TPU v7x, 32 devices: a whole 2x2x4 slice. The times are simulated.
32 devices in a mesh: fsdp: 8 (over z, core), seq: 4 (over y, x).
Axes of the slice: x: 2, y: 2, z: 4, core: 2. Of those that a mesh axis runs over, the one named last changes fastest.
Arguments:
- tokens: bfloat16 [4096, 1536], P(('fsdp', 'seq')), may hold values from -6 to 6
- cotangent: bfloat16 [4096, 1536], P(('fsdp', 'seq')), may hold values from -6 to 6
- condition: bfloat16 [8, 1024], P('fsdp'), may hold values from -6 to 6
- caption: bfloat16 [2048, 4096], P('fsdp'), may hold values from -6 to 6
- positions: int32 [3, 4096], P(None, 'fsdp'), may hold values from 0 to 63
- clip_lengths: int32 [8], P('fsdp'), may hold values from 448 to 512, as said below
- caption_lengths: int32 [8], P('fsdp'), may hold values from 32 to 256, as said below
- modulator: bfloat16 [1024, 6144], P('fsdp', 'seq'), may hold values from -0.1875 to 0.1875
- query_weight: bfloat16 [1536, 1536], P('fsdp', 'seq'), may hold values from -0.15625 to 0.15625
- key_weight: bfloat16 [1536, 1536], P('fsdp', 'seq'), may hold values from -0.15625 to 0.15625
- value_weight: bfloat16 [1536, 1536], P('fsdp', 'seq'), may hold values from -0.15625 to 0.15625
- output_weight: bfloat16 [1536, 1536], P('seq', 'fsdp'), may hold values from -1.25 to 1.25
- textkey_weight: bfloat16 [4096, 1536], P('fsdp', 'seq'), may hold values from -0.09375 to 0.09375
- textvalue_weight: bfloat16 [4096, 1536], P('fsdp', 'seq'), may hold values from -0.09375 to 0.09375
- gate_weight: bfloat16 [1536, 4096], P('fsdp', 'seq'), may hold values from -0.15625 to 0.15625
- up_weight: bfloat16 [1536, 4096], P('fsdp', 'seq'), may hold values from -0.15625 to 0.15625
- down_weight: bfloat16 [4096, 1536], P('seq', 'fsdp'), may hold values from -0.09375 to 0.09375
- attn_gain: float32 [1536], replicated, may hold values from 0.5 to 1.5
- ffn_gain: float32 [1536], replicated, may hold values from 0.5 to 1.5
- query_gain: float32 [64], replicated, may hold values from 0.5 to 1.5
- key_gain: float32 [64], replicated, may hold values from 0.5 to 1.5
- cross_gate: float32 [24], replicated, may hold values from -1.5 to 1.5
Outputs:
- block_out: bfloat16 [4096, 1536], P(('fsdp', 'seq'))
- token_grad: float32 [4096, 1536], P(('fsdp', 'seq'))
- modulator_grad: float32 [1024, 6144], P('fsdp', 'seq')
- query_grad: float32 [1536, 1536], P('fsdp', 'seq')
- key_grad: float32 [1536, 1536], P('fsdp', 'seq')
- value_grad: float32 [1536, 1536], P('fsdp', 'seq')
- output_grad: float32 [1536, 1536], P('seq', 'fsdp')
- textkey_grad: float32 [4096, 1536], P('fsdp', 'seq')
- textvalue_grad: float32 [4096, 1536], P('fsdp', 'seq')
- gate_grad: float32 [1536, 4096], P('fsdp', 'seq')
- up_grad: float32 [1536, 4096], P('fsdp', 'seq')
- down_grad: float32 [4096, 1536], P('seq', 'fsdp')
- attn_gain_grad: float32 [1536], replicated
- ffn_gain_grad: float32 [1536], replicated
- query_gain_grad: float32 [64], replicated
- key_gain_grad: float32 [64], replicated
- cross_gate_grad: float32 [24], replicated
- residual_rms: float32 [3, 8], P(None, 'fsdp')
Inputs may be any that keep to these rules, and one draw needn't show every extreme that they name: `clip_lengths`: each clip's valid tokens are its first slots; some clip is full and some clip has exactly the least length. `caption_lengths`: each caption's valid tokens are its first slots; some caption is full and some has exactly the least length.
All inputs are finite; a program needn't handle non-finite values.
Results may differ from a plain program's by a relative error of at most 0.019.
Values may be sent and summed in bfloat16 or wider, within the bound.
No kernel may reach another device: no remote copies, remote signals or barrier semaphores. Data moves between devices by JAX's collectives and lax.ppermute only.
A program may use at most 128 MiB of HBM per device.

v0:
```python
import math

import jax
import jax.numpy as jnp
from jax import lax
from jax.sharding import PartitionSpec as P

epsilon = 1e-06
masked_score = -1e30


def rope_tables(positions, head_size):
    half = head_size // 2
    pair_index = jnp.arange(half)
    frequency = jnp.exp(pair_index.astype(jnp.float32) * (-2.0 * math.log(10000.0) / head_size))
    angle = jnp.zeros((positions.shape[1], half), jnp.float32)
    for axis_number in range(3):
        chosen = jnp.where(pair_index % 3 == axis_number, frequency, jnp.zeros_like(frequency))
        angle = angle + positions[axis_number].astype(jnp.float32)[:, None] * chosen[None, :]
    return (jnp.cos(angle), jnp.sin(angle))


def rotate(values, cosine, sine):
    half = values.shape[-1] // 2
    first = values[..., :half]
    second = values[..., half:]
    return jnp.concatenate(
        [first * cosine - second * sine, first * sine + second * cosine], axis=-1
    )


def unrotate(grads, cosine, sine):
    half = grads.shape[-1] // 2
    first = grads[..., :half]
    second = grads[..., half:]
    return jnp.concatenate(
        [first * cosine + second * sine, second * cosine - first * sine], axis=-1
    )


def head_norm(values, gain):
    inverse = lax.rsqrt(jnp.mean(values * values, axis=-1, keepdims=True) + epsilon)
    unit = values * inverse
    return (unit * gain, unit, inverse)


def head_norm_back(grads, unit, inverse, gain):
    gain_grad = jnp.sum(grads * unit, axis=(0, 1))
    scaled = grads * gain
    return (inverse * (scaled - unit * jnp.mean(scaled * unit, axis=-1, keepdims=True)), gain_grad)


def softmax_rows(scores):
    peak = jnp.max(scores, axis=-1, keepdims=True)
    expo = jnp.exp(scores - peak)
    return expo / jnp.sum(expo, axis=-1, keepdims=True)


def local(
    tokens,
    cotangent,
    condition,
    caption,
    positions,
    clip_lengths,
    caption_lengths,
    modulator,
    query_weight,
    key_weight,
    value_weight,
    output_weight,
    textkey_weight,
    textvalue_weight,
    gate_weight,
    up_weight,
    down_weight,
    attn_gain,
    ffn_gain,
    query_gain,
    key_gain,
    cross_gate,
):
    fetched = (
        lax.all_gather(modulator, "fsdp", axis=0, tiled=True),
        lax.all_gather(query_weight, "fsdp", axis=0, tiled=True),
        lax.all_gather(key_weight, "fsdp", axis=0, tiled=True),
        lax.all_gather(value_weight, "fsdp", axis=0, tiled=True),
        lax.all_gather(textkey_weight, "fsdp", axis=0, tiled=True),
        lax.all_gather(textvalue_weight, "fsdp", axis=0, tiled=True),
        lax.all_gather(gate_weight, "fsdp", axis=0, tiled=True),
        lax.all_gather(up_weight, "fsdp", axis=0, tiled=True),
        lax.all_gather(output_weight, "fsdp", axis=1, tiled=True),
        lax.all_gather(down_weight, "fsdp", axis=1, tiled=True),
    )
    (
        full_mod,
        full_query,
        full_key,
        full_value,
        full_textkey,
        full_textvalue,
        full_gate,
        full_up,
        full_output,
        full_down,
    ) = fetched
    rows_local = tokens.shape[0]
    width = tokens.shape[1]
    head_size = query_gain.shape[0]
    local_heads = full_query.shape[1] // head_size
    clip_rows = positions.shape[1]
    text_rows = caption.shape[0]
    seq_index = lax.axis_index("seq")
    length = clip_lengths[0]
    text_length = caption_lengths[0]
    scale = head_size ** (-0.5)
    block = min(512, clip_rows)
    blocks = clip_rows // block
    cond_low = jax.nn.silu(condition.astype(jnp.float32)).astype(jnp.bfloat16)
    mod_part = jnp.dot(cond_low, full_mod, preferred_element_type=jnp.float32)
    modulation = lax.all_gather(mod_part, "seq", axis=1, tiled=True)[0]
    scale_attn = modulation[:width]
    gate_attn = modulation[width : 2 * width]
    scale_ffn = modulation[2 * width : 3 * width]
    gate_ffn = modulation[3 * width :]
    inputs = tokens.astype(jnp.float32)
    inv_attn = lax.rsqrt(jnp.mean(inputs * inputs, axis=-1, keepdims=True) + epsilon)
    unit_attn = inputs * inv_attn
    normed = (unit_attn * attn_gain * (1.0 + scale_attn)).astype(jnp.bfloat16)
    normed_all = lax.all_gather(normed, "seq", axis=0, tiled=True)
    query_raw = jnp.dot(normed_all, full_query, preferred_element_type=jnp.float32).reshape(
        clip_rows, local_heads, head_size
    )
    key_raw = jnp.dot(normed_all, full_key, preferred_element_type=jnp.float32).reshape(
        clip_rows, local_heads, head_size
    )
    value_heads = jnp.dot(normed_all, full_value, preferred_element_type=jnp.float32).astype(
        jnp.bfloat16
    )
    value_heads = value_heads.reshape(clip_rows, local_heads, head_size).transpose(1, 0, 2)
    cosine, sine = rope_tables(positions, head_size)
    cosine = cosine[:, None, :]
    sine = sine[:, None, :]
    query_normed, query_unit, query_inverse = head_norm(query_raw, query_gain)
    key_normed, key_unit, key_inverse = head_norm(key_raw, key_gain)
    query_heads = rotate(query_normed, cosine, sine).astype(jnp.bfloat16).transpose(1, 0, 2)
    key_heads = rotate(key_normed, cosine, sine).astype(jnp.bfloat16).transpose(1, 0, 2)
    key_valid = (jnp.arange(clip_rows) < length)[None, None, :]

    def self_block(index):
        query_block = lax.dynamic_slice_in_dim(query_heads, index * block, block, 1)
        scores = (
            jnp.einsum("hqd,hkd->hqk", query_block, key_heads, preferred_element_type=jnp.float32)
            * scale
        )
        scores = jnp.where(key_valid, scores, masked_score)
        peak = jnp.max(scores, axis=-1, keepdims=True)
        expo = jnp.exp(scores - peak)
        total = jnp.sum(expo, axis=-1, keepdims=True)
        output = jnp.einsum(
            "hqk,hkd->hqd",
            (expo / total).astype(jnp.bfloat16),
            value_heads,
            preferred_element_type=jnp.float32,
        )
        return (output, peak + jnp.log(total))

    self_blocks, self_lse = lax.map(self_block, jnp.arange(blocks))
    self_out = self_blocks.transpose(1, 0, 2, 3).reshape(local_heads, clip_rows, head_size)
    textkey_heads = jnp.dot(caption, full_textkey, preferred_element_type=jnp.float32).astype(
        jnp.bfloat16
    )
    textkey_heads = textkey_heads.reshape(text_rows, local_heads, head_size).transpose(1, 0, 2)
    textvalue_heads = jnp.dot(caption, full_textvalue, preferred_element_type=jnp.float32).astype(
        jnp.bfloat16
    )
    textvalue_heads = textvalue_heads.reshape(text_rows, local_heads, head_size).transpose(1, 0, 2)
    text_valid = (jnp.arange(text_rows) < text_length)[None, None, :]
    cross_scores = (
        jnp.einsum("hqd,hkd->hqk", query_heads, textkey_heads, preferred_element_type=jnp.float32)
        * scale
    )
    cross_probs = softmax_rows(jnp.where(text_valid, cross_scores, masked_score))
    cross_low = cross_probs.astype(jnp.bfloat16)
    cross_out = jnp.einsum(
        "hqk,hkd->hqd", cross_low, textvalue_heads, preferred_element_type=jnp.float32
    )
    gate_heads = jnp.tanh(
        lax.dynamic_slice_in_dim(cross_gate, seq_index * local_heads, local_heads)
    )
    mixed_heads = self_out + gate_heads[:, None, None] * cross_out
    mixed_rows = (
        mixed_heads.transpose(1, 0, 2)
        .reshape(clip_rows, local_heads * head_size)
        .astype(jnp.bfloat16)
    )
    attn_out = lax.psum_scatter(
        jnp.dot(mixed_rows, full_output, preferred_element_type=jnp.float32),
        "seq",
        scatter_dimension=0,
        tiled=True,
    )
    tanh_attn = jnp.tanh(gate_attn)
    branch_attn = tanh_attn * attn_out
    hidden_in = inputs + branch_attn
    inv_ffn = lax.rsqrt(jnp.mean(hidden_in * hidden_in, axis=-1, keepdims=True) + epsilon)
    unit_ffn = hidden_in * inv_ffn
    ffn_in = (unit_ffn * ffn_gain * (1.0 + scale_ffn)).astype(jnp.bfloat16)
    ffn_all = lax.all_gather(ffn_in, "seq", axis=0, tiled=True)
    gate_act = jnp.dot(ffn_all, full_gate, preferred_element_type=jnp.float32)
    up_act = jnp.dot(ffn_all, full_up, preferred_element_type=jnp.float32)
    sigmoid_gate = jax.nn.sigmoid(gate_act)
    silu_gate = gate_act * sigmoid_gate
    hidden = (silu_gate * up_act).astype(jnp.bfloat16)
    ffn_out = lax.psum_scatter(
        jnp.dot(hidden, full_down, preferred_element_type=jnp.float32).astype(jnp.bfloat16),
        "seq",
        scatter_dimension=0,
        tiled=True,
    ).astype(jnp.float32)
    tanh_ffn = jnp.tanh(gate_ffn)
    branch_ffn = tanh_ffn * ffn_out
    result = hidden_in + branch_ffn
    row_valid = (seq_index * rows_local + jnp.arange(rows_local) < length)[:, None]
    sums = jnp.stack(
        [
            jnp.sum(jnp.where(row_valid, result * result, 0.0)),
            jnp.sum(jnp.where(row_valid, branch_attn * branch_attn, 0.0)),
            jnp.sum(jnp.where(row_valid, branch_ffn * branch_ffn, 0.0)),
        ]
    )
    refetched = (
        lax.all_gather(query_weight, "fsdp", axis=0, tiled=True),
        lax.all_gather(key_weight, "fsdp", axis=0, tiled=True),
        lax.all_gather(value_weight, "fsdp", axis=0, tiled=True),
        lax.all_gather(gate_weight, "fsdp", axis=0, tiled=True),
        lax.all_gather(up_weight, "fsdp", axis=0, tiled=True),
        lax.all_gather(output_weight, "fsdp", axis=1, tiled=True),
        lax.all_gather(down_weight, "fsdp", axis=1, tiled=True),
    )
    back_query, back_key, back_value, back_gate, back_up, back_output, back_down = refetched
    grad_out = cotangent.astype(jnp.float32)
    ffn_back = (tanh_ffn * grad_out).astype(jnp.bfloat16)
    grad_gate_ffn = jnp.sum(grad_out * ffn_out, axis=0) * (1.0 - tanh_ffn * tanh_ffn)
    ffn_back_all = lax.all_gather(ffn_back, "seq", axis=0, tiled=True)
    down_part = jnp.einsum("nf,nd->fd", hidden, ffn_back_all, preferred_element_type=jnp.float32)
    grad_hidden = jnp.einsum(
        "nd,fd->nf", ffn_back_all, back_down, preferred_element_type=jnp.float32
    )
    grad_gate_act = (
        grad_hidden * up_act * sigmoid_gate * (1.0 + gate_act * (1.0 - sigmoid_gate))
    ).astype(jnp.bfloat16)
    grad_up_act = (grad_hidden * silu_gate).astype(jnp.bfloat16)
    gate_part = jnp.einsum("nd,nf->df", ffn_all, grad_gate_act, preferred_element_type=jnp.float32)
    up_part = jnp.einsum("nd,nf->df", ffn_all, grad_up_act, preferred_element_type=jnp.float32)
    grad_ffn_in = lax.psum_scatter(
        jnp.einsum("nf,df->nd", grad_gate_act, back_gate, preferred_element_type=jnp.float32)
        + jnp.einsum("nf,df->nd", grad_up_act, back_up, preferred_element_type=jnp.float32),
        "seq",
        scatter_dimension=0,
        tiled=True,
    )
    grad_ffn_gain = jnp.sum(grad_ffn_in * unit_ffn * (1.0 + scale_ffn), axis=0)
    grad_scale_ffn = jnp.sum(grad_ffn_in * unit_ffn * ffn_gain, axis=0)
    scaled_ffn = grad_ffn_in * ffn_gain * (1.0 + scale_ffn)
    grad_hidden_in = grad_out + inv_ffn * (
        scaled_ffn - unit_ffn * jnp.mean(scaled_ffn * unit_ffn, axis=-1, keepdims=True)
    )
    attn_back = (tanh_attn * grad_hidden_in).astype(jnp.bfloat16)
    grad_gate_attn = jnp.sum(grad_hidden_in * attn_out, axis=0) * (1.0 - tanh_attn * tanh_attn)
    attn_back_all = lax.all_gather(attn_back, "seq", axis=0, tiled=True)
    output_part = jnp.einsum(
        "nc,nd->cd", mixed_rows, attn_back_all, preferred_element_type=jnp.float32
    )
    grad_mixed = jnp.einsum(
        "nd,cd->nc", attn_back_all, back_output, preferred_element_type=jnp.float32
    )
    grad_mixed = (
        grad_mixed.astype(jnp.bfloat16)
        .reshape(clip_rows, local_heads, head_size)
        .transpose(1, 0, 2)
    )
    grad_mixed_wide = grad_mixed.astype(jnp.float32)
    grad_gate_heads = jnp.sum(grad_mixed_wide * cross_out, axis=(1, 2)) * (
        1.0 - gate_heads * gate_heads
    )
    cross_back = (gate_heads[:, None, None] * grad_mixed_wide).astype(jnp.bfloat16)
    grad_cross_probs = jnp.einsum(
        "hqd,hkd->hqk", cross_back, textvalue_heads, preferred_element_type=jnp.float32
    )
    cross_delta = jnp.sum(cross_probs * grad_cross_probs, axis=-1, keepdims=True)
    grad_cross_scores = (cross_probs * (grad_cross_probs - cross_delta)).astype(jnp.bfloat16)
    grad_query_cross = (
        jnp.einsum(
            "hqk,hkd->hqd", grad_cross_scores, textkey_heads, preferred_element_type=jnp.float32
        )
        * scale
    )
    grad_textkey = (
        jnp.einsum(
            "hqk,hqd->hkd", grad_cross_scores, query_heads, preferred_element_type=jnp.float32
        )
        * scale
    )
    grad_textvalue = jnp.einsum(
        "hqk,hqd->hkd", cross_low, cross_back, preferred_element_type=jnp.float32
    )

    def self_back(carry, index):
        grad_keys, grad_values = carry
        start = index * block
        query_block = lax.dynamic_slice_in_dim(query_heads, start, block, 1)
        back_block = lax.dynamic_slice_in_dim(grad_mixed, start, block, 1)
        lse_block = lax.dynamic_index_in_dim(self_lse, index, 0, keepdims=False)
        scores = (
            jnp.einsum("hqd,hkd->hqk", query_block, key_heads, preferred_element_type=jnp.float32)
            * scale
        )
        scores = jnp.where(key_valid, scores, masked_score)
        probs = jnp.exp(scores - lse_block)
        grad_probs = jnp.einsum(
            "hqd,hkd->hqk", back_block, value_heads, preferred_element_type=jnp.float32
        )
        delta = jnp.sum(probs * grad_probs, axis=-1, keepdims=True)
        grad_scores = (probs * (grad_probs - delta)).astype(jnp.bfloat16)
        grad_query_block = (
            jnp.einsum("hqk,hkd->hqd", grad_scores, key_heads, preferred_element_type=jnp.float32)
            * scale
        )
        grad_keys = (
            grad_keys
            + jnp.einsum(
                "hqk,hqd->hkd", grad_scores, query_block, preferred_element_type=jnp.float32
            )
            * scale
        )
        grad_values = grad_values + jnp.einsum(
            "hqk,hqd->hkd",
            probs.astype(jnp.bfloat16),
            back_block,
            preferred_element_type=jnp.float32,
        )
        return ((grad_keys, grad_values), grad_query_block)

    empty_heads = jnp.zeros((local_heads, clip_rows, head_size), jnp.float32)
    (grad_key_heads, grad_value_heads), grad_query_blocks = lax.scan(
        self_back, (empty_heads, empty_heads), jnp.arange(blocks)
    )
    grad_query_heads = grad_query_cross + grad_query_blocks.transpose(1, 0, 2, 3).reshape(
        local_heads, clip_rows, head_size
    )
    grad_query_normed = unrotate(grad_query_heads.transpose(1, 0, 2), cosine, sine)
    grad_key_normed = unrotate(grad_key_heads.transpose(1, 0, 2), cosine, sine)
    grad_query_raw, grad_query_gain = head_norm_back(
        grad_query_normed, query_unit, query_inverse, query_gain
    )
    grad_key_raw, grad_key_gain = head_norm_back(grad_key_normed, key_unit, key_inverse, key_gain)
    query_rows = grad_query_raw.reshape(clip_rows, local_heads * head_size).astype(jnp.bfloat16)
    key_rows = grad_key_raw.reshape(clip_rows, local_heads * head_size).astype(jnp.bfloat16)
    value_rows = (
        grad_value_heads.transpose(1, 0, 2)
        .reshape(clip_rows, local_heads * head_size)
        .astype(jnp.bfloat16)
    )
    textkey_rows = (
        grad_textkey.transpose(1, 0, 2)
        .reshape(text_rows, local_heads * head_size)
        .astype(jnp.bfloat16)
    )
    textvalue_rows = (
        grad_textvalue.transpose(1, 0, 2)
        .reshape(text_rows, local_heads * head_size)
        .astype(jnp.bfloat16)
    )
    query_part = jnp.einsum("nd,nc->dc", normed_all, query_rows, preferred_element_type=jnp.float32)
    key_part = jnp.einsum("nd,nc->dc", normed_all, key_rows, preferred_element_type=jnp.float32)
    value_part = jnp.einsum("nd,nc->dc", normed_all, value_rows, preferred_element_type=jnp.float32)
    textkey_part = jnp.einsum(
        "td,tc->dc", caption, textkey_rows, preferred_element_type=jnp.float32
    )
    textvalue_part = jnp.einsum(
        "td,tc->dc", caption, textvalue_rows, preferred_element_type=jnp.float32
    )
    total = jnp.einsum("nc,dc->nd", query_rows, back_query, preferred_element_type=jnp.float32)
    total = total + jnp.einsum("nc,dc->nd", key_rows, back_key, preferred_element_type=jnp.float32)
    grad_normed = lax.psum_scatter(
        (
            total
            + jnp.einsum("nc,dc->nd", value_rows, back_value, preferred_element_type=jnp.float32)
        ).astype(jnp.bfloat16),
        "seq",
        scatter_dimension=0,
        tiled=True,
    ).astype(jnp.float32)
    grad_attn_gain = jnp.sum(grad_normed * unit_attn * (1.0 + scale_attn), axis=0)
    grad_scale_attn = jnp.sum(grad_normed * unit_attn * attn_gain, axis=0)
    scaled_attn = grad_normed * attn_gain * (1.0 + scale_attn)
    token_grad = grad_hidden_in + inv_attn * (
        scaled_attn - unit_attn * jnp.mean(scaled_attn * unit_attn, axis=-1, keepdims=True)
    )
    grad_mod_part = jnp.concatenate(
        [grad_scale_attn, grad_gate_attn, grad_scale_ffn, grad_gate_ffn]
    )[None, :]
    grad_mod_all, totals = lax.psum((grad_mod_part, sums), "seq")
    mod_columns = full_mod.shape[1]
    grad_mod_low = lax.dynamic_slice_in_dim(
        grad_mod_all, seq_index * mod_columns, mod_columns, 1
    ).astype(jnp.bfloat16)
    modulator_part = jnp.einsum(
        "ia,ic->ac", cond_low, grad_mod_low, preferred_element_type=jnp.float32
    )
    residual_rms = jnp.sqrt(totals / (length.astype(jnp.float32) * width))[:, None]
    summed = (
        lax.psum_scatter(
            modulator_part.astype(jnp.bfloat16), "fsdp", scatter_dimension=0, tiled=True
        ).astype(jnp.float32),
        lax.psum_scatter(
            query_part.astype(jnp.bfloat16), "fsdp", scatter_dimension=0, tiled=True
        ).astype(jnp.float32),
        lax.psum_scatter(
            key_part.astype(jnp.bfloat16), "fsdp", scatter_dimension=0, tiled=True
        ).astype(jnp.float32),
        lax.psum_scatter(
            value_part.astype(jnp.bfloat16), "fsdp", scatter_dimension=0, tiled=True
        ).astype(jnp.float32),
        lax.psum_scatter(
            textkey_part.astype(jnp.bfloat16), "fsdp", scatter_dimension=0, tiled=True
        ).astype(jnp.float32),
        lax.psum_scatter(
            textvalue_part.astype(jnp.bfloat16), "fsdp", scatter_dimension=0, tiled=True
        ).astype(jnp.float32),
        lax.psum_scatter(
            gate_part.astype(jnp.bfloat16), "fsdp", scatter_dimension=0, tiled=True
        ).astype(jnp.float32),
        lax.psum_scatter(
            up_part.astype(jnp.bfloat16), "fsdp", scatter_dimension=0, tiled=True
        ).astype(jnp.float32),
        lax.psum_scatter(
            output_part.astype(jnp.bfloat16), "fsdp", scatter_dimension=1, tiled=True
        ).astype(jnp.float32),
        lax.psum_scatter(
            down_part.astype(jnp.bfloat16), "fsdp", scatter_dimension=1, tiled=True
        ).astype(jnp.float32),
    )
    gate_heads_full = lax.dynamic_update_slice_in_dim(
        jnp.zeros_like(cross_gate), grad_gate_heads, seq_index * local_heads, 0
    )
    small = lax.psum(
        (grad_attn_gain, grad_ffn_gain, grad_query_gain, grad_key_gain, gate_heads_full),
        ("fsdp", "seq"),
    )
    return (
        result.astype(jnp.bfloat16),
        token_grad,
        summed[0],
        summed[1],
        summed[2],
        summed[3],
        summed[8],
        summed[4],
        summed[5],
        summed[6],
        summed[7],
        summed[9],
        small[0],
        small[1],
        small[2],
        small[3],
        small[4],
        residual_rms,
    )


def solution(mesh):
    return jax.shard_map(
        local,
        mesh=mesh,
        in_specs=(
            P(("fsdp", "seq"), None),
            P(("fsdp", "seq"), None),
            P("fsdp", None),
            P("fsdp", None),
            P(None, "fsdp"),
            P("fsdp"),
            P("fsdp"),
            P("fsdp", "seq"),
            P("fsdp", "seq"),
            P("fsdp", "seq"),
            P("fsdp", "seq"),
            P("seq", "fsdp"),
            P("fsdp", "seq"),
            P("fsdp", "seq"),
            P("fsdp", "seq"),
            P("fsdp", "seq"),
            P("seq", "fsdp"),
            P(),
            P(),
            P(),
            P(),
            P(),
        ),
        out_specs=(
            P(("fsdp", "seq"), None),
            P(("fsdp", "seq"), None),
            P("fsdp", "seq"),
            P("fsdp", "seq"),
            P("fsdp", "seq"),
            P("fsdp", "seq"),
            P("seq", "fsdp"),
            P("fsdp", "seq"),
            P("fsdp", "seq"),
            P("fsdp", "seq"),
            P("fsdp", "seq"),
            P("seq", "fsdp"),
            P(),
            P(),
            P(),
            P(),
            P(),
            P(None, "fsdp"),
        ),
        check_vma=False,
    )
```

profile of v0, /device:TPU:0, one launch (start us, length us, event | category | flops | bytes accessed | tf_op | source)
XLA Modules:
  0.0 1065.9 jit_solution(14631658623483907987)
XLA Ops:
  11.3 39.5 %all-gather.17.cloned.1.call-done = bf16[1024,1536]{1,0:T(8,128)(2,1)} async-done(((bf16[128,1536]{1,0:T(8,128)(2,1)}), bf16[1024,1536]{1,0:T(8,128)(2,1)}) %all-gather.17.cloned.1.call-update) | async-done | bytes 3145744 | tf_op jit(solution)/shard_map/all_gather | solution.py:84
  50.7 2.4 convolution_bitcast_fusion
  53.1 8.1 all-gather.1
  69.6 20.0 %all-gather.27.cloned.1.call-done = bf16[4096,384]{1,0:T(8,128)(2,1)} async-done(((bf16[512,384]{1,0:T(8,128)(2,1)}), bf16[4096,384]{1,0:T(8,128)(2,1)}) %all-gather.27.cloned.1.call-update) | async-done | bytes 3145744 | tf_op jit(solution)/shard_map/all_gather | solution.py:88
  89.5 3.1 convolution_convert_fusion.14
  93.5 34.9 %all-gather.29.cloned.1.call-done = bf16[4096,384]{1,0:T(8,128)(2,1)} async-done(((bf16[512,384]{1,0:T(8,128)(2,1)}), bf16[4096,384]{1,0:T(8,128)(2,1)}) %all-gather.29.cloned.1.call-update) | async-done | bytes 3145744 | tf_op jit(solution)/shard_map/all_gather | solution.py:89
  128.4 3.1 convolution_convert_fusion.13
  132.3 19.1 %all-gather.23.cloned.1.call-done = bf16[1536,384]{1,0:T(8,128)(2,1)} async-done(((bf16[192,384]{1,0:T(8,128)(2,1)}), bf16[1536,384]{1,0:T(8,128)(2,1)}) %all-gather.23.cloned.1.call-update) | async-done | bytes 1179664 | tf_op jit(solution)/shard_map/all_gather | solution.py:86
  151.4 33.0 %all-gather.19.cloned.1.call-done = bf16[512,1536]{1,0:T(8,128)(2,1)} async-done(((bf16[128,1536]{1,0:T(8,128)(2,1)}), bf16[512,1536]{1,0:T(8,128)(2,1)}) %all-gather.19.cloned.1.call-update) | async-done | bytes 1572880 | tf_op jit(solution)/shard_map/all_gather | solution.py:130
  184.5 2.6 fusion.76
  188.0 20.6 %all-gather.21.cloned.1.call-done = bf16[1536,384]{1,0:T(8,128)(2,1)} async-done(((bf16[192,384]{1,0:T(8,128)(2,1)}), bf16[1536,384]{1,0:T(8,128)(2,1)}) %all-gather.21.cloned.1.call-update) | async-done | bytes 1179664 | tf_op jit(solution)/shard_map/all_gather | solution.py:85
  208.6 2.6 fusion.75
  212.9 4.6 fusion.74
  217.5 5.8 fusion.73
  223.3 9.4 all-gather.25.cloned.1.call-done
  232.7 2.6 convolution_convert_fusion.11
  235.4 3.8 fusion.1
  244.0 12.9 %all-gather.31.cloned.1.call-done = bf16[384,1536]{0,1:T(8,128)(2,1)} async-done(((bf16[384,192]{0,1:T(8,128)(2,1)}), bf16[384,1536]{0,1:T(8,128)(2,1)}) %all-gather.31.cloned.1.call-update) | async-done | bytes 1179664 | tf_op jit(solution)/shard_map/all_gather | solution.py:92
  256.8 4.4 fusion.77
  261.9 43.3 %reduce-scatter.15.cloned.1.call-done = f32[128,1536]{1,0:T(8,128)} async-done(((f32[512,1536]{1,0:T(8,128)}), f32[128,1536]{1,0:T(8,128)}) %reduce-scatter.15.cloned.1.call-update) | async-done | bytes 786448 | tf_op jit(solution)/shard_map/reduce_scatter | solution.py:197
  312.3 32.7 %all-gather.37.cloned.1.call-done = bf16[1536,1024]{1,0:T(8,128)(2,1)} async-done(((bf16[192,1024]{1,0:T(8,128)(2,1)}), bf16[1536,1024]{1,0:T(8,128)(2,1)}) %all-gather.37.cloned.1.call-update) | async-done | bytes 3145744 | tf_op jit(solution)/shard_map/all_gather | solution.py:91
  345.0 32.3 %all-gather.33.cloned.1.call-done = bf16[512,1536]{1,0:T(8,128)(2,1)} async-done(((bf16[128,1536]{1,0:T(8,128)(2,1)}), bf16[512,1536]{1,0:T(8,128)(2,1)}) %all-gather.33.cloned.1.call-update) | async-done | bytes 1572880 | tf_op jit(solution)/shard_map/all_gather | solution.py:209
  377.3 5.5 fusion.79
  382.8 34.3 %all-gather.35.cloned.1.call-done = bf16[1536,1024]{1,0:T(8,128)(2,1)} async-done(((bf16[192,1024]{1,0:T(8,128)(2,1)}), bf16[1536,1024]{1,0:T(8,128)(2,1)}) %all-gather.35.cloned.1.call-update) | async-done | bytes 3145744 | tf_op jit(solution)/shard_map/all_gather | solution.py:90
  417.1 5.5 fusion.78
  422.5 33.4 %all-gather.39.cloned.1.call-done = bf16[1024,1536]{0,1:T(8,128)(2,1)} async-done(((bf16[1024,192]{0,1:T(8,128)(2,1)}), bf16[1024,1536]{0,1:T(8,128)(2,1)}) %all-gather.39.cloned.1.call-update) | async-done | bytes 3145744 | tf_op jit(solution)/shard_map/all_gather | solution.py:93
  455.9 32.1 %all-gather.41.cloned.1.call-done = bf16[512,1536]{1,0:T(8,128)(2,1)} async-done(((bf16[128,1536]{1,0:T(8,128)(2,1)}), bf16[512,1536]{1,0:T(8,128)(2,1)}) %all-gather.41.cloned.1.call-update) | async-done | bytes 1572880 | tf_op jit(solution)/shard_map/all_gather | solution.py:245
  488.0 7.6 multiply_convert_fusion.3
  496.6 3.0 convolution_convert_fusion.5
  499.7 4.2 fusion.80
  503.9 3.5 convolution_add_fusion.2
  508.0 22.7 %reduce-scatter.17.cloned.1.call-done = bf16[128,1536]{1,0:T(8,128)(2,1)} async-done(((bf16[512,1536]{1,0:T(8,128)(2,1)}), bf16[128,1536]{1,0:T(8,128)(2,1)}) %reduce-scatter.17.cloned.1.call-update) | async-done | bytes 393232 | tf_op jit(solution)/shard_map/reduce_scatter | solution.py:215
  530.7 46.8 %reduce-scatter.19.cloned.1.call-done = f32[128,1536]{1,0:T(8,128)} async-done(((f32[512,1536]{1,0:T(8,128)}), f32[128,1536]{1,0:T(8,128)}) %reduce-scatter.19.cloned.1.call-update) | async-done | bytes 786448 | tf_op jit(solution)/shard_map/reduce_scatter | solution.py:256
  577.5 2.6 multiply_reduce_fusion.2
  580.2 4.1 select_reduce_fusion
  592.7 24.5 %all-gather.43.cloned.1.call-done = bf16[512,1536]{1,0:T(8,128)(2,1)} async-done(((bf16[128,1536]{1,0:T(8,128)(2,1)}), bf16[512,1536]{1,0:T(8,128)(2,1)}) %all-gather.43.cloned.1.call-update) | async-done | bytes 1572880 | tf_op jit(solution)/shard_map/all_gather | solution.py:271
  617.1 2.7 convolution_convert_fusion.10
  619.9 2.9 multiply_reduce_fusion.1
  630.8 2.1 fusion.17
  638.2 2.2 fusion.9
  640.6 5.2 convolution_convert_fusion.2
  645.9 5.5 convolution_convert_fusion.3
  651.4 5.3 convolution_convert_fusion.4
  657.7 3.5 convolution_convert_fusion.6
  661.3 3.6 convolution_convert_fusion.7
  665.0 3.5 convolution_convert_fusion.9
  668.5 3.7 convolution_convert_fusion.8
  672.3 2.5 convolution_convert_fusion.12
  674.8 2.7 fusion.3
  678.4 2.1 fusion.27
  680.6 2.6 fusion.2
  687.4 19.0 %all-reduce.1 = (bf16[1,6144]{1,0:T(2,128)(2,1)S(1)}, f32[3]{0:T(128)S(1)}) all-reduce(f32[1,6144]{1,0:T(1,128)S(1)} %bitcast.211, f32[3]{0:T(128)S(1)} %pad_maximum_fusion.3), channel_id=1, replica_groups=mesh['fsdp'=8,'seq'=4] {'seq'}, use_global_device_ids=true, to_apply=%region_22.23 | all-reduce | flops 6147 | bytes 36888 | tf_op jit(solution)/shard_map/psum | solution.py:404
  706.4 2.1 multiply_convert_fusion
  708.5 5.6 reduce-scatter.41.cloned.1.call-done
  716.1 39.6 %reduce-scatter.39.cloned.1.call-done = bf16[192,1024]{1,0:T(8,128)(2,1)} async-done(((bf16[1536,1024]{1,0:T(8,128)(2,1)}), bf16[192,1024]{1,0:T(8,128)(2,1)}) %reduce-scatter.39.cloned.1.call-update) | async-done | bytes 393232 | tf_op jit(solution)/shard_map/reduce_scatter | solution.py:435
  757.7 39.8 %reduce-scatter.37.cloned.1.call-done = bf16[192,1024]{1,0:T(8,128)(2,1)} async-done(((bf16[1536,1024]{1,0:T(8,128)(2,1)}), bf16[192,1024]{1,0:T(8,128)(2,1)}) %reduce-scatter.37.cloned.1.call-update) | async-done | bytes 393232 | tf_op jit(solution)/shard_map/reduce_scatter | solution.py:432
  801.2 30.3 %reduce-scatter.31.cloned.1.call-done = bf16[384,192]{0,1:T(8,128)(2,1)} async-done(((bf16[384,1536]{0,1:T(8,128)(2,1)}), bf16[384,192]{0,1:T(8,128)(2,1)}) %reduce-scatter.31.cloned.1.call-update) | async-done | bytes 147472 | tf_op jit(solution)/shard_map/reduce_scatter | solution.py:438
  833.2 31.7 %reduce-scatter.29.cloned.1.call-done = bf16[192,384]{1,0:T(8,128)(2,1)} async-done(((bf16[1536,384]{1,0:T(8,128)(2,1)}), bf16[192,384]{1,0:T(8,128)(2,1)}) %reduce-scatter.29.cloned.1.call-update) | async-done | bytes 147472 | tf_op jit(solution)/shard_map/reduce_scatter | solution.py:423
  866.6 31.7 %reduce-scatter.25.cloned.1.call-done = bf16[192,384]{1,0:T(8,128)(2,1)} async-done(((bf16[1536,384]{1,0:T(8,128)(2,1)}), bf16[192,384]{1,0:T(8,128)(2,1)}) %reduce-scatter.25.cloned.1.call-update) | async-done | bytes 147472 | tf_op jit(solution)/shard_map/reduce_scatter | solution.py:417
  899.9 31.7 %reduce-scatter.27.cloned.1.call-done = bf16[192,384]{1,0:T(8,128)(2,1)} async-done(((bf16[1536,384]{1,0:T(8,128)(2,1)}), bf16[192,384]{1,0:T(8,128)(2,1)}) %reduce-scatter.27.cloned.1.call-update) | async-done | bytes 147472 | tf_op jit(solution)/shard_map/reduce_scatter | solution.py:420
  933.2 39.9 %all-reduce = (f32[1536]{0:T(1024)}, f32[1536]{0:T(1024)}, f32[64]{0:T(128)}, f32[64]{0:T(128)}, f32[24]{0:T(128)}) all-reduce(f32[1536]{0:T(1024)S(1)} %get-tuple-element.144, f32[1536]{0:T(1024)S(1)} %copy-done.45, f32[64]{0:T(128)S(1)} %reduce_sum.252, f32[64]{0:T(128)S(1)} %reduce_sum.255, ...), channel_id=1, replica_groups=mesh['fsdp'=8,'seq'=4] {'fsdp','seq'}, use_global_device_ids=true, to_apply=%region_34.35 | all-reduce | flops 3224 | bytes 25792 | tf_op jit(solution)/shard_map/psum | solution.py:448
  973.7 2.2 fusion.37
  977.9 36.9 %reduce-scatter.33.cloned.1.call-done = bf16[512,384]{0,1:T(8,128)(2,1)} async-done(((bf16[4096,384]{0,1:T(8,128)(2,1)}), bf16[512,384]{0,1:T(8,128)(2,1)}) %reduce-scatter.33.cloned.1.call-update) | async-done | bytes 393232 | tf_op jit(solution)/shard_map/reduce_scatter | solution.py:426
  1016.9 39.7 %reduce-scatter.23.cloned.1.call-done = bf16[128,1536]{1,0:T(8,128)(2,1)} async-done(((bf16[1024,1536]{1,0:T(8,128)(2,1)}), bf16[128,1536]{1,0:T(8,128)(2,1)}) %reduce-scatter.23.cloned.1.call-update) | async-done | bytes 393232 | tf_op jit(solution)/shard_map/reduce_scatter | solution.py:414
  (283 shorter events, 77.9 us)
Async XLA Ops:
  7.2 82.4 %copy-start = (bf16[256,4096]{1,0:T(8,128)(2,1)S(1)}, bf16[256,4096]{1,0:T(8,128)(2,1)}, u32[]{:S(2)}) copy-start(bf16[256,4096]{1,0:T(8,128)(2,1)} %param.25) | copy-start | bytes 6291460
  7.2 55.3 %copy-start.5 = (bf16[128,1536]{1,0:T(8,128)(2,1)S(1)}, bf16[128,1536]{1,0:T(8,128)(2,1)}, u32[]{:S(2)}) copy-start(bf16[128,1536]{1,0:T(8,128)(2,1)} %param.22) | copy-start | bytes 1179652
  7.2 55.3 %copy-start.38 = (f32[1536]{0:T(1024)S(1)}, f32[1536]{0:T(1024)}, u32[]{:S(2)}) copy-start(f32[1536]{0:T(1024)} %param.39) | copy-start | bytes 18436
  7.2 43.5 %all-gather.17.cloned.1.call-start = ((), (), s32[]{:S(2)}) async-start(), calls=%async_computation.14 | async-start | bytes 3538944 | tf_op jit(solution)/shard_map/all_gather | solution.py:84
  8.0 60.0 %copy-start.55 = (s32[3,512]{1,0:T(4,128)S(1)}, s32[3,512]{1,0:T(4,128)}, u32[]{:S(2)}) copy-start(s32[3,512]{1,0:T(4,128)} %param.26) | copy-start | bytes 18436
  8.0 60.0 %copy-start.62 = (f32[24]{0:T(128)S(1)}, f32[24]{0:T(128)}, u32[]{:S(2)}) copy-start(f32[24]{0:T(128)} %param.43) | copy-start | bytes 292
  8.0 81.6 %all-gather.27.cloned.1.call-start = ((), (), s32[]{:S(2)}) async-start(), calls=%async_computation.19 | async-start | bytes 3538944 | tf_op jit(solution)/shard_map/all_gather | solution.py:88
  8.7 119.6 %all-gather.29.cloned.1.call-start = ((), (), s32[]{:S(2)}) async-start(), calls=%async_computation.20 | async-start | bytes 3538944 | tf_op jit(solution)/shard_map/all_gather | solution.py:89
  9.5 142.0 %all-gather.23.cloned.1.call-start = ((), (), s32[]{:S(2)}) async-start(), calls=%async_computation.17 | async-start | bytes 1327104 | tf_op jit(solution)/shard_map/all_gather | solution.py:86
  10.0 174.4 %all-gather.19.cloned.1.call-start = ((), (), s32[]{:S(2)}) async-start(), calls=%async_computation.15 | async-start | bytes 1966080 | tf_op jit(solution)/shard_map/all_gather | solution.py:130
  11.3 56.2 %copy-start.56 = (f32[128]{0:T(128)}, f32[128]{0:T(128)S(1)}, u32[]{:S(2)}) copy-start(f32[128]{0:T(128)S(1)} %add_rsqrt_fusion.3) | copy-start | bytes 1540
  63.5 145.1 %all-gather.21.cloned.1.call-start = ((), (), s32[]{:S(2)}) async-start(), calls=%async_computation.16 | async-start | bytes 1327104 | tf_op jit(solution)/shard_map/all_gather | solution.py:85
  64.1 168.7 %all-gather.25.cloned.1.call-start = ((), (), s32[]{:S(2)}) async-start(), calls=%async_computation.18 | async-start | bytes 1327104 | tf_op jit(solution)/shard_map/all_gather | solution.py:87
  64.8 192.0 %all-gather.31.cloned.1.call-start = ((), (), s32[]{:S(2)}) async-start(), calls=%async_computation.21 | async-start | bytes 1327104 | tf_op jit(solution)/shard_map/all_gather | solution.py:92
  65.6 239.6 %reduce-scatter.15.cloned.1.call-start = ((), (), s32[]{:S(2)}) async-start(), calls=%async_computation.22 | async-start | bytes 3932160 | tf_op jit(solution)/shard_map/reduce_scatter | solution.py:197
  187.0 24.4 %copy-start.58 = (f32[64]{0:T(128)S(1)}, f32[64]{0:T(128)}, u32[]{:S(2)}) copy-start(f32[64]{0:T(128)} %param.42) | copy-start | bytes 772
  187.1 24.4 %copy-start.60 = (f32[64]{0:T(128)S(1)}, f32[64]{0:T(128)}, u32[]{:S(2)}) copy-start(f32[64]{0:T(128)} %param.41) | copy-start | bytes 772
  188.0 23.8 %copy-start.31 = (f32[512,6]{0,1:T(8,128)}, f32[512,6]{0,1:T(8,128)S(1)}, u32[]{:S(2)}) copy-start(f32[512,6]{0,1:T(8,128)S(1)} %add_rsqrt_fusion) | copy-start | bytes 36868
  208.6 2.8 copy-start.2
  208.6 3.2 copy-start.26
  235.3 4.4 copy-start.28
  235.3 3.9 copy-start.12
  235.4 3.9 copy-start.34
  235.4 3.9 copy-start.48
  235.4 5.2 slice-start
  239.3 2.7 slice-start.1
  239.3 2.7 copy-start.66
  261.3 83.7 %all-gather.37.cloned.1.call-start = ((), (), s32[]{:S(2)}) async-start(), calls=%async_computation.25 | async-start | bytes 3538944 | tf_op jit(solution)/shard_map/all_gather | solution.py:91
  261.9 115.4 %all-gather.33.cloned.1.call-start = ((), (), s32[]{:S(2)}) async-start(), calls=%async_computation.23 | async-start | bytes 1966080 | tf_op jit(solution)/shard_map/all_gather | solution.py:209
  309.0 108.0 %all-gather.35.cloned.1.call-start = ((), (), s32[]{:S(2)}) async-start(), calls=%async_computation.24 | async-start | bytes 3538944 | tf_op jit(solution)/shard_map/all_gather | solution.py:90
  309.6 146.3 %all-gather.39.cloned.1.call-start = ((), (), s32[]{:S(2)}) async-start(), calls=%async_computation.26 | async-start | bytes 3538944 | tf_op jit(solution)/shard_map/all_gather | solution.py:93
  310.4 177.7 %all-gather.41.cloned.1.call-start = ((), (), s32[]{:S(2)}) async-start(), calls=%async_computation.28 | async-start | bytes 1966080 | tf_op jit(solution)/shard_map/all_gather | solution.py:245
  312.3 218.4 %reduce-scatter.17.cloned.1.call-start = ((), (), s32[]{:S(2)}) async-start(), calls=%async_computation.27 | async-start | bytes 1966080 | tf_op jit(solution)/shard_map/reduce_scatter | solution.py:215
  488.0 8.6 copy-start.65
  499.6 77.9 %reduce-scatter.19.cloned.1.call-start = ((), (), s32[]{:S(2)}) async-start(), calls=%async_computation.29 | async-start | bytes 3932160 | tf_op jit(solution)/shard_map/reduce_scatter | solution.py:256
  499.6 4.2 copy-start.64
  499.7 4.2 copy-start.68
  507.4 109.7 %all-gather.43.cloned.1.call-start = ((), (), s32[]{:S(2)}) async-start(), calls=%async_computation.30 | async-start | bytes 1966080 | tf_op jit(solution)/shard_map/all_gather | solution.py:271
  577.5 7.7 copy-start.37
  586.0 99.9 %reduce-scatter.21.cloned.1.call-start = ((), (), s32[]{:S(2)}) async-start(), calls=%async_computation.31 | async-start | bytes 1966080 | tf_op jit(solution)/shard_map/reduce_scatter | solution.py:386
  617.1 5.6 slice-start.2
  619.8 4.8 copy-start.9
  619.9 2.9 slice-start.3
  619.9 2.9 copy-start.33
  640.4 73.7 %reduce-scatter.41.cloned.1.call-start = ((), (), s32[]{:S(2)}) async-start(), calls=%async_computation.41 | async-start | bytes 3538944 | tf_op jit(solution)/shard_map/reduce_scatter | solution.py:441
  645.9 109.8 %reduce-scatter.39.cloned.1.call-start = ((), (), s32[]{:S(2)}) async-start(), calls=%async_computation.40 | async-start | bytes 3538944 | tf_op jit(solution)/shard_map/reduce_scatter | solution.py:435
  651.4 146.1 %reduce-scatter.37.cloned.1.call-start = ((), (), s32[]{:S(2)}) async-start(), calls=%async_computation.39 | async-start | bytes 3538944 | tf_op jit(solution)/shard_map/reduce_scatter | solution.py:432
  656.8 174.8 %reduce-scatter.31.cloned.1.call-start = ((), (), s32[]{:S(2)}) async-start(), calls=%async_computation.36 | async-start | bytes 1327104 | tf_op jit(solution)/shard_map/reduce_scatter | solution.py:438
  661.2 3.7 copy-start.16
  661.3 203.6 %reduce-scatter.29.cloned.1.call-start = ((), (), s32[]{:S(2)}) async-start(), calls=%async_computation.35 | async-start | bytes 1327104 | tf_op jit(solution)/shard_map/reduce_scatter | solution.py:423
  664.9 233.3 %reduce-scatter.25.cloned.1.call-start = ((), (), s32[]{:S(2)}) async-start(), calls=%async_computation.33 | async-start | bytes 1327104 | tf_op jit(solution)/shard_map/reduce_scatter | solution.py:417
  668.4 3.8 copy-start.10
  668.4 3.8 copy-start.50
  668.5 3.8 copy-start.67
  668.5 263.1 %reduce-scatter.27.cloned.1.call-start = ((), (), s32[]{:S(2)}) async-start(), calls=%async_computation.34 | async-start | bytes 1327104 | tf_op jit(solution)/shard_map/reduce_scatter | solution.py:420
  672.2 303.6 %reduce-scatter.35.cloned.1.call-start = ((), (), s32[]{:S(2)}) async-start(), calls=%async_computation.38 | async-start | bytes 3538944 | tf_op jit(solution)/shard_map/reduce_scatter | solution.py:429
  677.5 337.3 %reduce-scatter.33.cloned.1.call-start = ((), (), s32[]{:S(2)}) async-start(), calls=%async_computation.37 | async-start | bytes 3538944 | tf_op jit(solution)/shard_map/reduce_scatter | solution.py:426
  683.2 2.7 copy-start.36
  683.3 2.7 copy-start.39
  683.3 4.1 copy-start.42
  683.3 373.3 %reduce-scatter.23.cloned.1.call-start = ((), (), s32[]{:S(2)}) async-start(), calls=%async_computation.32 | async-start | bytes 3538944 | tf_op jit(solution)/shard_map/reduce_scatter | solution.py:414
  708.5 92.6 %copy-start.63 = (f32[24]{0:T(128)S(1)}, f32[24]{0:T(128)}, u32[]{:S(2)}) copy-start(f32[24]{0:T(128)} %param.43) | copy-start | bytes 292
  708.5 224.7 %copy-start.45 = (f32[1536]{0:T(1024)S(1)}, f32[1536]{0:T(1024)}, u32[]{:S(2)}) copy-start(f32[1536]{0:T(1024)} %get-tuple-element.141) | copy-start | bytes 18436
  708.5 265.2 %copy-start.7 = (f32[128,1536]{1,0:T(8,128)S(1)}, f32[128,1536]{1,0:T(8,128)}, u32[]{:S(2)}) copy-start(f32[128,1536]{1,0:T(8,128)} %copy-done.6) | copy-start | bytes 2359300
  (38 other events, 47.0 us)
Sparse Core Ops, SparseCore 0:
  9.7 40.9 all-gather.16
  52.4 37.1 all-gather.26
  91.2 37.1 all-gather.28
  129.9 21.5 all-gather.22
  153.7 30.7 all-gather.18
  186.0 22.6 all-gather.20
  210.3 22.4 all-gather.24
  234.4 22.4 all-gather.30
  261.4 43.7 reduce-scatter.14
  306.7 38.2 all-gather.36
  347.4 29.8 all-gather.32
  378.7 38.2 all-gather.34
  418.7 37.1 all-gather.38
  458.2 29.8 all-gather.40
  499.7 30.9 reduce-scatter.16
  533.5 43.9 reduce-scatter.18
  586.1 30.9 all-gather.42
  640.5 30.8 reduce-scatter.20
  673.7 40.3 reduce-scatter.40
  716.3 39.4 reduce-scatter.38
  758.0 39.4 reduce-scatter.36
  799.8 31.7 reduce-scatter.30
  833.8 31.0 reduce-scatter.28
  867.0 31.1 reduce-scatter.24
  900.5 30.9 reduce-scatter.26
  933.7 39.6 reduce-scatter.34
  975.5 39.2 reduce-scatter.32
  1017.1 39.4 reduce-scatter.22
where the time goes:
time: 1080 us; the launch traced here: 1070 us
  waiting for transfers between devices  785 us (73%)
  matrix products  120 us (11%)
  blocking collectives  67 us (6%)
  other arithmetic  53 us (5%)
  local copies, waits for them, and re-layouts  21.8 us (2%)
  between operations  17.2 us (2%)
    reduce_scatter x1, waiting for transfers between devices, local(): lax.psum_scatter(jnp.einsum('nf,df->nd', grad_gate_act, back_gate, prefer...  46.8 us
    reduce_scatter x1, waiting for transfers between devices, local(): lax.psum_scatter(jnp.dot(mixed_rows, full_output, preferred_element_type=...  43.3 us
    psum x1, blocking collectives, local(): lax.psum((grad_attn_gain, grad_ffn_gain, grad_query_gain, grad_key_gain,...  39.9 us
    reduce_scatter x1, waiting for transfers between devices, local(): lax.psum_scatter(gate_part.astype(jnp.bfloat16), 'fsdp', scatter_dimensio...  39.8 us
    reduce_scatter x1, waiting for transfers between devices, local(): lax.psum_scatter(modulator_part.astype(jnp.bfloat16), 'fsdp', scatter_dim...  39.7 us
    reduce_scatter x1, waiting for transfers between devices, local(): lax.psum_scatter(up_part.astype(jnp.bfloat16), 'fsdp', scatter_dimension=...  39.6 us
    all_gather x1, waiting for transfers between devices, local(): lax.all_gather(modulator, 'fsdp', axis=0, tiled=True)  39.5 us
    reduce_scatter x1, waiting for transfers between devices, local(): lax.psum_scatter(textkey_part.astype(jnp.bfloat16), 'fsdp', scatter_dimen...  36.9 us
  transfers between devices with their start and end apart: 28, of which 26 were waited for; matrix products, arithmetic and copies ran while one was open for 13% of the time, Pallas kernels for 0%

commit v1 on v0

v1 whole, which is shorter than its diff:
```python
import math

import jax
import jax.numpy as jnp
from jax import lax
from jax.sharding import PartitionSpec as P

epsilon = 1e-06
masked_score = -1e30
f32 = jnp.float32
bf16 = jnp.bfloat16


def rope_tables(positions, head_size):
    half = head_size // 2
    pair_index = jnp.arange(half)
    frequency = jnp.exp(pair_index.astype(f32) * (-2.0 * math.log(10000.0) / head_size))
    angle = jnp.zeros((positions.shape[1], half), f32)
    for axis_number in range(3):
        chosen = jnp.where(pair_index % 3 == axis_number, frequency, jnp.zeros_like(frequency))
        angle = angle + positions[axis_number].astype(f32)[:, None] * chosen[None, :]
    return (jnp.cos(angle), jnp.sin(angle))


def rotate(values, cosine, sine):
    half = values.shape[-1] // 2
    first = values[..., :half]
    second = values[..., half:]
    return jnp.concatenate(
        [first * cosine - second * sine, first * sine + second * cosine], axis=-1
    )


def unrotate(grads, cosine, sine):
    half = grads.shape[-1] // 2
    first = grads[..., :half]
    second = grads[..., half:]
    return jnp.concatenate(
        [first * cosine + second * sine, second * cosine - first * sine], axis=-1
    )


def head_norm(values, gain):
    inverse = lax.rsqrt(jnp.mean(values * values, axis=-1, keepdims=True) + epsilon)
    unit = values * inverse
    return (unit * gain, unit, inverse)


def head_norm_back(grads, unit, inverse, gain):
    gain_grad = jnp.sum(grads * unit, axis=(0, 1))
    scaled = grads * gain
    return (inverse * (scaled - unit * jnp.mean(scaled * unit, axis=-1, keepdims=True)), gain_grad)


def dot(left, right):
    return jnp.dot(left, right, preferred_element_type=f32)


def dot_nt(left, right):
    return lax.dot_general(left, right, (((1,), (1,)), ((), ())), preferred_element_type=f32)


def dot_tn(left, right):
    return lax.dot_general(left, right, (((0,), (0,)), ((), ())), preferred_element_type=f32)


def build(n_f, n_s):
    swaps = [[(i, i ^ k) for i in range(n_s)] for k in range(n_s)]

    def seq_gather(block):
        parts = [block] + [lax.ppermute(block, "seq", swaps[k]) for k in range(1, n_s)]
        return jnp.concatenate(parts, axis=0)

    def seq_scatter(total, rows):
        parts = [
            lax.ppermute(total[k * rows : (k + 1) * rows].astype(bf16), "seq", swaps[k])
            for k in range(1, n_s)
        ]
        result = total[:rows]
        for part in parts:
            result = result + part.astype(f32)
        return result

    def fsdp_gather(shard):
        return lax.all_gather(shard, "fsdp", axis=0, tiled=True)

    def fsdp_scatter(total):
        return lax.psum_scatter(total, "fsdp", scatter_dimension=0, tiled=True).astype(f32)

    def local(
        tokens,
        cotangent,
        condition,
        caption,
        positions,
        clip_lengths,
        caption_lengths,
        modulator,
        query_weight,
        key_weight,
        value_weight,
        output_weight,
        textkey_weight,
        textvalue_weight,
        gate_weight,
        up_weight,
        down_weight,
        attn_gain,
        ffn_gain,
        query_gain,
        key_gain,
        cross_gate,
    ):
        rows = tokens.shape[0]
        width = tokens.shape[1]
        head_size = query_gain.shape[0]
        columns = query_weight.shape[1]
        heads = columns // head_size
        units = gate_weight.shape[1]
        clip_rows = positions.shape[1]
        text_rows = caption.shape[0]
        seq_index = lax.axis_index("seq")
        fsdp_index = lax.axis_index("fsdp")
        length = clip_lengths[0]
        text_length = caption_lengths[0]
        scale = head_size ** (-0.5)

        attn_full = fsdp_gather(
            jnp.concatenate([query_weight, key_weight, value_weight, output_weight.T], axis=1)
        )
        text_full = fsdp_gather(jnp.concatenate([textkey_weight, textvalue_weight], axis=1))
        ffn_full = fsdp_gather(jnp.concatenate([gate_weight, up_weight, down_weight.T], axis=1))

        tokens_all = seq_gather(tokens).astype(f32)
        cotangent_all = seq_gather(cotangent).astype(f32)

        cond_low = jax.nn.silu(condition.astype(f32)).astype(bf16)
        cond_all = lax.all_gather(cond_low, "fsdp", axis=0, tiled=True)
        mod_rows = modulator.shape[0]
        cond_mine = lax.dynamic_slice_in_dim(cond_all, fsdp_index * mod_rows, mod_rows, 1)
        mod_part = dot(cond_mine, modulator)
        mod_part = lax.psum_scatter(mod_part, "fsdp", scatter_dimension=0, tiled=True)
        modulation = lax.all_gather(mod_part, "seq", axis=1, tiled=True)[0]
        scale_attn = modulation[:width]
        gate_attn = modulation[width : 2 * width]
        scale_ffn = modulation[2 * width : 3 * width]
        gate_ffn = modulation[3 * width :]
        tanh_attn = jnp.tanh(gate_attn)
        tanh_ffn = jnp.tanh(gate_ffn)

        order = [seq_index ^ k for k in range(n_s)]
        row_index = jnp.concatenate([order[k] * rows + jnp.arange(rows) for k in range(n_s)])
        places = jnp.concatenate(
            [lax.dynamic_slice_in_dim(positions, order[k] * rows, rows, 1) for k in range(n_s)],
            axis=1,
        )

        inv_attn_all = lax.rsqrt(jnp.mean(tokens_all * tokens_all, axis=-1, keepdims=True) + epsilon)
        normed_all = (tokens_all * inv_attn_all * attn_gain * (1.0 + scale_attn)).astype(bf16)
        inputs = tokens.astype(f32)
        inv_attn = inv_attn_all[:rows]
        unit_attn = inputs * inv_attn
        qkv = dot(normed_all, attn_full[:, : 3 * columns])
        query_raw = qkv[:, :columns].reshape(clip_rows, heads, head_size)
        key_raw = qkv[:, columns : 2 * columns].reshape(clip_rows, heads, head_size)
        value_heads = (
            qkv[:, 2 * columns :].astype(bf16).reshape(clip_rows, heads, head_size).transpose(1, 0, 2)
        )
        cosine, sine = rope_tables(places, head_size)
        cosine = cosine[:, None, :]
        sine = sine[:, None, :]
        query_normed, query_unit, query_inverse = head_norm(query_raw, query_gain)
        key_normed, key_unit, key_inverse = head_norm(key_raw, key_gain)
        query_heads = rotate(query_normed, cosine, sine).astype(bf16).transpose(1, 0, 2)
        key_heads = rotate(key_normed, cosine, sine).astype(bf16).transpose(1, 0, 2)
        key_valid = (row_index < length)[None, None, :]

        def softmax(scores):
            peak = jnp.max(scores, axis=-1, keepdims=True)
            expo = jnp.exp(scores - peak)
            return expo / jnp.sum(expo, axis=-1, keepdims=True)

        def bmm(spec, left, right):
            return jnp.einsum(spec, left, right, preferred_element_type=f32)

        scores = bmm("hqd,hkd->hqk", query_heads, key_heads) * scale
        probs = softmax(jnp.where(key_valid, scores, masked_score))
        probs_low = probs.astype(bf16)
        self_out = bmm("hqk,hkd->hqd", probs_low, value_heads)
        text_both = dot(caption, text_full).astype(bf16)
        textkey_heads = text_both[:, :columns].reshape(text_rows, heads, head_size).transpose(1, 0, 2)
        textvalue_heads = (
            text_both[:, columns:].reshape(text_rows, heads, head_size).transpose(1, 0, 2)
        )
        text_valid = (jnp.arange(text_rows) < text_length)[None, None, :]
        cross_scores = bmm("hqd,hkd->hqk", query_heads, textkey_heads) * scale
        cross_probs = softmax(jnp.where(text_valid, cross_scores, masked_score))
        cross_low = cross_probs.astype(bf16)
        cross_out = bmm("hqk,hkd->hqd", cross_low, textvalue_heads)
        gate_heads = jnp.tanh(lax.dynamic_slice_in_dim(cross_gate, seq_index * heads, heads))
        mixed_heads = self_out + gate_heads[:, None, None] * cross_out
        mixed_rows = mixed_heads.transpose(1, 0, 2).reshape(clip_rows, columns).astype(bf16)
        output_t = attn_full[:, 3 * columns :]
        attn_out = seq_scatter(dot_nt(mixed_rows, output_t), rows)
        branch_attn = tanh_attn * attn_out
        hidden_in = inputs + branch_attn
        inv_ffn = lax.rsqrt(jnp.mean(hidden_in * hidden_in, axis=-1, keepdims=True) + epsilon)
        unit_ffn = hidden_in * inv_ffn
        ffn_in = (unit_ffn * ffn_gain * (1.0 + scale_ffn)).astype(bf16)
        ffn_all = seq_gather(ffn_in)
        act = dot(ffn_all, ffn_full[:, : 2 * units])
        gate_act = act[:, :units]
        up_act = act[:, units:]
        down_t = ffn_full[:, 2 * units :]
        sigmoid_gate = jax.nn.sigmoid(gate_act)
        silu_gate = gate_act * sigmoid_gate
        hidden = (silu_gate * up_act).astype(bf16)
        ffn_back_all = (tanh_ffn * cotangent_all).astype(bf16)
        grad_hidden = dot(ffn_back_all, down_t)
        grad_gate_act = (
            grad_hidden * up_act * sigmoid_gate * (1.0 + gate_act * (1.0 - sigmoid_gate))
        ).astype(bf16)
        grad_up_act = (grad_hidden * silu_gate).astype(bf16)
        grad_act = jnp.concatenate([grad_gate_act, grad_up_act], axis=1)
        grad_ffn_in = seq_scatter(dot_nt(grad_act, ffn_full[:, : 2 * units]), rows)

        ffn_out = seq_scatter(dot_nt(hidden, down_t), rows)
        ffn_part = jnp.concatenate(
            [dot_tn(ffn_all, grad_act).astype(bf16), dot_tn(ffn_back_all, hidden).astype(bf16)], axis=1
        )
        ffn_grads = fsdp_scatter(ffn_part)

        branch_ffn = tanh_ffn * ffn_out
        result = hidden_in + branch_ffn
        row_valid = (seq_index * rows + jnp.arange(rows) < length)[:, None]
        sums = jnp.stack(
            [
                jnp.sum(jnp.where(row_valid, result * result, 0.0)),
                jnp.sum(jnp.where(row_valid, branch_attn * branch_attn, 0.0)),
                jnp.sum(jnp.where(row_valid, branch_ffn * branch_ffn, 0.0)),
            ]
        )
        grad_out = cotangent.astype(f32)
        grad_gate_ffn = jnp.sum(grad_out * ffn_out, axis=0) * (1.0 - tanh_ffn * tanh_ffn)

        grad_ffn_gain = jnp.sum(grad_ffn_in * unit_ffn * (1.0 + scale_ffn), axis=0)
        grad_scale_ffn = jnp.sum(grad_ffn_in * unit_ffn * ffn_gain, axis=0)
        scaled_ffn = grad_ffn_in * ffn_gain * (1.0 + scale_ffn)
        grad_hidden_in = grad_out + inv_ffn * (
            scaled_ffn - unit_ffn * jnp.mean(scaled_ffn * unit_ffn, axis=-1, keepdims=True)
        )
        attn_back = (tanh_attn * grad_hidden_in).astype(bf16)
        grad_gate_attn = jnp.sum(grad_hidden_in * attn_out, axis=0) * (1.0 - tanh_attn * tanh_attn)
        attn_back_all = seq_gather(attn_back)
        output_part = dot_tn(attn_back_all, mixed_rows).astype(bf16)
        grad_mixed = dot(attn_back_all, output_t).astype(bf16)
        grad_mixed = grad_mixed.reshape(clip_rows, heads, head_size).transpose(1, 0, 2)
        grad_mixed_wide = grad_mixed.astype(f32)
        grad_gate_heads = jnp.sum(grad_mixed_wide * cross_out, axis=(1, 2)) * (
            1.0 - gate_heads * gate_heads
        )
        cross_back = (gate_heads[:, None, None] * grad_mixed_wide).astype(bf16)
        grad_cross_probs = bmm("hqd,hkd->hqk", cross_back, textvalue_heads)
        cross_delta = jnp.sum(cross_probs * grad_cross_probs, axis=-1, keepdims=True)
        grad_cross_scores = (cross_probs * (grad_cross_probs - cross_delta)).astype(bf16)
        grad_query_cross = bmm("hqk,hkd->hqd", grad_cross_scores, textkey_heads) * scale
        grad_textkey = bmm("hqk,hqd->hkd", grad_cross_scores, query_heads) * scale
        grad_textvalue = bmm("hqk,hqd->hkd", cross_low, cross_back)

        grad_probs = bmm("hqd,hkd->hqk", grad_mixed, value_heads)
        delta = jnp.sum(probs * grad_probs, axis=-1, keepdims=True)
        grad_scores = (probs * (grad_probs - delta)).astype(bf16)
        grad_query_heads = grad_query_cross + bmm("hqk,hkd->hqd", grad_scores, key_heads) * scale
        grad_key_heads = bmm("hqk,hqd->hkd", grad_scores, query_heads) * scale
        grad_value_heads = bmm("hqk,hqd->hkd", probs_low, grad_mixed)

        grad_query_normed = unrotate(grad_query_heads.transpose(1, 0, 2), cosine, sine)
        grad_key_normed = unrotate(grad_key_heads.transpose(1, 0, 2), cosine, sine)
        grad_query_raw, grad_query_gain = head_norm_back(
            grad_query_normed, query_unit, query_inverse, query_gain
        )
        grad_key_raw, grad_key_gain = head_norm_back(
            grad_key_normed, key_unit, key_inverse, key_gain
        )
        qkv_rows = jnp.concatenate(
            [
                grad_query_raw.reshape(clip_rows, columns).astype(bf16),
                grad_key_raw.reshape(clip_rows, columns).astype(bf16),
                grad_value_heads.transpose(1, 0, 2).reshape(clip_rows, columns).astype(bf16),
            ],
            axis=1,
        )
        text_grads_rows = jnp.concatenate(
            [
                grad_textkey.transpose(1, 0, 2).reshape(text_rows, columns).astype(bf16),
                grad_textvalue.transpose(1, 0, 2).reshape(text_rows, columns).astype(bf16),
            ],
            axis=1,
        )
        text_grads = fsdp_scatter(dot_tn(caption, text_grads_rows).astype(bf16))
        attn_grads = fsdp_scatter(
            jnp.concatenate([dot_tn(normed_all, qkv_rows).astype(bf16), output_part], axis=1)
        )
        grad_normed = seq_scatter(dot_nt(qkv_rows, attn_full[:, : 3 * columns]), rows)
        grad_attn_gain = jnp.sum(grad_normed * unit_attn * (1.0 + scale_attn), axis=0)
        grad_scale_attn = jnp.sum(grad_normed * unit_attn * attn_gain, axis=0)
        scaled_attn = grad_normed * attn_gain * (1.0 + scale_attn)
        token_grad = grad_hidden_in + inv_attn * (
            scaled_attn - unit_attn * jnp.mean(scaled_attn * unit_attn, axis=-1, keepdims=True)
        )

        gate_heads_full = lax.dynamic_update_slice_in_dim(
            jnp.zeros_like(cross_gate), grad_gate_heads, seq_index * heads, 0
        )
        mod_grad = jnp.concatenate([grad_scale_attn, grad_gate_attn, grad_scale_ffn, grad_gate_ffn])
        mod_total, totals = lax.psum((mod_grad, sums), "seq")
        mod_columns = modulator.shape[1]
        mod_mine = lax.dynamic_slice_in_dim(mod_total, seq_index * mod_columns, mod_columns, 0)
        mod_mine = lax.all_gather(mod_mine.astype(bf16)[None, :], "fsdp", axis=0, tiled=True)
        modulator_grad = dot_tn(cond_mine, mod_mine)
        residual_rms = jnp.sqrt(totals / (length.astype(f32) * width))[:, None]
        small = lax.psum(
            (grad_attn_gain, grad_ffn_gain, grad_query_gain, grad_key_gain, gate_heads_full),
            ("fsdp", "seq"),
        )
        return (
            result.astype(bf16),
            token_grad,
            modulator_grad,
            attn_grads[:, :columns],
            attn_grads[:, columns : 2 * columns],
            attn_grads[:, 2 * columns : 3 * columns],
            attn_grads[:, 3 * columns :].T,
            text_grads[:, :columns],
            text_grads[:, columns:],
            ffn_grads[:, :units],
            ffn_grads[:, units : 2 * units],
            ffn_grads[:, 2 * units :].T,
            small[0],
            small[1],
            small[2],
            small[3],
            small[4],
            residual_rms,
        )

    return local


def solution(mesh):
    by_both = P(("fsdp", "seq"), None)
    return jax.shard_map(
        build(mesh.shape["fsdp"], mesh.shape["seq"]),
        mesh=mesh,
        in_specs=(
            by_both,
            by_both,
            P("fsdp", None),
            P("fsdp", None),
            P(None, "fsdp"),
            P("fsdp"),
            P("fsdp"),
            P("fsdp", "seq"),
            P("fsdp", "seq"),
            P("fsdp", "seq"),
            P("fsdp", "seq"),
            P("seq", "fsdp"),
            P("fsdp", "seq"),
            P("fsdp", "seq"),
            P("fsdp", "seq"),
            P("fsdp", "seq"),
            P("seq", "fsdp"),
            P(),
            P(),
            P(),
            P(),
            P(),
        ),
        out_specs=(
            by_both,
            by_both,
            P("fsdp", "seq"),
            P("fsdp", "seq"),
            P("fsdp", "seq"),
            P("fsdp", "seq"),
            P("seq", "fsdp"),
            P("fsdp", "seq"),
            P("fsdp", "seq"),
            P("fsdp", "seq"),
            P("fsdp", "seq"),
            P("seq", "fsdp"),
            P(),
            P(),
            P(),
            P(),
            P(),
            P(None, "fsdp"),
        ),
        check_vma=False,
    )
```

time: 1080 us -> 608 us (0.56)
  waiting for transfers between devices: 785 us -> 210 us
  blocking collectives: 67 us -> 123 us
  local copies, waits for them, and re-layouts: 21.8 us -> 61.8 us
  starting transfers between devices: 1.76 us -> 31.6 us
  matrix products: 120 us -> 93.6 us
    all_gather x14 -> x3, waiting for transfers between devices: 378 us -> 54.2 us  [fsdp_gather(): return lax.all_gather(shard, 'fsdp', axis=0, tiled=True)]
    reduce_scatter x14 -> x2, waiting for transfers between devices: 400 us -> 79 us  [fsdp_scatter(): lax.psum_scatter(total, 'fsdp', scatter_dimension=0, tiled=True).astype(f32)]
    ppermute x0 -> x24, waiting for transfers between devices: none -> 77.2 us  [the longest x12 58.3 us: seq_scatter(): lax.ppermute(total[k * rows:(k + 1) * rows].astype(bf16), 'seq', swaps[k])]
    dot_general x37 -> x26, matrix products: 116 us -> 82.2 us  [the longest x10 25.4 us: bmm(): return jnp.einsum(spec, left, right, preferred_element_type=f32)]
    ppermute x0 -> x24, starting transfers between devices: none -> 31.2 us  [the longest x12 16 us: seq_gather(): lax.ppermute(block, 'seq', swaps[k])]
    unnamed x0 -> x1, blocking collectives: none -> 30.9 us
    all_gather x0 -> x2, blocking collectives: none -> 29.4 us  [the longest x1 14.8 us: local(): cond_all = lax.all_gather(cond_low, 'fsdp', axis=0, tiled=True)]
    concatenate x0 -> x7, other arithmetic: none -> 16.7 us  [the longest x1 4.69 us: local(): jnp.concatenate([dot_tn(ffn_all, grad_act).astype(bf16), dot_tn(ffn_back_...]
  transfers between devices with their start and end apart: 28 -> 30, of which waited for: 26 -> 18; matrix products, arithmetic and copies ran while one was open for 13% -> 22% of each run, Pallas kernels for 0% -> 0%
where the time goes in v1:
time: 608 us; the launch traced here: 596 us
  waiting for transfers between devices  210 us (35%)
  blocking collectives  123 us (20%)
  matrix products  93.6 us (15%)
  local copies, waits for them, and re-layouts  61.8 us (10%)
  other arithmetic  58.1 us (10%)
  starting transfers between devices  31.6 us (5%)
  between operations  17.1 us (3%)
    reduce_scatter x2, waiting for transfers between devices, fsdp_scatter(): lax.psum_scatter(total, 'fsdp', scatter_dimension=0, tiled=True).astype(f32)  79 us
    ppermute x12, waiting for transfers between devices, seq_scatter(): lax.ppermute(total[k * rows:(k + 1) * rows].astype(bf16), 'seq', swaps[k])  58.3 us
    all_gather x3, waiting for transfers between devices, fsdp_gather(): return lax.all_gather(shard, 'fsdp', axis=0, tiled=True)  54.2 us
    psum x1, blocking collectives, local(): lax.psum((grad_attn_gain, grad_ffn_gain, grad_query_gain, grad_key_gain,...  39.6 us
    unnamed x1, blocking collectives  30.9 us
    unnamed x207, local copies, waits for them, and re-layouts  25.9 us
    dot_general x10, matrix products, bmm(): return jnp.einsum(spec, left, right, preferred_element_type=f32)  25.4 us
    dot_general x6, matrix products, dot(): return jnp.dot(left, right, preferred_element_type=f32)  23 us
  transfers between devices with their start and end apart: 30, of which 18 were waited for; matrix products, arithmetic and copies ran while one was open for 22% of the time, Pallas kernels for 0%

profile of v1, /device:TPU:0, one launch (start us, length us, event | category | flops | bytes accessed | tf_op | source)
XLA Modules:
  0.0 596.1 jit_solution(13379463111017192524)
XLA Ops:
  7.3 2.1 pad_maximum_fusion.13
  14.0 4.0 collective-permute-start.2
  20.5 14.8 %all-gather.1 = bf16[8,1,1024]{2,1,0:T(2,128)(2,1)S(1)} all-gather(bf16[1,1,1024]{2,1,0:T(2,128)(2,1)S(1)} %convert_bitcast_fusion), channel_id=1, replica_groups=mesh['fsdp'=8,'seq'=4] {'fsdp'}, dimensions={0}, use_global_device_ids=true | all-gather | bytes 18432 | tf_op jit(solution)/shard_map/all_gather | solution.py:138
  37.1 30.9 %all-reduce = f32[8,1536]{1,0:T(8,128)S(1)} all-reduce(f32[8,1536]{1,0:T(8,128)S(1)} %fusion.90), channel_id=3, replica_groups=mesh['fsdp'=8,'seq'=4] {'fsdp'}, use_global_device_ids=true, to_apply=%region_0.1.clone | all-reduce | flops 12288 | bytes 98304
  70.3 8.2 %all_gather.19 = f32[1,6144]{1,0:T(1,128)S(1)} all-gather(f32[1,1536]{1,0:T(1,128)S(1)} %constant_dynamic-slice_fusion.5), channel_id=1, replica_groups=mesh['fsdp'=8,'seq'=4] {'seq'}, dimensions={1}, use_global_device_ids=true | all-gather | bytes 30720 | tf_op jit(solution)/shard_map/all_gather | solution.py:143
  81.9 4.4 fusion.17
  88.7 2.4 fusion.120
  97.7 6.7 %fusion.130 = (f32[6,512]{1,0:T(8,128)}, f32[6,512,512]{1,2,0:T(8,128)}) fusion(pred[512]{0:T(512)(128)(4,1)} %add_compare_fusion, bf16[512,6,32]{0,2,1:T(8,128)(2,1)} %get-tuple-element.152, bf16[512,6,32]{0,2,1:T(8,128)(2,1)} %get-tuple-element.151, bf16[512,6,32]{0,2,1:T(8,128)(2,1)S(1)} %get-tuple-element.169, bf16[512,6,32]{0,2,1:T(8,128)(2,1)} %get-tuple-element.170), kind=kOutput, calls=%fused_computation.249 | convolution fusion | flops 209191424 | bytes 7090688 | tf_op jit(solution)/shard_map/sub | solution.py:180
  104.4 27.4 %all-gather.9.cloned.1.call-done = bf16[4096,768]{1,0:T(8,128)(2,1)} async-done(((bf16[512,768]{1,0:T(8,128)(2,1)}), bf16[4096,768]{1,0:T(8,128)(2,1)}) %all-gather.9.cloned.1.call-update) | async-done | bytes 6291472 | tf_op jit(solution)/shard_map/all_gather | solution.py:85
  131.8 4.6 fusion.44
  137.2 4.7 fusion.129
  141.9 2.5 fusion.68
  144.4 3.8 fusion.38
  148.2 2.5 fusion.131
  150.8 2.6 collective-permute-start.5
  154.4 9.4 %collective-permute-done.5 = bf16[128,1536]{1,0:T(8,128)(2,1)S(1)} collective-permute-done((bf16[128,1536]{1,0:T(8,128)(2,1)S(1)}, bf16[128,1536]{1,0:T(8,128)(2,1)S(1)}, u32[]{:S(2)}, u32[]{:S(2)}) %collective-permute-start.5) | collective-permute-done | bytes 393248 | tf_op jit(solution)/shard_map/ppermute | solution.py:76
  163.8 7.7 %collective-permute-done.4 = bf16[128,1536]{1,0:T(8,128)(2,1)S(1)} collective-permute-done((bf16[128,1536]{1,0:T(8,128)(2,1)S(1)}, bf16[128,1536]{1,0:T(8,128)(2,1)S(1)}, u32[]{:S(2)}, u32[]{:S(2)}) %collective-permute-start.4) | collective-permute-done | bytes 393248 | tf_op jit(solution)/shard_map/ppermute | solution.py:76
  180.3 6.5 %collective-permute-done.8 = bf16[128,1536]{1,0:T(8,128)(2,1)S(1)} collective-permute-done((bf16[128,1536]{1,0:T(8,128)(2,1)S(1)}, bf16[128,1536]{1,0:T(8,128)(2,1)S(1)}, u32[]{:S(2)}, u32[]{:S(2)}) %collective-permute-start.8) | collective-permute-done | bytes 393248 | tf_op jit(solution)/shard_map/ppermute | solution.py:71
  188.3 7.0 %collective-permute-done.7 = bf16[128,1536]{1,0:T(8,128)(2,1)S(1)} collective-permute-done((bf16[128,1536]{1,0:T(8,128)(2,1)S(1)}, bf16[128,1536]{1,0:T(8,128)(2,1)S(1)}, u32[]{:S(2)}, u32[]{:S(2)}) %collective-permute-start.7) | collective-permute-done | bytes 393248 | tf_op jit(solution)/shard_map/ppermute | solution.py:71
  196.1 26.8 %all-gather.11.cloned.1.call-done = bf16[1536,3072]{1,0:T(8,128)(2,1)} async-done(((bf16[192,3072]{1,0:T(8,128)(2,1)}), bf16[1536,3072]{1,0:T(8,128)(2,1)}) %all-gather.11.cloned.1.call-update) | async-done | bytes 9437200 | tf_op jit(solution)/shard_map/all_gather | solution.py:85
  222.9 6.1 %fusion.5 = f32[512,2048]{1,0:T(8,128)S(1)} fusion(bf16[1536,3072]{1,0:T(8,128)(2,1)} %all-gather.11.cloned.1.call-done, bf16[128,1536]{1,0:T(8,128)(2,1)} %copy-done.83, bf16[128,1536]{1,0:T(8,128)(2,1)} %copy-done.85, bf16[128,1536]{1,0:T(8,128)(2,1)} %collective-permute-done.6, bf16[128,1536]{1,0:T(8,128)(2,1)} %copy-done.32), kind=kOutput, calls=%fused_computation.13 | convolution fusion | flops 3227516928 | bytes 12058624 | tf_op jit(solution)/shard_map/dot_general | solution.py:56
  229.0 4.0 multiply_convert_fusion.4
  233.0 3.5 fusion.132
  236.6 2.5 collective-permute-start.17
  242.1 2.5 collective-permute-start.11
  245.2 4.4 collective-permute-done.17
  251.1 7.0 %collective-permute-done.16 = bf16[128,1536]{1,0:T(8,128)(2,1)S(1)} collective-permute-done((bf16[128,1536]{1,0:T(8,128)(2,1)S(1)}, bf16[128,1536]{1,0:T(8,128)(2,1)S(1)}, u32[]{:S(2)}, u32[]{:S(2)}) %collective-permute-start.16) | collective-permute-done | bytes 393248 | tf_op jit(solution)/shard_map/ppermute | solution.py:76
  258.1 8.4 %collective-permute-done.11 = bf16[128,1536]{1,0:T(8,128)(2,1)S(1)} collective-permute-done((bf16[128,1536]{1,0:T(8,128)(2,1)S(1)}, bf16[128,1536]{1,0:T(8,128)(2,1)S(1)}, u32[]{:S(2)}, u32[]{:S(2)}) %collective-permute-start.11) | collective-permute-done | bytes 393248 | tf_op jit(solution)/shard_map/ppermute | solution.py:76
  266.5 7.7 %collective-permute-done.10 = bf16[128,1536]{1,0:T(8,128)(2,1)S(1)} collective-permute-done((bf16[128,1536]{1,0:T(8,128)(2,1)S(1)}, bf16[128,1536]{1,0:T(8,128)(2,1)S(1)}, u32[]{:S(2)}, u32[]{:S(2)}) %collective-permute-start.10) | collective-permute-done | bytes 393248 | tf_op jit(solution)/shard_map/ppermute | solution.py:76
  274.3 2.8 select_reduce_fusion.2
  277.1 3.0 select_reduce_fusion.1
  291.6 2.3 copy.140
  294.8 2.3 copy.135
  297.1 5.3 collective-permute-done.19
  302.5 2.7 convolution_convert_fusion.5
  305.3 4.8 fusion.41
  310.1 3.0 multiply_reduce_fusion.1
  313.1 4.5 multiply_reduce_fusion
  319.5 3.9 multiply_convert_fusion.1
  324.3 4.6 multiply_convert_fusion
  333.0 2.3 copy.137
  335.3 2.1 pad_maximum_fusion.11
  337.4 2.3 copy.132
  342.2 3.4 multiply_reduce_fusion.2
  345.7 2.4 convolution_convert_fusion.4
  348.2 3.2 convolution_convert_fusion.1
  351.4 2.5 pad_maximum_fusion.1
  353.9 6.6 %copy.163 = bf16[1536,1536]{1,0:T(8,128)(2,1)} copy(bf16[1536,1536]{0,1:T(8,128)(2,1)} %pad_maximum_fusion.1) | data formatting | bytes 9437184
  363.5 2.8 convolution_convert_fusion.7
  366.3 4.4 fusion.2
  371.4 3.7 convolution_convert_fusion.3
  375.2 4.9 convolution_convert_fusion
  380.0 4.7 pad_maximum_fusion
  385.7 6.2 %fusion.134 = (bf16[512,1536]{1,0:T(8,128)(2,1)S(1)}, f32[512,1536]{1,0:T(8,128)}) fusion(bf16[1536,1536]{1,0:T(8,128)(2,1)} %all-gather.7.cloned.1.call-done, bf16[512,384]{1,0:T(8,128)(2,1)S(1)} %copy-done.27, bf16[512,384]{1,0:T(8,128)(2,1)} %copy-done.37, bf16[512,384]{1,0:T(8,128)(2,1)S(1)} %copy-done.36), kind=kOutput, calls=%fused_computation.253 | convolution fusion | flops 1816264704 | bytes 9437184 | tf_op jit(solution)/shard_map/dot_general | solution.py:60
  400.3 5.9 collective-permute-done.23
  406.2 7.5 %collective-permute-done.22 = bf16[128,1536]{1,0:T(8,128)(2,1)} collective-permute-done((bf16[128,1536]{1,0:T(8,128)(2,1)}, bf16[128,1536]{1,0:T(8,128)(2,1)}, u32[]{:S(2)}, u32[]{:S(2)}) %collective-permute-start.22) | collective-permute-done | bytes 393248 | tf_op jit(solution)/shard_map/ppermute | solution.py:76
  413.8 2.7 multiply_reduce_fusion.5
  416.6 15.3 %all-reduce.2 = (bf16[6144]{0:T(1024)(128)(2,1)S(1)}, f32[3]{0:T(128)S(1)}) all-reduce(f32[6144]{0:T(1024)S(1)} %pad_maximum_fusion.20, f32[3]{0:T(128)S(1)} %pad_maximum_fusion.21), channel_id=1, replica_groups=mesh['fsdp'=8,'seq'=4] {'seq'}, use_global_device_ids=true, to_apply=%region_19.20 | all-reduce | flops 6147 | bytes 36888 | tf_op jit(solution)/shard_map/psum | solution.py:316
  432.0 39.6 %all-reduce.1 = (f32[1536]{0:T(1024)}, f32[1536]{0:T(1024)}, f32[64]{0:T(128)}, f32[64]{0:T(128)}, f32[24]{0:T(128)}) all-reduce(f32[1536]{0:T(1024)S(1)} %get-tuple-element.95, f32[1536]{0:T(1024)S(1)} %copy-done.56, f32[64]{0:T(128)S(1)} %reduce_sum.250, f32[64]{0:T(128)S(1)} %reduce_sum.253, ...), channel_id=1, replica_groups=mesh['fsdp'=8,'seq'=4] {'fsdp','seq'}, use_global_device_ids=true, to_apply=%region_24.25 | all-reduce | flops 3224 | bytes 25792 | tf_op jit(solution)/shard_map/psum | solution.py:322
  471.5 14.6 %all-gather.2 = bf16[8,1,1536]{2,1,0:T(2,128)(2,1)S(1)} all-gather(bf16[1,1,1536]{2,1,0:T(2,128)(2,1)S(1)} %reshape.389), channel_id=2, replica_groups=mesh['fsdp'=8,'seq'=4] {'fsdp'}, dimensions={0}, use_global_device_ids=true | all-gather | bytes 27648 | tf_op jit(solution)/shard_map/all_gather | solution.py:319
  487.8 2.3 fusion.55
  500.3 2.2 fusion.126
  502.5 2.3 copy.152
  505.9 79.0 %reduce-scatter.8.cloned.1.call-done = bf16[192,3072]{1,0:T(8,128)(2,1)} async-done(((bf16[1536,3072]{1,0:T(8,128)(2,1)}), bf16[192,3072]{1,0:T(8,128)(2,1)}) %reduce-scatter.8.cloned.1.call-update) | async-done | bytes 1179664 | tf_op jit(solution)/shard_map/reduce_scatter | solution.py:88
  (335 shorter events, 92.1 us)
Async XLA Ops:
  7.2 124.6 %copy-start = (bf16[256,4096]{1,0:T(8,128)(2,1)S(1)}, bf16[256,4096]{1,0:T(8,128)(2,1)}, u32[]{:S(2)}) copy-start(bf16[256,4096]{1,0:T(8,128)(2,1)} %param.25) | copy-start | bytes 6291460
  7.2 74.6 %all-gather.7.cloned.1.call-start = ((), (), s32[]{:S(2)}) async-start(), calls=%async_computation.3 | async-start | bytes 5308416 | tf_op jit(solution)/shard_map/all_gather | solution.py:85
  9.4 10.5 %copy-start.90 = (u32[32]{0:T(128)S(1)}, u32[32]{0:T(128)}, u32[]{:S(2)}) copy-start(u32[32]{0:T(128)} %constant.95) | copy-start | bytes 388
  9.4 11.0 %copy-start.77 = (bf16[1,1024]{1,0:T(2,128)(2,1)S(1)}, bf16[1,1024]{1,0:T(2,128)(2,1)}, u32[]{:S(2)}) copy-start(bf16[1,1024]{1,0:T(2,128)(2,1)} %param.24) | copy-start | bytes 6148
  9.5 59.0 %copy-start.80 = (f32[24]{0:T(128)S(1)}, f32[24]{0:T(128)}, u32[]{:S(2)}) copy-start(f32[24]{0:T(128)} %param.43) | copy-start | bytes 292
  9.5 59.6 %copy-start.67 = (s32[3,512]{1,0:T(4,128)S(1)}, s32[3,512]{1,0:T(4,128)}, u32[]{:S(2)}) copy-start(s32[3,512]{1,0:T(4,128)} %param.26) | copy-start | bytes 18436
  9.5 122.3 %all-gather.9.cloned.1.call-start = ((), (), s32[]{:S(2)}) async-start(), calls=%async_computation.4 | async-start | bytes 7077888 | tf_op jit(solution)/shard_map/all_gather | solution.py:85
  11.7 70.2 %copy-start.51 = (f32[1536]{0:T(1024)S(1)}, f32[1536]{0:T(1024)}, u32[]{:S(2)}) copy-start(f32[1536]{0:T(1024)} %param.39) | copy-start | bytes 18436
  11.7 211.2 %all-gather.11.cloned.1.call-start = ((), (), s32[]{:S(2)}) async-start(), calls=%async_computation.5 | async-start | bytes 10616832 | tf_op jit(solution)/shard_map/all_gather | solution.py:85
  13.9 476.3 %reduce-scatter.10.cloned.1.call-start = ((), (), s32[]{:S(2)}) async-start(), calls=%async_computation.8 | async-start | bytes 5308416
  14.0 66.2 %collective-permute-start.2 = (bf16[128,1536]{1,0:T(8,128)(2,1)S(1)}, bf16[128,1536]{1,0:T(8,128)(2,1)S(1)}, u32[]{:S(2)}, u32[]{:S(2)}) collective-permute-start(bf16[128,1536]{1,0:T(8,128)(2,1)S(1)} %copy-done.7), channel_id=1, source_target_pairs={{0,3},{1,2},{2,1},{3,0},{4,7},{5,6},{6,5},{7,4},{8,11},{9,10},{10,... | collective-permute-start | bytes 1179656 | tf_op jit(solution)/shard_map/ppermute | solution.py:71
  17.9 62.2 %collective-permute-start.1 = (bf16[128,1536]{1,0:T(8,128)(2,1)S(1)}, bf16[128,1536]{1,0:T(8,128)(2,1)S(1)}, u32[]{:S(2)}, u32[]{:S(2)}) collective-permute-start(bf16[128,1536]{1,0:T(8,128)(2,1)S(1)} %copy-done.7), channel_id=1, source_target_pairs={{0,2},{1,3},{2,0},{3,1},{4,6},{5,7},{6,4},{7,5},{8,10},{9,11},{10,... | collective-permute-start | bytes 1179656 | tf_op jit(solution)/shard_map/ppermute | solution.py:71
  18.4 61.7 %collective-permute-start = (bf16[128,1536]{1,0:T(8,128)(2,1)S(1)}, bf16[128,1536]{1,0:T(8,128)(2,1)}, u32[]{:S(2)}, u32[]{:S(2)}) collective-permute-start(bf16[128,1536]{1,0:T(8,128)(2,1)S(1)} %copy-done.7), channel_id=1, source_target_pairs={{0,1},{1,0},{2,3},{3,2},{4,5},{5,4},{6,7},{7,6},{8,9},{9,8},{10,11... | collective-permute-start | bytes 1179656 | tf_op jit(solution)/shard_map/ppermute | solution.py:71
  79.2 7.1 %copy-start.47 = (f32[1536]{0:T(1024)}, f32[1536]{0:T(1024)S(1)}, u32[]{:S(2)}) copy-start(f32[1536]{0:T(1024)S(1)} %get-tuple-element.110) | copy-start | bytes 18436
  80.1 6.2 %copy-start.30 = (bf16[128,1536]{1,0:T(8,128)(2,1)}, bf16[128,1536]{1,0:T(8,128)(2,1)S(1)}, u32[]{:S(2)}) copy-start(bf16[128,1536]{1,0:T(8,128)(2,1)S(1)} %collective-permute-done.1) | copy-start | bytes 1179652
  148.2 23.4 %copy-start.41 = (f32[1536]{0:T(1024)S(1)}, f32[1536]{0:T(1024)}, u32[]{:S(2)}) copy-start(f32[1536]{0:T(1024)} %get-tuple-element.111) | copy-start | bytes 18436
  150.7 22.9 %copy-start.43 = (f32[1536]{0:T(1024)S(1)}, f32[1536]{0:T(1024)}, u32[]{:S(2)}) copy-start(f32[1536]{0:T(1024)} %get-tuple-element.108) | copy-start | bytes 18436
  150.7 22.9 %copy-start.45 = (f32[1536]{0:T(1024)S(1)}, f32[1536]{0:T(1024)}, u32[]{:S(2)}) copy-start(f32[1536]{0:T(1024)} %param.40) | copy-start | bytes 18436
  150.8 13.0 %collective-permute-start.5 = (bf16[128,1536]{1,0:T(8,128)(2,1)S(1)}, bf16[128,1536]{1,0:T(8,128)(2,1)S(1)}, u32[]{:S(2)}, u32[]{:S(2)}) collective-permute-start(bf16[128,1536]{1,0:T(8,128)(2,1)S(1)} %get-tuple-element.143), channel_id=1, source_target_pairs={{0,3},{1,2},{2,1},{3,0},{4,7},{5,6},{6,5},{7,4},{8,11},{9,10},{10,... | collective-permute-start | bytes 1179656 | tf_op jit(solution)/shard_map/ppermute | solution.py:76
  153.4 18.1 %collective-permute-start.4 = (bf16[128,1536]{1,0:T(8,128)(2,1)S(1)}, bf16[128,1536]{1,0:T(8,128)(2,1)S(1)}, u32[]{:S(2)}, u32[]{:S(2)}) collective-permute-start(bf16[128,1536]{1,0:T(8,128)(2,1)S(1)} %get-tuple-element.144), channel_id=1, source_target_pairs={{0,2},{1,3},{2,0},{3,1},{4,6},{5,7},{6,4},{7,5},{8,10},{9,11},{10,... | collective-permute-start | bytes 1179656 | tf_op jit(solution)/shard_map/ppermute | solution.py:76
  153.9 17.7 %collective-permute-start.3 = (bf16[128,1536]{1,0:T(8,128)(2,1)S(1)}, bf16[128,1536]{1,0:T(8,128)(2,1)S(1)}, u32[]{:S(2)}, u32[]{:S(2)}) collective-permute-start(bf16[128,1536]{1,0:T(8,128)(2,1)S(1)} %get-tuple-element.142), channel_id=1, source_target_pairs={{0,1},{1,0},{2,3},{3,2},{4,5},{5,4},{6,7},{7,6},{8,9},{9,8},{10,11... | collective-permute-start | bytes 1179656 | tf_op jit(solution)/shard_map/ppermute | solution.py:76
  172.8 22.5 %copy-start.70 = (f32[128]{0:T(128)}, f32[128]{0:T(128)S(1)}, u32[]{:S(2)}) copy-start(f32[128]{0:T(128)S(1)} %add_rsqrt_fusion.3) | copy-start | bytes 1540
  173.8 13.0 %collective-permute-start.8 = (bf16[128,1536]{1,0:T(8,128)(2,1)S(1)}, bf16[128,1536]{1,0:T(8,128)(2,1)S(1)}, u32[]{:S(2)}, u32[]{:S(2)}) collective-permute-start(bf16[128,1536]{1,0:T(8,128)(2,1)S(1)} %multiply_convert_fusion.9), channel_id=1, source_target_pairs={{0,3},{1,2},{2,1},{3,0},{4,7},{5,6},{6,5},{7,4},{8,11},{9,10},{10,... | collective-permute-start | bytes 1179656 | tf_op jit(solution)/shard_map/ppermute | solution.py:71
  175.5 19.8 %collective-permute-start.7 = (bf16[128,1536]{1,0:T(8,128)(2,1)S(1)}, bf16[128,1536]{1,0:T(8,128)(2,1)S(1)}, u32[]{:S(2)}, u32[]{:S(2)}) collective-permute-start(bf16[128,1536]{1,0:T(8,128)(2,1)S(1)} %multiply_convert_fusion.9), channel_id=1, source_target_pairs={{0,2},{1,3},{2,0},{3,1},{4,6},{5,7},{6,4},{7,5},{8,10},{9,11},{10,... | collective-permute-start | bytes 1179656 | tf_op jit(solution)/shard_map/ppermute | solution.py:71
  176.8 19.2 %collective-permute-start.6 = (bf16[128,1536]{1,0:T(8,128)(2,1)S(1)}, bf16[128,1536]{1,0:T(8,128)(2,1)}, u32[]{:S(2)}, u32[]{:S(2)}) collective-permute-start(bf16[128,1536]{1,0:T(8,128)(2,1)S(1)} %multiply_convert_fusion.9), channel_id=1, source_target_pairs={{0,1},{1,0},{2,3},{3,2},{4,5},{5,4},{6,7},{7,6},{8,9},{9,8},{10,11... | collective-permute-start | bytes 1179656 | tf_op jit(solution)/shard_map/ppermute | solution.py:71
  177.4 51.6 %collective-permute-start.14 = (bf16[128,1536]{1,0:T(8,128)(2,1)}, bf16[128,1536]{1,0:T(8,128)(2,1)}, u32[]{:S(2)}, u32[]{:S(2)}) collective-permute-start(bf16[128,1536]{1,0:T(8,128)(2,1)} %param.23), channel_id=1, source_target_pairs={{0,3},{1,2},{2,1},{3,0},{4,7},{5,6},{6,5},{7,4},{8,11},{9,10},{10,... | collective-permute-start | bytes 1179656 | tf_op jit(solution)/shard_map/ppermute | solution.py:71
  179.0 50.0 %collective-permute-start.13 = (bf16[128,1536]{1,0:T(8,128)(2,1)}, bf16[128,1536]{1,0:T(8,128)(2,1)}, u32[]{:S(2)}, u32[]{:S(2)}) collective-permute-start(bf16[128,1536]{1,0:T(8,128)(2,1)} %param.23), channel_id=1, source_target_pairs={{0,2},{1,3},{2,0},{3,1},{4,6},{5,7},{6,4},{7,5},{8,10},{9,11},{10,... | collective-permute-start | bytes 1179656 | tf_op jit(solution)/shard_map/ppermute | solution.py:71
  186.8 8.5 %copy-start.83 = (bf16[128,1536]{1,0:T(8,128)(2,1)}, bf16[128,1536]{1,0:T(8,128)(2,1)S(1)}, u32[]{:S(2)}) copy-start(bf16[128,1536]{1,0:T(8,128)(2,1)S(1)} %collective-permute-done.8) | copy-start | bytes 1179652
  186.8 42.2 %collective-permute-start.12 = (bf16[128,1536]{1,0:T(8,128)(2,1)}, bf16[128,1536]{1,0:T(8,128)(2,1)}, u32[]{:S(2)}, u32[]{:S(2)}) collective-permute-start(bf16[128,1536]{1,0:T(8,128)(2,1)} %param.23), channel_id=1, source_target_pairs={{0,1},{1,0},{2,3},{3,2},{4,5},{5,4},{6,7},{7,6},{8,9},{9,8},{10,11... | collective-permute-start | bytes 1179656 | tf_op jit(solution)/shard_map/ppermute | solution.py:71
  222.9 6.1 %copy-start.49 = (f32[1536]{0:T(1024)S(1)}, f32[1536]{0:T(1024)}, u32[]{:S(2)}) copy-start(f32[1536]{0:T(1024)} %get-tuple-element.109) | copy-start | bytes 18436
  222.9 6.1 %copy-start.82 = (bf16[1536,3072]{1,0:T(8,128)(2,1)S(1)}, bf16[1536,3072]{1,0:T(8,128)(2,1)}, u32[]{:S(2)}) copy-start(bf16[1536,3072]{1,0:T(8,128)(2,1)} %all-gather.11.cloned.1.call-done) | copy-start | bytes 28311556
  233.0 7.2 %copy-start.91 = (bf16[512,1024]{1,0:T(8,128)(2,1)}, bf16[512,1024]{1,0:T(8,128)(2,1)S(1)}, u32[]{:S(2)}) copy-start(bf16[512,1024]{1,0:T(8,128)(2,1)S(1)} %get-tuple-element.128) | copy-start | bytes 3145732
  236.6 13.0 %collective-permute-start.17 = (bf16[128,1536]{1,0:T(8,128)(2,1)S(1)}, bf16[128,1536]{1,0:T(8,128)(2,1)S(1)}, u32[]{:S(2)}, u32[]{:S(2)}) collective-permute-start(bf16[128,1536]{1,0:T(8,128)(2,1)S(1)} %get-tuple-element.140), channel_id=1, source_target_pairs={{0,3},{1,2},{2,1},{3,0},{4,7},{5,6},{6,5},{7,4},{8,11},{9,10},{10,... | collective-permute-start | bytes 1179656 | tf_op jit(solution)/shard_map/ppermute | solution.py:76
  239.1 19.0 %collective-permute-start.16 = (bf16[128,1536]{1,0:T(8,128)(2,1)S(1)}, bf16[128,1536]{1,0:T(8,128)(2,1)S(1)}, u32[]{:S(2)}, u32[]{:S(2)}) collective-permute-start(bf16[128,1536]{1,0:T(8,128)(2,1)S(1)} %get-tuple-element.141), channel_id=1, source_target_pairs={{0,2},{1,3},{2,0},{3,1},{4,6},{5,7},{6,4},{7,5},{8,10},{9,11},{10,... | collective-permute-start | bytes 1179656 | tf_op jit(solution)/shard_map/ppermute | solution.py:76
  239.6 18.4 %collective-permute-start.15 = (bf16[128,1536]{1,0:T(8,128)(2,1)S(1)}, bf16[128,1536]{1,0:T(8,128)(2,1)S(1)}, u32[]{:S(2)}, u32[]{:S(2)}) collective-permute-start(bf16[128,1536]{1,0:T(8,128)(2,1)S(1)} %get-tuple-element.139), channel_id=1, source_target_pairs={{0,1},{1,0},{2,3},{3,2},{4,5},{5,4},{6,7},{7,6},{8,9},{9,8},{10,11... | collective-permute-start | bytes 1179656 | tf_op jit(solution)/shard_map/ppermute | solution.py:76
  240.2 34.1 %copy-start.3 = (f32[128,1536]{1,0:T(8,128)S(1)}, f32[128,1536]{1,0:T(8,128)}, u32[]{:S(2)}) copy-start(f32[128,1536]{1,0:T(8,128)} %copy-done.2) | copy-start | bytes 2359300
  240.2 34.1 %copy-start.44 = (f32[1536]{0:T(1024)S(1)}, f32[1536]{0:T(1024)}, u32[]{:S(2)}) copy-start(f32[1536]{0:T(1024)} %get-tuple-element.108) | copy-start | bytes 18436
  240.2 34.1 %copy-start.46 = (f32[1536]{0:T(1024)S(1)}, f32[1536]{0:T(1024)}, u32[]{:S(2)}) copy-start(f32[1536]{0:T(1024)} %param.40) | copy-start | bytes 18436
  240.2 34.1 %copy-start.71 = (f32[128]{0:T(128)S(1)}, f32[128]{0:T(128)}, u32[]{:S(2)}) copy-start(f32[128]{0:T(128)} %copy-done.70) | copy-start | bytes 1540
  242.1 24.3 %collective-permute-start.11 = (bf16[128,1536]{1,0:T(8,128)(2,1)S(1)}, bf16[128,1536]{1,0:T(8,128)(2,1)S(1)}, u32[]{:S(2)}, u32[]{:S(2)}) collective-permute-start(bf16[128,1536]{1,0:T(8,128)(2,1)S(1)} %get-tuple-element.137), channel_id=1, source_target_pairs={{0,3},{1,2},{2,1},{3,0},{4,7},{5,6},{6,5},{7,4},{8,11},{9,10},{10,... | collective-permute-start | bytes 1179656 | tf_op jit(solution)/shard_map/ppermute | solution.py:76
  244.6 29.5 %collective-permute-start.10 = (bf16[128,1536]{1,0:T(8,128)(2,1)S(1)}, bf16[128,1536]{1,0:T(8,128)(2,1)S(1)}, u32[]{:S(2)}, u32[]{:S(2)}) collective-permute-start(bf16[128,1536]{1,0:T(8,128)(2,1)S(1)} %get-tuple-element.138), channel_id=1, source_target_pairs={{0,2},{1,3},{2,0},{3,1},{4,6},{5,7},{6,4},{7,5},{8,10},{9,11},{10,... | collective-permute-start | bytes 1179656 | tf_op jit(solution)/shard_map/ppermute | solution.py:76
  249.6 24.7 %collective-permute-start.9 = (bf16[128,1536]{1,0:T(8,128)(2,1)S(1)}, bf16[128,1536]{1,0:T(8,128)(2,1)S(1)}, u32[]{:S(2)}, u32[]{:S(2)}) collective-permute-start(bf16[128,1536]{1,0:T(8,128)(2,1)S(1)} %get-tuple-element.136), channel_id=1, source_target_pairs={{0,1},{1,0},{2,3},{3,2},{4,5},{5,4},{6,7},{7,6},{8,9},{9,8},{10,11... | collective-permute-start | bytes 1179656 | tf_op jit(solution)/shard_map/ppermute | solution.py:76
  277.1 8.2 %copy-start.75 = (f32[64]{0:T(128)S(1)}, f32[64]{0:T(128)}, u32[]{:S(2)}) copy-start(f32[64]{0:T(128)} %param.41) | copy-start | bytes 772
  281.8 15.3 %collective-permute-start.20 = (bf16[128,1536]{1,0:T(8,128)(2,1)}, bf16[128,1536]{1,0:T(8,128)(2,1)}, u32[]{:S(2)}, u32[]{:S(2)}) collective-permute-start(bf16[128,1536]{1,0:T(8,128)(2,1)} %multiply_convert_fusion.8), channel_id=1, source_target_pairs={{0,3},{1,2},{2,1},{3,0},{4,7},{5,6},{6,5},{7,4},{8,11},{9,10},{10,... | collective-permute-start | bytes 1179656 | tf_op jit(solution)/shard_map/ppermute | solution.py:71
  283.4 18.9 %collective-permute-start.19 = (bf16[128,1536]{1,0:T(8,128)(2,1)}, bf16[128,1536]{1,0:T(8,128)(2,1)}, u32[]{:S(2)}, u32[]{:S(2)}) collective-permute-start(bf16[128,1536]{1,0:T(8,128)(2,1)} %multiply_convert_fusion.8), channel_id=1, source_target_pairs={{0,2},{1,3},{2,0},{3,1},{4,6},{5,7},{6,4},{7,5},{8,10},{9,11},{10,... | collective-permute-start | bytes 1179656 | tf_op jit(solution)/shard_map/ppermute | solution.py:71
  284.8 17.7 %collective-permute-start.18 = (bf16[128,1536]{1,0:T(8,128)(2,1)}, bf16[128,1536]{1,0:T(8,128)(2,1)}, u32[]{:S(2)}, u32[]{:S(2)}) collective-permute-start(bf16[128,1536]{1,0:T(8,128)(2,1)} %multiply_convert_fusion.8), channel_id=1, source_target_pairs={{0,1},{1,0},{2,3},{3,2},{4,5},{5,4},{6,7},{7,6},{8,9},{9,8},{10,11... | collective-permute-start | bytes 1179656 | tf_op jit(solution)/shard_map/ppermute | solution.py:71
  297.1 8.1 %copy-start.64 = (f32[6,512]{1,0:T(8,128)S(1)}, f32[6,512]{1,0:T(8,128)}, u32[]{:S(2)}) copy-start(f32[6,512]{1,0:T(8,128)} %get-tuple-element.182) | copy-start | bytes 36868
  302.5 10.6 %slice-start = ((s8[6291456]{0:T(1024)(128)(4,1)}), s8[4194304]{0:T(1024)(128)(4,1)S(1)}, s32[]{:S(2)}) async-start(s8[6291456]{0:T(1024)(128)(4,1)} %bitcast.131), calls=%async_computation.9 | async-start | bytes 8388608
  305.2 7.9 %copy-start.34 = (bf16[512,384]{0,1:T(8,128)(2,1)}, bf16[512,384]{0,1:T(8,128)(2,1)S(1)}, u32[]{:S(2)}) copy-start(bf16[512,384]{0,1:T(8,128)(2,1)S(1)} %convolution_convert_fusion.5) | copy-start | bytes 1179652
  305.3 7.8 %slice-start.1 = ((s8[6291456]{0:T(1024)(128)(4,1)}), s8[2097152]{0:T(1024)(128)(4,1)S(1)}, s32[]{:S(2)}) async-start(s8[6291456]{0:T(1024)(128)(4,1)} %bitcast.131), calls=%async_computation.10 | async-start | bytes 4194304
  360.6 139.7 %reduce-scatter.6.cloned.1.call-start = ((), (), s32[]{:S(2)}) async-start(), calls=%async_computation.6 | async-start | bytes 7077888 | tf_op jit(solution)/shard_map/reduce_scatter | solution.py:88
  370.7 214.2 %reduce-scatter.8.cloned.1.call-start = ((), (), s32[]{:S(2)}) async-start(), calls=%async_computation.7 | async-start | bytes 10616832 | tf_op jit(solution)/shard_map/reduce_scatter | solution.py:88
  385.7 12.7 %copy-start.54 = (f32[1536]{0:T(1024)S(1)}, f32[1536]{0:T(1024)}, u32[]{:S(2)}) copy-start(f32[1536]{0:T(1024)} %get-tuple-element.100) | copy-start | bytes 18436
  385.7 12.7 %copy-start.58 = (f32[1536]{0:T(1024)S(1)}, f32[1536]{0:T(1024)}, u32[]{:S(2)}) copy-start(f32[1536]{0:T(1024)} %get-tuple-element.107) | copy-start | bytes 18436
  385.7 12.8 %copy-start.55 = (f32[1536]{0:T(1024)S(1)}, f32[1536]{0:T(1024)}, u32[]{:S(2)}) copy-start(f32[1536]{0:T(1024)} %get-tuple-element.105) | copy-start | bytes 18436
  385.7 12.8 %copy-start.57 = (f32[1536]{0:T(1024)S(1)}, f32[1536]{0:T(1024)}, u32[]{:S(2)}) copy-start(f32[1536]{0:T(1024)} %get-tuple-element.106) | copy-start | bytes 18436
  392.0 8.2 %copy-start.81 = (f32[24]{0:T(128)S(1)}, f32[24]{0:T(128)}, u32[]{:S(2)}) copy-start(f32[24]{0:T(128)} %param.43) | copy-start | bytes 292
  392.0 24.6 %copy-start.53 = (f32[1536]{0:T(1024)S(1)}, f32[1536]{0:T(1024)}, u32[]{:S(2)}) copy-start(f32[1536]{0:T(1024)} %get-tuple-element.101) | copy-start | bytes 18436
  392.0 40.0 %copy-start.56 = (f32[1536]{0:T(1024)S(1)}, f32[1536]{0:T(1024)}, u32[]{:S(2)}) copy-start(f32[1536]{0:T(1024)} %get-tuple-element.103) | copy-start | bytes 18436
  392.0 94.7 %copy-start.62 = (bf16[8,1,128]{2,1,0:T(2,128)(2,1)S(1)}, bf16[8,1,128]{2,1,0:T(2,128)(2,1)}, u32[]{:S(2)}) copy-start(bf16[8,1,128]{2,1,0:T(2,128)(2,1)} %copy-done.61) | copy-start | bytes 6148
  393.0 94.8 %copy-start.5 = (f32[128,1536]{1,0:T(8,128)S(1)}, f32[128,1536]{1,0:T(8,128)}, u32[]{:S(2)}) copy-start(f32[128,1536]{1,0:T(8,128)} %copy-done.4) | copy-start | bytes 2359300
  393.0 13.2 %collective-permute-start.23 = (bf16[128,1536]{1,0:T(8,128)(2,1)}, bf16[128,1536]{1,0:T(8,128)(2,1)}, u32[]{:S(2)}, u32[]{:S(2)}) collective-permute-start(bf16[128,1536]{1,0:T(8,128)(2,1)} %get-tuple-element.134), channel_id=1, source_target_pairs={{0,3},{1,2},{2,1},{3,0},{4,7},{5,6},{6,5},{7,4},{8,11},{9,10},{10,... | collective-permute-start | bytes 1179656 | tf_op jit(solution)/shard_map/ppermute | solution.py:76
  394.2 19.5 %collective-permute-start.22 = (bf16[128,1536]{1,0:T(8,128)(2,1)}, bf16[128,1536]{1,0:T(8,128)(2,1)}, u32[]{:S(2)}, u32[]{:S(2)}) collective-permute-start(bf16[128,1536]{1,0:T(8,128)(2,1)} %get-tuple-element.135), channel_id=1, source_target_pairs={{0,2},{1,3},{2,0},{3,1},{4,6},{5,7},{6,4},{7,5},{8,10},{9,11},{10,... | collective-permute-start | bytes 1179656 | tf_op jit(solution)/shard_map/ppermute | solution.py:76
  396.0 17.8 %collective-permute-start.21 = (bf16[128,1536]{1,0:T(8,128)(2,1)}, bf16[128,1536]{1,0:T(8,128)(2,1)}, u32[]{:S(2)}, u32[]{:S(2)}) collective-permute-start(bf16[128,1536]{1,0:T(8,128)(2,1)} %get-tuple-element.133), channel_id=1, source_target_pairs={{0,1},{1,0},{2,3},{3,2},{4,5},{5,4},{6,7},{7,6},{8,9},{9,8},{10,11... | collective-permute-start | bytes 1179656 | tf_op jit(solution)/shard_map/ppermute | solution.py:76
  (64 other events, 193.0 us)
Sparse Core Ops, SparseCore 0:
  10.3 55.6 all-gather.6
  68.2 63.5 all-gather.8
  133.4 89.3 all-gather.10
  360.7 52.4 reduce-scatter.9
  415.3 69.5 reduce-scatter.5
  487.1 97.7 reduce-scatter.7

commit v2 on v1

v2 whole, which is shorter than its diff:
```python
import math

import jax
import jax.numpy as jnp
from jax import lax
from jax.experimental import pallas as pl
from jax.experimental.pallas import tpu as pltpu
from jax.sharding import PartitionSpec as P

epsilon = 1e-06
masked_score = -1e30
f32 = jnp.float32
bf16 = jnp.bfloat16


def rope_tables(positions, head_size):
    half = head_size // 2
    pair_index = jnp.arange(half)
    frequency = jnp.exp(pair_index.astype(f32) * (-2.0 * math.log(10000.0) / head_size))
    angle = jnp.zeros((positions.shape[1], half), f32)
    for axis_number in range(3):
        chosen = jnp.where(pair_index % 3 == axis_number, frequency, jnp.zeros_like(frequency))
        angle = angle + positions[axis_number].astype(f32)[:, None] * chosen[None, :]
    return (jnp.cos(angle), jnp.sin(angle))


def dot(left, right):
    return jnp.dot(left, right, preferred_element_type=f32)


def dot_nt(left, right):
    return lax.dot_general(left, right, (((1,), (1,)), ((), ())), preferred_element_type=f32)


def dot_tn(left, right):
    return lax.dot_general(left, right, (((0,), (0,)), ((), ())), preferred_element_type=f32)


def attention_forward(qkv, text, cosine, sine, gains, mask, text_mask, gate, heads, head):
    rows = qkv.shape[0]
    columns = heads * head
    block = min(rows, 256)

    def kernel(qkv_ref, text_ref, cos_ref, sin_ref, gain_ref, mask_ref, tmask_ref, gate_ref,
               q_ref, k_ref, v_ref, mixed_ref, cross_ref, lse_ref):
        cos = cos_ref[...]
        sin = sin_ref[...]
        lse_ref[...] = jnp.zeros_like(lse_ref)

        def turned(raw, gain):
            inverse = lax.rsqrt(jnp.mean(raw * raw, axis=-1, keepdims=True) + epsilon)
            value = raw * inverse * gain
            swapped = jnp.concatenate([value[:, head // 2 :], value[:, : head // 2]], axis=1)
            return (value * cos + swapped * sin).astype(bf16)

        for h in range(heads):
            at = slice(h * head, (h + 1) * head)
            q_ref[:, at] = turned(qkv_ref[:, at], gain_ref[0:1, :head])
            k_ref[:, at] = turned(
                qkv_ref[:, columns + h * head : columns + (h + 1) * head], gain_ref[1:2, :head]
            )
            v_ref[:, at] = qkv_ref[:, 2 * columns + h * head : 2 * columns + (h + 1) * head].astype(bf16)

        def attend(query, keys, values, masks):
            scores = dot_nt(query, keys) + masks
            peak = jnp.max(scores, axis=-1, keepdims=True)
            expo = jnp.exp(scores - peak)
            total = jnp.sum(expo, axis=-1, keepdims=True)
            return dot(expo.astype(bf16), values) / total, peak + jnp.log(total)

        for h in range(heads):
            at = slice(h * head, (h + 1) * head)
            keys = k_ref[:, at]
            values = v_ref[:, at]
            text_keys = text_ref[:, at]
            text_values = text_ref[:, columns + h * head : columns + (h + 1) * head]
            for b in range(rows // block):
                here = slice(b * block, (b + 1) * block)
                query = q_ref[here, at] * jnp.asarray(head**-0.5, bf16)
                own, own_lse = attend(query, keys, values, mask_ref[...])
                other, other_lse = attend(query, text_keys, text_values, tmask_ref[...])
                cross_ref[here, at] = other
                mixed_ref[here, at] = (own + gate_ref[:, at] * other).astype(bf16)
                lse_ref[here, h : h + 1] = own_lse
                lse_ref[here, heads + h : heads + h + 1] = other_lse

    wide = jax.ShapeDtypeStruct((rows, columns), bf16)
    return pl.pallas_call(
        kernel,
        out_shape=(wide, wide, wide, wide, jax.ShapeDtypeStruct((rows, columns), f32),
                   jax.ShapeDtypeStruct((rows, 128), f32)),
        in_specs=[pl.BlockSpec(memory_space=pltpu.VMEM)] * 8,
        out_specs=(pl.BlockSpec(memory_space=pltpu.VMEM),) * 6,
        compiler_params=pltpu.CompilerParams(vmem_limit_bytes=48 * 1024 * 1024),
        cost_estimate=pl.CostEstimate(
            flops=4 * rows * (rows + text.shape[0]) * columns,
            bytes_accessed=8 * rows * columns * 4,
            transcendentals=heads * rows * (rows + text.shape[0]),
        ),
        name="attention_forward",
    )(qkv, text, cosine, sine, gains, mask, text_mask, gate)


def attention_backward(qkv, query, key, value, text, grad, lse, cross, cosine, sine, gains, mask, text_mask, gate, heads, head):
    rows = qkv.shape[0]
    text_rows = text.shape[0]
    columns = heads * head
    block = min(rows, 256)
    scale = head**-0.5

    def kernel(qkv_ref, q_ref, k_ref, v_ref, text_ref, grad_ref, lse_ref, cross_ref, cos_ref, sin_ref,
               gain_ref, mask_ref, tmask_ref, gate_ref, rows_ref, text_rows_ref, small_ref,
               dq_ref, dk_ref, dv_ref, dtk_ref, dtv_ref):
        cos = cos_ref[...]
        sin = sin_ref[...]
        small_ref[...] = jnp.zeros_like(small_ref)

        def soft_back(query, keys, values, masks, lse, back):
            probs = jnp.exp(dot_nt(query, keys) + masks - lse)
            grad_probs = dot_nt(back, values)
            delta = jnp.sum(probs * grad_probs, axis=-1, keepdims=True)
            return probs.astype(bf16), (probs * (grad_probs - delta)).astype(bf16)

        def raw_back(grad, raw, gain, row):
            swapped = jnp.concatenate([grad[:, head // 2 :], grad[:, : head // 2]], axis=1)
            turned = grad * cos - swapped * sin
            inverse = lax.rsqrt(jnp.mean(raw * raw, axis=-1, keepdims=True) + epsilon)
            unit = raw * inverse
            small_ref[row : row + 1, :head] += jnp.sum(turned * unit, axis=0, keepdims=True)
            scaled = turned * gain
            return (
                inverse * (scaled - unit * jnp.mean(scaled * unit, axis=-1, keepdims=True))
            ).astype(bf16)

        for h in range(heads):
            at = slice(h * head, (h + 1) * head)
            at_key = slice(columns + h * head, columns + (h + 1) * head)
            at_value = slice(2 * columns + h * head, 2 * columns + (h + 1) * head)
            keys = k_ref[:, at]
            values = v_ref[:, at]
            text_keys = text_ref[:, at]
            text_values = text_ref[:, at_key]
            gate_row = gate_ref[:, at]
            for b in range(rows // block):
                here = slice(b * block, (b + 1) * block)
                plain = q_ref[here, at]
                query = plain * jnp.asarray(scale, bf16)
                back = grad_ref[here, at]
                wide = back.astype(f32)
                probs, grads = soft_back(query, keys, values, mask_ref[...], lse_ref[here, h : h + 1], back)
                dq = dot(grads, keys)
                dk = dot_tn(grads, query)
                dv = dot_tn(probs, back)
                cross_back = (wide * gate_row).astype(bf16)
                probs, grads = soft_back(
                    query, text_keys, text_values, tmask_ref[...],
                    lse_ref[here, heads + h : heads + h + 1], cross_back,
                )
                dq_ref[here, :] = (dq + dot(grads, text_keys)) * scale
                dtk = dot_tn(grads, query)
                dtv = dot_tn(probs, cross_back)
                small_ref[2:3, h * head : (h + 1) * head] += jnp.sum(
                    wide * cross_ref[here, at], axis=0, keepdims=True
                )
                if b == 0:
                    dk_ref[...] = dk
                    dv_ref[...] = dv
                    dtk_ref[...] = dtk
                    dtv_ref[...] = dtv
                else:
                    dk_ref[...] += dk
                    dv_ref[...] += dv
                    dtk_ref[...] += dtk
                    dtv_ref[...] += dtv
            rows_ref[:, at] = raw_back(dq_ref[...], qkv_ref[:, at], gain_ref[0:1, :head], 0)
            rows_ref[:, at_key] = raw_back(dk_ref[...], qkv_ref[:, at_key], gain_ref[1:2, :head], 1)
            rows_ref[:, at_value] = dv_ref[...].astype(bf16)
            text_rows_ref[:, at] = dtk_ref[...].astype(bf16)
            text_rows_ref[:, at_key] = dtv_ref[...].astype(bf16)

    return pl.pallas_call(
        kernel,
        out_shape=(
            jax.ShapeDtypeStruct((rows, 3 * columns), bf16),
            jax.ShapeDtypeStruct((text_rows, 2 * columns), bf16),
            jax.ShapeDtypeStruct((8, max(columns, 128)), f32),
        ),
        in_specs=[pl.BlockSpec(memory_space=pltpu.VMEM)] * 14,
        out_specs=(pl.BlockSpec(memory_space=pltpu.VMEM),) * 3,
        scratch_shapes=[pltpu.VMEM((rows, head), f32)] * 3 + [pltpu.VMEM((text_rows, head), f32)] * 2,
        compiler_params=pltpu.CompilerParams(vmem_limit_bytes=48 * 1024 * 1024),
        cost_estimate=pl.CostEstimate(
            flops=10 * rows * (rows + text_rows) * columns,
            bytes_accessed=12 * rows * columns * 4,
            transcendentals=heads * rows * (rows + text_rows),
        ),
        name="attention_backward",
    )(qkv, query, key, value, text, grad, lse, cross, cosine, sine, gains, mask, text_mask, gate)


def ffn_forward(ffn_in, weights):
    rows, width = ffn_in.shape
    units = weights.shape[1] // 2
    tile = min(units, 256)
    tiles = units // tile

    def kernel(in_ref, gate_ref, up_ref, hidden_ref, by_gate_ref, by_up_ref):
        gate_act = dot(in_ref[...], gate_ref[...])
        up_act = dot(in_ref[...], up_ref[...])
        sigmoid = 1.0 / (1.0 + jnp.exp(-gate_act))
        silu = gate_act * sigmoid
        hidden_ref[...] = (silu * up_act).astype(bf16)
        by_gate_ref[...] = up_act * sigmoid * (1.0 + gate_act * (1.0 - sigmoid))
        by_up_ref[...] = silu

    part = pl.BlockSpec((rows, tile), lambda j: (0, j))
    wide = jax.ShapeDtypeStruct((rows, units), f32)
    return pl.pallas_call(
        kernel,
        grid=(tiles,),
        out_shape=(jax.ShapeDtypeStruct((rows, units), bf16), wide, wide),
        in_specs=[
            pl.BlockSpec((rows, width), lambda j: (0, 0)),
            pl.BlockSpec((width, tile), lambda j: (0, j)),
            pl.BlockSpec((width, tile), lambda j: (0, tiles + j)),
        ],
        out_specs=(part, part, part),
        compiler_params=pltpu.CompilerParams(vmem_limit_bytes=48 * 1024 * 1024),
        cost_estimate=pl.CostEstimate(
            flops=4 * rows * width * units,
            bytes_accessed=2 * rows * width + 4 * width * units + 10 * rows * units,
            transcendentals=rows * units,
        ),
        name="ffn_forward",
    )(ffn_in, weights, weights)


def ffn_backward(back, down, weights, by_gate, by_up):
    rows, width = back.shape
    units = down.shape[1]
    tile = min(units, 256)
    tiles = units // tile

    def kernel(back_ref, down_ref, gate_ref, up_ref, by_gate_ref, by_up_ref, act_ref, grad_ref, total):
        step = pl.program_id(0)

        @pl.when(step == 0)
        def _():
            total[...] = jnp.zeros_like(total)

        grad_hidden = dot(back_ref[...], down_ref[...])
        grad_gate = (grad_hidden * by_gate_ref[...]).astype(bf16)
        grad_up = (grad_hidden * by_up_ref[...]).astype(bf16)
        act_ref[:, pl.ds(pl.multiple_of(step * tile, tile), tile)] = grad_gate
        act_ref[:, pl.ds(pl.multiple_of(units + step * tile, tile), tile)] = grad_up
        total[...] += dot_nt(grad_gate, gate_ref[...]) + dot_nt(grad_up, up_ref[...])

        @pl.when(step == tiles - 1)
        def _():
            grad_ref[...] = total[...].astype(bf16)

    whole = pl.BlockSpec((rows, width), lambda j: (0, 0))
    part = pl.BlockSpec((rows, tile), lambda j: (0, j))
    return pl.pallas_call(
        kernel,
        grid=(tiles,),
        out_shape=(
            jax.ShapeDtypeStruct((rows, 2 * units), bf16),
            jax.ShapeDtypeStruct((rows, width), bf16),
        ),
        in_specs=[
            whole,
            pl.BlockSpec((width, tile), lambda j: (0, j)),
            pl.BlockSpec((width, tile), lambda j: (0, j)),
            pl.BlockSpec((width, tile), lambda j: (0, tiles + j)),
            part,
            part,
        ],
        out_specs=(pl.BlockSpec((rows, 2 * units), lambda j: (0, 0)), whole),
        scratch_shapes=[pltpu.VMEM((rows, width), f32)],
        compiler_params=pltpu.CompilerParams(vmem_limit_bytes=48 * 1024 * 1024),
        cost_estimate=pl.CostEstimate(
            flops=6 * rows * width * units,
            bytes_accessed=6 * rows * width + 6 * width * units + 12 * rows * units,
            transcendentals=0,
        ),
        name="ffn_backward",
    )(back, down, weights, weights, by_gate, by_up)


def widen(block, parts):
    rows = block.shape[0]
    columns = block.shape[1] // parts

    def kernel(block_ref, *part_refs):
        for i, part_ref in enumerate(part_refs):
            part_ref[...] = block_ref[:, i * columns : (i + 1) * columns].astype(f32)

    return pl.pallas_call(
        kernel,
        out_shape=[jax.ShapeDtypeStruct((rows, columns), f32)] * parts,
        in_specs=[pl.BlockSpec(memory_space=pltpu.VMEM)],
        out_specs=[pl.BlockSpec(memory_space=pltpu.VMEM)] * parts,
        name="widen",
    )(block)


def build(n_f, n_s):
    n_z = n_f // 2
    swaps = [[(i, i ^ k) for i in range(n_s)] for k in range(n_s)]

    def twin(block):
        return lax.ppermute(block, "fsdp", [(i, i ^ 1) for i in range(n_f)])

    def fsdp_xor(block, k):
        return lax.ppermute(block, "fsdp", [(i, i ^ k) for i in range(n_f)])

    def after(block, *earlier):
        return lax.optimization_barrier((block,) + earlier)[0]

    def stage(*values):
        return lax.optimization_barrier(values)

    def fsdp_scatter(total):
        return lax.psum_scatter(total, "fsdp", scatter_dimension=0, tiled=True)

    class Gather:
        def __init__(self, own, core):
            got = twin(own)
            first = core == 0
            pair = [jnp.where(first, own, got), jnp.where(first, got, own)]
            self.got = [jnp.concatenate(pair, axis=0)]
            self.twins = [None]

        def step(self, last=None):
            last = n_z - 1 if last is None else last
            while len(self.got) <= last:
                k = len(self.got)
                pairs = [(2 * z, 2 * z + 2) for z in range(k - 1, n_z - 1)]
                pairs += [(2 * z + 1, 2 * z - 1) for z in range(1, n_z - k + 1)]
                self.got.append(lax.ppermute(self.got[-1], "fsdp", pairs))

        def pass_on(self, last=None):
            last = n_z - 1 if last is None else last
            while len(self.twins) <= last:
                self.twins.append(twin(self.got[len(self.twins)]))

        def full(self, chip, core, place):
            rows, columns = self.got[0].shape
            whole = jnp.zeros((n_z, rows, columns), self.got[0].dtype)
            for k in range(n_z):
                block = self.got[0] if k == 0 else self.got[k] + self.twins[n_z - k]
                at = jnp.where(core == 0, lax.rem(chip + n_z - k, n_z), lax.rem(chip + k, n_z))
                whole = lax.dynamic_update_slice(whole, block[None], (place(at), 0, 0))
            return whole.reshape(n_z * rows, columns)

    def seq_near(block):
        return [lax.ppermute(block, "seq", swaps[k]) for k in (1, 2)]

    def seq_far(near, axis=0):
        half = near[0].shape[axis] // 2
        return [
            lax.ppermute(lax.slice_in_dim(near[0], 0, half, axis=axis), "seq", swaps[2]),
            lax.ppermute(lax.slice_in_dim(near[1], half, 2 * half, axis=axis), "seq", swaps[1]),
        ]

    def seq_gather(block, axis=0):
        if n_s != 4:
            parts = [block] + [lax.ppermute(block, "seq", swaps[k]) for k in range(1, n_s)]
        else:
            near = seq_near(block)
            far = jnp.concatenate(seq_far(near, axis + 1 if axis else 0), axis=axis + 1) if axis else None
            parts = [block] + near + ([far] if axis else seq_far(near))
        return jnp.concatenate(parts, axis=axis)

    def seq_send(total, rows):
        return [
            lax.ppermute(total[k * rows : (k + 1) * rows].astype(bf16), "seq", swaps[k])
            for k in range(1, n_s)
        ]

    def seq_sum(total, parts, rows):
        result = total[:rows].astype(f32)
        for part in parts:
            result = result + part.astype(f32)
        return result

    def by_seq(stacked, index):
        bit = 1
        while bit < n_s:
            split = stacked.reshape((n_s // (2 * bit), 2, bit) + stacked.shape[1:])
            turn = (index & bit) != 0
            first = jnp.where(turn, split[:, 1], split[:, 0])
            second = jnp.where(turn, split[:, 0], split[:, 1])
            stacked = jnp.stack([first, second], axis=1).reshape(stacked.shape)
            bit *= 2
        return stacked

    def all_sum(block, axis, size):
        bit = 1
        while bit < size:
            block = block + lax.ppermute(block, axis, [(i, i ^ bit) for i in range(size)])
            bit *= 2
        return block

    def local(
        tokens,
        cotangent,
        condition,
        caption,
        positions,
        clip_lengths,
        caption_lengths,
        modulator,
        query_weight,
        key_weight,
        value_weight,
        output_weight,
        textkey_weight,
        textvalue_weight,
        gate_weight,
        up_weight,
        down_weight,
        attn_gain,
        ffn_gain,
        query_gain,
        key_gain,
        cross_gate,
    ):
        rows = tokens.shape[0]
        width = tokens.shape[1]
        head_size = query_gain.shape[0]
        columns = query_weight.shape[1]
        heads = columns // head_size
        units = gate_weight.shape[1]
        clip_rows = positions.shape[1]
        text_rows = caption.shape[0]
        seq_index = lax.axis_index("seq")
        fsdp_index = lax.axis_index("fsdp")
        length = clip_lengths[0]
        text_length = caption_lengths[0]
        scale = head_size ** (-0.5)

        chip = fsdp_index // 2
        core = fsdp_index % 2

        def straight(t):
            return t

        def turned(t):
            return t ^ chip

        def fsdp_gather(*parts):
            return lax.all_gather(jnp.concatenate(parts, axis=1), "fsdp", axis=0, tiled=True)

        attn_full = fsdp_gather(query_weight, key_weight, value_weight, output_weight.T)
        text_full = fsdp_gather(textkey_weight, textvalue_weight)
        ffn_full = fsdp_gather(gate_weight, up_weight)
        down_t = lax.all_gather(down_weight.T, "fsdp", axis=0, tiled=True)
        qkv_full = attn_full[:, : 3 * columns]
        output_t = attn_full[:, 3 * columns :]
        cap_rows = text_rows // n_s
        cap_columns = textkey_weight.shape[0]
        cap_piece = lax.dynamic_slice_in_dim(caption, seq_index * cap_rows, cap_rows, 0)
        cap_mine = jnp.stack(
            [
                lax.dynamic_slice_in_dim(cap_piece, (fsdp_index ^ k) * cap_columns, cap_columns, 1)
                for k in range(n_f)
            ]
        )
        bit = 1
        while bit < n_f:
            split = cap_mine.reshape(n_f // (2 * bit), 2, bit, cap_rows, cap_columns)
            got = fsdp_xor(split[:, 1], bit)
            cap_mine = jnp.stack([split[:, 0], got], axis=1).reshape(n_f, cap_rows, cap_columns)
            bit *= 2
        cap_mine = cap_mine.reshape(n_z, 2, cap_rows, cap_columns)
        cap_mine = jnp.stack(
            [
                jnp.where(core == 0, cap_mine[:, 0], cap_mine[:, 1]),
                jnp.where(core == 0, cap_mine[:, 1], cap_mine[:, 0]),
            ],
            axis=1,
        )
        cap_mine = cap_mine.reshape(n_f, cap_rows, cap_columns)
        cond_low = jax.nn.silu(condition.astype(f32)).astype(bf16)
        cond_all = cond_low
        bit = 1
        while bit < n_f:
            cond_all = jnp.concatenate([cond_all, fsdp_xor(cond_all, bit)], axis=0)
            bit *= 2
        tokens_all = seq_gather(tokens)
        cond_all, cap_mine, tokens_all = stage(cond_all, cap_mine, tokens_all)

        mod_rows = modulator.shape[0]
        cond_mine = lax.dynamic_slice_in_dim(cond_all, fsdp_index * mod_rows, mod_rows, 1)
        mod_part = dot(cond_mine, modulator)
        half = n_f // 2
        while half:
            mod_part = mod_part[:half] + fsdp_xor(mod_part[half:], half)
            half //= 2
        cap_all = seq_gather(cap_mine[:, None], 1)
        modulation = mod_part
        bit = 1
        while bit < n_s:
            modulation = jnp.concatenate(
                [modulation, lax.ppermute(modulation, "seq", swaps[bit])], axis=0
            )
            bit *= 2
        modulation = by_seq(modulation, seq_index).reshape(-1)
        modulation, cap_all = stage(modulation, cap_all)
        cap_all = cap_all.reshape(n_f * text_rows, cap_columns)
        tokens_all = tokens_all.astype(f32)
        cotangent_all = seq_gather(after(cotangent, cap_all)).astype(f32)

        scale_attn = modulation[:width]
        gate_attn = modulation[width : 2 * width]
        scale_ffn = modulation[2 * width : 3 * width]
        gate_ffn = modulation[3 * width :]
        tanh_attn = jnp.tanh(gate_attn)
        tanh_ffn = jnp.tanh(gate_ffn)

        order = [seq_index ^ k for k in range(n_s)]
        row_index = jnp.concatenate([order[k] * rows + jnp.arange(rows) for k in range(n_s)])
        places = jnp.concatenate(
            [lax.dynamic_slice_in_dim(positions, order[k] * rows, rows, 1) for k in range(n_s)],
            axis=1,
        )

        inv_attn_all = lax.rsqrt(jnp.mean(tokens_all * tokens_all, axis=-1, keepdims=True) + epsilon)
        normed_all = (tokens_all * inv_attn_all * attn_gain * (1.0 + scale_attn)).astype(bf16)
        inputs = tokens.astype(f32)
        inv_attn = inv_attn_all[:rows]
        unit_attn = inputs * inv_attn
        qkv = dot(normed_all, qkv_full)
        text_both = dot(caption, text_full).astype(bf16)
        cosine, sine = rope_tables(places, head_size)
        cosine = jnp.concatenate([cosine, cosine], axis=1)
        sine = jnp.concatenate([-sine, sine], axis=1)
        gains = jnp.zeros((8, head_size), f32).at[0].set(query_gain).at[1].set(key_gain)
        mask = jnp.where(row_index < length, 0.0, masked_score).astype(f32)[None, :]
        text_mask = jnp.where(jnp.arange(text_rows) < text_length, 0.0, masked_score).astype(f32)[None, :]
        gate_heads = jnp.tanh(lax.dynamic_slice_in_dim(cross_gate, seq_index * heads, heads))
        gate_row = jnp.repeat(gate_heads, head_size)[None, :]
        query_rot, key_rot, value_low, mixed_rows, cross_out, lse = attention_forward(
            qkv, text_both, cosine, sine, gains, mask, text_mask, gate_row, heads, head_size
        )
        attn_sent = dot_nt(mixed_rows, output_t)
        attn_out = seq_sum(attn_sent, seq_send(attn_sent, rows), rows)
        branch_attn = tanh_attn * attn_out
        hidden_in = inputs + branch_attn
        inv_ffn = lax.rsqrt(jnp.mean(hidden_in * hidden_in, axis=-1, keepdims=True) + epsilon)
        unit_ffn = hidden_in * inv_ffn
        ffn_in = (unit_ffn * ffn_gain * (1.0 + scale_ffn)).astype(bf16)
        ffn_all = seq_gather(ffn_in)
        ffn_back_all = (tanh_ffn * cotangent_all).astype(bf16)
        hidden, by_gate, by_up = ffn_forward(ffn_all, ffn_full)
        down_part = dot_tn(ffn_back_all, hidden).astype(bf16)
        down_grads = fsdp_scatter(down_part)
        grad_act, grad_sent = ffn_backward(
            ffn_back_all, after(down_t, down_part), ffn_full, by_gate, by_up
        )
        parts = seq_send(grad_sent, rows)
        act_part = dot_tn(ffn_all, grad_act).astype(bf16)
        act_grads = fsdp_scatter(act_part)
        parts[0] = after(parts[0], act_part)
        grad_ffn_in = seq_sum(grad_sent, parts, rows)
        grad_out = cotangent.astype(f32)
        grad_ffn_gain = jnp.sum(grad_ffn_in * unit_ffn * (1.0 + scale_ffn), axis=0)
        grad_scale_ffn = jnp.sum(grad_ffn_in * unit_ffn * ffn_gain, axis=0)
        scaled_ffn = grad_ffn_in * ffn_gain * (1.0 + scale_ffn)
        grad_hidden_in = grad_out + inv_ffn * (
            scaled_ffn - unit_ffn * jnp.mean(scaled_ffn * unit_ffn, axis=-1, keepdims=True)
        )
        attn_back = (tanh_attn * grad_hidden_in).astype(bf16)
        grad_gate_attn = jnp.sum(grad_hidden_in * attn_out, axis=0) * (1.0 - tanh_attn * tanh_attn)
        attn_back_all = seq_gather(attn_back)
        grad_mixed = dot(attn_back_all, output_t).astype(bf16)
        output_part = dot_tn(attn_back_all, mixed_rows).astype(bf16)
        ffn_sent = dot_nt(after(hidden, attn_back_all), down_t)
        ffn_parts = seq_send(ffn_sent, rows)
        qkv_rows, text_grads_rows, head_sums = attention_backward(
            qkv, query_rot, key_rot, value_low, text_both, grad_mixed, lse, cross_out,
            cosine, sine, gains, mask, text_mask, gate_row, heads, head_size,
        )
        qkv_rows, text_grads_rows, *ffn_parts = stage(qkv_rows, text_grads_rows, *ffn_parts)

        text_order = [
            lax.dynamic_slice_in_dim(text_grads_rows, order[k] * cap_rows, cap_rows, 0)
            for k in range(n_s)
        ]
        text_back = Gather(jnp.concatenate(text_order, axis=0), core)
        text_back.step(1)
        normed_sent = dot_nt(qkv_rows, qkv_full)
        parts = seq_send(normed_sent, rows)
        qkv_part = dot_tn(normed_all, after(qkv_rows, normed_sent)).astype(bf16)
        attn_part = jnp.concatenate([qkv_part, output_part], axis=1)
        ffn_out = seq_sum(ffn_sent, ffn_parts, rows)
        branch_ffn = tanh_ffn * ffn_out
        result = hidden_in + branch_ffn
        row_valid = (seq_index * rows + jnp.arange(rows) < length)[:, None]
        sums = jnp.stack(
            [
                jnp.sum(jnp.where(row_valid, result * result, 0.0)),
                jnp.sum(jnp.where(row_valid, branch_attn * branch_attn, 0.0)),
                jnp.sum(jnp.where(row_valid, branch_ffn * branch_ffn, 0.0)),
            ]
        )
        grad_gate_ffn = jnp.sum(grad_out * ffn_out, axis=0) * (1.0 - tanh_ffn * tanh_ffn)

        grad_query_gain = head_sums[0, :head_size]
        grad_key_gain = head_sums[1, :head_size]
        grad_gate_heads = jnp.sum(
            head_sums[2, :columns].reshape(heads, head_size), axis=1
        ) * (1.0 - gate_heads * gate_heads)
        attn_grads = fsdp_scatter(after(attn_part, act_grads))
        *parts, text_back.got[1] = stage(*parts, text_back.got[1])

        text_back.step(2)
        text_back.pass_on(1)
        grad_normed = seq_sum(normed_sent, parts, rows)
        grad_attn_gain = jnp.sum(grad_normed * unit_attn * (1.0 + scale_attn), axis=0)
        grad_scale_attn = jnp.sum(grad_normed * unit_attn * attn_gain, axis=0)
        scaled_attn = grad_normed * attn_gain * (1.0 + scale_attn)
        token_grad = grad_hidden_in + inv_attn * (
            scaled_attn - unit_attn * jnp.mean(scaled_attn * unit_attn, axis=-1, keepdims=True)
        )

        gate_heads_full = lax.dynamic_update_slice_in_dim(
            jnp.zeros_like(cross_gate), grad_gate_heads, seq_index * heads, 0
        )
        sizes = jnp.concatenate(
            [grad_attn_gain, grad_ffn_gain, gate_heads_full, grad_query_gain, grad_key_gain, sums]
        )
        sizes = all_sum(sizes, "seq", n_s)
        mod_grad = jnp.concatenate([grad_scale_attn, grad_gate_attn, grad_scale_ffn, grad_gate_ffn])
        mod_mine = by_seq(mod_grad.reshape(n_s, -1), seq_index)
        half = n_s // 2
        while half:
            mod_mine = mod_mine[:half] + lax.ppermute(mod_mine[half:], "seq", swaps[half])
            half //= 2
        mod_mine = mod_mine.astype(bf16)
        sizes, mod_mine, text_back.got[2] = stage(sizes, mod_mine, text_back.got[2])

        text_back.step()
        text_back.pass_on(2)
        bit = 1
        while bit < n_f:
            mod_mine = jnp.concatenate([mod_mine, fsdp_xor(mod_mine, bit)], axis=0)
            bit *= 2
        modulator_grad = dot_tn(cond_mine, mod_mine)
        totals = sizes[-3:]
        residual_rms = jnp.sqrt(totals / (length.astype(f32) * width))[:, None]
        small = all_sum(sizes[:-3], "fsdp", n_f)
        small, modulator_grad, text_back.got[-1] = stage(
            small, modulator_grad, text_back.got[-1]
        )

        text_back.pass_on()
        text_grads = dot_tn(cap_all, text_back.full(chip, core, turned))
        attn_grads = widen(attn_grads, 4)
        act_grads = widen(act_grads, 2)
        down_grads = widen(down_grads, 1)[0]
        n_heads = cross_gate.shape[0]
        ends = [width, width, n_heads, head_size, head_size]
        ends = [sum(ends[:i]) for i in range(6)]
        small = [small[ends[i] : ends[i + 1]] for i in range(5)]
        small = (small[0], small[1], small[3], small[4], small[2])
        return (
            result.astype(bf16),
            token_grad,
            modulator_grad,
            *attn_grads[:3],
            attn_grads[3].T,
            text_grads[:, :columns],
            text_grads[:, columns:],
            *act_grads,
            down_grads.T,
            small[0],
            small[1],
            small[2],
            small[3],
            small[4],
            residual_rms,
        )

    return local


def solution(mesh):
    by_both = P(("fsdp", "seq"), None)
    return jax.shard_map(
        build(mesh.shape["fsdp"], mesh.shape["seq"]),
        mesh=mesh,
        in_specs=(
            by_both,
            by_both,
            P("fsdp", None),
            P("fsdp", None),
            P(None, "fsdp"),
            P("fsdp"),
            P("fsdp"),
            P("fsdp", "seq"),
            P("fsdp", "seq"),
            P("fsdp", "seq"),
            P("fsdp", "seq"),
            P("seq", "fsdp"),
            P("fsdp", "seq"),
            P("fsdp", "seq"),
            P("fsdp", "seq"),
            P("fsdp", "seq"),
            P("seq", "fsdp"),
            P(),
            P(),
            P(),
            P(),
            P(),
        ),
        out_specs=(
            by_both,
            by_both,
            P("fsdp", "seq"),
            P("fsdp", "seq"),
            P("fsdp", "seq"),
            P("fsdp", "seq"),
            P("seq", "fsdp"),
            P("fsdp", "seq"),
            P("fsdp", "seq"),
            P("fsdp", "seq"),
            P("fsdp", "seq"),
            P("seq", "fsdp"),
            P(),
            P(),
            P(),
            P(),
            P(),
            P(None, "fsdp"),
        ),
        check_vma=False,
    )
```

time: 608 us -> 488 us (0.80); the launches traced: 596 us -> 483 us
  blocking collectives: 123 us -> 0 us
  starting transfers between devices: 31.6 us -> 113 us
  Pallas kernels: 0 us -> 64.8 us
  matrix products: 93.6 us -> 39.2 us
  waiting for transfers between devices: 210 us -> 181 us
  other arithmetic: 58.1 us -> 30.1 us
  local copies, waits for them, and re-layouts: 61.8 us -> 37.3 us
    ppermute x24 -> x60, starting transfers between devices: 31.2 us -> 113 us  [the longest x12 58.6 us: fsdp_xor(): return lax.ppermute(block, 'fsdp', [(i, i ^ k) for i in range(n_f)])]
    reduce_scatter x2 -> x3, waiting for transfers between devices: 79 us -> 0.01 us  [fsdp_scatter(): return lax.psum_scatter(total, 'fsdp', scatter_dimension=0, tiled=True)]
    ppermute x24 -> x60, waiting for transfers between devices: 77.2 us -> 154 us  [the longest x12 47.6 us: fsdp_xor(): return lax.ppermute(block, 'fsdp', [(i, i ^ k) for i in range(n_f)])]
    pallas_call x0 -> x7, Pallas kernels: none -> 64.8 us  [the longest x1 23.6 us: attention_backward(): pl.pallas_call(kernel, out_shape=(jax.ShapeDtypeStruct((rows, 3 * columns...]
    psum x2 -> x0, blocking collectives: 54.9 us -> none  [the longest x1 39.6 us: local(): lax.psum((grad_attn_gain, grad_ffn_gain, grad_query_gain, grad_key_gain,...]
    all_gather x3 -> x0, blocking collectives: 37.6 us -> none  [the longest x1 14.8 us: local(): cond_all = lax.all_gather(cond_low, 'fsdp', axis=0, tiled=True)]
    unnamed x1 -> x0, blocking collectives: 30.9 us -> none
    all_gather x3 -> x4, waiting for transfers between devices: 54.2 us -> 26.3 us  [the longest x1 25.1 us: local(): down_t = lax.all_gather(down_weight.T, 'fsdp', axis=0, tiled=True)]
  transfers between devices with their start and end apart: 30 -> 67, of which waited for: 18 -> 35; matrix products, arithmetic and copies ran while one was open for 22% -> 19% of each run, Pallas kernels for 0% -> 11%
where the time goes in v2:
time: 488 us; the launch traced here: 483 us
  waiting for transfers between devices  181 us (37%)
  starting transfers between devices  113 us (23%)
  Pallas kernels  64.8 us (13%)
  matrix products  39.2 us (8%)
  local copies, waits for them, and re-layouts  37.3 us (8%)
  other arithmetic  30.1 us (6%)
  between operations  17.4 us (4%)
    ppermute x12, starting transfers between devices, fsdp_xor(): return lax.ppermute(block, 'fsdp', [(i, i ^ k) for i in range(n_f)])  58.6 us
    ppermute x12, waiting for transfers between devices, fsdp_xor(): return lax.ppermute(block, 'fsdp', [(i, i ^ k) for i in range(n_f)])  47.6 us
    ppermute x12, waiting for transfers between devices, seq_send(): lax.ppermute(total[k * rows:(k + 1) * rows].astype(bf16), 'seq', swaps[k])  45.5 us
    all_gather x1, waiting for transfers between devices, local(): down_t = lax.all_gather(down_weight.T, 'fsdp', axis=0, tiled=True)  25.1 us
    pallas_call x1, Pallas kernels, attention_backward(): pl.pallas_call(kernel, out_shape=(jax.ShapeDtypeStruct((rows, 3 * columns...  23.6 us
    ppermute x10, waiting for transfers between devices, seq_near(): return [lax.ppermute(block, 'seq', swaps[k]) for k in (1, 2)]  21.9 us
    unnamed x161, local copies, waits for them, and re-layouts  19.2 us
    dot_general x6, matrix products, dot_tn(): lax.dot_general(left, right, (((0,), (0,)), ((), ())), preferred_element_...  16.3 us
  transfers between devices with their start and end apart: 67, of which 35 were waited for; matrix products, arithmetic and copies ran while one was open for 19% of the time, Pallas kernels for 11%

profile of v2, /device:TPU:0, one launch (start us, length us, event | category | flops | bytes accessed | tf_op | source)
XLA Modules:
  0.0 482.7 jit_solution(4984884573237792356)
XLA Ops:
  7.3 2.1 pad_maximum_fusion.4
  11.6 3.0 collective-permute-start.6
  28.9 3.0 collective-permute-done.1
  31.9 2.0 collective-permute-start.2
  34.5 2.4 collective-permute-done.2
  43.7 19.2 %collective-permute-done.4 = bf16[2,2,64,512]{3,2,0,1:T(8,128)(2,1)S(1)} collective-permute-done((bf16[2,2,64,512]{3,2,0,1:T(8,128)(2,1)S(1)}, bf16[2,2,64,512]{3,2,0,1:T(8,128)(2,1)S(1)}, u32[]{:S(2)}, u32[]{:S(2)}) %collective-permute-start.4) | collective-permute-done | bytes 262176 | tf_op jit(solution)/shard_map/ppermute | solution.py:316
  63.6 14.2 %collective-permute-done.5 = bf16[1,4,64,512]{3,2,1,0:T(8,128)(2,1)S(1)} collective-permute-done((bf16[1,4,64,512]{3,2,1,0:T(8,128)(2,1)S(1)}, bf16[1,4,64,512]{3,2,1,0:T(8,128)(2,1)S(1)}, u32[]{:S(2)}, u32[]{:S(2)}) %collective-permute-start.5) | collective-permute-done | bytes 262176 | tf_op jit(solution)/shard_map/ppermute | solution.py:316
  78.9 4.1 collective-permute-done.10
  83.1 3.7 collective-permute-done.11
  87.4 1.7 collective-permute-start.15
  89.1 1.8 collective-permute-start.16
  91.6 10.3 %collective-permute-done.13 = f32[1,1536]{1,0:T(1,128)S(1)} collective-permute-done((f32[1,1536]{1,0:T(1,128)S(1)}, f32[1,1536]{1,0:T(1,128)S(1)}, u32[]{:S(2)}, u32[]{:S(2)}) %collective-permute-start.13) | collective-permute-done | bytes 6176 | tf_op jit(solution)/shard_map/ppermute | solution.py:507
  102.0 1.7 collective-permute-start.14
  103.7 2.0 collective-permute-done.14
  105.9 1.7 slice.367
  109.2 1.7 slice.368
  110.9 1.7 collective-permute-start.18
  112.7 2.3 collective-permute-done.17
  115.0 3.0 collective-permute-done.18
  118.0 3.0 maximum_maximum_fusion
  121.0 1.7 collective-permute-start.26
  123.8 6.1 %collective-permute-done.26 = bf16[128,1536]{1,0:T(8,128)(2,1)S(1)} collective-permute-done((bf16[128,1536]{1,0:T(8,128)(2,1)S(1)}, bf16[128,1536]{1,0:T(8,128)(2,1)S(1)}, u32[]{:S(2)}, u32[]{:S(2)}) %collective-permute-start.26) | collective-permute-done | bytes 393248 | tf_op jit(solution)/shard_map/ppermute | solution.py:358
  134.9 4.8 fusion.6.qkv_ref
  140.0 5.8 %fusion.8.text_ref = bf16[256,768]{1,0:T(8,128)(2,1)S(1)} fusion(bf16[256,4096]{1,0:T(8,128)(2,1)} %param.29, bf16[4096,768]{1,0:T(8,128)(2,1)} %all-gather.7.cloned.1.call-done), kind=kOutput, calls=%fused_computation.19 | convolution fusion | flops 1610809344 | bytes 8781824 | tf_op jit(solution)/shard_map/dot_general | solution.py:28
  145.8 16.0 %attention_forward.1 = (bf16[512,384]{1,0:T(8,128)(2,1)S(1)}, bf16[512,384]{1,0:T(8,128)(2,1)S(1)}, bf16[512,384]{1,0:T(8,128)(2,1)S(1)}, bf16[512,384]{1,0:T(8,...) custom-call(f32[512,1152]{1,0:T(8,128)S(1)} %fusion.6.qkv_ref, bf16[256,768]{1,0:T(8,128)(2,1)S(1)} %fusion.8.text_ref, ...), custom_call_target="tpu_custom_call" | custom-call | flops 603979776 | bytes 6291456 | tf_op jit(solution)/shard_map/attention_forward/pallas_call | solution.py:88
  161.9 3.2 fusion.64
  172.1 5.3 %collective-permute-done.19 = bf16[128,1536]{1,0:T(8,128)(2,1)S(1)} collective-permute-done((bf16[128,1536]{1,0:T(8,128)(2,1)S(1)}, bf16[128,1536]{1,0:T(8,128)(2,1)S(1)}, u32[]{:S(2)}, u32[]{:S(2)}) %collective-permute-start.19) | collective-permute-done | bytes 393248 | tf_op jit(solution)/shard_map/ppermute | solution.py:378
  177.4 8.2 %collective-permute-done.20 = bf16[128,1536]{1,0:T(8,128)(2,1)S(1)} collective-permute-done((bf16[128,1536]{1,0:T(8,128)(2,1)S(1)}, bf16[128,1536]{1,0:T(8,128)(2,1)S(1)}, u32[]{:S(2)}, u32[]{:S(2)}) %collective-permute-start.20) | collective-permute-done | bytes 393248 | tf_op jit(solution)/shard_map/ppermute | solution.py:378
  190.8 6.3 %collective-permute-done.22 = bf16[128,1536]{1,0:T(8,128)(2,1)S(1)} collective-permute-done((bf16[128,1536]{1,0:T(8,128)(2,1)S(1)}, bf16[128,1536]{1,0:T(8,128)(2,1)S(1)}, u32[]{:S(2)}, u32[]{:S(2)}) %collective-permute-start.22) | collective-permute-done | bytes 393248 | tf_op jit(solution)/shard_map/ppermute | solution.py:358
  197.1 1.8 collective-permute-start.24
  199.3 3.5 collective-permute-done.24
  202.8 1.8 collective-permute-done.25
  205.6 7.4 %ffn_forward.1 = (bf16[512,1024]{1,0:T(8,128)(2,1)S(1)}, f32[512,1024]{1,0:T(8,128)S(1)}, f32[512,1024]{1,0:T(8,128)}) custom-call(bf16[512,1536]{1,0:T(8,128)(2,1)S(1)} %constant_dynamic-update-slice_fusion.5.in_ref, bf16[1536,2048]{1,0:T(8,128)(2,1)} %all-gather.9.cloned.1.call-done.gate_ref.up_ref, ...), custom_call_target="tpu_custom_call" | custom-call | flops 3221225472 | bytes 13107200 | tf_op jit(solution)/shard_map/ffn_forward/pallas_call | solution.py:218
  215.4 3.5 convolution_convert_fusion.2
  219.0 25.1 %all-gather.11.cloned.1.call-done.down_ref = bf16[1536,1024]{1,0:T(8,128)(2,1)} async-done(((bf16[192,1024]{1,0:T(8,128)(2,1)}), bf16[1536,1024]{1,0:T(8,128)(2,1)}) %all-gather.11.cloned.1.call-update) | async-done | bytes 3145744 | tf_op jit(solution)/shard_map/all_gather | solution.py:459
  244.1 11.4 %ffn_backward.1 = (bf16[512,2048]{1,0:T(8,128)(2,1)S(1)}, bf16[512,1536]{1,0:T(8,128)(2,1)S(1)}) custom-call(bf16[512,1536]{1,0:T(8,128)(2,1)S(1)} %multiply_convert_fusion.back_ref, bf16[1536,1024]{1,0:T(8,128)(2,1)} %all-gather.11.cloned.1.call-done.down_ref, bf16[1536,2048]{1,0:T(8,128)(2,1)} %all-gather.9.cloned.1.call-done.gate_ref.up_ref, ...), custom_call_target="tpu_custom_call" | custom-call | flops 4831838208 | bytes 20447232 | tf_op jit(solution)/shard_map/ffn_backward/pallas_call | solution.py:264
  256.7 5.4 %convolution_convert_fusion = bf16[1536,2048]{1,0:T(8,128)(2,1)} fusion(bf16[512,1536]{1,0:T(8,128)(2,1)S(1)} %constant_dynamic-update-slice_fusion.5.in_ref, bf16[512,2048]{1,0:T(8,128)(2,1)S(1)} %get-tuple-element.100), kind=kOutput, calls=%fused_computation | convolution fusion | flops 3224371200 | bytes 9961472 | tf_op jit(solution)/shard_map/dot_general | solution.py:36
  267.2 8.5 %collective-permute-done.30 = bf16[128,1536]{1,0:T(8,128)(2,1)S(1)} collective-permute-done((bf16[128,1536]{1,0:T(8,128)(2,1)S(1)}, bf16[128,1536]{1,0:T(8,128)(2,1)S(1)}, u32[]{:S(2)}, u32[]{:S(2)}) %collective-permute-start.30) | collective-permute-done | bytes 393248 | tf_op jit(solution)/shard_map/ppermute | solution.py:378
  275.7 8.9 %collective-permute-done.31 = bf16[128,1536]{1,0:T(8,128)(2,1)S(1)} collective-permute-done((bf16[128,1536]{1,0:T(8,128)(2,1)S(1)}, bf16[128,1536]{1,0:T(8,128)(2,1)S(1)}, u32[]{:S(2)}, u32[]{:S(2)}) %collective-permute-start.31) | collective-permute-done | bytes 393248 | tf_op jit(solution)/shard_map/ppermute | solution.py:378
  289.0 8.3 %collective-permute-done.33 = bf16[128,1536]{1,0:T(8,128)(2,1)S(1)} collective-permute-done((bf16[128,1536]{1,0:T(8,128)(2,1)S(1)}, bf16[128,1536]{1,0:T(8,128)(2,1)S(1)}, u32[]{:S(2)}, u32[]{:S(2)}) %collective-permute-start.33) | collective-permute-done | bytes 393248 | tf_op jit(solution)/shard_map/ppermute | solution.py:358
  299.6 3.5 collective-permute-done.35
  304.6 3.5 fusion.65
  312.9 23.6 %attention_backward.1 = (bf16[512,1152]{1,0:T(8,128)(2,1)S(1)}, bf16[256,768]{1,0:T(8,128)(2,1)S(1)}, f32[8,384]{1,0:T(8,128)S(1)}) custom-call(f32[512,1152]{1,0:T(8,128)} %copy-done.2, bf16[512,384]{1,0:T(8,128)(2,1)S(1)} %copy-done.15, bf16[512,384]{1,0:T(8,128)(2,1)S(1)} %copy-done.17, bf16[512,384]{1,0:T(8,128)(2,1)S(1)} %copy-done.19, ...), custom_call_target="tpu_custom_call" | custom-call | flops 1509949440 | bytes 9437184 | tf_op jit(solution)/shard_map/attention_backward/pallas_call | solution.py:181
  337.6 4.4 fusion.66
  342.1 2.7 convolution_convert_fusion.1
  344.8 2.6 pad_maximum_fusion
  347.6 1.7 collective-permute-done.43
  350.4 2.6 collective-permute-start.44
  358.5 7.9 %collective-permute-done.40 = bf16[128,1536]{1,0:T(8,128)(2,1)} collective-permute-done((bf16[128,1536]{1,0:T(8,128)(2,1)}, bf16[128,1536]{1,0:T(8,128)(2,1)}, u32[]{:S(2)}, u32[]{:S(2)}) %collective-permute-start.40) | collective-permute-done | bytes 393248 | tf_op jit(solution)/shard_map/ppermute | solution.py:378
  366.4 6.6 %collective-permute-done.41 = bf16[128,1536]{1,0:T(8,128)(2,1)} collective-permute-done((bf16[128,1536]{1,0:T(8,128)(2,1)}, bf16[128,1536]{1,0:T(8,128)(2,1)}, u32[]{:S(2)}, u32[]{:S(2)}) %collective-permute-start.41) | collective-permute-done | bytes 393248 | tf_op jit(solution)/shard_map/ppermute | solution.py:378
  373.1 2.7 collective-permute-done.44
  375.7 2.3 multiply_reduce_fusion.2
  378.2 3.5 multiply_reduce_fusion.1
  383.6 2.0 concatenate.127
  389.9 2.4 collective-permute-done.48
  393.2 31.6 %collective-permute-start.53 = (bf16[1,1536]{1,0:T(2,128)(2,1)S(1)}, bf16[1,1536]{1,0:T(2,128)(2,1)S(1)}, u32[]{:S(2)}, u32[]{:S(2)}) collective-permute-start(bf16[1,1536]{1,0:T(2,128)(2,1)S(1)} %fusion.43), channel_id=1, source_target_pairs={{0,4},{4,0},{8,12},{12,8},{16,20},{20,16},{24,28},{28,24},{1,5},{5... | collective-permute-start | bytes 9224 | tf_op jit(solution)/shard_map/ppermute | solution.py:316
  430.3 19.6 %collective-permute-start.55 = (bf16[4,1536]{1,0:T(4,128)(2,1)S(1)}, bf16[4,1536]{1,0:T(4,128)(2,1)S(1)}, u32[]{:S(2)}, u32[]{:S(2)}) collective-permute-start(bf16[4,1536]{1,0:T(4,128)(2,1)S(1)} %pad_maximum_fusion.17), channel_id=1, source_target_pairs={{0,16},{4,20},{8,24},{12,28},{16,0},{20,4},{24,8},{28,12},{1,17},{... | collective-permute-start | bytes 36872 | tf_op jit(solution)/shard_map/ppermute | solution.py:316
  449.9 2.5 collective-permute-start.51
  454.2 1.8 fusion.34
  456.0 2.8 collective-permute-done.52
  466.0 1.9 fusion.67
  469.1 1.9 widen.5
  471.0 2.3 widen.4
  473.3 2.1 widen.3
  (379 shorter events, 99.2 us)
Async XLA Ops:
  7.2 127.7 %all-gather.5.cloned.1.call-start = ((), (), s32[]{:S(2)}) async-start(), calls=%async_computation.3 | async-start | bytes 5308416 | tf_op jit(solution)/shard_map/all_gather | solution.py:454
  9.4 130.6 %all-gather.7.cloned.1.call-start = ((), (), s32[]{:S(2)}) async-start(), calls=%async_computation.4 | async-start | bytes 7077888 | tf_op jit(solution)/shard_map/all_gather | solution.py:454
  10.4 195.2 %all-gather.9.cloned.1.call-start = ((), (), s32[]{:S(2)}) async-start(), calls=%async_computation.5 | async-start | bytes 7077888 | tf_op jit(solution)/shard_map/all_gather | solution.py:454
  11.6 232.5 %all-gather.11.cloned.1.call-start = ((), (), s32[]{:S(2)}) async-start(), calls=%async_computation.6 | async-start | bytes 3538944 | tf_op jit(solution)/shard_map/all_gather | solution.py:459
  11.6 27.6 %collective-permute-start.6 = (bf16[128,1536]{1,0:T(8,128)(2,1)S(1)}, bf16[128,1536]{1,0:T(8,128)(2,1)}, u32[]{:S(2)}, u32[]{:S(2)}) collective-permute-start(bf16[128,1536]{1,0:T(8,128)(2,1)S(1)} %copy-done.26), channel_id=1, source_target_pairs={{0,1},{1,0},{2,3},{3,2},{4,5},{5,4},{6,7},{7,6},{8,9},{9,8},{10,11... | collective-permute-start | bytes 1179656 | tf_op jit(solution)/shard_map/ppermute | solution.py:358
  14.6 25.6 %collective-permute-start.7 = (bf16[128,1536]{1,0:T(8,128)(2,1)S(1)}, bf16[128,1536]{1,0:T(8,128)(2,1)}, u32[]{:S(2)}, u32[]{:S(2)}) collective-permute-start(bf16[128,1536]{1,0:T(8,128)(2,1)S(1)} %copy-done.26), channel_id=1, source_target_pairs={{0,2},{1,3},{2,0},{3,1},{4,6},{5,7},{6,4},{7,5},{8,10},{9,11},{10,... | collective-permute-start | bytes 1179656 | tf_op jit(solution)/shard_map/ppermute | solution.py:358
  25.0 11.9 %collective-permute-start.3 = (bf16[4,1,64,512]{3,2,0,1:T(8,128)(2,1)}, bf16[4,1,64,512]{3,2,0,1:T(8,128)(2,1)}, u32[]{:S(2)}, u32[]{:S(2)}) collective-permute-start(bf16[4,1,64,512]{3,2,0,1:T(8,128)(2,1)} %get-tuple-element.183), channel_id=1, source_target_pairs={{0,4},{4,0},{8,12},{12,8},{16,20},{20,16},{24,28},{28,24},{1,5},{5... | collective-permute-start | bytes 786440 | tf_op jit(solution)/shard_map/ppermute | solution.py:316
  25.7 321.7 %reduce-scatter.4.cloned.1.call-start = ((), (), s32[]{:S(2)}) async-start(), calls=%async_computation.7 | async-start | bytes 7077888 | tf_op jit(solution)/shard_map/reduce_scatter | solution.py:325
  27.2 4.6 collective-permute-start.1
  31.9 5.0 %collective-permute-start.2 = (bf16[4,1024]{1,0:T(4,128)(2,1)S(1)}, bf16[4,1024]{1,0:T(4,128)(2,1)S(1)}, u32[]{:S(2)}, u32[]{:S(2)}) collective-permute-start(bf16[4,1024]{1,0:T(4,128)(2,1)S(1)} %pad_maximum_fusion.18), channel_id=1, source_target_pairs={{0,16},{4,20},{8,24},{12,28},{16,0},{20,4},{24,8},{28,12},{1,17},{... | collective-permute-start | bytes 24584 | tf_op jit(solution)/shard_map/ppermute | solution.py:316
  38.1 24.7 %collective-permute-start.4 = (bf16[2,2,64,512]{3,2,0,1:T(8,128)(2,1)S(1)}, bf16[2,2,64,512]{3,2,0,1:T(8,128)(2,1)S(1)}, u32[]{:S(2)}, u32[]{:S(2)}) collective-permute-start(bf16[2,2,64,512]{3,2,0,1:T(8,128)(2,1)S(1)} %get-tuple-element.181), channel_id=1, source_target_pairs={{0,8},{4,12},{8,0},{12,4},{16,24},{20,28},{24,16},{28,20},{1,9},{5... | collective-permute-start | bytes 786440 | tf_op jit(solution)/shard_map/ppermute | solution.py:316
  40.2 23.4 %collective-permute-start.8 = (bf16[64,1536]{1,0:T(8,128)(2,1)S(1)}, bf16[64,1536]{1,0:T(8,128)(2,1)S(1)}, u32[]{:S(2)}, u32[]{:S(2)}) collective-permute-start(bf16[64,1536]{1,0:T(8,128)(2,1)S(1)} %slice.355), channel_id=1, source_target_pairs={{0,2},{1,3},{2,0},{3,1},{4,6},{5,7},{6,4},{7,5},{8,10},{9,11},{10,... | collective-permute-start | bytes 589832 | tf_op jit(solution)/shard_map/ppermute | solution.py:363
  41.2 22.4 %collective-permute-start.9 = (bf16[64,1536]{1,0:T(8,128)(2,1)S(1)}, bf16[64,1536]{1,0:T(8,128)(2,1)S(1)}, u32[]{:S(2)}, u32[]{:S(2)}) collective-permute-start(bf16[64,1536]{1,0:T(8,128)(2,1)S(1)} %slice.356), channel_id=1, source_target_pairs={{0,1},{1,0},{2,3},{3,2},{4,5},{5,4},{6,7},{7,6},{8,9},{9,8},{10,11... | collective-permute-start | bytes 589832 | tf_op jit(solution)/shard_map/ppermute | solution.py:364
  63.0 14.8 %collective-permute-start.5 = (bf16[1,4,64,512]{3,2,1,0:T(8,128)(2,1)S(1)}, bf16[1,4,64,512]{3,2,1,0:T(8,128)(2,1)S(1)}, u32[]{:S(2)}, u32[]{:S(2)}) collective-permute-start(bf16[1,4,64,512]{3,2,1,0:T(8,128)(2,1)S(1)} %get-tuple-element.179), channel_id=1, source_target_pairs={{0,16},{4,20},{8,24},{12,28},{16,0},{20,4},{24,8},{28,12},{1,17},{... | collective-permute-start | bytes 786440 | tf_op jit(solution)/shard_map/ppermute | solution.py:316
  78.2 4.8 collective-permute-start.10
  83.0 3.8 collective-permute-start.11
  86.8 4.0 collective-permute-start.12
  87.4 18.4 %collective-permute-start.15 = (bf16[8,1,64,512]{3,2,1,0:T(8,128)(2,1)S(1)}, bf16[8,1,64,512]{3,2,1,0:T(8,128)(2,1)}, u32[]{:S(2)}, u32[]{:S(2)}) collective-permute-start(bf16[8,1,64,512]{3,2,1,0:T(8,128)(2,1)S(1)} %bitcast.107), channel_id=1, source_target_pairs={{0,1},{1,0},{2,3},{3,2},{4,5},{5,4},{6,7},{7,6},{8,9},{9,8},{10,11... | collective-permute-start | bytes 1572872 | tf_op jit(solution)/shard_map/ppermute | solution.py:358
  89.1 20.1 %collective-permute-start.16 = (bf16[8,1,64,512]{3,2,1,0:T(8,128)(2,1)S(1)}, bf16[8,1,64,512]{3,2,1,0:T(8,128)(2,1)}, u32[]{:S(2)}, u32[]{:S(2)}) collective-permute-start(bf16[8,1,64,512]{3,2,1,0:T(8,128)(2,1)S(1)} %bitcast.108), channel_id=1, source_target_pairs={{0,2},{1,3},{2,0},{3,1},{4,6},{5,7},{6,4},{7,5},{8,10},{9,11},{10,... | collective-permute-start | bytes 1572872 | tf_op jit(solution)/shard_map/ppermute | solution.py:358
  90.9 11.1 %collective-permute-start.13 = (f32[1,1536]{1,0:T(1,128)S(1)}, f32[1,1536]{1,0:T(1,128)S(1)}, u32[]{:S(2)}, u32[]{:S(2)}) collective-permute-start(f32[1,1536]{1,0:T(1,128)S(1)} %slice_add_fusion.8), channel_id=1, source_target_pairs={{0,1},{1,0},{2,3},{3,2},{4,5},{5,4},{6,7},{7,6},{8,9},{9,8},{10,11... | collective-permute-start | bytes 18440 | tf_op jit(solution)/shard_map/ppermute | solution.py:507
  102.0 3.8 collective-permute-start.14
  107.5 7.4 %collective-permute-start.17 = (bf16[8,1,32,512]{3,2,1,0:T(8,128)(2,1)}, bf16[8,1,32,512]{3,2,1,0:T(8,128)(2,1)S(1)}, u32[]{:S(2)}, u32[]{:S(2)}) collective-permute-start(bf16[8,1,32,512]{3,2,1,0:T(8,128)(2,1)} %slice.367), channel_id=1, source_target_pairs={{0,2},{1,3},{2,0},{3,1},{4,6},{5,7},{6,4},{7,5},{8,10},{9,11},{10,... | collective-permute-start | bytes 786440 | tf_op jit(solution)/shard_map/ppermute | solution.py:363
  110.9 7.2 %collective-permute-start.18 = (bf16[8,1,32,512]{3,2,1,0:T(8,128)(2,1)}, bf16[8,1,32,512]{3,2,1,0:T(8,128)(2,1)S(1)}, u32[]{:S(2)}, u32[]{:S(2)}) collective-permute-start(bf16[8,1,32,512]{3,2,1,0:T(8,128)(2,1)} %slice.368), channel_id=1, source_target_pairs={{0,1},{1,0},{2,3},{3,2},{4,5},{5,4},{6,7},{7,6},{8,9},{9,8},{10,11... | collective-permute-start | bytes 786440 | tf_op jit(solution)/shard_map/ppermute | solution.py:364
  121.0 8.9 %collective-permute-start.26 = (bf16[128,1536]{1,0:T(8,128)(2,1)S(1)}, bf16[128,1536]{1,0:T(8,128)(2,1)S(1)}, u32[]{:S(2)}, u32[]{:S(2)}) collective-permute-start(bf16[128,1536]{1,0:T(8,128)(2,1)S(1)} %copy-done.29), channel_id=1, source_target_pairs={{0,1},{1,0},{2,3},{3,2},{4,5},{5,4},{6,7},{7,6},{8,9},{9,8},{10,11... | collective-permute-start | bytes 1179656 | tf_op jit(solution)/shard_map/ppermute | solution.py:358
  122.7 9.5 %collective-permute-start.27 = (bf16[128,1536]{1,0:T(8,128)(2,1)S(1)}, bf16[128,1536]{1,0:T(8,128)(2,1)S(1)}, u32[]{:S(2)}, u32[]{:S(2)}) collective-permute-start(bf16[128,1536]{1,0:T(8,128)(2,1)S(1)} %copy-done.29), channel_id=1, source_target_pairs={{0,2},{1,3},{2,0},{3,1},{4,6},{5,7},{6,4},{7,5},{8,10},{9,11},{10,... | collective-permute-start | bytes 1179656 | tf_op jit(solution)/shard_map/ppermute | solution.py:358
  130.6 38.2 %collective-permute-start.28 = (bf16[64,1536]{1,0:T(8,128)(2,1)}, bf16[64,1536]{1,0:T(8,128)(2,1)}, u32[]{:S(2)}, u32[]{:S(2)}) collective-permute-start(bf16[64,1536]{1,0:T(8,128)(2,1)} %slice.377), channel_id=1, source_target_pairs={{0,2},{1,3},{2,0},{3,1},{4,6},{5,7},{6,4},{7,5},{8,10},{9,11},{10,... | collective-permute-start | bytes 589832 | tf_op jit(solution)/shard_map/ppermute | solution.py:363
  132.9 37.6 %collective-permute-start.29 = (bf16[64,1536]{1,0:T(8,128)(2,1)}, bf16[64,1536]{1,0:T(8,128)(2,1)}, u32[]{:S(2)}, u32[]{:S(2)}) collective-permute-start(bf16[64,1536]{1,0:T(8,128)(2,1)} %slice.378), channel_id=1, source_target_pairs={{0,1},{1,0},{2,3},{3,2},{4,5},{5,4},{6,7},{7,6},{8,9},{9,8},{10,11... | collective-permute-start | bytes 589832 | tf_op jit(solution)/shard_map/ppermute | solution.py:364
  165.3 12.1 %collective-permute-start.19 = (bf16[128,1536]{1,0:T(8,128)(2,1)S(1)}, bf16[128,1536]{1,0:T(8,128)(2,1)S(1)}, u32[]{:S(2)}, u32[]{:S(2)}) collective-permute-start(bf16[128,1536]{1,0:T(8,128)(2,1)S(1)} %get-tuple-element.170), channel_id=1, source_target_pairs={{0,1},{1,0},{2,3},{3,2},{4,5},{5,4},{6,7},{7,6},{8,9},{9,8},{10,11... | collective-permute-start | bytes 1179656 | tf_op jit(solution)/shard_map/ppermute | solution.py:378
  166.9 18.7 %collective-permute-start.20 = (bf16[128,1536]{1,0:T(8,128)(2,1)S(1)}, bf16[128,1536]{1,0:T(8,128)(2,1)S(1)}, u32[]{:S(2)}, u32[]{:S(2)}) collective-permute-start(bf16[128,1536]{1,0:T(8,128)(2,1)S(1)} %get-tuple-element.172), channel_id=1, source_target_pairs={{0,2},{1,3},{2,0},{3,1},{4,6},{5,7},{6,4},{7,5},{8,10},{9,11},{10,... | collective-permute-start | bytes 1179656 | tf_op jit(solution)/shard_map/ppermute | solution.py:378
  167.7 17.9 %collective-permute-start.21 = (bf16[128,1536]{1,0:T(8,128)(2,1)S(1)}, bf16[128,1536]{1,0:T(8,128)(2,1)S(1)}, u32[]{:S(2)}, u32[]{:S(2)}) collective-permute-start(bf16[128,1536]{1,0:T(8,128)(2,1)S(1)} %get-tuple-element.171), channel_id=1, source_target_pairs={{0,3},{1,2},{2,1},{3,0},{4,7},{5,6},{6,5},{7,4},{8,11},{9,10},{10,... | collective-permute-start | bytes 1179656 | tf_op jit(solution)/shard_map/ppermute | solution.py:378
  187.0 10.0 %collective-permute-start.22 = (bf16[128,1536]{1,0:T(8,128)(2,1)S(1)}, bf16[128,1536]{1,0:T(8,128)(2,1)S(1)}, u32[]{:S(2)}, u32[]{:S(2)}) collective-permute-start(bf16[128,1536]{1,0:T(8,128)(2,1)S(1)} %get-tuple-element.155), channel_id=1, source_target_pairs={{0,1},{1,0},{2,3},{3,2},{4,5},{5,4},{6,7},{7,6},{8,9},{9,8},{10,11... | collective-permute-start | bytes 1179656 | tf_op jit(solution)/shard_map/ppermute | solution.py:358
  188.2 10.6 %collective-permute-start.23 = (bf16[128,1536]{1,0:T(8,128)(2,1)S(1)}, bf16[128,1536]{1,0:T(8,128)(2,1)S(1)}, u32[]{:S(2)}, u32[]{:S(2)}) collective-permute-start(bf16[128,1536]{1,0:T(8,128)(2,1)S(1)} %get-tuple-element.155), channel_id=1, source_target_pairs={{0,2},{1,3},{2,0},{3,1},{4,6},{5,7},{6,4},{7,5},{8,10},{9,11},{10,... | collective-permute-start | bytes 1179656 | tf_op jit(solution)/shard_map/ppermute | solution.py:358
  197.1 5.7 %collective-permute-start.24 = (bf16[64,1536]{1,0:T(8,128)(2,1)S(1)}, bf16[64,1536]{1,0:T(8,128)(2,1)S(1)}, u32[]{:S(2)}, u32[]{:S(2)}) collective-permute-start(bf16[64,1536]{1,0:T(8,128)(2,1)S(1)} %slice.375), channel_id=1, source_target_pairs={{0,2},{1,3},{2,0},{3,1},{4,6},{5,7},{6,4},{7,5},{8,10},{9,11},{10,... | collective-permute-start | bytes 589832 | tf_op jit(solution)/shard_map/ppermute | solution.py:363
  198.9 5.7 %collective-permute-start.25 = (bf16[64,1536]{1,0:T(8,128)(2,1)S(1)}, bf16[64,1536]{1,0:T(8,128)(2,1)S(1)}, u32[]{:S(2)}, u32[]{:S(2)}) collective-permute-start(bf16[64,1536]{1,0:T(8,128)(2,1)S(1)} %slice.376), channel_id=1, source_target_pairs={{0,1},{1,0},{2,3},{3,2},{4,5},{5,4},{6,7},{7,6},{8,9},{9,8},{10,11... | collective-permute-start | bytes 589832 | tf_op jit(solution)/shard_map/ppermute | solution.py:364
  262.2 206.9 %reduce-scatter.8.cloned.1.call-start = ((), (), s32[]{:S(2)}) async-start(), calls=%async_computation.9 | async-start | bytes 3538944 | tf_op jit(solution)/shard_map/reduce_scatter | solution.py:325
  262.8 210.6 %reduce-scatter.6.cloned.1.call-start = ((), (), s32[]{:S(2)}) async-start(), calls=%async_computation.8 | async-start | bytes 5308416 | tf_op jit(solution)/shard_map/reduce_scatter | solution.py:325
  263.7 12.0 %collective-permute-start.30 = (bf16[128,1536]{1,0:T(8,128)(2,1)S(1)}, bf16[128,1536]{1,0:T(8,128)(2,1)S(1)}, u32[]{:S(2)}, u32[]{:S(2)}) collective-permute-start(bf16[128,1536]{1,0:T(8,128)(2,1)S(1)} %get-tuple-element.167), channel_id=1, source_target_pairs={{0,1},{1,0},{2,3},{3,2},{4,5},{5,4},{6,7},{7,6},{8,9},{9,8},{10,11... | collective-permute-start | bytes 1179656 | tf_op jit(solution)/shard_map/ppermute | solution.py:378
  265.2 19.4 %collective-permute-start.31 = (bf16[128,1536]{1,0:T(8,128)(2,1)S(1)}, bf16[128,1536]{1,0:T(8,128)(2,1)S(1)}, u32[]{:S(2)}, u32[]{:S(2)}) collective-permute-start(bf16[128,1536]{1,0:T(8,128)(2,1)S(1)} %get-tuple-element.169), channel_id=1, source_target_pairs={{0,2},{1,3},{2,0},{3,1},{4,6},{5,7},{6,4},{7,5},{8,10},{9,11},{10,... | collective-permute-start | bytes 1179656 | tf_op jit(solution)/shard_map/ppermute | solution.py:378
  266.7 17.9 %collective-permute-start.32 = (bf16[128,1536]{1,0:T(8,128)(2,1)S(1)}, bf16[128,1536]{1,0:T(8,128)(2,1)S(1)}, u32[]{:S(2)}, u32[]{:S(2)}) collective-permute-start(bf16[128,1536]{1,0:T(8,128)(2,1)S(1)} %get-tuple-element.168), channel_id=1, source_target_pairs={{0,3},{1,2},{2,1},{3,0},{4,7},{5,6},{6,5},{7,4},{8,11},{9,10},{10,... | collective-permute-start | bytes 1179656 | tf_op jit(solution)/shard_map/ppermute | solution.py:378
  287.0 10.3 %collective-permute-start.33 = (bf16[128,1536]{1,0:T(8,128)(2,1)S(1)}, bf16[128,1536]{1,0:T(8,128)(2,1)S(1)}, u32[]{:S(2)}, u32[]{:S(2)}) collective-permute-start(bf16[128,1536]{1,0:T(8,128)(2,1)S(1)} %get-tuple-element.151), channel_id=1, source_target_pairs={{0,1},{1,0},{2,3},{3,2},{4,5},{5,4},{6,7},{7,6},{8,9},{9,8},{10,11... | collective-permute-start | bytes 1179656 | tf_op jit(solution)/shard_map/ppermute | solution.py:358
  288.2 10.6 %collective-permute-start.34 = (bf16[128,1536]{1,0:T(8,128)(2,1)S(1)}, bf16[128,1536]{1,0:T(8,128)(2,1)S(1)}, u32[]{:S(2)}, u32[]{:S(2)}) collective-permute-start(bf16[128,1536]{1,0:T(8,128)(2,1)S(1)} %get-tuple-element.151), channel_id=1, source_target_pairs={{0,2},{1,3},{2,0},{3,1},{4,6},{5,7},{6,4},{7,5},{8,10},{9,11},{10,... | collective-permute-start | bytes 1179656 | tf_op jit(solution)/shard_map/ppermute | solution.py:358
  297.3 5.7 %collective-permute-start.35 = (bf16[64,1536]{1,0:T(8,128)(2,1)S(1)}, bf16[64,1536]{1,0:T(8,128)(2,1)S(1)}, u32[]{:S(2)}, u32[]{:S(2)}) collective-permute-start(bf16[64,1536]{1,0:T(8,128)(2,1)S(1)} %slice.379), channel_id=1, source_target_pairs={{0,2},{1,3},{2,0},{3,1},{4,6},{5,7},{6,4},{7,5},{8,10},{9,11},{10,... | collective-permute-start | bytes 589832 | tf_op jit(solution)/shard_map/ppermute | solution.py:363
  298.8 5.7 %collective-permute-start.36 = (bf16[64,1536]{1,0:T(8,128)(2,1)S(1)}, bf16[64,1536]{1,0:T(8,128)(2,1)S(1)}, u32[]{:S(2)}, u32[]{:S(2)}) collective-permute-start(bf16[64,1536]{1,0:T(8,128)(2,1)S(1)} %slice.380), channel_id=1, source_target_pairs={{0,1},{1,0},{2,3},{3,2},{4,5},{5,4},{6,7},{7,6},{8,9},{9,8},{10,11... | collective-permute-start | bytes 589832 | tf_op jit(solution)/shard_map/ppermute | solution.py:364
  308.2 29.4 %collective-permute-start.37 = (bf16[128,1536]{1,0:T(8,128)(2,1)S(1)}, bf16[128,1536]{1,0:T(8,128)(2,1)S(1)}, u32[]{:S(2)}, u32[]{:S(2)}) collective-permute-start(bf16[128,1536]{1,0:T(8,128)(2,1)S(1)} %get-tuple-element.166), channel_id=1, source_target_pairs={{0,1},{1,0},{2,3},{3,2},{4,5},{5,4},{6,7},{7,6},{8,9},{9,8},{10,11... | collective-permute-start | bytes 1179656 | tf_op jit(solution)/shard_map/ppermute | solution.py:378
  308.9 28.7 %collective-permute-start.38 = (bf16[128,1536]{1,0:T(8,128)(2,1)S(1)}, bf16[128,1536]{1,0:T(8,128)(2,1)S(1)}, u32[]{:S(2)}, u32[]{:S(2)}) collective-permute-start(bf16[128,1536]{1,0:T(8,128)(2,1)S(1)} %get-tuple-element.165), channel_id=1, source_target_pairs={{0,2},{1,3},{2,0},{3,1},{4,6},{5,7},{6,4},{7,5},{8,10},{9,11},{10,... | collective-permute-start | bytes 1179656 | tf_op jit(solution)/shard_map/ppermute | solution.py:378
  310.4 27.2 %collective-permute-start.39 = (bf16[128,1536]{1,0:T(8,128)(2,1)S(1)}, bf16[128,1536]{1,0:T(8,128)(2,1)S(1)}, u32[]{:S(2)}, u32[]{:S(2)}) collective-permute-start(bf16[128,1536]{1,0:T(8,128)(2,1)S(1)} %get-tuple-element.164), channel_id=1, source_target_pairs={{0,3},{1,2},{2,1},{3,0},{4,7},{5,6},{6,5},{7,4},{8,11},{9,10},{10,... | collective-permute-start | bytes 1179656 | tf_op jit(solution)/shard_map/ppermute | solution.py:378
  350.4 25.4 %collective-permute-start.44 = (bf16[512,768]{1,0:T(8,128)(2,1)}, bf16[512,768]{1,0:T(8,128)(2,1)S(1)}, u32[]{:S(2)}, u32[]{:S(2)}) collective-permute-start(bf16[512,768]{1,0:T(8,128)(2,1)} %pad_maximum_fusion.3), channel_id=1, source_target_pairs={{0,8},{8,16},{16,24},{12,4},{20,12},{28,20},{1,9},{9,17},{17,25},{... | collective-permute-start | bytes 2359304 | tf_op jit(solution)/shard_map/ppermute | solution.py:341
  354.0 12.4 %collective-permute-start.40 = (bf16[128,1536]{1,0:T(8,128)(2,1)}, bf16[128,1536]{1,0:T(8,128)(2,1)}, u32[]{:S(2)}, u32[]{:S(2)}) collective-permute-start(bf16[128,1536]{1,0:T(8,128)(2,1)} %get-tuple-element.163), channel_id=1, source_target_pairs={{0,1},{1,0},{2,3},{3,2},{4,5},{5,4},{6,7},{7,6},{8,9},{9,8},{10,11... | collective-permute-start | bytes 1179656 | tf_op jit(solution)/shard_map/ppermute | solution.py:378
  354.6 18.5 %collective-permute-start.41 = (bf16[128,1536]{1,0:T(8,128)(2,1)}, bf16[128,1536]{1,0:T(8,128)(2,1)}, u32[]{:S(2)}, u32[]{:S(2)}) collective-permute-start(bf16[128,1536]{1,0:T(8,128)(2,1)} %get-tuple-element.162), channel_id=1, source_target_pairs={{0,2},{1,3},{2,0},{3,1},{4,6},{5,7},{6,4},{7,5},{8,10},{9,11},{10,... | collective-permute-start | bytes 1179656 | tf_op jit(solution)/shard_map/ppermute | solution.py:378
  356.0 17.1 %collective-permute-start.42 = (bf16[128,1536]{1,0:T(8,128)(2,1)}, bf16[128,1536]{1,0:T(8,128)(2,1)}, u32[]{:S(2)}, u32[]{:S(2)}) collective-permute-start(bf16[128,1536]{1,0:T(8,128)(2,1)} %get-tuple-element.161), channel_id=1, source_target_pairs={{0,3},{1,2},{2,1},{3,0},{4,7},{5,6},{6,5},{7,4},{8,11},{9,10},{10,... | collective-permute-start | bytes 1179656 | tf_op jit(solution)/shard_map/ppermute | solution.py:378
  381.8 6.8 %collective-permute-start.47 = (f32[2,1536]{1,0:T(2,128)S(1)}, f32[2,1536]{1,0:T(2,128)S(1)}, u32[]{:S(2)}, u32[]{:S(2)}) collective-permute-start(f32[2,1536]{1,0:T(2,128)S(1)} %select_bitcast_fusion), channel_id=1, source_target_pairs={{0,2},{1,3},{2,0},{3,1},{4,6},{5,7},{6,4},{7,5},{8,10},{9,11},{10,... | collective-permute-start | bytes 36872 | tf_op jit(solution)/shard_map/ppermute | solution.py:640
  385.6 3.7 collective-permute-start.45
  387.1 6.1 %collective-permute-start.49 = (bf16[512,768]{1,0:T(8,128)(2,1)}, bf16[512,768]{1,0:T(8,128)(2,1)}, u32[]{:S(2)}, u32[]{:S(2)}) collective-permute-start(bf16[512,768]{1,0:T(8,128)(2,1)} %copy-done.39), channel_id=1, source_target_pairs={{8,16},{16,24},{12,4},{20,12},{9,17},{17,25},{13,5},{21,13},{10,18... | collective-permute-start | bytes 2359304 | tf_op jit(solution)/shard_map/ppermute | solution.py:341
  388.6 3.7 collective-permute-start.48
  389.3 3.8 collective-permute-start.46
  393.2 33.1 %collective-permute-start.53 = (bf16[1,1536]{1,0:T(2,128)(2,1)S(1)}, bf16[1,1536]{1,0:T(2,128)(2,1)S(1)}, u32[]{:S(2)}, u32[]{:S(2)}) collective-permute-start(bf16[1,1536]{1,0:T(2,128)(2,1)S(1)} %fusion.43), channel_id=1, source_target_pairs={{0,4},{4,0},{8,12},{12,8},{16,20},{20,16},{24,28},{28,24},{1,5},{5... | collective-permute-start | bytes 9224 | tf_op jit(solution)/shard_map/ppermute | solution.py:316
  424.8 34.1 %collective-permute-start.56 = (bf16[512,768]{1,0:T(8,128)(2,1)}, bf16[512,768]{1,0:T(8,128)(2,1)}, u32[]{:S(2)}, u32[]{:S(2)}) collective-permute-start(bf16[512,768]{1,0:T(8,128)(2,1)} %collective-permute-done.49), channel_id=1, source_target_pairs={{16,24},{12,4},{17,25},{13,5},{18,26},{14,6},{19,27},{15,7}} | collective-permute-start | bytes 2359304 | tf_op jit(solution)/shard_map/ppermute | solution.py:341
  426.3 4.0 collective-permute-start.54
  427.6 22.3 %collective-permute-start.50 = (f32[3224]{0:T(1024)S(1)}, f32[3224]{0:T(1024)S(1)}, u32[]{:S(2)}, u32[]{:S(2)}) collective-permute-start(f32[3224]{0:T(1024)S(1)} %bitcast.119), channel_id=1, source_target_pairs={{0,4},{4,0},{8,12},{12,8},{16,20},{20,16},{24,28},{28,24},{1,5},{5... | collective-permute-start | bytes 38696 | tf_op jit(solution)/shard_map/ppermute | solution.py:402
  430.3 23.9 %collective-permute-start.55 = (bf16[4,1536]{1,0:T(4,128)(2,1)S(1)}, bf16[4,1536]{1,0:T(4,128)(2,1)S(1)}, u32[]{:S(2)}, u32[]{:S(2)}) collective-permute-start(bf16[4,1536]{1,0:T(4,128)(2,1)S(1)} %pad_maximum_fusion.17), channel_id=1, source_target_pairs={{0,16},{4,20},{8,24},{12,28},{16,0},{20,4},{24,8},{28,12},{1,17},{... | collective-permute-start | bytes 36872 | tf_op jit(solution)/shard_map/ppermute | solution.py:316
  449.9 4.3 collective-permute-start.51
  453.8 10.3 %collective-permute-start.59 = (bf16[512,768]{1,0:T(8,128)(2,1)S(1)}, bf16[512,768]{1,0:T(8,128)(2,1)S(1)}, u32[]{:S(2)}, u32[]{:S(2)}) collective-permute-start(bf16[512,768]{1,0:T(8,128)(2,1)S(1)} %copy-done.40), channel_id=1, source_target_pairs={{0,4},{4,0},{8,12},{12,8},{16,20},{20,16},{24,28},{28,24},{1,5},{5... | collective-permute-start | bytes 2359304 | tf_op jit(solution)/shard_map/ppermute | solution.py:313
  454.2 4.6 collective-permute-start.52
  458.8 3.7 collective-permute-start.57
  (73 other events, 1314.5 us)
Sparse Core Ops, SparseCore 0:
  10.3 59.8 all-gather.4
  72.4 67.5 all-gather.6
  142.2 63.3 all-gather.8
  207.1 36.9 all-gather.10
  262.3 68.6 reduce-scatter.3
  333.1 45.9 reduce-scatter.7
  381.4 62.6 reduce-scatter.5

commit v3 on v2

--- a/solution.py
+++ b/solution.py
@@ -345,13 +345,13 @@
             while len(self.twins) <= last:
                 self.twins.append(twin(self.got[len(self.twins)]))
 
-        def full(self, chip, core, place):
+        def full(self, chip, core):
             rows, columns = self.got[0].shape
             whole = jnp.zeros((n_z, rows, columns), self.got[0].dtype)
             for k in range(n_z):
                 block = self.got[0] if k == 0 else self.got[k] + self.twins[n_z - k]
                 at = jnp.where(core == 0, lax.rem(chip + n_z - k, n_z), lax.rem(chip + k, n_z))
-                whole = lax.dynamic_update_slice(whole, block[None], (place(at), 0, 0))
+                whole = lax.dynamic_update_slice(whole, block[None], (at, 0, 0))
             return whole.reshape(n_z * rows, columns)
 
     def seq_near(block):
@@ -444,54 +444,24 @@
         chip = fsdp_index // 2
         core = fsdp_index % 2
 
-        def straight(t):
-            return t
-
-        def turned(t):
-            return t ^ chip
-
         def fsdp_gather(*parts):
             return lax.all_gather(jnp.concatenate(parts, axis=1), "fsdp", axis=0, tiled=True)
 
         attn_full = fsdp_gather(query_weight, key_weight, value_weight, output_weight.T)
-        text_full = fsdp_gather(textkey_weight, textvalue_weight)
-        ffn_full = fsdp_gather(gate_weight, up_weight)
-        down_t = lax.all_gather(down_weight.T, "fsdp", axis=0, tiled=True)
         qkv_full = attn_full[:, : 3 * columns]
         output_t = attn_full[:, 3 * columns :]
         cap_rows = text_rows // n_s
         cap_columns = textkey_weight.shape[0]
         cap_piece = lax.dynamic_slice_in_dim(caption, seq_index * cap_rows, cap_rows, 0)
-        cap_mine = jnp.stack(
-            [
-                lax.dynamic_slice_in_dim(cap_piece, (fsdp_index ^ k) * cap_columns, cap_columns, 1)
-                for k in range(n_f)
-            ]
-        )
-        bit = 1
-        while bit < n_f:
-            split = cap_mine.reshape(n_f // (2 * bit), 2, bit, cap_rows, cap_columns)
-            got = fsdp_xor(split[:, 1], bit)
-            cap_mine = jnp.stack([split[:, 0], got], axis=1).reshape(n_f, cap_rows, cap_columns)
-            bit *= 2
-        cap_mine = cap_mine.reshape(n_z, 2, cap_rows, cap_columns)
-        cap_mine = jnp.stack(
-            [
-                jnp.where(core == 0, cap_mine[:, 0], cap_mine[:, 1]),
-                jnp.where(core == 0, cap_mine[:, 1], cap_mine[:, 0]),
-            ],
-            axis=1,
-        )
-        cap_mine = cap_mine.reshape(n_f, cap_rows, cap_columns)
-        cond_low = jax.nn.silu(condition.astype(f32)).astype(bf16)
+        cap_mine = cap_piece.reshape(cap_rows, n_f, cap_columns).transpose(1, 0, 2)
+        cap_mine = lax.all_to_all(cap_mine, "fsdp", 0, 0)
+        cond_low = jax.nn.silu(after(condition, cap_mine).astype(f32)).astype(bf16)
         cond_all = cond_low
         bit = 1
         while bit < n_f:
             cond_all = jnp.concatenate([cond_all, fsdp_xor(cond_all, bit)], axis=0)
             bit *= 2
         tokens_all = seq_gather(tokens)
-        cond_all, cap_mine, tokens_all = stage(cond_all, cap_mine, tokens_all)
-
         mod_rows = modulator.shape[0]
         cond_mine = lax.dynamic_slice_in_dim(cond_all, fsdp_index * mod_rows, mod_rows, 1)
         mod_part = dot(cond_mine, modulator)
@@ -508,8 +478,12 @@
             )
             bit *= 2
         modulation = by_seq(modulation, seq_index).reshape(-1)
-        modulation, cap_all = stage(modulation, cap_all)
         cap_all = cap_all.reshape(n_f * text_rows, cap_columns)
+        text_own = jnp.concatenate([textkey_weight, textvalue_weight], axis=1)
+        text_part = dot(cap_all, text_own).astype(bf16)
+        text_both = fsdp_scatter(text_part)
+        ffn_full = fsdp_gather(after(gate_weight, text_part), up_weight)
+        down_t = lax.all_gather(down_weight.T, "fsdp", axis=0, tiled=True)
         tokens_all = tokens_all.astype(f32)
         cotangent_all = seq_gather(after(cotangent, cap_all)).astype(f32)
 
@@ -522,6 +496,9 @@
 
         order = [seq_index ^ k for k in range(n_s)]
         row_index = jnp.concatenate([order[k] * rows + jnp.arange(rows) for k in range(n_s)])
+        text_index = jnp.concatenate(
+            [order[k] * cap_rows + jnp.arange(cap_rows) for k in range(n_s)]
+        )
         places = jnp.concatenate(
             [lax.dynamic_slice_in_dim(positions, order[k] * rows, rows, 1) for k in range(n_s)],
             axis=1,
@@ -533,13 +510,12 @@
         inv_attn = inv_attn_all[:rows]
         unit_attn = inputs * inv_attn
         qkv = dot(normed_all, qkv_full)
-        text_both = dot(caption, text_full).astype(bf16)
         cosine, sine = rope_tables(places, head_size)
         cosine = jnp.concatenate([cosine, cosine], axis=1)
         sine = jnp.concatenate([-sine, sine], axis=1)
         gains = jnp.zeros((8, head_size), f32).at[0].set(query_gain).at[1].set(key_gain)
         mask = jnp.where(row_index < length, 0.0, masked_score).astype(f32)[None, :]
-        text_mask = jnp.where(jnp.arange(text_rows) < text_length, 0.0, masked_score).astype(f32)[None, :]
+        text_mask = jnp.where(text_index < text_length, 0.0, masked_score).astype(f32)[None, :]
         gate_heads = jnp.tanh(lax.dynamic_slice_in_dim(cross_gate, seq_index * heads, heads))
         gate_row = jnp.repeat(gate_heads, head_size)[None, :]
         query_rot, key_rot, value_low, mixed_rows, cross_out, lse = attention_forward(
@@ -562,8 +538,8 @@
         )
         parts = seq_send(grad_sent, rows)
         act_part = dot_tn(ffn_all, grad_act).astype(bf16)
-        act_grads = fsdp_scatter(act_part)
-        parts[0] = after(parts[0], act_part)
+        *parts, act_part = stage(*parts, act_part)
+        act_grads = fsdp_scatter(after(act_part, down_grads))
         grad_ffn_in = seq_sum(grad_sent, parts, rows)
         grad_out = cotangent.astype(f32)
         grad_ffn_gain = jnp.sum(grad_ffn_in * unit_ffn * (1.0 + scale_ffn), axis=0)
@@ -585,11 +561,7 @@
         )
         qkv_rows, text_grads_rows, *ffn_parts = stage(qkv_rows, text_grads_rows, *ffn_parts)
 
-        text_order = [
-            lax.dynamic_slice_in_dim(text_grads_rows, order[k] * cap_rows, cap_rows, 0)
-            for k in range(n_s)
-        ]
-        text_back = Gather(jnp.concatenate(text_order, axis=0), core)
+        text_back = Gather(text_grads_rows, core)
         text_back.step(1)
         normed_sent = dot_nt(qkv_rows, qkv_full)
         parts = seq_send(normed_sent, rows)
@@ -613,11 +585,13 @@
         grad_gate_heads = jnp.sum(
             head_sums[2, :columns].reshape(heads, head_size), axis=1
         ) * (1.0 - gate_heads * gate_heads)
-        attn_grads = fsdp_scatter(after(attn_part, act_grads))
-        *parts, text_back.got[1] = stage(*parts, text_back.got[1])
-
-        text_back.step(2)
-        text_back.pass_on(1)
+        attn_part, act_grads, text_back.got[1] = stage(attn_part, act_grads, text_back.got[1])
+        attn_grads = fsdp_scatter(attn_part)
+        act_grads = widen(act_grads, 2)
+        down_grads = widen(down_grads, 1)[0]
+        *parts, down_grads, gate_grads, up_grads = stage(*parts, down_grads, *act_grads)
+        text_back.step()
+        text_back.pass_on()
         grad_normed = seq_sum(normed_sent, parts, rows)
         grad_attn_gain = jnp.sum(grad_normed * unit_attn * (1.0 + scale_attn), axis=0)
         grad_scale_attn = jnp.sum(grad_normed * unit_attn * attn_gain, axis=0)
@@ -640,10 +614,6 @@
             mod_mine = mod_mine[:half] + lax.ppermute(mod_mine[half:], "seq", swaps[half])
             half //= 2
         mod_mine = mod_mine.astype(bf16)
-        sizes, mod_mine, text_back.got[2] = stage(sizes, mod_mine, text_back.got[2])
-
-        text_back.step()
-        text_back.pass_on(2)
         bit = 1
         while bit < n_f:
             mod_mine = jnp.concatenate([mod_mine, fsdp_xor(mod_mine, bit)], axis=0)
@@ -652,15 +622,8 @@
         totals = sizes[-3:]
         residual_rms = jnp.sqrt(totals / (length.astype(f32) * width))[:, None]
         small = all_sum(sizes[:-3], "fsdp", n_f)
-        small, modulator_grad, text_back.got[-1] = stage(
-            small, modulator_grad, text_back.got[-1]
-        )
-
-        text_back.pass_on()
-        text_grads = dot_tn(cap_all, text_back.full(chip, core, turned))
+        text_grads = dot_tn(cap_all, text_back.full(chip, core))
         attn_grads = widen(attn_grads, 4)
-        act_grads = widen(act_grads, 2)
-        down_grads = widen(down_grads, 1)[0]
         n_heads = cross_gate.shape[0]
         ends = [width, width, n_heads, head_size, head_size]
         ends = [sum(ends[:i]) for i in range(6)]
@@ -674,7 +637,8 @@
             attn_grads[3].T,
             text_grads[:, :columns],
             text_grads[:, columns:],
-            *act_grads,
+            gate_grads,
+            up_grads,
             down_grads.T,
             small[0],
             small[1],

time: 488 us -> 438 us (0.90)
  waiting for transfers between devices: 181 us -> 123 us
  blocking collectives: 0 us -> 31.5 us
  starting transfers between devices: 113 us -> 95.7 us
  other arithmetic: 30.1 us -> 24.6 us
    ppermute x12 -> x9, waiting for transfers between devices: 47.6 us -> 7.42 us  [fsdp_xor(): return lax.ppermute(block, 'fsdp', [(i, i ^ k) for i in range(n_f)])]
    ppermute x12 -> x9, starting transfers between devices: 58.6 us -> 21 us  [fsdp_xor(): return lax.ppermute(block, 'fsdp', [(i, i ^ k) for i in range(n_f)])]
    all_to_all x0 -> x1, blocking collectives: none -> 31.5 us  [local(): cap_mine = lax.all_to_all(cap_mine, 'fsdp', 0, 0)]
    ppermute x5, starting transfers between devices: 6.06 us -> 20.4 us  [all_sum(): lax.ppermute(block, axis, [(i, i ^ bit) for i in range(size)])]
    ppermute x12, waiting for transfers between devices: 45.5 us -> 34.1 us  [seq_send(): lax.ppermute(total[k * rows:(k + 1) * rows].astype(bf16), 'seq', swaps[k])]
    ppermute x2, waiting for transfers between devices: 12.4 us -> 4.01 us  [local(): lax.ppermute(modulation, 'seq', swaps[bit])]
    ppermute x10, waiting for transfers between devices: 21.9 us -> 30.1 us  [seq_near(): return [lax.ppermute(block, 'seq', swaps[k]) for k in (1, 2)]]
    ppermute x4, starting transfers between devices: 0.64 us -> 7.67 us  [twin(): return lax.ppermute(block, 'fsdp', [(i, i ^ 1) for i in range(n_f)])]
  transfers between devices with their start and end apart: 67 -> 64, of which waited for: 35 -> 32; matrix products, arithmetic and copies ran while one was open for 19% -> 20% of each run, Pallas kernels for 11% -> 15%
where the time goes in v3:
time: 438 us; the launch traced here: 433 us
  waiting for transfers between devices  123 us (28%)
  starting transfers between devices  95.7 us (22%)
  Pallas kernels  64.9 us (15%)
  matrix products  39.3 us (9%)
  local copies, waits for them, and re-layouts  35.7 us (8%)
  blocking collectives  31.5 us (7%)
  other arithmetic  24.6 us (6%)
  between operations  17.5 us (4%)
    ppermute x12, waiting for transfers between devices, seq_send(): lax.ppermute(total[k * rows:(k + 1) * rows].astype(bf16), 'seq', swaps[k])  34.1 us
    all_to_all x1, blocking collectives, local(): cap_mine = lax.all_to_all(cap_mine, 'fsdp', 0, 0)  31.5 us
    ppermute x10, waiting for transfers between devices, seq_near(): return [lax.ppermute(block, 'seq', swaps[k]) for k in (1, 2)]  30.1 us
    pallas_call x1, Pallas kernels, attention_backward(): pl.pallas_call(kernel, out_shape=(jax.ShapeDtypeStruct((rows, 3 * columns...  23.6 us
    ppermute x9, starting transfers between devices, fsdp_xor(): return lax.ppermute(block, 'fsdp', [(i, i ^ k) for i in range(n_f)])  21 us
    ppermute x5, starting transfers between devices, all_sum(): lax.ppermute(block, axis, [(i, i ^ bit) for i in range(size)])  20.4 us
    all_gather x1, waiting for transfers between devices, local(): down_t = lax.all_gather(down_weight.T, 'fsdp', axis=0, tiled=True)  19.7 us
    unnamed x177, local copies, waits for them, and re-layouts  18.6 us
  transfers between devices with their start and end apart: 64, of which 32 were waited for; matrix products, arithmetic and copies ran while one was open for 20% of the time, Pallas kernels for 15%

profile of v3, /device:TPU:0, one launch (start us, length us, event | category | flops | bytes accessed | tf_op | source)
XLA Modules:
  0.0 432.6 jit_solution(10152879652473163484)
XLA Ops:
  7.3 2.1 pad_maximum_fusion.3
  9.9 31.5 %all_to_all.5 = bf16[8,64,512]{2,1,0:T(8,128)(2,1)S(1)} all-to-all(bf16[8,64,512]{2,1,0:T(8,128)(2,1)S(1)} %copy.50), channel_id=1, replica_groups=mesh['fsdp'=8,'seq'=4] {'fsdp'}, dimensions={0} | all-to-all | bytes 1048576 | tf_op jit(solution)/shard_map/all_to_all | solution.py:457
  44.4 8.3 %collective-permute-done.12 = bf16[8,1,64,512]{3,2,1,0:T(8,128)(2,1)S(1)} collective-permute-done((bf16[8,1,64,512]{3,2,1,0:T(8,128)(2,1)S(1)}, bf16[8,1,64,512]{3,2,1,0:T(8,128)(2,1)S(1)}, u32[]{:S(2)}, u32[]{:S(2)}) %collective-permute-start.12) | collective-permute-done | bytes 524320 | tf_op jit(solution)/shard_map/ppermute | solution.py:358
  52.7 1.6 collective-permute-start.14
  56.1 3.4 collective-permute-done.14
  59.5 2.7 collective-permute-done.15
  63.8 3.5 convolution_convert_fusion.3
  81.0 5.2 %collective-permute-start.2 = (bf16[4,1024]{1,0:T(4,128)(2,1)S(1)}, bf16[4,1024]{1,0:T(4,128)(2,1)S(1)}, u32[]{:S(2)}, u32[]{:S(2)}) collective-permute-start(bf16[4,1024]{1,0:T(4,128)(2,1)S(1)} %pad_maximum_fusion.11), channel_id=1, source_target_pairs={{0,16},{4,20},{8,24},{12,28},{16,0},{20,4},{24,8},{28,12},{1,17},{... | collective-permute-start | bytes 24584 | tf_op jit(solution)/shard_map/ppermute | solution.py:316
  89.5 2.7 collective-permute-start.3
  93.3 2.0 collective-permute-done.3
  95.3 2.2 collective-permute-start.4
  97.5 2.2 collective-permute-done.4
  102.8 1.8 collective-permute-done.6
  104.7 1.6 collective-permute-start.7
  106.3 2.2 collective-permute-done.7
  111.7 6.8 %collective-permute-done.23 = bf16[128,1536]{1,0:T(8,128)(2,1)S(1)} collective-permute-done((bf16[128,1536]{1,0:T(8,128)(2,1)S(1)}, bf16[128,1536]{1,0:T(8,128)(2,1)S(1)}, u32[]{:S(2)}, u32[]{:S(2)}) %collective-permute-start.23) | collective-permute-done | bytes 393248 | tf_op jit(solution)/shard_map/ppermute | solution.py:358
  123.5 5.0 %fusion.6.qkv_ref = f32[512,1152]{1,0:T(8,128)S(1)} fusion(bf16[1536,1536]{1,0:T(8,128)(2,1)} %all-gather.4.cloned.1.call-done, bf16[512,1536]{1,0:T(8,128)(2,1)} %copy-done.32, f32[1536]{0:T(1024)S(1)} %get-tuple-element.179, f32[1536]{0:T(1024)S(1)} %copy-done.60, f32[512]{0:T(512)S(1)} %add_rsqrt_fusion), kind=kOutput, calls=%fused_computation.14 | convolution fusion | flops 1815871488 | bytes 7485440 | tf_op jit(solution)/shard_map/dot_general | solution.py:28
  129.8 16.0 %attention_forward.1 = (bf16[512,384]{1,0:T(8,128)(2,1)S(1)}, bf16[512,384]{1,0:T(8,128)(2,1)S(1)}, bf16[512,384]{1,0:T(8,128)(2,1)S(1)}, bf16[512,384]{1,0:T(8,...) custom-call(f32[512,1152]{1,0:T(8,128)S(1)} %fusion.6.qkv_ref, bf16[256,768]{1,0:T(8,128)(2,1)S(1)} %copy-done.9, ...), custom_call_target="tpu_custom_call" | custom-call | flops 603979776 | bytes 6291456 | tf_op jit(solution)/shard_map/attention_forward/pallas_call | solution.py:88
  145.9 3.2 fusion.69
  149.3 1.8 collective-permute-start.16
  152.9 1.6 constant_dynamic-update-slice_fusion.11
  154.5 1.6 constant_dynamic-update-slice_fusion.10
  156.1 5.3 %collective-permute-done.16 = bf16[128,1536]{1,0:T(8,128)(2,1)S(1)} collective-permute-done((bf16[128,1536]{1,0:T(8,128)(2,1)S(1)}, bf16[128,1536]{1,0:T(8,128)(2,1)S(1)}, u32[]{:S(2)}, u32[]{:S(2)}) %collective-permute-start.16) | collective-permute-done | bytes 393248 | tf_op jit(solution)/shard_map/ppermute | solution.py:378
  161.4 5.8 %collective-permute-done.17 = bf16[128,1536]{1,0:T(8,128)(2,1)S(1)} collective-permute-done((bf16[128,1536]{1,0:T(8,128)(2,1)S(1)}, bf16[128,1536]{1,0:T(8,128)(2,1)S(1)}, u32[]{:S(2)}, u32[]{:S(2)}) %collective-permute-start.17) | collective-permute-done | bytes 393248 | tf_op jit(solution)/shard_map/ppermute | solution.py:378
  170.8 1.7 multiply_convert_fusion.back_ref
  172.5 5.3 %collective-permute-done.19 = bf16[128,1536]{1,0:T(8,128)(2,1)S(1)} collective-permute-done((bf16[128,1536]{1,0:T(8,128)(2,1)S(1)}, bf16[128,1536]{1,0:T(8,128)(2,1)S(1)}, u32[]{:S(2)}, u32[]{:S(2)}) %collective-permute-start.19) | collective-permute-done | bytes 393248 | tf_op jit(solution)/shard_map/ppermute | solution.py:358
  180.8 2.7 collective-permute-done.21
  185.0 7.5 %ffn_forward.1 = (bf16[512,1024]{1,0:T(8,128)(2,1)S(1)}, f32[512,1024]{1,0:T(8,128)S(1)}, f32[512,1024]{1,0:T(8,128)}) custom-call(bf16[512,1536]{1,0:T(8,128)(2,1)S(1)} %constant_dynamic-update-slice_fusion.5.in_ref, bf16[1536,2048]{1,0:T(8,128)(2,1)} %all-gather.6.cloned.1.call-done.gate_ref.up_ref, ...), custom_call_target="tpu_custom_call" | custom-call | flops 3221225472 | bytes 13107200 | tf_op jit(solution)/shard_map/ffn_forward/pallas_call | solution.py:218
  194.9 3.5 convolution_convert_fusion.2
  198.5 19.7 %all-gather.8.cloned.1.call-done.down_ref = bf16[1536,1024]{1,0:T(8,128)(2,1)} async-done(((bf16[192,1024]{1,0:T(8,128)(2,1)}), bf16[1536,1024]{1,0:T(8,128)(2,1)}) %all-gather.8.cloned.1.call-update) | async-done | bytes 3145744 | tf_op jit(solution)/shard_map/all_gather | solution.py:486
  218.2 11.4 %ffn_backward.1 = (bf16[512,2048]{1,0:T(8,128)(2,1)S(1)}, bf16[512,1536]{1,0:T(8,128)(2,1)S(1)}) custom-call(bf16[512,1536]{1,0:T(8,128)(2,1)S(1)} %multiply_convert_fusion.back_ref, bf16[1536,1024]{1,0:T(8,128)(2,1)} %all-gather.8.cloned.1.call-done.down_ref, bf16[1536,2048]{1,0:T(8,128)(2,1)} %all-gather.6.cloned.1.call-done.gate_ref.up_ref, ...), custom_call_target="tpu_custom_call" | custom-call | flops 4831838208 | bytes 20447232 | tf_op jit(solution)/shard_map/ffn_backward/pallas_call | solution.py:264
  235.3 5.4 %convolution_convert_fusion = bf16[1536,2048]{1,0:T(8,128)(2,1)} fusion(bf16[512,1536]{1,0:T(8,128)(2,1)S(1)} %constant_dynamic-update-slice_fusion.5.in_ref, bf16[512,2048]{1,0:T(8,128)(2,1)S(1)} %get-tuple-element.96), kind=kOutput, calls=%fused_computation | convolution fusion | flops 3224371200 | bytes 9961472 | tf_op jit(solution)/shard_map/dot_general | solution.py:36
  240.7 3.3 collective-permute-done.27
  244.0 8.9 %collective-permute-done.28 = bf16[128,1536]{1,0:T(8,128)(2,1)} collective-permute-done((bf16[128,1536]{1,0:T(8,128)(2,1)}, bf16[128,1536]{1,0:T(8,128)(2,1)}, u32[]{:S(2)}, u32[]{:S(2)}) %collective-permute-start.28) | collective-permute-done | bytes 393248 | tf_op jit(solution)/shard_map/ppermute | solution.py:378
  253.0 6.6 %reduce-scatter.7.cloned.1.call-done.block_ref = bf16[192,1024]{1,0:T(8,128)(2,1)} async-done(((bf16[1536,1024]{1,0:T(8,128)(2,1)}), bf16[192,1024]{1,0:T(8,128)(2,1)}) %reduce-scatter.7.cloned.1.call-update) | async-done | bytes 393232 | tf_op jit(solution)/shard_map/reduce_scatter | solution.py:325
  259.8 2.5 multiply_reduce_fusion
  266.6 5.4 %collective-permute-done.30 = bf16[128,1536]{1,0:T(8,128)(2,1)S(1)} collective-permute-done((bf16[128,1536]{1,0:T(8,128)(2,1)S(1)}, bf16[128,1536]{1,0:T(8,128)(2,1)S(1)}, u32[]{:S(2)}, u32[]{:S(2)}) %collective-permute-start.30) | collective-permute-done | bytes 393248 | tf_op jit(solution)/shard_map/ppermute | solution.py:358
  273.6 1.6 collective-permute-done.31
  278.5 2.5 collective-permute-done.33
  281.7 5.5 %fusion.70 = (bf16[512,1536]{1,0:T(8,128)(2,1)S(1)}, f32[512,1536]{1,0:T(8,128)}) fusion(bf16[512,1024]{1,0:T(8,128)(2,1)S(1)} %copy-done.22, bf16[1536,1024]{1,0:T(8,128)(2,1)} %all-gather.8.cloned.1.call-done.down_ref), kind=kOutput, calls=%fused_computation.200 | convolution fusion | flops 1611399168 | bytes 8912896 | tf_op jit(solution)/shard_map/dot_general | solution.py:32
  289.0 2.0 collective-permute-start.36
  292.0 23.6 %attention_backward.1 = (bf16[512,1152]{1,0:T(8,128)(2,1)S(1)}, bf16[256,768]{1,0:T(8,128)(2,1)S(1)}, f32[8,384]{1,0:T(8,128)S(1)}) custom-call(f32[512,1152]{1,0:T(8,128)} %copy-done.2, bf16[512,384]{1,0:T(8,128)(2,1)S(1)} %copy-done.14, bf16[512,384]{1,0:T(8,128)(2,1)S(1)} %copy-done.16, bf16[512,384]{1,0:T(8,128)(2,1)S(1)} %copy-done.18, ...), custom_call_target="tpu_custom_call" | custom-call | flops 1509949440 | bytes 9437184 | tf_op jit(solution)/shard_map/attention_backward/pallas_call | solution.py:181
  316.8 4.4 %fusion.71 = (bf16[512,1536]{1,0:T(8,128)(2,1)}, f32[512,1536]{1,0:T(8,128)}) fusion(bf16[512,1152]{1,0:T(8,128)(2,1)S(1)} %get-tuple-element.112, bf16[1536,1536]{1,0:T(8,128)(2,1)S(1)} %bitcast.91), kind=kOutput, calls=%fused_computation.201 | convolution fusion | flops 1812725760 | bytes 9437184 | tf_op jit(solution)/shard_map/dot_general | solution.py:32
  322.3 2.0 collective-permute-start.41
  324.4 2.4 convolution_convert_fusion.1
  326.8 2.6 pad_maximum_fusion
  329.3 4.9 %collective-permute-done.41 = bf16[512,768]{1,0:T(8,128)(2,1)S(1)} collective-permute-done((bf16[512,768]{1,0:T(8,128)(2,1)}, bf16[512,768]{1,0:T(8,128)(2,1)S(1)}, u32[]{:S(2)}, u32[]{:S(2)}) %collective-permute-start.41) | collective-permute-done | bytes 786464 | tf_op jit(solution)/shard_map/ppermute | solution.py:341
  334.2 2.4 fusion.63
  336.7 1.7 collective-permute-start.37
  342.4 2.0 widen.3
  344.4 2.3 widen.4
  347.4 10.0 %collective-permute-done.38 = bf16[128,1536]{1,0:T(8,128)(2,1)} collective-permute-done((bf16[128,1536]{1,0:T(8,128)(2,1)}, bf16[128,1536]{1,0:T(8,128)(2,1)}, u32[]{:S(2)}, u32[]{:S(2)}) %collective-permute-start.38) | collective-permute-done | bytes 393248 | tf_op jit(solution)/shard_map/ppermute | solution.py:378
  357.4 2.2 multiply_reduce_fusion.1
  359.8 3.6 select_reduce_fusion
  363.5 2.5 collective-permute-start.42
  369.2 2.0 concatenate.150
  375.0 1.9 collective-permute-start.53
  376.9 5.4 %collective-permute-start.45 = (bf16[2,1536]{1,0:T(2,128)(2,1)S(1)}, bf16[2,1536]{1,0:T(2,128)(2,1)S(1)}, u32[]{:S(2)}, u32[]{:S(2)}) collective-permute-start(bf16[2,1536]{1,0:T(2,128)(2,1)S(1)} %pad_maximum_fusion.12), channel_id=1, source_target_pairs={{0,8},{4,12},{8,0},{12,4},{16,24},{20,28},{24,16},{28,20},{1,9},{5... | collective-permute-start | bytes 18440 | tf_op jit(solution)/shard_map/ppermute | solution.py:316
  383.9 16.2 %collective-permute-start.54 = (f32[3224]{0:T(1024)S(1)}, f32[3224]{0:T(1024)S(1)}, u32[]{:S(2)}, u32[]{:S(2)}) collective-permute-start(f32[3224]{0:T(1024)S(1)} %bitcast.93), channel_id=1, source_target_pairs={{0,4},{4,0},{8,12},{12,8},{16,20},{20,16},{24,28},{28,24},{1,5},{5... | collective-permute-start | bytes 38696 | tf_op jit(solution)/shard_map/ppermute | solution.py:402
  400.1 3.5 collective-permute-start.46
  403.7 7.4 %collective-permute-start.49 = (bf16[512,768]{1,0:T(8,128)(2,1)S(1)}, bf16[512,768]{1,0:T(8,128)(2,1)S(1)}, u32[]{:S(2)}, u32[]{:S(2)}) collective-permute-start(bf16[512,768]{1,0:T(8,128)(2,1)S(1)} %collective-permute-done.48), channel_id=1, source_target_pairs={{0,4},{4,0},{8,12},{12,8},{16,20},{20,16},{24,28},{28,24},{1,5},{5... | collective-permute-start | bytes 2359304 | tf_op jit(solution)/shard_map/ppermute | solution.py:313
  414.6 1.7 collective-permute-done.56
  420.1 1.9 fusion.72
  423.2 2.1 widen.5
  (381 shorter events, 90.8 us)
Async XLA Ops:
  7.2 116.3 %all-gather.4.cloned.1.call-start = ((), (), s32[]{:S(2)}) async-start(), calls=%async_computation.5 | async-start | bytes 5308416 | tf_op jit(solution)/shard_map/all_gather | solution.py:448
  9.4 119.1 %reduce-scatter.5.cloned.1.call-start = ((), (), s32[]{:S(2)}) async-start(), calls=%async_computation.6 | async-start | bytes 3538944 | tf_op jit(solution)/shard_map/reduce_scatter | solution.py:325
  41.4 11.3 %collective-permute-start.12 = (bf16[8,1,64,512]{3,2,1,0:T(8,128)(2,1)S(1)}, bf16[8,1,64,512]{3,2,1,0:T(8,128)(2,1)S(1)}, u32[]{:S(2)}, u32[]{:S(2)}) collective-permute-start(bf16[8,1,64,512]{3,2,1,0:T(8,128)(2,1)S(1)} %bitcast.85), channel_id=1, source_target_pairs={{0,1},{1,0},{2,3},{3,2},{4,5},{5,4},{6,7},{7,6},{8,9},{9,8},{10,11... | collective-permute-start | bytes 1572872 | tf_op jit(solution)/shard_map/ppermute | solution.py:358
  42.9 12.8 %collective-permute-start.13 = (bf16[8,1,64,512]{3,2,1,0:T(8,128)(2,1)S(1)}, bf16[8,1,64,512]{3,2,1,0:T(8,128)(2,1)S(1)}, u32[]{:S(2)}, u32[]{:S(2)}) collective-permute-start(bf16[8,1,64,512]{3,2,1,0:T(8,128)(2,1)S(1)} %bitcast.86), channel_id=1, source_target_pairs={{0,2},{1,3},{2,0},{3,1},{4,6},{5,7},{6,4},{7,5},{8,10},{9,11},{10,... | collective-permute-start | bytes 1572872 | tf_op jit(solution)/shard_map/ppermute | solution.py:358
  52.7 6.8 %collective-permute-start.14 = (bf16[8,1,32,512]{3,2,1,0:T(8,128)(2,1)S(1)}, bf16[8,1,32,512]{3,2,1,0:T(8,128)(2,1)S(1)}, u32[]{:S(2)}, u32[]{:S(2)}) collective-permute-start(bf16[8,1,32,512]{3,2,1,0:T(8,128)(2,1)S(1)} %slice.328), channel_id=1, source_target_pairs={{0,2},{1,3},{2,0},{3,1},{4,6},{5,7},{6,4},{7,5},{8,10},{9,11},{10,... | collective-permute-start | bytes 786440 | tf_op jit(solution)/shard_map/ppermute | solution.py:363
  55.7 6.4 %collective-permute-start.15 = (bf16[8,1,32,512]{3,2,1,0:T(8,128)(2,1)S(1)}, bf16[8,1,32,512]{3,2,1,0:T(8,128)(2,1)S(1)}, u32[]{:S(2)}, u32[]{:S(2)}) collective-permute-start(bf16[8,1,32,512]{3,2,1,0:T(8,128)(2,1)S(1)} %slice.329), channel_id=1, source_target_pairs={{0,1},{1,0},{2,3},{3,2},{4,5},{5,4},{6,7},{7,6},{8,9},{9,8},{10,11... | collective-permute-start | bytes 786440 | tf_op jit(solution)/shard_map/ppermute | solution.py:364
  67.3 117.8 %all-gather.6.cloned.1.call-start = ((), (), s32[]{:S(2)}) async-start(), calls=%async_computation.7 | async-start | bytes 7077888 | tf_op jit(solution)/shard_map/all_gather | solution.py:448
  69.3 148.9 %all-gather.8.cloned.1.call-start = ((), (), s32[]{:S(2)}) async-start(), calls=%async_computation.8 | async-start | bytes 3538944 | tf_op jit(solution)/shard_map/all_gather | solution.py:486
  69.4 7.9 %collective-permute-start.8 = (bf16[128,1536]{1,0:T(8,128)(2,1)S(1)}, bf16[128,1536]{1,0:T(8,128)(2,1)}, u32[]{:S(2)}, u32[]{:S(2)}) collective-permute-start(bf16[128,1536]{1,0:T(8,128)(2,1)S(1)} %copy-done.25), channel_id=1, source_target_pairs={{0,1},{1,0},{2,3},{3,2},{4,5},{5,4},{6,7},{7,6},{8,9},{9,8},{10,11... | collective-permute-start | bytes 1179656 | tf_op jit(solution)/shard_map/ppermute | solution.py:358
  69.8 10.1 %collective-permute-start.9 = (bf16[128,1536]{1,0:T(8,128)(2,1)S(1)}, bf16[128,1536]{1,0:T(8,128)(2,1)}, u32[]{:S(2)}, u32[]{:S(2)}) collective-permute-start(bf16[128,1536]{1,0:T(8,128)(2,1)S(1)} %copy-done.25), channel_id=1, source_target_pairs={{0,2},{1,3},{2,0},{3,1},{4,6},{5,7},{6,4},{7,5},{8,10},{9,11},{10,... | collective-permute-start | bytes 1179656 | tf_op jit(solution)/shard_map/ppermute | solution.py:358
  71.1 188.5 %reduce-scatter.7.cloned.1.call-start = ((), (), s32[]{:S(2)}) async-start(), calls=%async_computation.9 | async-start | bytes 3538944 | tf_op jit(solution)/shard_map/reduce_scatter | solution.py:325
  74.0 1.2 collective-permute-start
  75.3 5.7 %collective-permute-start.1 = (bf16[2,1024]{1,0:T(2,128)(2,1)S(1)}, bf16[2,1024]{1,0:T(2,128)(2,1)S(1)}, u32[]{:S(2)}, u32[]{:S(2)}) collective-permute-start(bf16[2,1024]{1,0:T(2,128)(2,1)S(1)} %pad_maximum_fusion.13), channel_id=1, source_target_pairs={{0,8},{4,12},{8,0},{12,4},{16,24},{20,28},{24,16},{28,20},{1,9},{5... | collective-permute-start | bytes 12296 | tf_op jit(solution)/shard_map/ppermute | solution.py:316
  78.3 19.2 %collective-permute-start.10 = (bf16[64,1536]{1,0:T(8,128)(2,1)S(1)}, bf16[64,1536]{1,0:T(8,128)(2,1)S(1)}, u32[]{:S(2)}, u32[]{:S(2)}) collective-permute-start(bf16[64,1536]{1,0:T(8,128)(2,1)S(1)} %slice.324), channel_id=1, source_target_pairs={{0,2},{1,3},{2,0},{3,1},{4,6},{5,7},{6,4},{7,5},{8,10},{9,11},{10,... | collective-permute-start | bytes 589832 | tf_op jit(solution)/shard_map/ppermute | solution.py:363
  80.8 19.1 %collective-permute-start.11 = (bf16[64,1536]{1,0:T(8,128)(2,1)S(1)}, bf16[64,1536]{1,0:T(8,128)(2,1)S(1)}, u32[]{:S(2)}, u32[]{:S(2)}) collective-permute-start(bf16[64,1536]{1,0:T(8,128)(2,1)S(1)} %slice.325), channel_id=1, source_target_pairs={{0,1},{1,0},{2,3},{3,2},{4,5},{5,4},{6,7},{7,6},{8,9},{9,8},{10,11... | collective-permute-start | bytes 589832 | tf_op jit(solution)/shard_map/ppermute | solution.py:364
  81.0 7.3 %collective-permute-start.2 = (bf16[4,1024]{1,0:T(4,128)(2,1)S(1)}, bf16[4,1024]{1,0:T(4,128)(2,1)S(1)}, u32[]{:S(2)}, u32[]{:S(2)}) collective-permute-start(bf16[4,1024]{1,0:T(4,128)(2,1)S(1)} %pad_maximum_fusion.11), channel_id=1, source_target_pairs={{0,16},{4,20},{8,24},{12,28},{16,0},{20,4},{24,8},{28,12},{1,17},{... | collective-permute-start | bytes 24584 | tf_op jit(solution)/shard_map/ppermute | solution.py:316
  89.5 5.7 %collective-permute-start.3 = (f32[4,1536]{1,0:T(4,128)S(1)}, f32[4,1536]{1,0:T(4,128)S(1)}, u32[]{:S(2)}, u32[]{:S(2)}) collective-permute-start(f32[4,1536]{1,0:T(4,128)S(1)} %slice.314), channel_id=1, source_target_pairs={{0,16},{4,20},{8,24},{12,28},{16,0},{20,4},{24,8},{28,12},{1,17},{... | collective-permute-start | bytes 73736 | tf_op jit(solution)/shard_map/ppermute | solution.py:316
  95.3 4.4 %collective-permute-start.4 = (f32[2,1536]{1,0:T(2,128)S(1)}, f32[2,1536]{1,0:T(2,128)S(1)}, u32[]{:S(2)}, u32[]{:S(2)}) collective-permute-start(f32[2,1536]{1,0:T(2,128)S(1)} %slice.316), channel_id=1, source_target_pairs={{0,8},{4,12},{8,0},{12,4},{16,24},{20,28},{24,16},{28,20},{1,9},{5... | collective-permute-start | bytes 36872 | tf_op jit(solution)/shard_map/ppermute | solution.py:316
  99.7 1.2 collective-permute-start.5
  101.0 3.7 collective-permute-start.6
  104.7 3.8 collective-permute-start.7
  108.7 9.7 %collective-permute-start.23 = (bf16[128,1536]{1,0:T(8,128)(2,1)S(1)}, bf16[128,1536]{1,0:T(8,128)(2,1)S(1)}, u32[]{:S(2)}, u32[]{:S(2)}) collective-permute-start(bf16[128,1536]{1,0:T(8,128)(2,1)S(1)} %copy-done.28), channel_id=1, source_target_pairs={{0,1},{1,0},{2,3},{3,2},{4,5},{5,4},{6,7},{7,6},{8,9},{9,8},{10,11... | collective-permute-start | bytes 1179656 | tf_op jit(solution)/shard_map/ppermute | solution.py:358
  110.1 10.5 %collective-permute-start.24 = (bf16[128,1536]{1,0:T(8,128)(2,1)S(1)}, bf16[128,1536]{1,0:T(8,128)(2,1)S(1)}, u32[]{:S(2)}, u32[]{:S(2)}) collective-permute-start(bf16[128,1536]{1,0:T(8,128)(2,1)S(1)} %copy-done.28), channel_id=1, source_target_pairs={{0,2},{1,3},{2,0},{3,1},{4,6},{5,7},{6,4},{7,5},{8,10},{9,11},{10,... | collective-permute-start | bytes 1179656 | tf_op jit(solution)/shard_map/ppermute | solution.py:358
  119.1 33.8 %collective-permute-start.25 = (bf16[64,1536]{1,0:T(8,128)(2,1)}, bf16[64,1536]{1,0:T(8,128)(2,1)}, u32[]{:S(2)}, u32[]{:S(2)}) collective-permute-start(bf16[64,1536]{1,0:T(8,128)(2,1)} %slice.339), channel_id=1, source_target_pairs={{0,2},{1,3},{2,0},{3,1},{4,6},{5,7},{6,4},{7,5},{8,10},{9,11},{10,... | collective-permute-start | bytes 589832 | tf_op jit(solution)/shard_map/ppermute | solution.py:363
  121.3 33.2 %collective-permute-start.26 = (bf16[64,1536]{1,0:T(8,128)(2,1)}, bf16[64,1536]{1,0:T(8,128)(2,1)}, u32[]{:S(2)}, u32[]{:S(2)}) collective-permute-start(bf16[64,1536]{1,0:T(8,128)(2,1)} %slice.340), channel_id=1, source_target_pairs={{0,1},{1,0},{2,3},{3,2},{4,5},{5,4},{6,7},{7,6},{8,9},{9,8},{10,11... | collective-permute-start | bytes 589832 | tf_op jit(solution)/shard_map/ppermute | solution.py:364
  149.3 12.1 %collective-permute-start.16 = (bf16[128,1536]{1,0:T(8,128)(2,1)S(1)}, bf16[128,1536]{1,0:T(8,128)(2,1)S(1)}, u32[]{:S(2)}, u32[]{:S(2)}) collective-permute-start(bf16[128,1536]{1,0:T(8,128)(2,1)S(1)} %get-tuple-element.167), channel_id=1, source_target_pairs={{0,1},{1,0},{2,3},{3,2},{4,5},{5,4},{6,7},{7,6},{8,9},{9,8},{10,11... | collective-permute-start | bytes 1179656 | tf_op jit(solution)/shard_map/ppermute | solution.py:378
  151.1 16.2 %collective-permute-start.17 = (bf16[128,1536]{1,0:T(8,128)(2,1)S(1)}, bf16[128,1536]{1,0:T(8,128)(2,1)S(1)}, u32[]{:S(2)}, u32[]{:S(2)}) collective-permute-start(bf16[128,1536]{1,0:T(8,128)(2,1)S(1)} %get-tuple-element.169), channel_id=1, source_target_pairs={{0,2},{1,3},{2,0},{3,1},{4,6},{5,7},{6,4},{7,5},{8,10},{9,11},{10,... | collective-permute-start | bytes 1179656 | tf_op jit(solution)/shard_map/ppermute | solution.py:378
  151.8 15.5 %collective-permute-start.18 = (bf16[128,1536]{1,0:T(8,128)(2,1)S(1)}, bf16[128,1536]{1,0:T(8,128)(2,1)S(1)}, u32[]{:S(2)}, u32[]{:S(2)}) collective-permute-start(bf16[128,1536]{1,0:T(8,128)(2,1)S(1)} %get-tuple-element.168), channel_id=1, source_target_pairs={{0,3},{1,2},{2,1},{3,0},{4,7},{5,6},{6,5},{7,4},{8,11},{9,10},{10,... | collective-permute-start | bytes 1179656 | tf_op jit(solution)/shard_map/ppermute | solution.py:378
  168.7 9.1 %collective-permute-start.19 = (bf16[128,1536]{1,0:T(8,128)(2,1)S(1)}, bf16[128,1536]{1,0:T(8,128)(2,1)S(1)}, u32[]{:S(2)}, u32[]{:S(2)}) collective-permute-start(bf16[128,1536]{1,0:T(8,128)(2,1)S(1)} %get-tuple-element.152), channel_id=1, source_target_pairs={{0,1},{1,0},{2,3},{3,2},{4,5},{5,4},{6,7},{7,6},{8,9},{9,8},{10,11... | collective-permute-start | bytes 1179656 | tf_op jit(solution)/shard_map/ppermute | solution.py:358
  169.4 9.9 %collective-permute-start.20 = (bf16[128,1536]{1,0:T(8,128)(2,1)S(1)}, bf16[128,1536]{1,0:T(8,128)(2,1)S(1)}, u32[]{:S(2)}, u32[]{:S(2)}) collective-permute-start(bf16[128,1536]{1,0:T(8,128)(2,1)S(1)} %get-tuple-element.152), channel_id=1, source_target_pairs={{0,2},{1,3},{2,0},{3,1},{4,6},{5,7},{6,4},{7,5},{8,10},{9,11},{10,... | collective-permute-start | bytes 1179656 | tf_op jit(solution)/shard_map/ppermute | solution.py:358
  177.8 5.7 %collective-permute-start.21 = (bf16[64,1536]{1,0:T(8,128)(2,1)S(1)}, bf16[64,1536]{1,0:T(8,128)(2,1)S(1)}, u32[]{:S(2)}, u32[]{:S(2)}) collective-permute-start(bf16[64,1536]{1,0:T(8,128)(2,1)S(1)} %slice.337), channel_id=1, source_target_pairs={{0,2},{1,3},{2,0},{3,1},{4,6},{5,7},{6,4},{7,5},{8,10},{9,11},{10,... | collective-permute-start | bytes 589832 | tf_op jit(solution)/shard_map/ppermute | solution.py:363
  179.3 5.7 %collective-permute-start.22 = (bf16[64,1536]{1,0:T(8,128)(2,1)S(1)}, bf16[64,1536]{1,0:T(8,128)(2,1)S(1)}, u32[]{:S(2)}, u32[]{:S(2)}) collective-permute-start(bf16[64,1536]{1,0:T(8,128)(2,1)S(1)} %slice.338), channel_id=1, source_target_pairs={{0,1},{1,0},{2,3},{3,2},{4,5},{5,4},{6,7},{7,6},{8,9},{9,8},{10,11... | collective-permute-start | bytes 589832 | tf_op jit(solution)/shard_map/ppermute | solution.py:364
  198.4 135.8 %reduce-scatter.9.cloned.1.call-start = ((), (), s32[]{:S(2)}) async-start(), calls=%async_computation.10 | async-start | bytes 7077888 | tf_op jit(solution)/shard_map/reduce_scatter | solution.py:325
  231.8 12.3 %collective-permute-start.27 = (bf16[128,1536]{1,0:T(8,128)(2,1)}, bf16[128,1536]{1,0:T(8,128)(2,1)}, u32[]{:S(2)}, u32[]{:S(2)}) collective-permute-start(bf16[128,1536]{1,0:T(8,128)(2,1)} %get-tuple-element.166), channel_id=1, source_target_pairs={{0,1},{1,0},{2,3},{3,2},{4,5},{5,4},{6,7},{7,6},{8,9},{9,8},{10,11... | collective-permute-start | bytes 1179656 | tf_op jit(solution)/shard_map/ppermute | solution.py:378
  233.2 19.7 %collective-permute-start.28 = (bf16[128,1536]{1,0:T(8,128)(2,1)}, bf16[128,1536]{1,0:T(8,128)(2,1)}, u32[]{:S(2)}, u32[]{:S(2)}) collective-permute-start(bf16[128,1536]{1,0:T(8,128)(2,1)} %get-tuple-element.165), channel_id=1, source_target_pairs={{0,2},{1,3},{2,0},{3,1},{4,6},{5,7},{6,4},{7,5},{8,10},{9,11},{10,... | collective-permute-start | bytes 1179656 | tf_op jit(solution)/shard_map/ppermute | solution.py:378
  234.7 18.2 %collective-permute-start.29 = (bf16[128,1536]{1,0:T(8,128)(2,1)S(1)}, bf16[128,1536]{1,0:T(8,128)(2,1)}, u32[]{:S(2)}, u32[]{:S(2)}) collective-permute-start(bf16[128,1536]{1,0:T(8,128)(2,1)S(1)} %get-tuple-element.164), channel_id=1, source_target_pairs={{0,3},{1,2},{2,1},{3,0},{4,7},{5,6},{6,5},{7,4},{8,11},{9,10},{10,... | collective-permute-start | bytes 1179656 | tf_op jit(solution)/shard_map/ppermute | solution.py:378
  259.6 163.6 %reduce-scatter.11.cloned.1.call-start = ((), (), s32[]{:S(2)}) async-start(), calls=%async_computation.11 | async-start | bytes 5308416 | tf_op jit(solution)/shard_map/reduce_scatter | solution.py:325
  263.7 8.3 %collective-permute-start.30 = (bf16[128,1536]{1,0:T(8,128)(2,1)S(1)}, bf16[128,1536]{1,0:T(8,128)(2,1)S(1)}, u32[]{:S(2)}, u32[]{:S(2)}) collective-permute-start(bf16[128,1536]{1,0:T(8,128)(2,1)S(1)} %get-tuple-element.148), channel_id=1, source_target_pairs={{0,1},{1,0},{2,3},{3,2},{4,5},{5,4},{6,7},{7,6},{8,9},{9,8},{10,11... | collective-permute-start | bytes 1179656 | tf_op jit(solution)/shard_map/ppermute | solution.py:358
  265.1 10.1 %collective-permute-start.31 = (bf16[128,1536]{1,0:T(8,128)(2,1)S(1)}, bf16[128,1536]{1,0:T(8,128)(2,1)S(1)}, u32[]{:S(2)}, u32[]{:S(2)}) collective-permute-start(bf16[128,1536]{1,0:T(8,128)(2,1)S(1)} %get-tuple-element.148), channel_id=1, source_target_pairs={{0,2},{1,3},{2,0},{3,1},{4,6},{5,7},{6,4},{7,5},{8,10},{9,11},{10,... | collective-permute-start | bytes 1179656 | tf_op jit(solution)/shard_map/ppermute | solution.py:358
  272.0 5.7 %collective-permute-start.32 = (bf16[64,1536]{1,0:T(8,128)(2,1)S(1)}, bf16[64,1536]{1,0:T(8,128)(2,1)S(1)}, u32[]{:S(2)}, u32[]{:S(2)}) collective-permute-start(bf16[64,1536]{1,0:T(8,128)(2,1)S(1)} %slice.341), channel_id=1, source_target_pairs={{0,2},{1,3},{2,0},{3,1},{4,6},{5,7},{6,4},{7,5},{8,10},{9,11},{10,... | collective-permute-start | bytes 589832 | tf_op jit(solution)/shard_map/ppermute | solution.py:363
  275.2 5.7 %collective-permute-start.33 = (bf16[64,1536]{1,0:T(8,128)(2,1)S(1)}, bf16[64,1536]{1,0:T(8,128)(2,1)S(1)}, u32[]{:S(2)}, u32[]{:S(2)}) collective-permute-start(bf16[64,1536]{1,0:T(8,128)(2,1)S(1)} %slice.342), channel_id=1, source_target_pairs={{0,1},{1,0},{2,3},{3,2},{4,5},{5,4},{6,7},{7,6},{8,9},{9,8},{10,11... | collective-permute-start | bytes 589832 | tf_op jit(solution)/shard_map/ppermute | solution.py:364
  287.3 29.4 %collective-permute-start.34 = (bf16[128,1536]{1,0:T(8,128)(2,1)S(1)}, bf16[128,1536]{1,0:T(8,128)(2,1)S(1)}, u32[]{:S(2)}, u32[]{:S(2)}) collective-permute-start(bf16[128,1536]{1,0:T(8,128)(2,1)S(1)} %get-tuple-element.163), channel_id=1, source_target_pairs={{0,1},{1,0},{2,3},{3,2},{4,5},{5,4},{6,7},{7,6},{8,9},{9,8},{10,11... | collective-permute-start | bytes 1179656 | tf_op jit(solution)/shard_map/ppermute | solution.py:378
  287.8 28.9 %collective-permute-start.35 = (bf16[128,1536]{1,0:T(8,128)(2,1)S(1)}, bf16[128,1536]{1,0:T(8,128)(2,1)S(1)}, u32[]{:S(2)}, u32[]{:S(2)}) collective-permute-start(bf16[128,1536]{1,0:T(8,128)(2,1)S(1)} %get-tuple-element.162), channel_id=1, source_target_pairs={{0,2},{1,3},{2,0},{3,1},{4,6},{5,7},{6,4},{7,5},{8,10},{9,11},{10,... | collective-permute-start | bytes 1179656 | tf_op jit(solution)/shard_map/ppermute | solution.py:378
  289.0 27.7 %collective-permute-start.36 = (bf16[128,1536]{1,0:T(8,128)(2,1)S(1)}, bf16[128,1536]{1,0:T(8,128)(2,1)S(1)}, u32[]{:S(2)}, u32[]{:S(2)}) collective-permute-start(bf16[128,1536]{1,0:T(8,128)(2,1)S(1)} %get-tuple-element.161), channel_id=1, source_target_pairs={{0,3},{1,2},{2,1},{3,0},{4,7},{5,6},{6,5},{7,4},{8,11},{9,10},{10,... | collective-permute-start | bytes 1179656 | tf_op jit(solution)/shard_map/ppermute | solution.py:378
  316.8 4.5 %collective-permute-start.40 = (bf16[256,768]{1,0:T(8,128)(2,1)S(1)}, bf16[256,768]{1,0:T(8,128)(2,1)S(1)}, u32[]{:S(2)}, u32[]{:S(2)}) collective-permute-start(bf16[256,768]{1,0:T(8,128)(2,1)S(1)} %get-tuple-element.115), channel_id=1, source_target_pairs={{0,4},{4,0},{8,12},{12,8},{16,20},{20,16},{24,28},{28,24},{1,5},{5... | collective-permute-start | bytes 1179656 | tf_op jit(solution)/shard_map/ppermute | solution.py:313
  322.3 11.9 %collective-permute-start.41 = (bf16[512,768]{1,0:T(8,128)(2,1)}, bf16[512,768]{1,0:T(8,128)(2,1)S(1)}, u32[]{:S(2)}, u32[]{:S(2)}) collective-permute-start(bf16[512,768]{1,0:T(8,128)(2,1)} %pad_maximum_fusion.2), channel_id=1, source_target_pairs={{0,8},{8,16},{16,24},{12,4},{20,12},{28,20},{1,9},{9,17},{17,25},{... | collective-permute-start | bytes 2359304 | tf_op jit(solution)/shard_map/ppermute | solution.py:341
  336.7 10.7 %collective-permute-start.37 = (bf16[128,1536]{1,0:T(8,128)(2,1)}, bf16[128,1536]{1,0:T(8,128)(2,1)}, u32[]{:S(2)}, u32[]{:S(2)}) collective-permute-start(bf16[128,1536]{1,0:T(8,128)(2,1)} %get-tuple-element.160), channel_id=1, source_target_pairs={{0,1},{1,0},{2,3},{3,2},{4,5},{5,4},{6,7},{7,6},{8,9},{9,8},{10,11... | collective-permute-start | bytes 1179656 | tf_op jit(solution)/shard_map/ppermute | solution.py:378
  338.4 18.9 %collective-permute-start.38 = (bf16[128,1536]{1,0:T(8,128)(2,1)}, bf16[128,1536]{1,0:T(8,128)(2,1)}, u32[]{:S(2)}, u32[]{:S(2)}) collective-permute-start(bf16[128,1536]{1,0:T(8,128)(2,1)} %get-tuple-element.159), channel_id=1, source_target_pairs={{0,2},{1,3},{2,0},{3,1},{4,6},{5,7},{6,4},{7,5},{8,10},{9,11},{10,... | collective-permute-start | bytes 1179656 | tf_op jit(solution)/shard_map/ppermute | solution.py:378
  339.9 17.5 %collective-permute-start.39 = (bf16[128,1536]{1,0:T(8,128)(2,1)S(1)}, bf16[128,1536]{1,0:T(8,128)(2,1)}, u32[]{:S(2)}, u32[]{:S(2)}) collective-permute-start(bf16[128,1536]{1,0:T(8,128)(2,1)S(1)} %get-tuple-element.158), channel_id=1, source_target_pairs={{0,3},{1,2},{2,1},{3,0},{4,7},{5,6},{6,5},{7,4},{8,11},{9,10},{10,... | collective-permute-start | bytes 1179656 | tf_op jit(solution)/shard_map/ppermute | solution.py:378
  363.5 4.2 collective-permute-start.42
  367.8 5.0 %collective-permute-start.43 = (f32[1,1536]{1,0:T(1,128)S(1)}, f32[1,1536]{1,0:T(1,128)S(1)}, u32[]{:S(2)}, u32[]{:S(2)}) collective-permute-start(f32[1,1536]{1,0:T(1,128)S(1)} %slice.356), channel_id=1, source_target_pairs={{0,1},{1,0},{2,3},{3,2},{4,5},{5,4},{6,7},{7,6},{8,9},{9,8},{10,11... | collective-permute-start | bytes 18440 | tf_op jit(solution)/shard_map/ppermute | solution.py:614
  371.2 3.8 collective-permute-start.52
  372.1 10.3 %collective-permute-start.47 = (bf16[512,768]{1,0:T(8,128)(2,1)}, bf16[512,768]{1,0:T(8,128)(2,1)S(1)}, u32[]{:S(2)}, u32[]{:S(2)}) collective-permute-start(bf16[512,768]{1,0:T(8,128)(2,1)} %copy-done.36), channel_id=1, source_target_pairs={{8,16},{16,24},{12,4},{20,12},{9,17},{17,25},{13,5},{21,13},{10,18... | collective-permute-start | bytes 2359304 | tf_op jit(solution)/shard_map/ppermute | solution.py:341
  372.8 4.1 collective-permute-start.44
  375.0 43.5 %collective-permute-start.51 = (bf16[512,768]{1,0:T(8,128)(2,1)S(1)}, bf16[512,768]{1,0:T(8,128)(2,1)S(1)}, u32[]{:S(2)}, u32[]{:S(2)}) collective-permute-start(bf16[512,768]{1,0:T(8,128)(2,1)S(1)} %copy-done.37), channel_id=1, source_target_pairs={{0,4},{4,0},{8,12},{12,8},{16,20},{20,16},{24,28},{28,24},{1,5},{5... | collective-permute-start | bytes 2359304 | tf_op jit(solution)/shard_map/ppermute | solution.py:313
  375.0 8.9 %collective-permute-start.53 = (f32[3227]{0:T(1024)S(1)}, f32[3227]{0:T(1024)S(1)}, u32[]{:S(2)}, u32[]{:S(2)}) collective-permute-start(f32[3227]{0:T(1024)S(1)} %add.397), channel_id=1, source_target_pairs={{0,2},{1,3},{2,0},{3,1},{4,6},{5,7},{6,4},{7,5},{8,10},{9,11},{10,... | collective-permute-start | bytes 38732 | tf_op jit(solution)/shard_map/ppermute | solution.py:402
  376.9 23.2 %collective-permute-start.45 = (bf16[2,1536]{1,0:T(2,128)(2,1)S(1)}, bf16[2,1536]{1,0:T(2,128)(2,1)S(1)}, u32[]{:S(2)}, u32[]{:S(2)}) collective-permute-start(bf16[2,1536]{1,0:T(2,128)(2,1)S(1)} %pad_maximum_fusion.12), channel_id=1, source_target_pairs={{0,8},{4,12},{8,0},{12,4},{16,24},{20,28},{24,16},{28,20},{1,9},{5... | collective-permute-start | bytes 18440 | tf_op jit(solution)/shard_map/ppermute | solution.py:316
  382.3 21.3 %collective-permute-start.48 = (bf16[512,768]{1,0:T(8,128)(2,1)S(1)}, bf16[512,768]{1,0:T(8,128)(2,1)S(1)}, u32[]{:S(2)}, u32[]{:S(2)}) collective-permute-start(bf16[512,768]{1,0:T(8,128)(2,1)S(1)} %collective-permute-done.47), channel_id=1, source_target_pairs={{16,24},{12,4},{17,25},{13,5},{18,26},{14,6},{19,27},{15,7}} | collective-permute-start | bytes 2359304 | tf_op jit(solution)/shard_map/ppermute | solution.py:341
  383.9 19.7 %collective-permute-start.54 = (f32[3224]{0:T(1024)S(1)}, f32[3224]{0:T(1024)S(1)}, u32[]{:S(2)}, u32[]{:S(2)}) collective-permute-start(f32[3224]{0:T(1024)S(1)} %bitcast.93), channel_id=1, source_target_pairs={{0,4},{4,0},{8,12},{12,8},{16,20},{20,16},{24,28},{28,24},{1,5},{5... | collective-permute-start | bytes 38696 | tf_op jit(solution)/shard_map/ppermute | solution.py:402
  400.1 13.2 %collective-permute-start.46 = (bf16[4,1536]{1,0:T(4,128)(2,1)S(1)}, bf16[4,1536]{1,0:T(4,128)(2,1)S(1)}, u32[]{:S(2)}, u32[]{:S(2)}) collective-permute-start(bf16[4,1536]{1,0:T(4,128)(2,1)S(1)} %pad_maximum_fusion.10), channel_id=1, source_target_pairs={{0,16},{4,20},{8,24},{12,28},{16,0},{20,4},{24,8},{28,12},{1,17},{... | collective-permute-start | bytes 36872 | tf_op jit(solution)/shard_map/ppermute | solution.py:316
  403.6 8.0 %collective-permute-start.55 = (f32[3224]{0:T(1024)S(1)}, f32[3224]{0:T(1024)S(1)}, u32[]{:S(2)}, u32[]{:S(2)}) collective-permute-start(f32[3224]{0:T(1024)S(1)} %slice_add_fusion.9), channel_id=1, source_target_pairs={{0,8},{4,12},{8,0},{12,4},{16,24},{20,28},{24,16},{28,20},{1,9},{5... | collective-permute-start | bytes 38696 | tf_op jit(solution)/shard_map/ppermute | solution.py:402
  403.7 14.4 %collective-permute-start.49 = (bf16[512,768]{1,0:T(8,128)(2,1)S(1)}, bf16[512,768]{1,0:T(8,128)(2,1)S(1)}, u32[]{:S(2)}, u32[]{:S(2)}) collective-permute-start(bf16[512,768]{1,0:T(8,128)(2,1)S(1)} %collective-permute-done.48), channel_id=1, source_target_pairs={{0,4},{4,0},{8,12},{12,8},{16,20},{20,16},{24,28},{28,24},{1,5},{5... | collective-permute-start | bytes 2359304 | tf_op jit(solution)/shard_map/ppermute | solution.py:313
  411.6 4.7 %collective-permute-start.56 = (f32[3224]{0:T(1024)S(1)}, f32[3224]{0:T(1024)S(1)}, u32[]{:S(2)}, u32[]{:S(2)}) collective-permute-start(f32[3224]{0:T(1024)S(1)} %add.400), channel_id=1, source_target_pairs={{0,16},{4,20},{8,24},{12,28},{16,0},{20,4},{24,8},{28,12},{1,17},{... | collective-permute-start | bytes 38696 | tf_op jit(solution)/shard_map/ppermute | solution.py:402
  413.1 5.2 %collective-permute-start.50 = (bf16[512,768]{1,0:T(8,128)(2,1)S(1)}, bf16[512,768]{1,0:T(8,128)(2,1)S(1)}, u32[]{:S(2)}, u32[]{:S(2)}) collective-permute-start(bf16[512,768]{1,0:T(8,128)(2,1)S(1)} %collective-permute-done.47), channel_id=1, source_target_pairs={{0,4},{4,0},{8,12},{12,8},{16,20},{20,16},{24,28},{28,24},{1,5},{5... | collective-permute-start | bytes 2359304 | tf_op jit(solution)/shard_map/ppermute | solution.py:313
  (81 other events, 1281.5 us)
Sparse Core Ops, SparseCore 0:
  10.3 60.8 all-gather.3
  73.5 40.2 reduce-scatter.4
  116.0 63.6 all-gather.5
  181.2 36.9 all-gather.7
  220.3 39.2 reduce-scatter.6
  261.7 68.9 reduce-scatter.8
  334.3 57.1 reduce-scatter.10

commit v4 on v3

--- a/solution.py
+++ b/solution.py
@@ -101,25 +101,81 @@
     )(qkv, text, cosine, sine, gains, mask, text_mask, gate)
 
 
-def attention_backward(qkv, query, key, value, text, grad, lse, cross, cosine, sine, gains, mask, text_mask, gate, heads, head):
-    rows = qkv.shape[0]
+def soft_back(query, keys, values, masks, lse, back):
+    probs = jnp.exp(dot_nt(query, keys) + masks - lse)
+    grad_probs = dot_nt(back, values)
+    delta = jnp.sum(probs * grad_probs, axis=-1, keepdims=True)
+    return probs.astype(bf16), (probs * (grad_probs - delta)).astype(bf16)
+
+
+def cross_backward(query, text, grad, lse, cross, text_mask, gate, heads, head):
+    rows = query.shape[0]
     text_rows = text.shape[0]
     columns = heads * head
     block = min(rows, 256)
     scale = head**-0.5
 
-    def kernel(qkv_ref, q_ref, k_ref, v_ref, text_ref, grad_ref, lse_ref, cross_ref, cos_ref, sin_ref,
-               gain_ref, mask_ref, tmask_ref, gate_ref, rows_ref, text_rows_ref, small_ref,
-               dq_ref, dk_ref, dv_ref, dtk_ref, dtv_ref):
+    def kernel(q_ref, text_ref, grad_ref, lse_ref, cross_ref, tmask_ref, gate_ref,
+               text_rows_ref, dq_ref, small_ref, dtk_ref, dtv_ref):
+        small_ref[...] = jnp.zeros_like(small_ref)
+        for h in range(heads):
+            at = slice(h * head, (h + 1) * head)
+            at_value = slice(columns + h * head, columns + (h + 1) * head)
+            text_keys = text_ref[:, at]
+            text_values = text_ref[:, at_value]
+            for b in range(rows // block):
+                here = slice(b * block, (b + 1) * block)
+                query = q_ref[here, at] * jnp.asarray(scale, bf16)
+                wide = grad_ref[here, at].astype(f32)
+                cross_back = (wide * gate_ref[:, at]).astype(bf16)
+                probs, grads = soft_back(
+                    query, text_keys, text_values, tmask_ref[...],
+                    lse_ref[here, heads + h : heads + h + 1], cross_back,
+                )
+                dq_ref[here, at] = dot(grads, text_keys)
+                dtk = dot_tn(grads, query)
+                dtv = dot_tn(probs, cross_back)
+                small_ref[0:1, at] += jnp.sum(wide * cross_ref[here, at], axis=0, keepdims=True)
+                if b == 0:
+                    dtk_ref[...] = dtk
+                    dtv_ref[...] = dtv
+                else:
+                    dtk_ref[...] += dtk
+                    dtv_ref[...] += dtv
+            text_rows_ref[:, at] = dtk_ref[...].astype(bf16)
+            text_rows_ref[:, at_value] = dtv_ref[...].astype(bf16)
+
+    return pl.pallas_call(
+        kernel,
+        out_shape=(
+            jax.ShapeDtypeStruct((text_rows, 2 * columns), bf16),
+            jax.ShapeDtypeStruct((rows, columns), f32),
+            jax.ShapeDtypeStruct((8, columns), f32),
+        ),
+        in_specs=[pl.BlockSpec(memory_space=pltpu.VMEM)] * 7,
+        out_specs=(pl.BlockSpec(memory_space=pltpu.VMEM),) * 3,
+        scratch_shapes=[pltpu.VMEM((text_rows, head), f32)] * 2,
+        compiler_params=pltpu.CompilerParams(vmem_limit_bytes=48 * 1024 * 1024),
+        cost_estimate=pl.CostEstimate(
+            flops=10 * rows * text_rows * columns,
+            bytes_accessed=6 * rows * columns * 4,
+            transcendentals=heads * rows * text_rows,
+        ),
+        name="cross_backward",
+    )(query, text, grad, lse, cross, text_mask, gate)
+
+
+def self_backward(qkv, query, key, value, grad, lse, cross_query, cosine, sine, gains, mask, heads, head):
+    rows = qkv.shape[0]
+    columns = heads * head
+    block = min(rows, 256)
+    scale = head**-0.5
+
+    def kernel(qkv_ref, q_ref, k_ref, v_ref, grad_ref, lse_ref, cross_ref, cos_ref, sin_ref,
+               gain_ref, mask_ref, rows_ref, small_ref, dq_ref, dk_ref, dv_ref):
         cos = cos_ref[...]
         sin = sin_ref[...]
         small_ref[...] = jnp.zeros_like(small_ref)
-
-        def soft_back(query, keys, values, masks, lse, back):
-            probs = jnp.exp(dot_nt(query, keys) + masks - lse)
-            grad_probs = dot_nt(back, values)
-            delta = jnp.sum(probs * grad_probs, axis=-1, keepdims=True)
-            return probs.astype(bf16), (probs * (grad_probs - delta)).astype(bf16)
 
         def raw_back(grad, raw, gain, row):
             swapped = jnp.concatenate([grad[:, head // 2 :], grad[:, : head // 2]], axis=1)
@@ -138,64 +194,43 @@
             at_value = slice(2 * columns + h * head, 2 * columns + (h + 1) * head)
             keys = k_ref[:, at]
             values = v_ref[:, at]
-            text_keys = text_ref[:, at]
-            text_values = text_ref[:, at_key]
-            gate_row = gate_ref[:, at]
             for b in range(rows // block):
                 here = slice(b * block, (b + 1) * block)
-                plain = q_ref[here, at]
-                query = plain * jnp.asarray(scale, bf16)
+                query = q_ref[here, at] * jnp.asarray(scale, bf16)
                 back = grad_ref[here, at]
-                wide = back.astype(f32)
-                probs, grads = soft_back(query, keys, values, mask_ref[...], lse_ref[here, h : h + 1], back)
-                dq = dot(grads, keys)
+                probs, grads = soft_back(
+                    query, keys, values, mask_ref[...], lse_ref[here, h : h + 1], back
+                )
+                dq_ref[here, :] = (dot(grads, keys) + cross_ref[here, at]) * scale
                 dk = dot_tn(grads, query)
                 dv = dot_tn(probs, back)
-                cross_back = (wide * gate_row).astype(bf16)
-                probs, grads = soft_back(
-                    query, text_keys, text_values, tmask_ref[...],
-                    lse_ref[here, heads + h : heads + h + 1], cross_back,
-                )
-                dq_ref[here, :] = (dq + dot(grads, text_keys)) * scale
-                dtk = dot_tn(grads, query)
-                dtv = dot_tn(probs, cross_back)
-                small_ref[2:3, h * head : (h + 1) * head] += jnp.sum(
-                    wide * cross_ref[here, at], axis=0, keepdims=True
-                )
                 if b == 0:
                     dk_ref[...] = dk
                     dv_ref[...] = dv
-                    dtk_ref[...] = dtk
-                    dtv_ref[...] = dtv
                 else:
                     dk_ref[...] += dk
                     dv_ref[...] += dv
-                    dtk_ref[...] += dtk
-                    dtv_ref[...] += dtv
             rows_ref[:, at] = raw_back(dq_ref[...], qkv_ref[:, at], gain_ref[0:1, :head], 0)
             rows_ref[:, at_key] = raw_back(dk_ref[...], qkv_ref[:, at_key], gain_ref[1:2, :head], 1)
             rows_ref[:, at_value] = dv_ref[...].astype(bf16)
-            text_rows_ref[:, at] = dtk_ref[...].astype(bf16)
-            text_rows_ref[:, at_key] = dtv_ref[...].astype(bf16)
 
     return pl.pallas_call(
         kernel,
         out_shape=(
             jax.ShapeDtypeStruct((rows, 3 * columns), bf16),
-            jax.ShapeDtypeStruct((text_rows, 2 * columns), bf16),
-            jax.ShapeDtypeStruct((8, max(columns, 128)), f32),
-        ),
-        in_specs=[pl.BlockSpec(memory_space=pltpu.VMEM)] * 14,
-        out_specs=(pl.BlockSpec(memory_space=pltpu.VMEM),) * 3,
-        scratch_shapes=[pltpu.VMEM((rows, head), f32)] * 3 + [pltpu.VMEM((text_rows, head), f32)] * 2,
+            jax.ShapeDtypeStruct((8, 128), f32),
+        ),
+        in_specs=[pl.BlockSpec(memory_space=pltpu.VMEM)] * 11,
+        out_specs=(pl.BlockSpec(memory_space=pltpu.VMEM),) * 2,
+        scratch_shapes=[pltpu.VMEM((rows, head), f32)] * 3,
         compiler_params=pltpu.CompilerParams(vmem_limit_bytes=48 * 1024 * 1024),
         cost_estimate=pl.CostEstimate(
-            flops=10 * rows * (rows + text_rows) * columns,
-            bytes_accessed=12 * rows * columns * 4,
-            transcendentals=heads * rows * (rows + text_rows),
-        ),
-        name="attention_backward",
-    )(qkv, query, key, value, text, grad, lse, cross, cosine, sine, gains, mask, text_mask, gate)
+            flops=10 * rows * rows * columns,
+            bytes_accessed=10 * rows * columns * 4,
+            transcendentals=heads * rows * rows,
+        ),
+        name="self_backward",
+    )(qkv, query, key, value, grad, lse, cross_query, cosine, sine, gains, mask)
 
 
 def ffn_forward(ffn_in, weights):
@@ -539,7 +574,6 @@
         parts = seq_send(grad_sent, rows)
         act_part = dot_tn(ffn_all, grad_act).astype(bf16)
         *parts, act_part = stage(*parts, act_part)
-        act_grads = fsdp_scatter(after(act_part, down_grads))
         grad_ffn_in = seq_sum(grad_sent, parts, rows)
         grad_out = cotangent.astype(f32)
         grad_ffn_gain = jnp.sum(grad_ffn_in * unit_ffn * (1.0 + scale_ffn), axis=0)
@@ -550,22 +584,34 @@
         )
         attn_back = (tanh_attn * grad_hidden_in).astype(bf16)
         grad_gate_attn = jnp.sum(grad_hidden_in * attn_out, axis=0) * (1.0 - tanh_attn * tanh_attn)
+        attn_back, act_part = stage(attn_back, act_part)
+        act_grads = fsdp_scatter(after(act_part, down_grads))
         attn_back_all = seq_gather(attn_back)
         grad_mixed = dot(attn_back_all, output_t).astype(bf16)
         output_part = dot_tn(attn_back_all, mixed_rows).astype(bf16)
         ffn_sent = dot_nt(after(hidden, attn_back_all), down_t)
         ffn_parts = seq_send(ffn_sent, rows)
-        qkv_rows, text_grads_rows, head_sums = attention_backward(
-            qkv, query_rot, key_rot, value_low, text_both, grad_mixed, lse, cross_out,
-            cosine, sine, gains, mask, text_mask, gate_row, heads, head_size,
-        )
-        qkv_rows, text_grads_rows, *ffn_parts = stage(qkv_rows, text_grads_rows, *ffn_parts)
-
+        text_grads_rows, cross_query, gate_sums = cross_backward(
+            query_rot, text_both, grad_mixed, lse, cross_out, text_mask, gate_row, heads, head_size
+        )
         text_back = Gather(text_grads_rows, core)
+        cross_query, text_back.got[0] = stage(cross_query, text_back.got[0])
         text_back.step(1)
+        qkv_rows, head_sums = self_backward(
+            qkv, query_rot, key_rot, value_low, grad_mixed, lse, cross_query,
+            cosine, sine, gains, mask, heads, head_size,
+        )
+        qkv_rows, text_back.got[1], *ffn_parts = stage(qkv_rows, text_back.got[1], *ffn_parts)
+        text_back.step(2)
+        text_back.pass_on(1)
         normed_sent = dot_nt(qkv_rows, qkv_full)
         parts = seq_send(normed_sent, rows)
         qkv_part = dot_tn(normed_all, after(qkv_rows, normed_sent)).astype(bf16)
+        qkv_part, text_back.got[2], text_back.twins[1] = stage(
+            qkv_part, text_back.got[2], text_back.twins[1]
+        )
+        text_back.step()
+        text_back.pass_on(2)
         attn_part = jnp.concatenate([qkv_part, output_part], axis=1)
         ffn_out = seq_sum(ffn_sent, ffn_parts, rows)
         branch_ffn = tanh_ffn * ffn_out
@@ -583,15 +629,19 @@
         grad_query_gain = head_sums[0, :head_size]
         grad_key_gain = head_sums[1, :head_size]
         grad_gate_heads = jnp.sum(
-            head_sums[2, :columns].reshape(heads, head_size), axis=1
+            gate_sums[0].reshape(heads, head_size), axis=1
         ) * (1.0 - gate_heads * gate_heads)
-        attn_part, act_grads, text_back.got[1] = stage(attn_part, act_grads, text_back.got[1])
+        attn_part, act_grads, text_back.got[-1], parts[0] = stage(
+            attn_part, act_grads, text_back.got[-1], parts[0]
+        )
+        text_back.pass_on()
+        text_grads = dot_tn(cap_all, text_back.full(chip, core))
         attn_grads = fsdp_scatter(attn_part)
         act_grads = widen(act_grads, 2)
         down_grads = widen(down_grads, 1)[0]
-        *parts, down_grads, gate_grads, up_grads = stage(*parts, down_grads, *act_grads)
-        text_back.step()
-        text_back.pass_on()
+        *parts, text_grads, down_grads, gate_grads, up_grads = stage(
+            *parts, text_grads, down_grads, *act_grads
+        )
         grad_normed = seq_sum(normed_sent, parts, rows)
         grad_attn_gain = jnp.sum(grad_normed * unit_attn * (1.0 + scale_attn), axis=0)
         grad_scale_attn = jnp.sum(grad_normed * unit_attn * attn_gain, axis=0)
@@ -622,7 +672,6 @@
         totals = sizes[-3:]
         residual_rms = jnp.sqrt(totals / (length.astype(f32) * width))[:, None]
         small = all_sum(sizes[:-3], "fsdp", n_f)
-        text_grads = dot_tn(cap_all, text_back.full(chip, core))
         attn_grads = widen(attn_grads, 4)
         n_heads = cross_gate.shape[0]
         ends = [width, width, n_heads, head_size, head_size]

time: 438 us -> 434 us (level)
  starting transfers between devices: 95.7 us -> 87.1 us
  other arithmetic: 24.6 us -> 30.6 us
    ppermute x5, starting transfers between devices: 20.4 us -> 4.68 us  [all_sum(): lax.ppermute(block, axis, [(i, i ^ bit) for i in range(size)])]
    ppermute x4, starting transfers between devices: 7.67 us -> 18.2 us  [twin(): return lax.ppermute(block, 'fsdp', [(i, i ^ 1) for i in range(n_f)])]
    dynamic_update_slice x4 -> x3, other arithmetic: 0.73 us -> 7.13 us  [full(): whole = lax.dynamic_update_slice(whole, block[None], (at, 0, 0))]
    ppermute x9, starting transfers between devices: 21 us -> 15.8 us  [fsdp_xor(): return lax.ppermute(block, 'fsdp', [(i, i ^ k) for i in range(n_f)])]
    ppermute x12, waiting for transfers between devices: 34.1 us -> 28.9 us  [seq_send(): lax.ppermute(total[k * rows:(k + 1) * rows].astype(bf16), 'seq', swaps[k])]
    ppermute x5, waiting for transfers between devices: 1.75 us -> 6.29 us  [all_sum(): lax.ppermute(block, axis, [(i, i ^ bit) for i in range(size)])]
    pallas_call x1 -> x2, Pallas kernels: 23.6 us -> 22.3 us  [the longest x1 16.7 us: self_backward(): pl.pallas_call(kernel, out_shape=(jax.ShapeDtypeStruct((rows, 3 * columns...]
    unnamed x177 -> x212, local copies, waits for them, and re-layouts: 18.6 us -> 17.3 us
  transfers between devices with their start and end apart: 64 -> 64, of which waited for: 32 -> 34; matrix products, arithmetic and copies ran while one was open for 20% -> 23% of each run, Pallas kernels for 15% -> 14%
where the time goes in v4:
time: 434 us; the launch traced here: 429 us
  waiting for transfers between devices  120 us (28%)
  starting transfers between devices  87.1 us (20%)
  Pallas kernels  63.5 us (15%)
  matrix products  41.1 us (9%)
  local copies, waits for them, and re-layouts  36.9 us (9%)
  blocking collectives  31.5 us (7%)
  other arithmetic  30.6 us (7%)
  between operations  17.6 us (4%)
    all_to_all x1, blocking collectives, local(): cap_mine = lax.all_to_all(cap_mine, 'fsdp', 0, 0)  31.5 us
    ppermute x10, waiting for transfers between devices, seq_near(): return [lax.ppermute(block, 'seq', swaps[k]) for k in (1, 2)]  29.8 us
    ppermute x12, waiting for transfers between devices, seq_send(): lax.ppermute(total[k * rows:(k + 1) * rows].astype(bf16), 'seq', swaps[k])  28.9 us
    all_gather x1, waiting for transfers between devices, local(): down_t = lax.all_gather(down_weight.T, 'fsdp', axis=0, tiled=True)  19.4 us
    dot_general x6, matrix products, dot_tn(): lax.dot_general(left, right, (((0,), (0,)), ((), ())), preferred_element_...  18.6 us
    ppermute x4, starting transfers between devices, twin(): return lax.ppermute(block, 'fsdp', [(i, i ^ 1) for i in range(n_f)])  18.2 us
    unnamed x212, local copies, waits for them, and re-layouts  17.3 us
    pallas_call x1, Pallas kernels, self_backward(): pl.pallas_call(kernel, out_shape=(jax.ShapeDtypeStruct((rows, 3 * columns...  16.7 us
  transfers between devices with their start and end apart: 64, of which 34 were waited for; matrix products, arithmetic and copies ran while one was open for 23% of the time, Pallas kernels for 14%

profile of v4, /device:TPU:0, one launch (start us, length us, event | category | flops | bytes accessed | tf_op | source)
XLA Modules:
  0.0 428.6 jit_solution(4915173808646140981)
XLA Ops:
  7.3 2.1 pad_maximum_fusion.3
  9.9 31.5 %all_to_all.5 = bf16[8,64,512]{2,1,0:T(8,128)(2,1)S(1)} all-to-all(bf16[8,64,512]{2,1,0:T(8,128)(2,1)S(1)} %copy.46), channel_id=1, replica_groups=mesh['fsdp'=8,'seq'=4] {'fsdp'}, dimensions={0} | all-to-all | bytes 1048576 | tf_op jit(solution)/shard_map/all_to_all | solution.py:492
  44.4 8.3 %collective-permute-done.12 = bf16[8,1,64,512]{3,2,1,0:T(8,128)(2,1)S(1)} collective-permute-done((bf16[8,1,64,512]{3,2,1,0:T(8,128)(2,1)S(1)}, bf16[8,1,64,512]{3,2,1,0:T(8,128)(2,1)S(1)}, u32[]{:S(2)}, u32[]{:S(2)}) %collective-permute-start.12) | collective-permute-done | bytes 524320 | tf_op jit(solution)/shard_map/ppermute | solution.py:393
  56.1 3.4 collective-permute-done.14
  59.5 2.7 collective-permute-done.15
  63.8 3.5 convolution_convert_fusion.3
  81.0 5.2 %collective-permute-start.2 = (bf16[4,1024]{1,0:T(4,128)(2,1)S(1)}, bf16[4,1024]{1,0:T(4,128)(2,1)S(1)}, u32[]{:S(2)}, u32[]{:S(2)}) collective-permute-start(bf16[4,1024]{1,0:T(4,128)(2,1)S(1)} %pad_maximum_fusion.11), channel_id=1, source_target_pairs={{0,16},{4,20},{8,24},{12,28},{16,0},{20,4},{24,8},{28,12},{1,17},{... | collective-permute-start | bytes 24584 | tf_op jit(solution)/shard_map/ppermute | solution.py:351
  89.6 2.9 collective-permute-start.3
  93.5 1.8 collective-permute-done.3
  95.3 2.3 collective-permute-start.4
  97.7 2.1 collective-permute-done.4
  102.9 1.9 collective-permute-done.6
  106.3 2.2 collective-permute-done.7
  112.3 6.2 %collective-permute-done.23 = bf16[128,1536]{1,0:T(8,128)(2,1)S(1)} collective-permute-done((bf16[128,1536]{1,0:T(8,128)(2,1)S(1)}, bf16[128,1536]{1,0:T(8,128)(2,1)S(1)}, u32[]{:S(2)}, u32[]{:S(2)}) %collective-permute-start.23) | collective-permute-done | bytes 393248 | tf_op jit(solution)/shard_map/ppermute | solution.py:393
  123.6 4.9 %fusion.6.qkv_ref = f32[512,1152]{1,0:T(8,128)S(1)} fusion(bf16[1536,1536]{1,0:T(8,128)(2,1)} %all-gather.4.cloned.1.call-done, bf16[512,1536]{1,0:T(8,128)(2,1)} %copy-done.32, f32[1536]{0:T(1024)S(1)} %get-tuple-element.200, f32[1536]{0:T(1024)S(1)} %copy-done.73, f32[512]{0:T(512)S(1)} %add_rsqrt_fusion), kind=kOutput, calls=%fused_computation.14 | convolution fusion | flops 1815871488 | bytes 7485440 | tf_op jit(solution)/shard_map/dot_general | solution.py:28
  129.9 16.0 %attention_forward.1 = (bf16[512,384]{1,0:T(8,128)(2,1)S(1)}, bf16[512,384]{1,0:T(8,128)(2,1)S(1)}, bf16[512,384]{1,0:T(8,128)(2,1)S(1)}, bf16[512,384]{1,0:T(8,...) custom-call(f32[512,1152]{1,0:T(8,128)S(1)} %fusion.6.qkv_ref, bf16[256,768]{1,0:T(8,128)(2,1)S(1)} %copy-done.19, ...), custom_call_target="tpu_custom_call" | custom-call | flops 603979776 | bytes 6291456 | tf_op jit(solution)/shard_map/attention_forward/pallas_call | solution.py:88
  145.9 3.1 fusion.69
  149.2 1.8 collective-permute-start.16
  156.0 5.3 %collective-permute-done.16 = bf16[128,1536]{1,0:T(8,128)(2,1)S(1)} collective-permute-done((bf16[128,1536]{1,0:T(8,128)(2,1)S(1)}, bf16[128,1536]{1,0:T(8,128)(2,1)S(1)}, u32[]{:S(2)}, u32[]{:S(2)}) %collective-permute-start.16) | collective-permute-done | bytes 393248 | tf_op jit(solution)/shard_map/ppermute | solution.py:413
  161.3 5.9 %collective-permute-done.17 = bf16[128,1536]{1,0:T(8,128)(2,1)S(1)} collective-permute-done((bf16[128,1536]{1,0:T(8,128)(2,1)S(1)}, bf16[128,1536]{1,0:T(8,128)(2,1)S(1)}, u32[]{:S(2)}, u32[]{:S(2)}) %collective-permute-start.17) | collective-permute-done | bytes 393248 | tf_op jit(solution)/shard_map/ppermute | solution.py:413
  170.9 1.7 multiply_convert_fusion.back_ref
  172.6 5.3 %collective-permute-done.19 = bf16[128,1536]{1,0:T(8,128)(2,1)S(1)} collective-permute-done((bf16[128,1536]{1,0:T(8,128)(2,1)S(1)}, bf16[128,1536]{1,0:T(8,128)(2,1)S(1)}, u32[]{:S(2)}, u32[]{:S(2)}) %collective-permute-start.19) | collective-permute-done | bytes 393248 | tf_op jit(solution)/shard_map/ppermute | solution.py:393
  181.1 2.6 collective-permute-done.21
  185.4 7.5 %ffn_forward.1 = (bf16[512,1024]{1,0:T(8,128)(2,1)S(1)}, f32[512,1024]{1,0:T(8,128)S(1)}, f32[512,1024]{1,0:T(8,128)}) custom-call(bf16[512,1536]{1,0:T(8,128)(2,1)S(1)} %constant_dynamic-update-slice_fusion.5.in_ref, bf16[1536,2048]{1,0:T(8,128)(2,1)} %all-gather.6.cloned.1.call-done.gate_ref.up_ref, ...), custom_call_target="tpu_custom_call" | custom-call | flops 3221225472 | bytes 13107200 | tf_op jit(solution)/shard_map/ffn_forward/pallas_call | solution.py:253
  195.2 3.5 convolution_convert_fusion.2
  198.8 19.4 %all-gather.8.cloned.1.call-done.down_ref = bf16[1536,1024]{1,0:T(8,128)(2,1)} async-done(((bf16[192,1024]{1,0:T(8,128)(2,1)}), bf16[1536,1024]{1,0:T(8,128)(2,1)}) %all-gather.8.cloned.1.call-update) | async-done | bytes 3145744 | tf_op jit(solution)/shard_map/all_gather | solution.py:521
  218.2 11.4 %ffn_backward.1 = (bf16[512,2048]{1,0:T(8,128)(2,1)S(1)}, bf16[512,1536]{1,0:T(8,128)(2,1)S(1)}) custom-call(bf16[512,1536]{1,0:T(8,128)(2,1)S(1)} %multiply_convert_fusion.back_ref, bf16[1536,1024]{1,0:T(8,128)(2,1)} %all-gather.8.cloned.1.call-done.down_ref, bf16[1536,2048]{1,0:T(8,128)(2,1)} %all-gather.6.cloned.1.call-done.gate_ref.up_ref, ...), custom_call_target="tpu_custom_call" | custom-call | flops 4831838208 | bytes 20447232 | tf_op jit(solution)/shard_map/ffn_backward/pallas_call | solution.py:299
  235.3 5.4 %convolution_convert_fusion = bf16[1536,2048]{1,0:T(8,128)(2,1)} fusion(bf16[512,1536]{1,0:T(8,128)(2,1)S(1)} %constant_dynamic-update-slice_fusion.5.in_ref, bf16[512,2048]{1,0:T(8,128)(2,1)S(1)} %get-tuple-element.107), kind=kOutput, calls=%fused_computation | convolution fusion | flops 3224371200 | bytes 9961472 | tf_op jit(solution)/shard_map/dot_general | solution.py:36
  240.8 3.3 collective-permute-done.27
  244.1 8.9 %collective-permute-done.28 = bf16[128,1536]{1,0:T(8,128)(2,1)} collective-permute-done((bf16[128,1536]{1,0:T(8,128)(2,1)}, bf16[128,1536]{1,0:T(8,128)(2,1)}, u32[]{:S(2)}, u32[]{:S(2)}) %collective-permute-start.28) | collective-permute-done | bytes 393248 | tf_op jit(solution)/shard_map/ppermute | solution.py:413
  253.1 2.5 multiply_reduce_fusion
  256.6 2.9 reduce-scatter.7.cloned.1.call-done.block_ref
  262.8 5.4 %collective-permute-done.30 = bf16[128,1536]{1,0:T(8,128)(2,1)S(1)} collective-permute-done((bf16[128,1536]{1,0:T(8,128)(2,1)S(1)}, bf16[128,1536]{1,0:T(8,128)(2,1)S(1)}, u32[]{:S(2)}, u32[]{:S(2)}) %collective-permute-start.30) | collective-permute-done | bytes 393248 | tf_op jit(solution)/shard_map/ppermute | solution.py:393
  269.7 1.8 collective-permute-done.31
  274.0 4.2 collective-permute-done.33
  279.3 2.4 convolution_convert_fusion.5.grad_ref
  281.8 5.6 %cross_backward.1 = (bf16[256,768]{1,0:T(8,128)(2,1)S(1)}, f32[512,384]{1,0:T(8,128)S(1)}, f32[8,384]{1,0:T(8,128)S(1)}) custom-call(bf16[512,384]{1,0:T(8,128)(2,1)S(1)} %get-tuple-element.114.q_ref, bf16[256,768]{1,0:T(8,128)(2,1)S(1)} %copy-done.20, bf16[512,384]{1,0:T(8,128)(2,1)S(1)} %convolution_convert_fusion.5.grad_ref, f32[512,128]{1,0:T(8,128)S(1)} %copy-done.10, ...), custom_call_target="tpu_custom_call" | custom-call | flops 503316480 | bytes 4718592 | tf_op jit(solution)/shard_map/cross_backward/pallas_call | solution.py:148
  287.5 3.5 fusion.70
  291.1 3.6 collective-permute-start.35
  296.6 1.9 collective-permute-start.38
  299.5 16.7 %self_backward.1 = (bf16[512,1152]{1,0:T(8,128)(2,1)S(1)}, f32[8,128]{1,0:T(8,128)S(1)}) custom-call(f32[512,1152]{1,0:T(8,128)} %copy-done.2, bf16[512,384]{1,0:T(8,128)(2,1)S(1)} %get-tuple-element.114.q_ref, bf16[512,384]{1,0:T(8,128)(2,1)S(1)} %copy-done.14, bf16[512,384]{1,0:T(8,128)(2,1)S(1)} %copy-done.16, ...), custom_call_target="tpu_custom_call" | custom-call | flops 1006632960 | bytes 7864320 | tf_op jit(solution)/shard_map/self_backward/pallas_call | solution.py:217
  316.3 4.7 %collective-permute-done.35 = bf16[512,768]{1,0:T(8,128)(2,1)S(1)} collective-permute-done((bf16[512,768]{1,0:T(8,128)(2,1)S(1)}, bf16[512,768]{1,0:T(8,128)(2,1)S(1)}, u32[]{:S(2)}, u32[]{:S(2)}) %collective-permute-start.35) | collective-permute-done | bytes 786464 | tf_op jit(solution)/shard_map/ppermute | solution.py:376
  323.9 3.9 fusion.71
  327.8 2.4 convolution_convert_fusion.1
  333.2 2.6 pad_maximum_fusion
  335.8 4.7 %collective-permute-done.42 = bf16[128,1536]{1,0:T(8,128)(2,1)S(1)} collective-permute-done((bf16[128,1536]{1,0:T(8,128)(2,1)S(1)}, bf16[128,1536]{1,0:T(8,128)(2,1)S(1)}, u32[]{:S(2)}, u32[]{:S(2)}) %collective-permute-start.42) | collective-permute-done | bytes 393248 | tf_op jit(solution)/shard_map/ppermute | solution.py:413
  341.3 16.8 %collective-permute-start.45 = (bf16[512,768]{1,0:T(8,128)(2,1)}, bf16[512,768]{1,0:T(8,128)(2,1)}, u32[]{:S(2)}, u32[]{:S(2)}) collective-permute-start(bf16[512,768]{1,0:T(8,128)(2,1)} %collective-permute-done.41), channel_id=1, source_target_pairs={{0,4},{4,0},{8,12},{12,8},{16,20},{20,16},{24,28},{28,24},{1,5},{5... | collective-permute-start | bytes 2359304 | tf_op jit(solution)/shard_map/ppermute | solution.py:348
  360.7 1.9 broadcast_in_dim.96
  366.4 1.9 widen.3
  368.4 2.3 widen.4
  370.7 2.2 bitcast_dynamic-update-slice_fusion.2
  372.9 2.5 bitcast_dynamic-update-slice_fusion.1
  375.5 2.4 bitcast_dynamic-update-slice_fusion
  377.9 5.0 %fusion.72 = f32[512,768]{1,0:T(8,128)} fusion(bf16[2048,512]{1,0:T(8,128)(2,1)S(1)} %bitcast.81, bf16[2048,768]{1,0:T(8,128)(2,1)} %bitcast.25), kind=kOutput, calls=%fused_computation.202 | convolution fusion | flops 1610612736 | bytes 6815744 | tf_op jit(solution)/shard_map/dot_general | solution.py:36
  383.7 1.8 multiply_reduce_fusion.1
  385.7 3.5 select_reduce_fusion
  391.1 2.1 collective-permute-done.47
  394.7 2.0 concatenate.150
  398.2 2.2 collective-permute-done.52
  403.3 2.8 fusion.62
  406.2 2.8 collective-permute-start.51
  410.8 2.1 collective-permute-done.55
  415.6 1.9 collective-permute-done.56
  419.2 2.1 widen.5
  (417 shorter events, 101.6 us)
Async XLA Ops:
  7.2 116.4 %all-gather.4.cloned.1.call-start = ((), (), s32[]{:S(2)}) async-start(), calls=%async_computation.5 | async-start | bytes 5308416 | tf_op jit(solution)/shard_map/all_gather | solution.py:483
  9.4 119.2 %reduce-scatter.5.cloned.1.call-start = ((), (), s32[]{:S(2)}) async-start(), calls=%async_computation.6 | async-start | bytes 3538944 | tf_op jit(solution)/shard_map/reduce_scatter | solution.py:360
  41.4 11.3 %collective-permute-start.12 = (bf16[8,1,64,512]{3,2,1,0:T(8,128)(2,1)S(1)}, bf16[8,1,64,512]{3,2,1,0:T(8,128)(2,1)S(1)}, u32[]{:S(2)}, u32[]{:S(2)}) collective-permute-start(bf16[8,1,64,512]{3,2,1,0:T(8,128)(2,1)S(1)} %bitcast.84), channel_id=1, source_target_pairs={{0,1},{1,0},{2,3},{3,2},{4,5},{5,4},{6,7},{7,6},{8,9},{9,8},{10,11... | collective-permute-start | bytes 1572872 | tf_op jit(solution)/shard_map/ppermute | solution.py:393
  42.9 12.8 %collective-permute-start.13 = (bf16[8,1,64,512]{3,2,1,0:T(8,128)(2,1)S(1)}, bf16[8,1,64,512]{3,2,1,0:T(8,128)(2,1)S(1)}, u32[]{:S(2)}, u32[]{:S(2)}) collective-permute-start(bf16[8,1,64,512]{3,2,1,0:T(8,128)(2,1)S(1)} %bitcast.85), channel_id=1, source_target_pairs={{0,2},{1,3},{2,0},{3,1},{4,6},{5,7},{6,4},{7,5},{8,10},{9,11},{10,... | collective-permute-start | bytes 1572872 | tf_op jit(solution)/shard_map/ppermute | solution.py:393
  52.7 6.8 %collective-permute-start.14 = (bf16[8,1,32,512]{3,2,1,0:T(8,128)(2,1)S(1)}, bf16[8,1,32,512]{3,2,1,0:T(8,128)(2,1)S(1)}, u32[]{:S(2)}, u32[]{:S(2)}) collective-permute-start(bf16[8,1,32,512]{3,2,1,0:T(8,128)(2,1)S(1)} %slice.328), channel_id=1, source_target_pairs={{0,2},{1,3},{2,0},{3,1},{4,6},{5,7},{6,4},{7,5},{8,10},{9,11},{10,... | collective-permute-start | bytes 786440 | tf_op jit(solution)/shard_map/ppermute | solution.py:398
  55.7 6.4 %collective-permute-start.15 = (bf16[8,1,32,512]{3,2,1,0:T(8,128)(2,1)S(1)}, bf16[8,1,32,512]{3,2,1,0:T(8,128)(2,1)S(1)}, u32[]{:S(2)}, u32[]{:S(2)}) collective-permute-start(bf16[8,1,32,512]{3,2,1,0:T(8,128)(2,1)S(1)} %slice.329), channel_id=1, source_target_pairs={{0,1},{1,0},{2,3},{3,2},{4,5},{5,4},{6,7},{7,6},{8,9},{9,8},{10,11... | collective-permute-start | bytes 786440 | tf_op jit(solution)/shard_map/ppermute | solution.py:399
  67.3 118.1 %all-gather.6.cloned.1.call-start = ((), (), s32[]{:S(2)}) async-start(), calls=%async_computation.7 | async-start | bytes 7077888 | tf_op jit(solution)/shard_map/all_gather | solution.py:483
  69.3 148.9 %all-gather.8.cloned.1.call-start = ((), (), s32[]{:S(2)}) async-start(), calls=%async_computation.8 | async-start | bytes 3538944 | tf_op jit(solution)/shard_map/all_gather | solution.py:521
  69.4 7.9 %collective-permute-start.8 = (bf16[128,1536]{1,0:T(8,128)(2,1)S(1)}, bf16[128,1536]{1,0:T(8,128)(2,1)}, u32[]{:S(2)}, u32[]{:S(2)}) collective-permute-start(bf16[128,1536]{1,0:T(8,128)(2,1)S(1)} %copy-done.25), channel_id=1, source_target_pairs={{0,1},{1,0},{2,3},{3,2},{4,5},{5,4},{6,7},{7,6},{8,9},{9,8},{10,11... | collective-permute-start | bytes 1179656 | tf_op jit(solution)/shard_map/ppermute | solution.py:393
  69.8 10.1 %collective-permute-start.9 = (bf16[128,1536]{1,0:T(8,128)(2,1)S(1)}, bf16[128,1536]{1,0:T(8,128)(2,1)}, u32[]{:S(2)}, u32[]{:S(2)}) collective-permute-start(bf16[128,1536]{1,0:T(8,128)(2,1)S(1)} %copy-done.25), channel_id=1, source_target_pairs={{0,2},{1,3},{2,0},{3,1},{4,6},{5,7},{6,4},{7,5},{8,10},{9,11},{10,... | collective-permute-start | bytes 1179656 | tf_op jit(solution)/shard_map/ppermute | solution.py:393
  71.1 188.4 %reduce-scatter.7.cloned.1.call-start = ((), (), s32[]{:S(2)}) async-start(), calls=%async_computation.9 | async-start | bytes 3538944 | tf_op jit(solution)/shard_map/reduce_scatter | solution.py:360
  74.1 1.2 collective-permute-start
  75.3 5.7 %collective-permute-start.1 = (bf16[2,1024]{1,0:T(2,128)(2,1)S(1)}, bf16[2,1024]{1,0:T(2,128)(2,1)S(1)}, u32[]{:S(2)}, u32[]{:S(2)}) collective-permute-start(bf16[2,1024]{1,0:T(2,128)(2,1)S(1)} %pad_maximum_fusion.13), channel_id=1, source_target_pairs={{0,8},{4,12},{8,0},{12,4},{16,24},{20,28},{24,16},{28,20},{1,9},{5... | collective-permute-start | bytes 12296 | tf_op jit(solution)/shard_map/ppermute | solution.py:351
  78.3 19.4 %collective-permute-start.10 = (bf16[64,1536]{1,0:T(8,128)(2,1)S(1)}, bf16[64,1536]{1,0:T(8,128)(2,1)S(1)}, u32[]{:S(2)}, u32[]{:S(2)}) collective-permute-start(bf16[64,1536]{1,0:T(8,128)(2,1)S(1)} %slice.324), channel_id=1, source_target_pairs={{0,2},{1,3},{2,0},{3,1},{4,6},{5,7},{6,4},{7,5},{8,10},{9,11},{10,... | collective-permute-start | bytes 589832 | tf_op jit(solution)/shard_map/ppermute | solution.py:398
  80.8 19.1 %collective-permute-start.11 = (bf16[64,1536]{1,0:T(8,128)(2,1)S(1)}, bf16[64,1536]{1,0:T(8,128)(2,1)S(1)}, u32[]{:S(2)}, u32[]{:S(2)}) collective-permute-start(bf16[64,1536]{1,0:T(8,128)(2,1)S(1)} %slice.325), channel_id=1, source_target_pairs={{0,1},{1,0},{2,3},{3,2},{4,5},{5,4},{6,7},{7,6},{8,9},{9,8},{10,11... | collective-permute-start | bytes 589832 | tf_op jit(solution)/shard_map/ppermute | solution.py:399
  81.0 7.3 %collective-permute-start.2 = (bf16[4,1024]{1,0:T(4,128)(2,1)S(1)}, bf16[4,1024]{1,0:T(4,128)(2,1)S(1)}, u32[]{:S(2)}, u32[]{:S(2)}) collective-permute-start(bf16[4,1024]{1,0:T(4,128)(2,1)S(1)} %pad_maximum_fusion.11), channel_id=1, source_target_pairs={{0,16},{4,20},{8,24},{12,28},{16,0},{20,4},{24,8},{28,12},{1,17},{... | collective-permute-start | bytes 24584 | tf_op jit(solution)/shard_map/ppermute | solution.py:351
  89.6 5.7 %collective-permute-start.3 = (f32[4,1536]{1,0:T(4,128)S(1)}, f32[4,1536]{1,0:T(4,128)S(1)}, u32[]{:S(2)}, u32[]{:S(2)}) collective-permute-start(f32[4,1536]{1,0:T(4,128)S(1)} %slice.314), channel_id=1, source_target_pairs={{0,16},{4,20},{8,24},{12,28},{16,0},{20,4},{24,8},{28,12},{1,17},{... | collective-permute-start | bytes 73736 | tf_op jit(solution)/shard_map/ppermute | solution.py:351
  95.3 4.5 %collective-permute-start.4 = (f32[2,1536]{1,0:T(2,128)S(1)}, f32[2,1536]{1,0:T(2,128)S(1)}, u32[]{:S(2)}, u32[]{:S(2)}) collective-permute-start(f32[2,1536]{1,0:T(2,128)S(1)} %slice.316), channel_id=1, source_target_pairs={{0,8},{4,12},{8,0},{12,4},{16,24},{20,28},{24,16},{28,20},{1,9},{5... | collective-permute-start | bytes 36872 | tf_op jit(solution)/shard_map/ppermute | solution.py:351
  99.8 1.2 collective-permute-start.5
  101.1 3.7 collective-permute-start.6
  104.8 3.8 collective-permute-start.7
  108.7 9.7 %collective-permute-start.23 = (bf16[128,1536]{1,0:T(8,128)(2,1)S(1)}, bf16[128,1536]{1,0:T(8,128)(2,1)S(1)}, u32[]{:S(2)}, u32[]{:S(2)}) collective-permute-start(bf16[128,1536]{1,0:T(8,128)(2,1)S(1)} %copy-done.28), channel_id=1, source_target_pairs={{0,1},{1,0},{2,3},{3,2},{4,5},{5,4},{6,7},{7,6},{8,9},{9,8},{10,11... | collective-permute-start | bytes 1179656 | tf_op jit(solution)/shard_map/ppermute | solution.py:393
  110.2 10.5 %collective-permute-start.24 = (bf16[128,1536]{1,0:T(8,128)(2,1)S(1)}, bf16[128,1536]{1,0:T(8,128)(2,1)S(1)}, u32[]{:S(2)}, u32[]{:S(2)}) collective-permute-start(bf16[128,1536]{1,0:T(8,128)(2,1)S(1)} %copy-done.28), channel_id=1, source_target_pairs={{0,2},{1,3},{2,0},{3,1},{4,6},{5,7},{6,4},{7,5},{8,10},{9,11},{10,... | collective-permute-start | bytes 1179656 | tf_op jit(solution)/shard_map/ppermute | solution.py:393
  119.2 33.5 %collective-permute-start.25 = (bf16[64,1536]{1,0:T(8,128)(2,1)}, bf16[64,1536]{1,0:T(8,128)(2,1)}, u32[]{:S(2)}, u32[]{:S(2)}) collective-permute-start(bf16[64,1536]{1,0:T(8,128)(2,1)} %slice.339), channel_id=1, source_target_pairs={{0,2},{1,3},{2,0},{3,1},{4,6},{5,7},{6,4},{7,5},{8,10},{9,11},{10,... | collective-permute-start | bytes 589832 | tf_op jit(solution)/shard_map/ppermute | solution.py:398
  121.3 33.0 %collective-permute-start.26 = (bf16[64,1536]{1,0:T(8,128)(2,1)}, bf16[64,1536]{1,0:T(8,128)(2,1)}, u32[]{:S(2)}, u32[]{:S(2)}) collective-permute-start(bf16[64,1536]{1,0:T(8,128)(2,1)} %slice.340), channel_id=1, source_target_pairs={{0,1},{1,0},{2,3},{3,2},{4,5},{5,4},{6,7},{7,6},{8,9},{9,8},{10,11... | collective-permute-start | bytes 589832 | tf_op jit(solution)/shard_map/ppermute | solution.py:399
  149.2 12.1 %collective-permute-start.16 = (bf16[128,1536]{1,0:T(8,128)(2,1)S(1)}, bf16[128,1536]{1,0:T(8,128)(2,1)S(1)}, u32[]{:S(2)}, u32[]{:S(2)}) collective-permute-start(bf16[128,1536]{1,0:T(8,128)(2,1)S(1)} %get-tuple-element.188), channel_id=1, source_target_pairs={{0,1},{1,0},{2,3},{3,2},{4,5},{5,4},{6,7},{7,6},{8,9},{9,8},{10,11... | collective-permute-start | bytes 1179656 | tf_op jit(solution)/shard_map/ppermute | solution.py:413
  150.9 16.2 %collective-permute-start.17 = (bf16[128,1536]{1,0:T(8,128)(2,1)S(1)}, bf16[128,1536]{1,0:T(8,128)(2,1)S(1)}, u32[]{:S(2)}, u32[]{:S(2)}) collective-permute-start(bf16[128,1536]{1,0:T(8,128)(2,1)S(1)} %get-tuple-element.190), channel_id=1, source_target_pairs={{0,2},{1,3},{2,0},{3,1},{4,6},{5,7},{6,4},{7,5},{8,10},{9,11},{10,... | collective-permute-start | bytes 1179656 | tf_op jit(solution)/shard_map/ppermute | solution.py:413
  151.7 15.5 %collective-permute-start.18 = (bf16[128,1536]{1,0:T(8,128)(2,1)S(1)}, bf16[128,1536]{1,0:T(8,128)(2,1)S(1)}, u32[]{:S(2)}, u32[]{:S(2)}) collective-permute-start(bf16[128,1536]{1,0:T(8,128)(2,1)S(1)} %get-tuple-element.189), channel_id=1, source_target_pairs={{0,3},{1,2},{2,1},{3,0},{4,7},{5,6},{6,5},{7,4},{8,11},{9,10},{10,... | collective-permute-start | bytes 1179656 | tf_op jit(solution)/shard_map/ppermute | solution.py:413
  169.0 9.0 %collective-permute-start.19 = (bf16[128,1536]{1,0:T(8,128)(2,1)S(1)}, bf16[128,1536]{1,0:T(8,128)(2,1)S(1)}, u32[]{:S(2)}, u32[]{:S(2)}) collective-permute-start(bf16[128,1536]{1,0:T(8,128)(2,1)S(1)} %get-tuple-element.173), channel_id=1, source_target_pairs={{0,1},{1,0},{2,3},{3,2},{4,5},{5,4},{6,7},{7,6},{8,9},{9,8},{10,11... | collective-permute-start | bytes 1179656 | tf_op jit(solution)/shard_map/ppermute | solution.py:393
  169.7 9.9 %collective-permute-start.20 = (bf16[128,1536]{1,0:T(8,128)(2,1)S(1)}, bf16[128,1536]{1,0:T(8,128)(2,1)S(1)}, u32[]{:S(2)}, u32[]{:S(2)}) collective-permute-start(bf16[128,1536]{1,0:T(8,128)(2,1)S(1)} %get-tuple-element.173), channel_id=1, source_target_pairs={{0,2},{1,3},{2,0},{3,1},{4,6},{5,7},{6,4},{7,5},{8,10},{9,11},{10,... | collective-permute-start | bytes 1179656 | tf_op jit(solution)/shard_map/ppermute | solution.py:393
  178.0 5.7 %collective-permute-start.21 = (bf16[64,1536]{1,0:T(8,128)(2,1)S(1)}, bf16[64,1536]{1,0:T(8,128)(2,1)S(1)}, u32[]{:S(2)}, u32[]{:S(2)}) collective-permute-start(bf16[64,1536]{1,0:T(8,128)(2,1)S(1)} %slice.337), channel_id=1, source_target_pairs={{0,2},{1,3},{2,0},{3,1},{4,6},{5,7},{6,4},{7,5},{8,10},{9,11},{10,... | collective-permute-start | bytes 589832 | tf_op jit(solution)/shard_map/ppermute | solution.py:398
  179.6 5.7 %collective-permute-start.22 = (bf16[64,1536]{1,0:T(8,128)(2,1)S(1)}, bf16[64,1536]{1,0:T(8,128)(2,1)S(1)}, u32[]{:S(2)}, u32[]{:S(2)}) collective-permute-start(bf16[64,1536]{1,0:T(8,128)(2,1)S(1)} %slice.338), channel_id=1, source_target_pairs={{0,1},{1,0},{2,3},{3,2},{4,5},{5,4},{6,7},{7,6},{8,9},{9,8},{10,11... | collective-permute-start | bytes 589832 | tf_op jit(solution)/shard_map/ppermute | solution.py:399
  198.7 141.8 %reduce-scatter.9.cloned.1.call-start = ((), (), s32[]{:S(2)}) async-start(), calls=%async_computation.10 | async-start | bytes 7077888 | tf_op jit(solution)/shard_map/reduce_scatter | solution.py:360
  231.8 12.3 %collective-permute-start.27 = (bf16[128,1536]{1,0:T(8,128)(2,1)}, bf16[128,1536]{1,0:T(8,128)(2,1)}, u32[]{:S(2)}, u32[]{:S(2)}) collective-permute-start(bf16[128,1536]{1,0:T(8,128)(2,1)} %get-tuple-element.187), channel_id=1, source_target_pairs={{0,1},{1,0},{2,3},{3,2},{4,5},{5,4},{6,7},{7,6},{8,9},{9,8},{10,11... | collective-permute-start | bytes 1179656 | tf_op jit(solution)/shard_map/ppermute | solution.py:413
  233.3 19.7 %collective-permute-start.28 = (bf16[128,1536]{1,0:T(8,128)(2,1)}, bf16[128,1536]{1,0:T(8,128)(2,1)}, u32[]{:S(2)}, u32[]{:S(2)}) collective-permute-start(bf16[128,1536]{1,0:T(8,128)(2,1)} %get-tuple-element.186), channel_id=1, source_target_pairs={{0,2},{1,3},{2,0},{3,1},{4,6},{5,7},{6,4},{7,5},{8,10},{9,11},{10,... | collective-permute-start | bytes 1179656 | tf_op jit(solution)/shard_map/ppermute | solution.py:413
  234.8 18.2 %collective-permute-start.29 = (bf16[128,1536]{1,0:T(8,128)(2,1)}, bf16[128,1536]{1,0:T(8,128)(2,1)}, u32[]{:S(2)}, u32[]{:S(2)}) collective-permute-start(bf16[128,1536]{1,0:T(8,128)(2,1)} %get-tuple-element.185), channel_id=1, source_target_pairs={{0,3},{1,2},{2,1},{3,0},{4,7},{5,6},{6,5},{7,4},{8,11},{9,10},{10,... | collective-permute-start | bytes 1179656 | tf_op jit(solution)/shard_map/ppermute | solution.py:413
  259.6 159.7 %reduce-scatter.11.cloned.1.call-start = ((), (), s32[]{:S(2)}) async-start(), calls=%async_computation.11 | async-start | bytes 5308416 | tf_op jit(solution)/shard_map/reduce_scatter | solution.py:360
  259.8 8.4 %collective-permute-start.30 = (bf16[128,1536]{1,0:T(8,128)(2,1)S(1)}, bf16[128,1536]{1,0:T(8,128)(2,1)S(1)}, u32[]{:S(2)}, u32[]{:S(2)}) collective-permute-start(bf16[128,1536]{1,0:T(8,128)(2,1)S(1)} %copy-done.36), channel_id=1, source_target_pairs={{0,1},{1,0},{2,3},{3,2},{4,5},{5,4},{6,7},{7,6},{8,9},{9,8},{10,11... | collective-permute-start | bytes 1179656 | tf_op jit(solution)/shard_map/ppermute | solution.py:393
  261.3 10.2 %collective-permute-start.31 = (bf16[128,1536]{1,0:T(8,128)(2,1)S(1)}, bf16[128,1536]{1,0:T(8,128)(2,1)}, u32[]{:S(2)}, u32[]{:S(2)}) collective-permute-start(bf16[128,1536]{1,0:T(8,128)(2,1)S(1)} %copy-done.36), channel_id=1, source_target_pairs={{0,2},{1,3},{2,0},{3,1},{4,6},{5,7},{6,4},{7,5},{8,10},{9,11},{10,... | collective-permute-start | bytes 1179656 | tf_op jit(solution)/shard_map/ppermute | solution.py:393
  268.2 5.7 %collective-permute-start.32 = (bf16[64,1536]{1,0:T(8,128)(2,1)S(1)}, bf16[64,1536]{1,0:T(8,128)(2,1)S(1)}, u32[]{:S(2)}, u32[]{:S(2)}) collective-permute-start(bf16[64,1536]{1,0:T(8,128)(2,1)S(1)} %slice.341), channel_id=1, source_target_pairs={{0,2},{1,3},{2,0},{3,1},{4,6},{5,7},{6,4},{7,5},{8,10},{9,11},{10,... | collective-permute-start | bytes 589832 | tf_op jit(solution)/shard_map/ppermute | solution.py:398
  272.4 5.7 %collective-permute-start.33 = (bf16[64,1536]{1,0:T(8,128)(2,1)S(1)}, bf16[64,1536]{1,0:T(8,128)(2,1)S(1)}, u32[]{:S(2)}, u32[]{:S(2)}) collective-permute-start(bf16[64,1536]{1,0:T(8,128)(2,1)S(1)} %slice.342), channel_id=1, source_target_pairs={{0,1},{1,0},{2,3},{3,2},{4,5},{5,4},{6,7},{7,6},{8,9},{9,8},{10,11... | collective-permute-start | bytes 589832 | tf_op jit(solution)/shard_map/ppermute | solution.py:399
  287.4 3.6 collective-permute-start.34
  291.1 29.8 %collective-permute-start.35 = (bf16[512,768]{1,0:T(8,128)(2,1)S(1)}, bf16[512,768]{1,0:T(8,128)(2,1)S(1)}, u32[]{:S(2)}, u32[]{:S(2)}) collective-permute-start(bf16[512,768]{1,0:T(8,128)(2,1)S(1)} %pad_maximum_fusion.2), channel_id=1, source_target_pairs={{0,8},{8,16},{16,24},{12,4},{20,12},{28,20},{1,9},{9,17},{17,25},{... | collective-permute-start | bytes 2359304 | tf_op jit(solution)/shard_map/ppermute | solution.py:376
  294.8 21.4 %collective-permute-start.36 = (bf16[128,1536]{1,0:T(8,128)(2,1)S(1)}, bf16[128,1536]{1,0:T(8,128)(2,1)S(1)}, u32[]{:S(2)}, u32[]{:S(2)}) collective-permute-start(bf16[128,1536]{1,0:T(8,128)(2,1)S(1)} %get-tuple-element.184), channel_id=1, source_target_pairs={{0,1},{1,0},{2,3},{3,2},{4,5},{5,4},{6,7},{7,6},{8,9},{9,8},{10,11... | collective-permute-start | bytes 1179656 | tf_op jit(solution)/shard_map/ppermute | solution.py:413
  295.4 20.8 %collective-permute-start.37 = (bf16[128,1536]{1,0:T(8,128)(2,1)S(1)}, bf16[128,1536]{1,0:T(8,128)(2,1)S(1)}, u32[]{:S(2)}, u32[]{:S(2)}) collective-permute-start(bf16[128,1536]{1,0:T(8,128)(2,1)S(1)} %get-tuple-element.183), channel_id=1, source_target_pairs={{0,2},{1,3},{2,0},{3,1},{4,6},{5,7},{6,4},{7,5},{8,10},{9,11},{10,... | collective-permute-start | bytes 1179656 | tf_op jit(solution)/shard_map/ppermute | solution.py:413
  296.6 19.7 %collective-permute-start.38 = (bf16[128,1536]{1,0:T(8,128)(2,1)S(1)}, bf16[128,1536]{1,0:T(8,128)(2,1)S(1)}, u32[]{:S(2)}, u32[]{:S(2)}) collective-permute-start(bf16[128,1536]{1,0:T(8,128)(2,1)S(1)} %get-tuple-element.182), channel_id=1, source_target_pairs={{0,3},{1,2},{2,1},{3,0},{4,7},{5,6},{6,5},{7,4},{8,11},{9,10},{10,... | collective-permute-start | bytes 1179656 | tf_op jit(solution)/shard_map/ppermute | solution.py:413
  321.0 9.2 %collective-permute-start.39 = (bf16[512,768]{1,0:T(8,128)(2,1)S(1)}, bf16[512,768]{1,0:T(8,128)(2,1)}, u32[]{:S(2)}, u32[]{:S(2)}) collective-permute-start(bf16[512,768]{1,0:T(8,128)(2,1)S(1)} %collective-permute-done.35), channel_id=1, source_target_pairs={{8,16},{16,24},{12,4},{20,12},{9,17},{17,25},{13,5},{21,13},{10,18... | collective-permute-start | bytes 2359304 | tf_op jit(solution)/shard_map/ppermute | solution.py:376
  322.6 7.6 %collective-permute-start.40 = (bf16[512,768]{1,0:T(8,128)(2,1)S(1)}, bf16[512,768]{1,0:T(8,128)(2,1)S(1)}, u32[]{:S(2)}, u32[]{:S(2)}) collective-permute-start(bf16[512,768]{1,0:T(8,128)(2,1)S(1)} %collective-permute-done.35), channel_id=1, source_target_pairs={{0,4},{4,0},{8,12},{12,8},{16,20},{20,16},{24,28},{28,24},{1,5},{5... | collective-permute-start | bytes 2359304 | tf_op jit(solution)/shard_map/ppermute | solution.py:348
  330.2 10.3 %collective-permute-start.41 = (bf16[512,768]{1,0:T(8,128)(2,1)}, bf16[512,768]{1,0:T(8,128)(2,1)}, u32[]{:S(2)}, u32[]{:S(2)}) collective-permute-start(bf16[512,768]{1,0:T(8,128)(2,1)} %collective-permute-done.39), channel_id=1, source_target_pairs={{16,24},{12,4},{17,25},{13,5},{18,26},{14,6},{19,27},{15,7}} | collective-permute-start | bytes 2359304 | tf_op jit(solution)/shard_map/ppermute | solution.py:376
  332.8 7.8 %collective-permute-start.42 = (bf16[128,1536]{1,0:T(8,128)(2,1)S(1)}, bf16[128,1536]{1,0:T(8,128)(2,1)S(1)}, u32[]{:S(2)}, u32[]{:S(2)}) collective-permute-start(bf16[128,1536]{1,0:T(8,128)(2,1)S(1)} %get-tuple-element.181), channel_id=1, source_target_pairs={{0,1},{1,0},{2,3},{3,2},{4,5},{5,4},{6,7},{7,6},{8,9},{9,8},{10,11... | collective-permute-start | bytes 1179656 | tf_op jit(solution)/shard_map/ppermute | solution.py:413
  341.3 29.4 %collective-permute-start.45 = (bf16[512,768]{1,0:T(8,128)(2,1)}, bf16[512,768]{1,0:T(8,128)(2,1)}, u32[]{:S(2)}, u32[]{:S(2)}) collective-permute-start(bf16[512,768]{1,0:T(8,128)(2,1)} %collective-permute-done.41), channel_id=1, source_target_pairs={{0,4},{4,0},{8,12},{12,8},{16,20},{20,16},{24,28},{28,24},{1,5},{5... | collective-permute-start | bytes 2359304 | tf_op jit(solution)/shard_map/ppermute | solution.py:348
  358.2 14.8 %collective-permute-start.46 = (bf16[512,768]{1,0:T(8,128)(2,1)}, bf16[512,768]{1,0:T(8,128)(2,1)}, u32[]{:S(2)}, u32[]{:S(2)}) collective-permute-start(bf16[512,768]{1,0:T(8,128)(2,1)} %collective-permute-done.39), channel_id=1, source_target_pairs={{0,4},{4,0},{8,12},{12,8},{16,20},{20,16},{24,28},{28,24},{1,5},{5... | collective-permute-start | bytes 2359304 | tf_op jit(solution)/shard_map/ppermute | solution.py:348
  363.5 20.1 %collective-permute-start.43 = (bf16[128,1536]{1,0:T(8,128)(2,1)}, bf16[128,1536]{1,0:T(8,128)(2,1)S(1)}, u32[]{:S(2)}, u32[]{:S(2)}) collective-permute-start(bf16[128,1536]{1,0:T(8,128)(2,1)} %get-tuple-element.180), channel_id=1, source_target_pairs={{0,2},{1,3},{2,0},{3,1},{4,6},{5,7},{6,4},{7,5},{8,10},{9,11},{10,... | collective-permute-start | bytes 1179656 | tf_op jit(solution)/shard_map/ppermute | solution.py:413
  365.0 18.6 %collective-permute-start.44 = (bf16[128,1536]{1,0:T(8,128)(2,1)}, bf16[128,1536]{1,0:T(8,128)(2,1)S(1)}, u32[]{:S(2)}, u32[]{:S(2)}) collective-permute-start(bf16[128,1536]{1,0:T(8,128)(2,1)} %get-tuple-element.179), channel_id=1, source_target_pairs={{0,3},{1,2},{2,1},{3,0},{4,7},{5,6},{6,5},{7,4},{8,11},{9,10},{10,... | collective-permute-start | bytes 1179656 | tf_op jit(solution)/shard_map/ppermute | solution.py:413
  389.4 3.8 collective-permute-start.47
  393.2 4.1 collective-permute-start.48
  396.7 3.7 collective-permute-start.52
  397.3 4.6 %collective-permute-start.49 = (bf16[1,1536]{1,0:T(2,128)(2,1)S(1)}, bf16[1,1536]{1,0:T(2,128)(2,1)S(1)}, u32[]{:S(2)}, u32[]{:S(2)}) collective-permute-start(bf16[1,1536]{1,0:T(2,128)(2,1)S(1)} %fusion.42), channel_id=1, source_target_pairs={{0,4},{4,0},{8,12},{12,8},{16,20},{20,16},{24,28},{28,24},{1,5},{5... | collective-permute-start | bytes 9224 | tf_op jit(solution)/shard_map/ppermute | solution.py:351
  400.5 5.6 %collective-permute-start.53 = (f32[3227]{0:T(1024)S(1)}, f32[3227]{0:T(1024)S(1)}, u32[]{:S(2)}, u32[]{:S(2)}) collective-permute-start(f32[3227]{0:T(1024)S(1)} %add.397), channel_id=1, source_target_pairs={{0,2},{1,3},{2,0},{3,1},{4,6},{5,7},{6,4},{7,5},{8,10},{9,11},{10,... | collective-permute-start | bytes 38732 | tf_op jit(solution)/shard_map/ppermute | solution.py:437
  402.0 4.1 collective-permute-start.50
  406.0 2.9 collective-permute-start.54
  406.2 8.1 %collective-permute-start.51 = (bf16[4,1536]{1,0:T(4,128)(2,1)S(1)}, bf16[4,1536]{1,0:T(4,128)(2,1)S(1)}, u32[]{:S(2)}, u32[]{:S(2)}) collective-permute-start(bf16[4,1536]{1,0:T(4,128)(2,1)S(1)} %pad_maximum_fusion.10), channel_id=1, source_target_pairs={{0,16},{4,20},{8,24},{12,28},{16,0},{20,4},{24,8},{28,12},{1,17},{... | collective-permute-start | bytes 36872 | tf_op jit(solution)/shard_map/ppermute | solution.py:351
  409.0 3.9 collective-permute-start.55
  412.9 4.6 %collective-permute-start.56 = (f32[3224]{0:T(1024)S(1)}, f32[3224]{0:T(1024)S(1)}, u32[]{:S(2)}, u32[]{:S(2)}) collective-permute-start(f32[3224]{0:T(1024)S(1)} %add.400), channel_id=1, source_target_pairs={{0,16},{4,20},{8,24},{12,28},{16,0},{20,4},{24,8},{28,12},{1,17},{... | collective-permute-start | bytes 38696 | tf_op jit(solution)/shard_map/ppermute | solution.py:437
  (98 other events, 835.9 us)
Sparse Core Ops, SparseCore 0:
  10.3 60.8 all-gather.3
  73.5 40.2 reduce-scatter.4
  116.0 63.6 all-gather.5
  181.2 36.9 all-gather.7
  220.3 39.1 reduce-scatter.6
  261.7 77.3 reduce-scatter.8
  341.4 73.3 reduce-scatter.10

commit v5 on v4

--- a/solution.py
+++ b/solution.py
@@ -631,17 +631,14 @@
         grad_gate_heads = jnp.sum(
             gate_sums[0].reshape(heads, head_size), axis=1
         ) * (1.0 - gate_heads * gate_heads)
-        attn_part, act_grads, text_back.got[-1], parts[0] = stage(
-            attn_part, act_grads, text_back.got[-1], parts[0]
-        )
-        text_back.pass_on()
-        text_grads = dot_tn(cap_all, text_back.full(chip, core))
+        attn_part, act_grads, parts[0] = stage(attn_part, act_grads, parts[0])
         attn_grads = fsdp_scatter(attn_part)
         act_grads = widen(act_grads, 2)
         down_grads = widen(down_grads, 1)[0]
-        *parts, text_grads, down_grads, gate_grads, up_grads = stage(
-            *parts, text_grads, down_grads, *act_grads
-        )
+        *parts, down_grads, gate_grads, up_grads, text_back.got[-1] = stage(
+            *parts, down_grads, *act_grads, text_back.got[-1]
+        )
+        text_back.pass_on()
         grad_normed = seq_sum(normed_sent, parts, rows)
         grad_attn_gain = jnp.sum(grad_normed * unit_attn * (1.0 + scale_attn), axis=0)
         grad_scale_attn = jnp.sum(grad_normed * unit_attn * attn_gain, axis=0)
@@ -663,6 +660,7 @@
         while half:
             mod_mine = mod_mine[:half] + lax.ppermute(mod_mine[half:], "seq", swaps[half])
             half //= 2
+        text_grads = dot_tn(cap_all, text_back.full(chip, core))
         mod_mine = mod_mine.astype(bf16)
         bit = 1
         while bit < n_f:

time: 434 us -> 434 us (level)
  waiting for transfers between devices: 120 us -> 129 us
  other arithmetic: 30.6 us -> 25.4 us
    ppermute x9, starting transfers between devices: 15.8 us -> 32.9 us  [fsdp_xor(): return lax.ppermute(block, 'fsdp', [(i, i ^ k) for i in range(n_f)])]
    ppermute x4, starting transfers between devices: 18.2 us -> 3.9 us  [twin(): return lax.ppermute(block, 'fsdp', [(i, i ^ 1) for i in range(n_f)])]
    ppermute x12, waiting for transfers between devices: 28.9 us -> 35.4 us  [seq_send(): lax.ppermute(total[k * rows:(k + 1) * rows].astype(bf16), 'seq', swaps[k])]
    dynamic_update_slice x3, other arithmetic: 7.13 us -> 1.95 us  [full(): whole = lax.dynamic_update_slice(whole, block[None], (at, 0, 0))]
  transfers between devices with their start and end apart: 64 -> 64, of which waited for: 34 -> 35; matrix products, arithmetic and copies ran while one was open for 23% -> 20% of each run, Pallas kernels for 14% -> 14%
where the time goes in v5:
time: 434 us; the launch traced here: 428 us
  waiting for transfers between devices  129 us (30%)
  starting transfers between devices  86.7 us (20%)
  Pallas kernels  63.6 us (15%)
  matrix products  37.9 us (9%)
  local copies, waits for them, and re-layouts  36.6 us (8%)
  blocking collectives  31.5 us (7%)
  other arithmetic  25.4 us (6%)
  between operations  17.7 us (4%)
    ppermute x12, waiting for transfers between devices, seq_send(): lax.ppermute(total[k * rows:(k + 1) * rows].astype(bf16), 'seq', swaps[k])  35.4 us
    ppermute x9, starting transfers between devices, fsdp_xor(): return lax.ppermute(block, 'fsdp', [(i, i ^ k) for i in range(n_f)])  32.9 us
    all_to_all x1, blocking collectives, local(): cap_mine = lax.all_to_all(cap_mine, 'fsdp', 0, 0)  31.5 us
    ppermute x10, waiting for transfers between devices, seq_near(): return [lax.ppermute(block, 'seq', swaps[k]) for k in (1, 2)]  30 us
    unnamed x212, local copies, waits for them, and re-layouts  20.1 us
    all_gather x1, waiting for transfers between devices, local(): down_t = lax.all_gather(down_weight.T, 'fsdp', axis=0, tiled=True)  19.4 us
    pallas_call x1, Pallas kernels, self_backward(): pl.pallas_call(kernel, out_shape=(jax.ShapeDtypeStruct((rows, 3 * columns...  16.7 us
    pallas_call x1, Pallas kernels, attention_forward(): pl.pallas_call(kernel, out_shape=(wide, wide, wide, wide, jax.ShapeDtypeS...  16 us
  transfers between devices with their start and end apart: 64, of which 35 were waited for; matrix products, arithmetic and copies ran while one was open for 20% of the time, Pallas kernels for 14%

profile of v5, /device:TPU:0, one launch (start us, length us, event | category | flops | bytes accessed | tf_op | source)
XLA Modules:
  0.0 428.5 jit_solution(7408366817054912488)
XLA Ops:
  7.3 2.1 pad_maximum_fusion.3
  9.9 31.5 %all_to_all.5 = bf16[8,64,512]{2,1,0:T(8,128)(2,1)S(1)} all-to-all(bf16[8,64,512]{2,1,0:T(8,128)(2,1)S(1)} %copy.46), channel_id=1, replica_groups=mesh['fsdp'=8,'seq'=4] {'fsdp'}, dimensions={0} | all-to-all | bytes 1048576 | tf_op jit(solution)/shard_map/all_to_all | solution.py:492
  44.4 8.3 %collective-permute-done.12 = bf16[8,1,64,512]{3,2,1,0:T(8,128)(2,1)S(1)} collective-permute-done((bf16[8,1,64,512]{3,2,1,0:T(8,128)(2,1)S(1)}, bf16[8,1,64,512]{3,2,1,0:T(8,128)(2,1)S(1)}, u32[]{:S(2)}, u32[]{:S(2)}) %collective-permute-start.12) | collective-permute-done | bytes 524320 | tf_op jit(solution)/shard_map/ppermute | solution.py:393
  56.1 3.4 collective-permute-done.14
  59.5 2.7 collective-permute-done.15
  63.8 3.5 convolution_convert_fusion.3
  81.0 5.2 %collective-permute-start.2 = (bf16[4,1024]{1,0:T(4,128)(2,1)S(1)}, bf16[4,1024]{1,0:T(4,128)(2,1)S(1)}, u32[]{:S(2)}, u32[]{:S(2)}) collective-permute-start(bf16[4,1024]{1,0:T(4,128)(2,1)S(1)} %pad_maximum_fusion.11), channel_id=1, source_target_pairs={{0,16},{4,20},{8,24},{12,28},{16,0},{20,4},{24,8},{28,12},{1,17},{... | collective-permute-start | bytes 24584 | tf_op jit(solution)/shard_map/ppermute | solution.py:351
  89.6 2.9 collective-permute-start.3
  93.5 1.8 collective-permute-done.3
  95.3 2.3 collective-permute-start.4
  97.7 2.1 collective-permute-done.4
  102.9 1.9 collective-permute-done.6
  106.3 2.2 collective-permute-done.7
  112.3 6.2 %collective-permute-done.23 = bf16[128,1536]{1,0:T(8,128)(2,1)S(1)} collective-permute-done((bf16[128,1536]{1,0:T(8,128)(2,1)S(1)}, bf16[128,1536]{1,0:T(8,128)(2,1)S(1)}, u32[]{:S(2)}, u32[]{:S(2)}) %collective-permute-start.23) | collective-permute-done | bytes 393248 | tf_op jit(solution)/shard_map/ppermute | solution.py:393
  123.6 4.9 %fusion.6.qkv_ref = f32[512,1152]{1,0:T(8,128)S(1)} fusion(bf16[1536,1536]{1,0:T(8,128)(2,1)} %all-gather.4.cloned.1.call-done, bf16[512,1536]{1,0:T(8,128)(2,1)} %copy-done.34, f32[1536]{0:T(1024)S(1)} %get-tuple-element.198, f32[1536]{0:T(1024)S(1)} %copy-done.74, f32[512]{0:T(512)S(1)} %add_rsqrt_fusion), kind=kOutput, calls=%fused_computation.14 | convolution fusion | flops 1815871488 | bytes 7485440 | tf_op jit(solution)/shard_map/dot_general | solution.py:28
  129.9 16.0 %attention_forward.1 = (bf16[512,384]{1,0:T(8,128)(2,1)S(1)}, bf16[512,384]{1,0:T(8,128)(2,1)S(1)}, bf16[512,384]{1,0:T(8,128)(2,1)S(1)}, bf16[512,384]{1,0:T(8,...) custom-call(f32[512,1152]{1,0:T(8,128)S(1)} %fusion.6.qkv_ref, bf16[256,768]{1,0:T(8,128)(2,1)S(1)} %copy-done.19, ...), custom_call_target="tpu_custom_call" | custom-call | flops 603979776 | bytes 6291456 | tf_op jit(solution)/shard_map/attention_forward/pallas_call | solution.py:88
  145.9 3.1 fusion.69
  149.2 1.8 collective-permute-start.16
  152.7 1.6 constant_dynamic-update-slice_fusion.11
  154.3 1.6 constant_dynamic-update-slice_fusion.10
  156.0 5.3 %collective-permute-done.16 = bf16[128,1536]{1,0:T(8,128)(2,1)S(1)} collective-permute-done((bf16[128,1536]{1,0:T(8,128)(2,1)S(1)}, bf16[128,1536]{1,0:T(8,128)(2,1)S(1)}, u32[]{:S(2)}, u32[]{:S(2)}) %collective-permute-start.16) | collective-permute-done | bytes 393248 | tf_op jit(solution)/shard_map/ppermute | solution.py:413
  161.3 5.9 %collective-permute-done.17 = bf16[128,1536]{1,0:T(8,128)(2,1)S(1)} collective-permute-done((bf16[128,1536]{1,0:T(8,128)(2,1)S(1)}, bf16[128,1536]{1,0:T(8,128)(2,1)S(1)}, u32[]{:S(2)}, u32[]{:S(2)}) %collective-permute-start.17) | collective-permute-done | bytes 393248 | tf_op jit(solution)/shard_map/ppermute | solution.py:413
  170.9 1.7 multiply_convert_fusion.back_ref
  172.6 5.3 %collective-permute-done.19 = bf16[128,1536]{1,0:T(8,128)(2,1)S(1)} collective-permute-done((bf16[128,1536]{1,0:T(8,128)(2,1)S(1)}, bf16[128,1536]{1,0:T(8,128)(2,1)S(1)}, u32[]{:S(2)}, u32[]{:S(2)}) %collective-permute-start.19) | collective-permute-done | bytes 393248 | tf_op jit(solution)/shard_map/ppermute | solution.py:393
  181.1 2.6 collective-permute-done.21
  185.4 7.5 %ffn_forward.1 = (bf16[512,1024]{1,0:T(8,128)(2,1)S(1)}, f32[512,1024]{1,0:T(8,128)S(1)}, f32[512,1024]{1,0:T(8,128)}) custom-call(bf16[512,1536]{1,0:T(8,128)(2,1)S(1)} %constant_dynamic-update-slice_fusion.5.in_ref, bf16[1536,2048]{1,0:T(8,128)(2,1)} %all-gather.6.cloned.1.call-done.gate_ref.up_ref, ...), custom_call_target="tpu_custom_call" | custom-call | flops 3221225472 | bytes 13107200 | tf_op jit(solution)/shard_map/ffn_forward/pallas_call | solution.py:253
  195.2 3.5 convolution_convert_fusion.2
  198.8 19.4 %all-gather.8.cloned.1.call-done.down_ref = bf16[1536,1024]{1,0:T(8,128)(2,1)} async-done(((bf16[192,1024]{1,0:T(8,128)(2,1)}), bf16[1536,1024]{1,0:T(8,128)(2,1)}) %all-gather.8.cloned.1.call-update) | async-done | bytes 3145744 | tf_op jit(solution)/shard_map/all_gather | solution.py:521
  218.2 11.4 %ffn_backward.1 = (bf16[512,2048]{1,0:T(8,128)(2,1)S(1)}, bf16[512,1536]{1,0:T(8,128)(2,1)S(1)}) custom-call(bf16[512,1536]{1,0:T(8,128)(2,1)S(1)} %multiply_convert_fusion.back_ref, bf16[1536,1024]{1,0:T(8,128)(2,1)} %all-gather.8.cloned.1.call-done.down_ref, bf16[1536,2048]{1,0:T(8,128)(2,1)} %all-gather.6.cloned.1.call-done.gate_ref.up_ref, ...), custom_call_target="tpu_custom_call" | custom-call | flops 4831838208 | bytes 20447232 | tf_op jit(solution)/shard_map/ffn_backward/pallas_call | solution.py:299
  235.3 5.4 %convolution_convert_fusion = bf16[1536,2048]{1,0:T(8,128)(2,1)} fusion(bf16[512,1536]{1,0:T(8,128)(2,1)S(1)} %constant_dynamic-update-slice_fusion.5.in_ref, bf16[512,2048]{1,0:T(8,128)(2,1)S(1)} %get-tuple-element.106), kind=kOutput, calls=%fused_computation | convolution fusion | flops 3224371200 | bytes 9961472 | tf_op jit(solution)/shard_map/dot_general | solution.py:36
  240.7 3.3 collective-permute-done.27
  244.0 8.9 %collective-permute-done.28 = bf16[128,1536]{1,0:T(8,128)(2,1)} collective-permute-done((bf16[128,1536]{1,0:T(8,128)(2,1)}, bf16[128,1536]{1,0:T(8,128)(2,1)}, u32[]{:S(2)}, u32[]{:S(2)}) %collective-permute-start.28) | collective-permute-done | bytes 393248 | tf_op jit(solution)/shard_map/ppermute | solution.py:413
  253.0 2.5 multiply_reduce_fusion
  255.8 3.7 reduce-scatter.7.cloned.1.call-done.block_ref
  262.8 5.4 %collective-permute-done.30 = bf16[128,1536]{1,0:T(8,128)(2,1)S(1)} collective-permute-done((bf16[128,1536]{1,0:T(8,128)(2,1)S(1)}, bf16[128,1536]{1,0:T(8,128)(2,1)S(1)}, u32[]{:S(2)}, u32[]{:S(2)}) %collective-permute-start.30) | collective-permute-done | bytes 393248 | tf_op jit(solution)/shard_map/ppermute | solution.py:393
  269.7 1.9 collective-permute-done.31
  273.9 4.4 %collective-permute-done.33 = bf16[64,1536]{1,0:T(8,128)(2,1)S(1)} collective-permute-done((bf16[64,1536]{1,0:T(8,128)(2,1)S(1)}, bf16[64,1536]{1,0:T(8,128)(2,1)S(1)}, u32[]{:S(2)}, u32[]{:S(2)}) %collective-permute-start.33) | collective-permute-done | bytes 196640 | tf_op jit(solution)/shard_map/ppermute | solution.py:399
  279.5 2.4 convolution_convert_fusion.5.grad_ref
  282.0 5.6 %cross_backward.1 = (bf16[256,768]{1,0:T(8,128)(2,1)S(1)}, f32[512,384]{1,0:T(8,128)S(1)}, f32[8,384]{1,0:T(8,128)S(1)}) custom-call(bf16[512,384]{1,0:T(8,128)(2,1)S(1)} %get-tuple-element.113.q_ref, bf16[256,768]{1,0:T(8,128)(2,1)S(1)} %copy-done.20, bf16[512,384]{1,0:T(8,128)(2,1)S(1)} %convolution_convert_fusion.5.grad_ref, f32[512,128]{1,0:T(8,128)S(1)} %copy-done.10, ...), custom_call_target="tpu_custom_call" | custom-call | flops 503316480 | bytes 4718592 | tf_op jit(solution)/shard_map/cross_backward/pallas_call | solution.py:148
  287.6 3.5 fusion.70
  291.3 2.7 collective-permute-start.35
  298.8 16.7 %self_backward.1 = (bf16[512,1152]{1,0:T(8,128)(2,1)S(1)}, f32[8,128]{1,0:T(8,128)S(1)}) custom-call(f32[512,1152]{1,0:T(8,128)} %copy-done.2, bf16[512,384]{1,0:T(8,128)(2,1)S(1)} %get-tuple-element.113.q_ref, bf16[512,384]{1,0:T(8,128)(2,1)S(1)} %copy-done.14, bf16[512,384]{1,0:T(8,128)(2,1)S(1)} %copy-done.16, ...), custom_call_target="tpu_custom_call" | custom-call | flops 1006632960 | bytes 7864320 | tf_op jit(solution)/shard_map/self_backward/pallas_call | solution.py:217
  315.6 4.6 %collective-permute-done.35 = bf16[512,768]{1,0:T(8,128)(2,1)S(1)} collective-permute-done((bf16[512,768]{1,0:T(8,128)(2,1)S(1)}, bf16[512,768]{1,0:T(8,128)(2,1)S(1)}, u32[]{:S(2)}, u32[]{:S(2)}) %collective-permute-start.35) | collective-permute-done | bytes 786464 | tf_op jit(solution)/shard_map/ppermute | solution.py:376
  320.9 3.0 collective-permute-start.40
  323.9 3.9 fusion.71
  329.4 2.4 convolution_convert_fusion.1
  332.8 2.6 pad_maximum_fusion
  335.4 4.5 %collective-permute-done.41 = bf16[128,1536]{1,0:T(8,128)(2,1)} collective-permute-done((bf16[128,1536]{1,0:T(8,128)(2,1)S(1)}, bf16[128,1536]{1,0:T(8,128)(2,1)}, u32[]{:S(2)}, u32[]{:S(2)}) %collective-permute-start.41) | collective-permute-done | bytes 393248 | tf_op jit(solution)/shard_map/ppermute | solution.py:413
  339.9 1.7 collective-permute-start.44
  347.5 1.9 widen.3
  349.4 2.3 widen.4
  351.7 7.4 %collective-permute-done.42 = bf16[128,1536]{1,0:T(8,128)(2,1)} collective-permute-done((bf16[128,1536]{1,0:T(8,128)(2,1)}, bf16[128,1536]{1,0:T(8,128)(2,1)}, u32[]{:S(2)}, u32[]{:S(2)}) %collective-permute-start.42) | collective-permute-done | bytes 393248 | tf_op jit(solution)/shard_map/ppermute | solution.py:413
  359.2 2.1 multiply_reduce_fusion.1
  361.5 3.5 select_reduce_fusion
  367.0 2.0 collective-permute-done.45
  369.1 2.0 concatenate.150
  371.2 2.0 collective-permute-start.52
  373.2 15.8 %collective-permute-start.47 = (bf16[1,1536]{1,0:T(2,128)(2,1)S(1)}, bf16[1,1536]{1,0:T(2,128)(2,1)S(1)}, u32[]{:S(2)}, u32[]{:S(2)}) collective-permute-start(bf16[1,1536]{1,0:T(2,128)(2,1)S(1)} %fusion.42), channel_id=1, source_target_pairs={{0,4},{4,0},{8,12},{12,8},{16,20},{20,16},{24,28},{28,24},{1,5},{5... | collective-permute-start | bytes 9224 | tf_op jit(solution)/shard_map/ppermute | solution.py:351
  395.1 1.8 collective-permute-done.48
  396.9 5.3 %collective-permute-start.49 = (bf16[4,1536]{1,0:T(4,128)(2,1)S(1)}, bf16[4,1536]{1,0:T(4,128)(2,1)S(1)}, u32[]{:S(2)}, u32[]{:S(2)}) collective-permute-start(bf16[4,1536]{1,0:T(4,128)(2,1)S(1)} %pad_maximum_fusion.10), channel_id=1, source_target_pairs={{0,16},{4,20},{8,24},{12,28},{16,0},{20,4},{24,8},{28,12},{1,17},{... | collective-permute-start | bytes 36872 | tf_op jit(solution)/shard_map/ppermute | solution.py:351
  402.2 2.1 collective-permute-start.55
  407.8 3.2 collective-permute-done.56
  415.9 1.9 fusion.72
  419.0 2.1 widen.5
  (417 shorter events, 98.1 us)
Async XLA Ops:
  7.2 116.4 %all-gather.4.cloned.1.call-start = ((), (), s32[]{:S(2)}) async-start(), calls=%async_computation.5 | async-start | bytes 5308416 | tf_op jit(solution)/shard_map/all_gather | solution.py:483
  9.4 119.2 %reduce-scatter.5.cloned.1.call-start = ((), (), s32[]{:S(2)}) async-start(), calls=%async_computation.6 | async-start | bytes 3538944 | tf_op jit(solution)/shard_map/reduce_scatter | solution.py:360
  41.4 11.3 %collective-permute-start.12 = (bf16[8,1,64,512]{3,2,1,0:T(8,128)(2,1)S(1)}, bf16[8,1,64,512]{3,2,1,0:T(8,128)(2,1)S(1)}, u32[]{:S(2)}, u32[]{:S(2)}) collective-permute-start(bf16[8,1,64,512]{3,2,1,0:T(8,128)(2,1)S(1)} %bitcast.85), channel_id=1, source_target_pairs={{0,1},{1,0},{2,3},{3,2},{4,5},{5,4},{6,7},{7,6},{8,9},{9,8},{10,11... | collective-permute-start | bytes 1572872 | tf_op jit(solution)/shard_map/ppermute | solution.py:393
  42.9 12.8 %collective-permute-start.13 = (bf16[8,1,64,512]{3,2,1,0:T(8,128)(2,1)S(1)}, bf16[8,1,64,512]{3,2,1,0:T(8,128)(2,1)S(1)}, u32[]{:S(2)}, u32[]{:S(2)}) collective-permute-start(bf16[8,1,64,512]{3,2,1,0:T(8,128)(2,1)S(1)} %bitcast.86), channel_id=1, source_target_pairs={{0,2},{1,3},{2,0},{3,1},{4,6},{5,7},{6,4},{7,5},{8,10},{9,11},{10,... | collective-permute-start | bytes 1572872 | tf_op jit(solution)/shard_map/ppermute | solution.py:393
  52.7 6.8 %collective-permute-start.14 = (bf16[8,1,32,512]{3,2,1,0:T(8,128)(2,1)S(1)}, bf16[8,1,32,512]{3,2,1,0:T(8,128)(2,1)S(1)}, u32[]{:S(2)}, u32[]{:S(2)}) collective-permute-start(bf16[8,1,32,512]{3,2,1,0:T(8,128)(2,1)S(1)} %slice.328), channel_id=1, source_target_pairs={{0,2},{1,3},{2,0},{3,1},{4,6},{5,7},{6,4},{7,5},{8,10},{9,11},{10,... | collective-permute-start | bytes 786440 | tf_op jit(solution)/shard_map/ppermute | solution.py:398
  55.7 6.4 %collective-permute-start.15 = (bf16[8,1,32,512]{3,2,1,0:T(8,128)(2,1)S(1)}, bf16[8,1,32,512]{3,2,1,0:T(8,128)(2,1)S(1)}, u32[]{:S(2)}, u32[]{:S(2)}) collective-permute-start(bf16[8,1,32,512]{3,2,1,0:T(8,128)(2,1)S(1)} %slice.329), channel_id=1, source_target_pairs={{0,1},{1,0},{2,3},{3,2},{4,5},{5,4},{6,7},{7,6},{8,9},{9,8},{10,11... | collective-permute-start | bytes 786440 | tf_op jit(solution)/shard_map/ppermute | solution.py:399
  67.3 118.1 %all-gather.6.cloned.1.call-start = ((), (), s32[]{:S(2)}) async-start(), calls=%async_computation.7 | async-start | bytes 7077888 | tf_op jit(solution)/shard_map/all_gather | solution.py:483
  69.3 148.9 %all-gather.8.cloned.1.call-start = ((), (), s32[]{:S(2)}) async-start(), calls=%async_computation.8 | async-start | bytes 3538944 | tf_op jit(solution)/shard_map/all_gather | solution.py:521
  69.4 7.9 %collective-permute-start.8 = (bf16[128,1536]{1,0:T(8,128)(2,1)S(1)}, bf16[128,1536]{1,0:T(8,128)(2,1)}, u32[]{:S(2)}, u32[]{:S(2)}) collective-permute-start(bf16[128,1536]{1,0:T(8,128)(2,1)S(1)} %copy-done.25), channel_id=1, source_target_pairs={{0,1},{1,0},{2,3},{3,2},{4,5},{5,4},{6,7},{7,6},{8,9},{9,8},{10,11... | collective-permute-start | bytes 1179656 | tf_op jit(solution)/shard_map/ppermute | solution.py:393
  69.8 10.1 %collective-permute-start.9 = (bf16[128,1536]{1,0:T(8,128)(2,1)S(1)}, bf16[128,1536]{1,0:T(8,128)(2,1)}, u32[]{:S(2)}, u32[]{:S(2)}) collective-permute-start(bf16[128,1536]{1,0:T(8,128)(2,1)S(1)} %copy-done.25), channel_id=1, source_target_pairs={{0,2},{1,3},{2,0},{3,1},{4,6},{5,7},{6,4},{7,5},{8,10},{9,11},{10,... | collective-permute-start | bytes 1179656 | tf_op jit(solution)/shard_map/ppermute | solution.py:393
  71.1 188.4 %reduce-scatter.7.cloned.1.call-start = ((), (), s32[]{:S(2)}) async-start(), calls=%async_computation.9 | async-start | bytes 3538944 | tf_op jit(solution)/shard_map/reduce_scatter | solution.py:360
  74.1 1.2 collective-permute-start
  75.3 5.7 %collective-permute-start.1 = (bf16[2,1024]{1,0:T(2,128)(2,1)S(1)}, bf16[2,1024]{1,0:T(2,128)(2,1)S(1)}, u32[]{:S(2)}, u32[]{:S(2)}) collective-permute-start(bf16[2,1024]{1,0:T(2,128)(2,1)S(1)} %pad_maximum_fusion.13), channel_id=1, source_target_pairs={{0,8},{4,12},{8,0},{12,4},{16,24},{20,28},{24,16},{28,20},{1,9},{5... | collective-permute-start | bytes 12296 | tf_op jit(solution)/shard_map/ppermute | solution.py:351
  78.3 19.4 %collective-permute-start.10 = (bf16[64,1536]{1,0:T(8,128)(2,1)S(1)}, bf16[64,1536]{1,0:T(8,128)(2,1)S(1)}, u32[]{:S(2)}, u32[]{:S(2)}) collective-permute-start(bf16[64,1536]{1,0:T(8,128)(2,1)S(1)} %slice.324), channel_id=1, source_target_pairs={{0,2},{1,3},{2,0},{3,1},{4,6},{5,7},{6,4},{7,5},{8,10},{9,11},{10,... | collective-permute-start | bytes 589832 | tf_op jit(solution)/shard_map/ppermute | solution.py:398
  80.8 19.1 %collective-permute-start.11 = (bf16[64,1536]{1,0:T(8,128)(2,1)S(1)}, bf16[64,1536]{1,0:T(8,128)(2,1)S(1)}, u32[]{:S(2)}, u32[]{:S(2)}) collective-permute-start(bf16[64,1536]{1,0:T(8,128)(2,1)S(1)} %slice.325), channel_id=1, source_target_pairs={{0,1},{1,0},{2,3},{3,2},{4,5},{5,4},{6,7},{7,6},{8,9},{9,8},{10,11... | collective-permute-start | bytes 589832 | tf_op jit(solution)/shard_map/ppermute | solution.py:399
  81.0 7.3 %collective-permute-start.2 = (bf16[4,1024]{1,0:T(4,128)(2,1)S(1)}, bf16[4,1024]{1,0:T(4,128)(2,1)S(1)}, u32[]{:S(2)}, u32[]{:S(2)}) collective-permute-start(bf16[4,1024]{1,0:T(4,128)(2,1)S(1)} %pad_maximum_fusion.11), channel_id=1, source_target_pairs={{0,16},{4,20},{8,24},{12,28},{16,0},{20,4},{24,8},{28,12},{1,17},{... | collective-permute-start | bytes 24584 | tf_op jit(solution)/shard_map/ppermute | solution.py:351
  89.6 5.7 %collective-permute-start.3 = (f32[4,1536]{1,0:T(4,128)S(1)}, f32[4,1536]{1,0:T(4,128)S(1)}, u32[]{:S(2)}, u32[]{:S(2)}) collective-permute-start(f32[4,1536]{1,0:T(4,128)S(1)} %slice.314), channel_id=1, source_target_pairs={{0,16},{4,20},{8,24},{12,28},{16,0},{20,4},{24,8},{28,12},{1,17},{... | collective-permute-start | bytes 73736 | tf_op jit(solution)/shard_map/ppermute | solution.py:351
  95.3 4.5 %collective-permute-start.4 = (f32[2,1536]{1,0:T(2,128)S(1)}, f32[2,1536]{1,0:T(2,128)S(1)}, u32[]{:S(2)}, u32[]{:S(2)}) collective-permute-start(f32[2,1536]{1,0:T(2,128)S(1)} %slice.316), channel_id=1, source_target_pairs={{0,8},{4,12},{8,0},{12,4},{16,24},{20,28},{24,16},{28,20},{1,9},{5... | collective-permute-start | bytes 36872 | tf_op jit(solution)/shard_map/ppermute | solution.py:351
  99.8 1.2 collective-permute-start.5
  101.1 3.7 collective-permute-start.6
  104.8 3.8 collective-permute-start.7
  108.7 9.7 %collective-permute-start.23 = (bf16[128,1536]{1,0:T(8,128)(2,1)S(1)}, bf16[128,1536]{1,0:T(8,128)(2,1)S(1)}, u32[]{:S(2)}, u32[]{:S(2)}) collective-permute-start(bf16[128,1536]{1,0:T(8,128)(2,1)S(1)} %copy-done.28), channel_id=1, source_target_pairs={{0,1},{1,0},{2,3},{3,2},{4,5},{5,4},{6,7},{7,6},{8,9},{9,8},{10,11... | collective-permute-start | bytes 1179656 | tf_op jit(solution)/shard_map/ppermute | solution.py:393
  110.2 10.5 %collective-permute-start.24 = (bf16[128,1536]{1,0:T(8,128)(2,1)S(1)}, bf16[128,1536]{1,0:T(8,128)(2,1)S(1)}, u32[]{:S(2)}, u32[]{:S(2)}) collective-permute-start(bf16[128,1536]{1,0:T(8,128)(2,1)S(1)} %copy-done.28), channel_id=1, source_target_pairs={{0,2},{1,3},{2,0},{3,1},{4,6},{5,7},{6,4},{7,5},{8,10},{9,11},{10,... | collective-permute-start | bytes 1179656 | tf_op jit(solution)/shard_map/ppermute | solution.py:393
  119.2 33.5 %collective-permute-start.25 = (bf16[64,1536]{1,0:T(8,128)(2,1)}, bf16[64,1536]{1,0:T(8,128)(2,1)}, u32[]{:S(2)}, u32[]{:S(2)}) collective-permute-start(bf16[64,1536]{1,0:T(8,128)(2,1)} %slice.339), channel_id=1, source_target_pairs={{0,2},{1,3},{2,0},{3,1},{4,6},{5,7},{6,4},{7,5},{8,10},{9,11},{10,... | collective-permute-start | bytes 589832 | tf_op jit(solution)/shard_map/ppermute | solution.py:398
  121.3 33.0 %collective-permute-start.26 = (bf16[64,1536]{1,0:T(8,128)(2,1)}, bf16[64,1536]{1,0:T(8,128)(2,1)}, u32[]{:S(2)}, u32[]{:S(2)}) collective-permute-start(bf16[64,1536]{1,0:T(8,128)(2,1)} %slice.340), channel_id=1, source_target_pairs={{0,1},{1,0},{2,3},{3,2},{4,5},{5,4},{6,7},{7,6},{8,9},{9,8},{10,11... | collective-permute-start | bytes 589832 | tf_op jit(solution)/shard_map/ppermute | solution.py:399
  149.2 12.1 %collective-permute-start.16 = (bf16[128,1536]{1,0:T(8,128)(2,1)S(1)}, bf16[128,1536]{1,0:T(8,128)(2,1)S(1)}, u32[]{:S(2)}, u32[]{:S(2)}) collective-permute-start(bf16[128,1536]{1,0:T(8,128)(2,1)S(1)} %get-tuple-element.186), channel_id=1, source_target_pairs={{0,1},{1,0},{2,3},{3,2},{4,5},{5,4},{6,7},{7,6},{8,9},{9,8},{10,11... | collective-permute-start | bytes 1179656 | tf_op jit(solution)/shard_map/ppermute | solution.py:413
  150.9 16.2 %collective-permute-start.17 = (bf16[128,1536]{1,0:T(8,128)(2,1)S(1)}, bf16[128,1536]{1,0:T(8,128)(2,1)S(1)}, u32[]{:S(2)}, u32[]{:S(2)}) collective-permute-start(bf16[128,1536]{1,0:T(8,128)(2,1)S(1)} %get-tuple-element.188), channel_id=1, source_target_pairs={{0,2},{1,3},{2,0},{3,1},{4,6},{5,7},{6,4},{7,5},{8,10},{9,11},{10,... | collective-permute-start | bytes 1179656 | tf_op jit(solution)/shard_map/ppermute | solution.py:413
  151.7 15.5 %collective-permute-start.18 = (bf16[128,1536]{1,0:T(8,128)(2,1)S(1)}, bf16[128,1536]{1,0:T(8,128)(2,1)S(1)}, u32[]{:S(2)}, u32[]{:S(2)}) collective-permute-start(bf16[128,1536]{1,0:T(8,128)(2,1)S(1)} %get-tuple-element.187), channel_id=1, source_target_pairs={{0,3},{1,2},{2,1},{3,0},{4,7},{5,6},{6,5},{7,4},{8,11},{9,10},{10,... | collective-permute-start | bytes 1179656 | tf_op jit(solution)/shard_map/ppermute | solution.py:413
  169.0 9.0 %collective-permute-start.19 = (bf16[128,1536]{1,0:T(8,128)(2,1)S(1)}, bf16[128,1536]{1,0:T(8,128)(2,1)S(1)}, u32[]{:S(2)}, u32[]{:S(2)}) collective-permute-start(bf16[128,1536]{1,0:T(8,128)(2,1)S(1)} %get-tuple-element.171), channel_id=1, source_target_pairs={{0,1},{1,0},{2,3},{3,2},{4,5},{5,4},{6,7},{7,6},{8,9},{9,8},{10,11... | collective-permute-start | bytes 1179656 | tf_op jit(solution)/shard_map/ppermute | solution.py:393
  169.7 9.9 %collective-permute-start.20 = (bf16[128,1536]{1,0:T(8,128)(2,1)S(1)}, bf16[128,1536]{1,0:T(8,128)(2,1)S(1)}, u32[]{:S(2)}, u32[]{:S(2)}) collective-permute-start(bf16[128,1536]{1,0:T(8,128)(2,1)S(1)} %get-tuple-element.171), channel_id=1, source_target_pairs={{0,2},{1,3},{2,0},{3,1},{4,6},{5,7},{6,4},{7,5},{8,10},{9,11},{10,... | collective-permute-start | bytes 1179656 | tf_op jit(solution)/shard_map/ppermute | solution.py:393
  178.0 5.7 %collective-permute-start.21 = (bf16[64,1536]{1,0:T(8,128)(2,1)S(1)}, bf16[64,1536]{1,0:T(8,128)(2,1)S(1)}, u32[]{:S(2)}, u32[]{:S(2)}) collective-permute-start(bf16[64,1536]{1,0:T(8,128)(2,1)S(1)} %slice.337), channel_id=1, source_target_pairs={{0,2},{1,3},{2,0},{3,1},{4,6},{5,7},{6,4},{7,5},{8,10},{9,11},{10,... | collective-permute-start | bytes 589832 | tf_op jit(solution)/shard_map/ppermute | solution.py:398
  179.6 5.7 %collective-permute-start.22 = (bf16[64,1536]{1,0:T(8,128)(2,1)S(1)}, bf16[64,1536]{1,0:T(8,128)(2,1)S(1)}, u32[]{:S(2)}, u32[]{:S(2)}) collective-permute-start(bf16[64,1536]{1,0:T(8,128)(2,1)S(1)} %slice.338), channel_id=1, source_target_pairs={{0,1},{1,0},{2,3},{3,2},{4,5},{5,4},{6,7},{7,6},{8,9},{9,8},{10,11... | collective-permute-start | bytes 589832 | tf_op jit(solution)/shard_map/ppermute | solution.py:399
  198.7 141.2 %reduce-scatter.9.cloned.1.call-start = ((), (), s32[]{:S(2)}) async-start(), calls=%async_computation.10 | async-start | bytes 7077888 | tf_op jit(solution)/shard_map/reduce_scatter | solution.py:360
  231.8 12.3 %collective-permute-start.27 = (bf16[128,1536]{1,0:T(8,128)(2,1)}, bf16[128,1536]{1,0:T(8,128)(2,1)}, u32[]{:S(2)}, u32[]{:S(2)}) collective-permute-start(bf16[128,1536]{1,0:T(8,128)(2,1)} %get-tuple-element.185), channel_id=1, source_target_pairs={{0,1},{1,0},{2,3},{3,2},{4,5},{5,4},{6,7},{7,6},{8,9},{9,8},{10,11... | collective-permute-start | bytes 1179656 | tf_op jit(solution)/shard_map/ppermute | solution.py:413
  233.2 19.7 %collective-permute-start.28 = (bf16[128,1536]{1,0:T(8,128)(2,1)}, bf16[128,1536]{1,0:T(8,128)(2,1)}, u32[]{:S(2)}, u32[]{:S(2)}) collective-permute-start(bf16[128,1536]{1,0:T(8,128)(2,1)} %get-tuple-element.184), channel_id=1, source_target_pairs={{0,2},{1,3},{2,0},{3,1},{4,6},{5,7},{6,4},{7,5},{8,10},{9,11},{10,... | collective-permute-start | bytes 1179656 | tf_op jit(solution)/shard_map/ppermute | solution.py:413
  234.7 18.2 %collective-permute-start.29 = (bf16[128,1536]{1,0:T(8,128)(2,1)S(1)}, bf16[128,1536]{1,0:T(8,128)(2,1)}, u32[]{:S(2)}, u32[]{:S(2)}) collective-permute-start(bf16[128,1536]{1,0:T(8,128)(2,1)S(1)} %get-tuple-element.183), channel_id=1, source_target_pairs={{0,3},{1,2},{2,1},{3,0},{4,7},{5,6},{6,5},{7,4},{8,11},{9,10},{10,... | collective-permute-start | bytes 1179656 | tf_op jit(solution)/shard_map/ppermute | solution.py:413
  259.6 159.5 %reduce-scatter.11.cloned.1.call-start = ((), (), s32[]{:S(2)}) async-start(), calls=%async_computation.11 | async-start | bytes 5308416 | tf_op jit(solution)/shard_map/reduce_scatter | solution.py:360
  259.8 8.4 %collective-permute-start.30 = (bf16[128,1536]{1,0:T(8,128)(2,1)S(1)}, bf16[128,1536]{1,0:T(8,128)(2,1)S(1)}, u32[]{:S(2)}, u32[]{:S(2)}) collective-permute-start(bf16[128,1536]{1,0:T(8,128)(2,1)S(1)} %get-tuple-element.111), channel_id=1, source_target_pairs={{0,1},{1,0},{2,3},{3,2},{4,5},{5,4},{6,7},{7,6},{8,9},{9,8},{10,11... | collective-permute-start | bytes 1179656 | tf_op jit(solution)/shard_map/ppermute | solution.py:393
  261.3 10.3 %collective-permute-start.31 = (bf16[128,1536]{1,0:T(8,128)(2,1)S(1)}, bf16[128,1536]{1,0:T(8,128)(2,1)}, u32[]{:S(2)}, u32[]{:S(2)}) collective-permute-start(bf16[128,1536]{1,0:T(8,128)(2,1)S(1)} %get-tuple-element.111), channel_id=1, source_target_pairs={{0,2},{1,3},{2,0},{3,1},{4,6},{5,7},{6,4},{7,5},{8,10},{9,11},{10,... | collective-permute-start | bytes 1179656 | tf_op jit(solution)/shard_map/ppermute | solution.py:393
  268.2 5.7 %collective-permute-start.32 = (bf16[64,1536]{1,0:T(8,128)(2,1)S(1)}, bf16[64,1536]{1,0:T(8,128)(2,1)S(1)}, u32[]{:S(2)}, u32[]{:S(2)}) collective-permute-start(bf16[64,1536]{1,0:T(8,128)(2,1)S(1)} %slice.341), channel_id=1, source_target_pairs={{0,2},{1,3},{2,0},{3,1},{4,6},{5,7},{6,4},{7,5},{8,10},{9,11},{10,... | collective-permute-start | bytes 589832 | tf_op jit(solution)/shard_map/ppermute | solution.py:398
  272.6 5.7 %collective-permute-start.33 = (bf16[64,1536]{1,0:T(8,128)(2,1)S(1)}, bf16[64,1536]{1,0:T(8,128)(2,1)S(1)}, u32[]{:S(2)}, u32[]{:S(2)}) collective-permute-start(bf16[64,1536]{1,0:T(8,128)(2,1)S(1)} %slice.342), channel_id=1, source_target_pairs={{0,1},{1,0},{2,3},{3,2},{4,5},{5,4},{6,7},{7,6},{8,9},{9,8},{10,11... | collective-permute-start | bytes 589832 | tf_op jit(solution)/shard_map/ppermute | solution.py:399
  287.6 3.6 collective-permute-start.34
  291.3 28.9 %collective-permute-start.35 = (bf16[512,768]{1,0:T(8,128)(2,1)S(1)}, bf16[512,768]{1,0:T(8,128)(2,1)S(1)}, u32[]{:S(2)}, u32[]{:S(2)}) collective-permute-start(bf16[512,768]{1,0:T(8,128)(2,1)S(1)} %pad_maximum_fusion.2), channel_id=1, source_target_pairs={{0,8},{8,16},{16,24},{12,4},{20,12},{28,20},{1,9},{9,17},{17,25},{... | collective-permute-start | bytes 2359304 | tf_op jit(solution)/shard_map/ppermute | solution.py:376
  294.1 21.5 %collective-permute-start.36 = (bf16[128,1536]{1,0:T(8,128)(2,1)S(1)}, bf16[128,1536]{1,0:T(8,128)(2,1)S(1)}, u32[]{:S(2)}, u32[]{:S(2)}) collective-permute-start(bf16[128,1536]{1,0:T(8,128)(2,1)S(1)} %get-tuple-element.182), channel_id=1, source_target_pairs={{0,1},{1,0},{2,3},{3,2},{4,5},{5,4},{6,7},{7,6},{8,9},{9,8},{10,11... | collective-permute-start | bytes 1179656 | tf_op jit(solution)/shard_map/ppermute | solution.py:413
  294.8 20.8 %collective-permute-start.37 = (bf16[128,1536]{1,0:T(8,128)(2,1)S(1)}, bf16[128,1536]{1,0:T(8,128)(2,1)S(1)}, u32[]{:S(2)}, u32[]{:S(2)}) collective-permute-start(bf16[128,1536]{1,0:T(8,128)(2,1)S(1)} %get-tuple-element.181), channel_id=1, source_target_pairs={{0,2},{1,3},{2,0},{3,1},{4,6},{5,7},{6,4},{7,5},{8,10},{9,11},{10,... | collective-permute-start | bytes 1179656 | tf_op jit(solution)/shard_map/ppermute | solution.py:413
  296.1 19.5 %collective-permute-start.38 = (bf16[128,1536]{1,0:T(8,128)(2,1)S(1)}, bf16[128,1536]{1,0:T(8,128)(2,1)S(1)}, u32[]{:S(2)}, u32[]{:S(2)}) collective-permute-start(bf16[128,1536]{1,0:T(8,128)(2,1)S(1)} %get-tuple-element.180), channel_id=1, source_target_pairs={{0,3},{1,2},{2,1},{3,0},{4,7},{5,6},{6,5},{7,4},{8,11},{9,10},{10,... | collective-permute-start | bytes 1179656 | tf_op jit(solution)/shard_map/ppermute | solution.py:413
  320.2 11.6 %collective-permute-start.39 = (bf16[512,768]{1,0:T(8,128)(2,1)S(1)}, bf16[512,768]{1,0:T(8,128)(2,1)S(1)}, u32[]{:S(2)}, u32[]{:S(2)}) collective-permute-start(bf16[512,768]{1,0:T(8,128)(2,1)S(1)} %collective-permute-done.35), channel_id=1, source_target_pairs={{8,16},{16,24},{12,4},{20,12},{9,17},{17,25},{13,5},{21,13},{10,18... | collective-permute-start | bytes 2359304 | tf_op jit(solution)/shard_map/ppermute | solution.py:376
  320.9 10.9 %collective-permute-start.40 = (bf16[512,768]{1,0:T(8,128)(2,1)S(1)}, bf16[512,768]{1,0:T(8,128)(2,1)S(1)}, u32[]{:S(2)}, u32[]{:S(2)}) collective-permute-start(bf16[512,768]{1,0:T(8,128)(2,1)S(1)} %collective-permute-done.35), channel_id=1, source_target_pairs={{0,4},{4,0},{8,12},{12,8},{16,20},{20,16},{24,28},{28,24},{1,5},{5... | collective-permute-start | bytes 2359304 | tf_op jit(solution)/shard_map/ppermute | solution.py:348
  328.7 11.2 %collective-permute-start.41 = (bf16[128,1536]{1,0:T(8,128)(2,1)S(1)}, bf16[128,1536]{1,0:T(8,128)(2,1)}, u32[]{:S(2)}, u32[]{:S(2)}) collective-permute-start(bf16[128,1536]{1,0:T(8,128)(2,1)S(1)} %get-tuple-element.179), channel_id=1, source_target_pairs={{0,1},{1,0},{2,3},{3,2},{4,5},{5,4},{6,7},{7,6},{8,9},{9,8},{10,11... | collective-permute-start | bytes 1179656 | tf_op jit(solution)/shard_map/ppermute | solution.py:413
  339.9 19.2 %collective-permute-start.44 = (bf16[512,768]{1,0:T(8,128)(2,1)S(1)}, bf16[512,768]{1,0:T(8,128)(2,1)}, u32[]{:S(2)}, u32[]{:S(2)}) collective-permute-start(bf16[512,768]{1,0:T(8,128)(2,1)S(1)} %collective-permute-done.39), channel_id=1, source_target_pairs={{16,24},{12,4},{17,25},{13,5},{18,26},{14,6},{19,27},{15,7}} | collective-permute-start | bytes 2359304 | tf_op jit(solution)/shard_map/ppermute | solution.py:376
  341.6 17.5 %collective-permute-start.42 = (bf16[128,1536]{1,0:T(8,128)(2,1)}, bf16[128,1536]{1,0:T(8,128)(2,1)}, u32[]{:S(2)}, u32[]{:S(2)}) collective-permute-start(bf16[128,1536]{1,0:T(8,128)(2,1)} %get-tuple-element.178), channel_id=1, source_target_pairs={{0,2},{1,3},{2,0},{3,1},{4,6},{5,7},{6,4},{7,5},{8,10},{9,11},{10,... | collective-permute-start | bytes 1179656 | tf_op jit(solution)/shard_map/ppermute | solution.py:413
  343.0 16.1 %collective-permute-start.43 = (bf16[128,1536]{1,0:T(8,128)(2,1)S(1)}, bf16[128,1536]{1,0:T(8,128)(2,1)}, u32[]{:S(2)}, u32[]{:S(2)}) collective-permute-start(bf16[128,1536]{1,0:T(8,128)(2,1)S(1)} %get-tuple-element.177), channel_id=1, source_target_pairs={{0,3},{1,2},{2,1},{3,0},{4,7},{5,6},{6,5},{7,4},{8,11},{9,10},{10,... | collective-permute-start | bytes 1179656 | tf_op jit(solution)/shard_map/ppermute | solution.py:413
  365.2 3.8 collective-permute-start.45
  369.0 4.1 collective-permute-start.46
  371.2 20.1 %collective-permute-start.52 = (f32[3227]{0:T(1024)S(1)}, f32[3227]{0:T(1024)S(1)}, u32[]{:S(2)}, u32[]{:S(2)}) collective-permute-start(f32[3227]{0:T(1024)S(1)} %concatenate.150), channel_id=1, source_target_pairs={{0,1},{1,0},{2,3},{3,2},{4,5},{5,4},{6,7},{7,6},{8,9},{9,8},{10,11... | collective-permute-start | bytes 38732 | tf_op jit(solution)/shard_map/ppermute | solution.py:437
  373.2 19.6 %collective-permute-start.47 = (bf16[1,1536]{1,0:T(2,128)(2,1)S(1)}, bf16[1,1536]{1,0:T(2,128)(2,1)S(1)}, u32[]{:S(2)}, u32[]{:S(2)}) collective-permute-start(bf16[1,1536]{1,0:T(2,128)(2,1)S(1)} %fusion.42), channel_id=1, source_target_pairs={{0,4},{4,0},{8,12},{12,8},{16,20},{20,16},{24,28},{28,24},{1,5},{5... | collective-permute-start | bytes 9224 | tf_op jit(solution)/shard_map/ppermute | solution.py:351
  390.4 22.6 %collective-permute-start.51 = (bf16[512,768]{1,0:T(8,128)(2,1)S(1)}, bf16[512,768]{1,0:T(8,128)(2,1)S(1)}, u32[]{:S(2)}, u32[]{:S(2)}) collective-permute-start(bf16[512,768]{1,0:T(8,128)(2,1)S(1)} %copy-done.43), channel_id=1, source_target_pairs={{0,4},{4,0},{8,12},{12,8},{16,20},{20,16},{24,28},{28,24},{1,5},{5... | collective-permute-start | bytes 2359304 | tf_op jit(solution)/shard_map/ppermute | solution.py:348
  391.2 21.5 %collective-permute-start.50 = (bf16[512,768]{1,0:T(8,128)(2,1)}, bf16[512,768]{1,0:T(8,128)(2,1)S(1)}, u32[]{:S(2)}, u32[]{:S(2)}) collective-permute-start(bf16[512,768]{1,0:T(8,128)(2,1)} %collective-permute-done.44), channel_id=1, source_target_pairs={{0,4},{4,0},{8,12},{12,8},{16,20},{20,16},{24,28},{28,24},{1,5},{5... | collective-permute-start | bytes 2359304 | tf_op jit(solution)/shard_map/ppermute | solution.py:348
  391.2 3.8 collective-permute-start.53
  392.8 4.1 collective-permute-start.48
  395.1 7.2 %collective-permute-start.54 = (f32[3224]{0:T(1024)S(1)}, f32[3224]{0:T(1024)S(1)}, u32[]{:S(2)}, u32[]{:S(2)}) collective-permute-start(f32[3224]{0:T(1024)S(1)} %bitcast.93), channel_id=1, source_target_pairs={{0,4},{4,0},{8,12},{12,8},{16,20},{20,16},{24,28},{28,24},{1,5},{5... | collective-permute-start | bytes 38696 | tf_op jit(solution)/shard_map/ppermute | solution.py:437
  396.9 9.6 %collective-permute-start.49 = (bf16[4,1536]{1,0:T(4,128)(2,1)S(1)}, bf16[4,1536]{1,0:T(4,128)(2,1)S(1)}, u32[]{:S(2)}, u32[]{:S(2)}) collective-permute-start(bf16[4,1536]{1,0:T(4,128)(2,1)S(1)} %pad_maximum_fusion.10), channel_id=1, source_target_pairs={{0,16},{4,20},{8,24},{12,28},{16,0},{20,4},{24,8},{28,12},{1,17},{... | collective-permute-start | bytes 36872 | tf_op jit(solution)/shard_map/ppermute | solution.py:351
  402.2 4.1 collective-permute-start.55
  406.4 4.6 %collective-permute-start.56 = (f32[3224]{0:T(1024)S(1)}, f32[3224]{0:T(1024)S(1)}, u32[]{:S(2)}, u32[]{:S(2)}) collective-permute-start(f32[3224]{0:T(1024)S(1)} %add.400), channel_id=1, source_target_pairs={{0,16},{4,20},{8,24},{12,28},{16,0},{20,4},{24,8},{28,12},{1,17},{... | collective-permute-start | bytes 38696 | tf_op jit(solution)/shard_map/ppermute | solution.py:437
  (98 other events, 858.0 us)
Sparse Core Ops, SparseCore 0:
  10.3 60.8 all-gather.3
  73.5 40.2 reduce-scatter.4
  116.0 63.6 all-gather.5
  181.2 36.9 all-gather.7
  220.3 39.1 reduce-scatter.6
  261.7 77.3 reduce-scatter.8
  341.4 64.3 reduce-scatter.10

commit v6 on v4

--- a/solution.py
+++ b/solution.py
@@ -233,9 +233,8 @@
     )(qkv, query, key, value, grad, lse, cross_query, cosine, sine, gains, mask)
 
 
-def ffn_forward(ffn_in, weights):
+def ffn_forward(ffn_in, weights, units):
     rows, width = ffn_in.shape
-    units = weights.shape[1] // 2
     tile = min(units, 256)
     tiles = units // tile
 
@@ -270,9 +269,9 @@
     )(ffn_in, weights, weights)
 
 
-def ffn_backward(back, down, weights, by_gate, by_up):
+def ffn_backward(back, weights, by_gate, by_up):
     rows, width = back.shape
-    units = down.shape[1]
+    units = by_up.shape[1]
     tile = min(units, 256)
     tiles = units // tile
 
@@ -305,7 +304,7 @@
         ),
         in_specs=[
             whole,
-            pl.BlockSpec((width, tile), lambda j: (0, j)),
+            pl.BlockSpec((width, tile), lambda j: (0, 2 * tiles + j)),
             pl.BlockSpec((width, tile), lambda j: (0, j)),
             pl.BlockSpec((width, tile), lambda j: (0, tiles + j)),
             part,
@@ -320,7 +319,7 @@
             transcendentals=0,
         ),
         name="ffn_backward",
-    )(back, down, weights, weights, by_gate, by_up)
+    )(back, weights, weights, weights, by_gate, by_up)
 
 
 def widen(block, parts):
@@ -517,8 +516,8 @@
         text_own = jnp.concatenate([textkey_weight, textvalue_weight], axis=1)
         text_part = dot(cap_all, text_own).astype(bf16)
         text_both = fsdp_scatter(text_part)
-        ffn_full = fsdp_gather(after(gate_weight, text_part), up_weight)
-        down_t = lax.all_gather(down_weight.T, "fsdp", axis=0, tiled=True)
+        ffn_full = fsdp_gather(after(gate_weight, text_part), up_weight, down_weight.T)
+        down_t = ffn_full[:, 2 * units :]
         tokens_all = tokens_all.astype(f32)
         cotangent_all = seq_gather(after(cotangent, cap_all)).astype(f32)
 
@@ -565,11 +564,11 @@
         ffn_in = (unit_ffn * ffn_gain * (1.0 + scale_ffn)).astype(bf16)
         ffn_all = seq_gather(ffn_in)
         ffn_back_all = (tanh_ffn * cotangent_all).astype(bf16)
-        hidden, by_gate, by_up = ffn_forward(ffn_all, ffn_full)
+        hidden, by_gate, by_up = ffn_forward(ffn_all, ffn_full, units)
         down_part = dot_tn(ffn_back_all, hidden).astype(bf16)
         down_grads = fsdp_scatter(down_part)
         grad_act, grad_sent = ffn_backward(
-            ffn_back_all, after(down_t, down_part), ffn_full, by_gate, by_up
+            after(ffn_back_all, down_part), ffn_full, by_gate, by_up
         )
         parts = seq_send(grad_sent, rows)
         act_part = dot_tn(ffn_all, grad_act).astype(bf16)

time: 434 us -> 432 us (level)
    all_gather x2, waiting for transfers between devices: 0.02 us -> 20.4 us  [fsdp_gather(): lax.all_gather(jnp.concatenate(parts, axis=1), 'fsdp', axis=0, tiled=True)]
    all_gather x1 -> x0, waiting for transfers between devices: 19.4 us -> none  [local(): down_t = lax.all_gather(down_weight.T, 'fsdp', axis=0, tiled=True)]
    ppermute x9, waiting for transfers between devices: 7.15 us -> 11.6 us  [fsdp_xor(): return lax.ppermute(block, 'fsdp', [(i, i ^ k) for i in range(n_f)])]
    unnamed x212 -> x208, local copies, waits for them, and re-layouts: 17.3 us -> 15.7 us
  transfers between devices with their start and end apart: 64 -> 63, of which waited for: 34 -> 33; matrix products, arithmetic and copies ran while one was open for 23% -> 22% of each run, Pallas kernels for 14% -> 13%
where the time goes in v6:
time: 432 us; the launch traced here: 427 us
  waiting for transfers between devices  122 us (28%)
  starting transfers between devices  83.3 us (19%)
  Pallas kernels  63.5 us (15%)
  matrix products  42.7 us (10%)
  local copies, waits for them, and re-layouts  35.4 us (8%)
  blocking collectives  31.5 us (7%)
  other arithmetic  30.8 us (7%)
  between operations  17.4 us (4%)
    all_to_all x1, blocking collectives, local(): cap_mine = lax.all_to_all(cap_mine, 'fsdp', 0, 0)  31.5 us
    ppermute x10, waiting for transfers between devices, seq_near(): return [lax.ppermute(block, 'seq', swaps[k]) for k in (1, 2)]  29.6 us
    ppermute x12, waiting for transfers between devices, seq_send(): lax.ppermute(total[k * rows:(k + 1) * rows].astype(bf16), 'seq', swaps[k])  27.8 us
    all_gather x2, waiting for transfers between devices, fsdp_gather(): lax.all_gather(jnp.concatenate(parts, axis=1), 'fsdp', axis=0, tiled=True)  20.4 us
    dot_general x6, matrix products, dot_tn(): lax.dot_general(left, right, (((0,), (0,)), ((), ())), preferred_element_...  18.6 us
    pallas_call x1, Pallas kernels, self_backward(): pl.pallas_call(kernel, out_shape=(jax.ShapeDtypeStruct((rows, 3 * columns...  16.7 us
    ppermute x4, starting transfers between devices, twin(): return lax.ppermute(block, 'fsdp', [(i, i ^ 1) for i in range(n_f)])  16.5 us
    pallas_call x1, Pallas kernels, attention_forward(): pl.pallas_call(kernel, out_shape=(wide, wide, wide, wide, jax.ShapeDtypeS...  16 us
  transfers between devices with their start and end apart: 63, of which 33 were waited for; matrix products, arithmetic and copies ran while one was open for 22% of the time, Pallas kernels for 13%

profile of v6, /device:TPU:0, one launch (start us, length us, event | category | flops | bytes accessed | tf_op | source)
XLA Modules:
  0.0 426.6 jit_solution(11418560420191366847)
XLA Ops:
  7.3 2.1 pad_maximum_fusion.3
  9.9 31.5 %all_to_all.5 = bf16[8,64,512]{2,1,0:T(8,128)(2,1)S(1)} all-to-all(bf16[8,64,512]{2,1,0:T(8,128)(2,1)S(1)} %copy.46), channel_id=1, replica_groups=mesh['fsdp'=8,'seq'=4] {'fsdp'}, dimensions={0} | all-to-all | bytes 1048576 | tf_op jit(solution)/shard_map/all_to_all | solution.py:491
  44.4 8.3 %collective-permute-done.12 = bf16[8,1,64,512]{3,2,1,0:T(8,128)(2,1)S(1)} collective-permute-done((bf16[8,1,64,512]{3,2,1,0:T(8,128)(2,1)S(1)}, bf16[8,1,64,512]{3,2,1,0:T(8,128)(2,1)S(1)}, u32[]{:S(2)}, u32[]{:S(2)}) %collective-permute-start.12) | collective-permute-done | bytes 524320 | tf_op jit(solution)/shard_map/ppermute | solution.py:392
  56.1 3.4 collective-permute-done.14
  59.5 2.7 collective-permute-done.15
  63.8 3.5 convolution_convert_fusion.3
  81.4 5.2 %collective-permute-start.2 = (bf16[4,1024]{1,0:T(4,128)(2,1)S(1)}, bf16[4,1024]{1,0:T(4,128)(2,1)S(1)}, u32[]{:S(2)}, u32[]{:S(2)}) collective-permute-start(bf16[4,1024]{1,0:T(4,128)(2,1)S(1)} %pad_maximum_fusion.11), channel_id=1, source_target_pairs={{0,16},{4,20},{8,24},{12,28},{16,0},{20,4},{24,8},{28,12},{1,17},{... | collective-permute-start | bytes 24584 | tf_op jit(solution)/shard_map/ppermute | solution.py:350
  86.6 2.1 collective-permute-done.2
  89.0 2.8 collective-permute-start.3
  91.8 3.2 collective-permute-done.3
  95.2 4.1 collective-permute-done.4
  102.4 1.8 collective-permute-done.6
  105.4 2.7 collective-permute-done.7
  111.8 6.2 %collective-permute-done.23 = bf16[128,1536]{1,0:T(8,128)(2,1)S(1)} collective-permute-done((bf16[128,1536]{1,0:T(8,128)(2,1)S(1)}, bf16[128,1536]{1,0:T(8,128)(2,1)S(1)}, u32[]{:S(2)}, u32[]{:S(2)}) %collective-permute-start.23) | collective-permute-done | bytes 393248 | tf_op jit(solution)/shard_map/ppermute | solution.py:392
  123.0 5.5 %fusion.8.qkv_ref = f32[512,1152]{1,0:T(8,128)S(1)} fusion(bf16[1536,1536]{1,0:T(8,128)(2,1)} %all-gather.3.cloned.1.call-done, bf16[512,1536]{1,0:T(8,128)(2,1)} %copy-done.31, f32[1536]{0:T(1024)S(1)} %get-tuple-element.200, f32[1536]{0:T(1024)S(1)} %copy-done.74, f32[512]{0:T(512)S(1)} %add_rsqrt_fusion), kind=kOutput, calls=%fused_computation.16 | convolution fusion | flops 1815871488 | bytes 7485440 | tf_op jit(solution)/shard_map/dot_general | solution.py:28
  129.9 16.0 %attention_forward.1 = (bf16[512,384]{1,0:T(8,128)(2,1)S(1)}, bf16[512,384]{1,0:T(8,128)(2,1)S(1)}, bf16[512,384]{1,0:T(8,128)(2,1)S(1)}, bf16[512,384]{1,0:T(8,...) custom-call(f32[512,1152]{1,0:T(8,128)S(1)} %fusion.8.qkv_ref, bf16[256,768]{1,0:T(8,128)(2,1)S(1)} %copy-done.19, ...), custom_call_target="tpu_custom_call" | custom-call | flops 603979776 | bytes 6291456 | tf_op jit(solution)/shard_map/attention_forward/pallas_call | solution.py:88
  145.9 3.0 fusion.71
  156.0 5.3 %collective-permute-done.16 = bf16[128,1536]{1,0:T(8,128)(2,1)S(1)} collective-permute-done((bf16[128,1536]{1,0:T(8,128)(2,1)S(1)}, bf16[128,1536]{1,0:T(8,128)(2,1)S(1)}, u32[]{:S(2)}, u32[]{:S(2)}) %collective-permute-start.16) | collective-permute-done | bytes 393248 | tf_op jit(solution)/shard_map/ppermute | solution.py:412
  162.2 4.2 collective-permute-done.18
  170.5 1.7 multiply_convert_fusion.back_ref
  172.1 5.2 %collective-permute-done.19 = bf16[128,1536]{1,0:T(8,128)(2,1)S(1)} collective-permute-done((bf16[128,1536]{1,0:T(8,128)(2,1)S(1)}, bf16[128,1536]{1,0:T(8,128)(2,1)S(1)}, u32[]{:S(2)}, u32[]{:S(2)}) %collective-permute-start.19) | collective-permute-done | bytes 393248 | tf_op jit(solution)/shard_map/ppermute | solution.py:392
  180.2 2.9 collective-permute-done.21
  183.1 1.7 collective-permute-done.22
  184.8 20.4 %all-gather.5.cloned.1.call-done.gate_ref.up_ref.down_ref = bf16[1536,3072]{1,0:T(8,128)(2,1)} async-done(((bf16[192,3072]{1,0:T(8,128)(2,1)}), bf16[1536,3072]{1,0:T(8,128)(2,1)}) %all-gather.5.cloned.1.call-update) | async-done | bytes 9437200 | tf_op jit(solution)/shard_map/all_gather | solution.py:482
  205.2 7.4 %ffn_forward.1 = (bf16[512,1024]{1,0:T(8,128)(2,1)S(1)}, f32[512,1024]{1,0:T(8,128)S(1)}, f32[512,1024]{1,0:T(8,128)}) custom-call(bf16[512,1536]{1,0:T(8,128)(2,1)S(1)} %constant_dynamic-update-slice_fusion.5.in_ref, bf16[1536,3072]{1,0:T(8,128)(2,1)} %all-gather.5.cloned.1.call-done.gate_ref.up_ref.down_ref, ...), custom_call_target="tpu_custom_call" | custom-call | flops 3221225472 | bytes 13107200 | tf_op jit(solution)/shard_map/ffn_forward/pallas_call | solution.py:252
  215.0 3.5 convolution_convert_fusion.2
  218.6 11.4 %ffn_backward.1 = (bf16[512,2048]{1,0:T(8,128)(2,1)S(1)}, bf16[512,1536]{1,0:T(8,128)(2,1)S(1)}) custom-call(bf16[512,1536]{1,0:T(8,128)(2,1)S(1)} %multiply_convert_fusion.back_ref, bf16[1536,3072]{1,0:T(8,128)(2,1)} %all-gather.5.cloned.1.call-done.gate_ref.up_ref.down_ref, bf16[1536,3072]{1,0:T(8,128)(2,1)} %all-gather.5.cloned.1.call-done.gate_ref.up_ref.down_ref, ...), custom_call_target="tpu_custom_call" | custom-call | flops 4831838208 | bytes 20447232 | tf_op jit(solution)/shard_map/ffn_backward/pallas_call | solution.py:298
  235.7 5.4 %convolution_convert_fusion = bf16[1536,2048]{1,0:T(8,128)(2,1)} fusion(bf16[512,1536]{1,0:T(8,128)(2,1)S(1)} %constant_dynamic-update-slice_fusion.5.in_ref, bf16[512,2048]{1,0:T(8,128)(2,1)S(1)} %get-tuple-element.107), kind=kOutput, calls=%fused_computation | convolution fusion | flops 3224371200 | bytes 9961472 | tf_op jit(solution)/shard_map/dot_general | solution.py:36
  241.1 3.4 collective-permute-done.27
  244.5 9.0 %collective-permute-done.28 = bf16[128,1536]{1,0:T(8,128)(2,1)} collective-permute-done((bf16[128,1536]{1,0:T(8,128)(2,1)}, bf16[128,1536]{1,0:T(8,128)(2,1)}, u32[]{:S(2)}, u32[]{:S(2)}) %collective-permute-start.28) | collective-permute-done | bytes 393248 | tf_op jit(solution)/shard_map/ppermute | solution.py:412
  253.5 2.5 multiply_reduce_fusion
  260.8 7.5 %collective-permute-done.30 = bf16[128,1536]{1,0:T(8,128)(2,1)S(1)} collective-permute-done((bf16[128,1536]{1,0:T(8,128)(2,1)S(1)}, bf16[128,1536]{1,0:T(8,128)(2,1)S(1)}, u32[]{:S(2)}, u32[]{:S(2)}) %collective-permute-start.30) | collective-permute-done | bytes 393248 | tf_op jit(solution)/shard_map/ppermute | solution.py:392
  274.0 2.4 collective-permute-done.33
  277.6 2.4 convolution_convert_fusion.5.grad_ref
  280.0 5.6 %cross_backward.1 = (bf16[256,768]{1,0:T(8,128)(2,1)S(1)}, f32[512,384]{1,0:T(8,128)S(1)}, f32[8,384]{1,0:T(8,128)S(1)}) custom-call(bf16[512,384]{1,0:T(8,128)(2,1)S(1)} %get-tuple-element.114.q_ref, bf16[256,768]{1,0:T(8,128)(2,1)S(1)} %copy-done.20, bf16[512,384]{1,0:T(8,128)(2,1)S(1)} %convolution_convert_fusion.5.grad_ref, f32[512,128]{1,0:T(8,128)S(1)} %copy-done.10, ...), custom_call_target="tpu_custom_call" | custom-call | flops 503316480 | bytes 4718592 | tf_op jit(solution)/shard_map/cross_backward/pallas_call | solution.py:148
  285.7 5.5 %fusion.72 = (bf16[512,1536]{1,0:T(8,128)(2,1)S(1)}, f32[512,1536]{1,0:T(8,128)}) fusion(bf16[512,1024]{1,0:T(8,128)(2,1)S(1)} %copy-done.22, bf16[1536,3072]{1,0:T(8,128)(2,1)} %all-gather.5.cloned.1.call-done.gate_ref.up_ref.down_ref), kind=kOutput, calls=%fused_computation.202 | convolution fusion | flops 1611399168 | bytes 8912896 | tf_op jit(solution)/shard_map/dot_general | solution.py:32
  291.3 2.9 collective-permute-start.35
  294.3 1.8 collective-permute-start.36
  299.0 16.7 %self_backward.1 = (bf16[512,1152]{1,0:T(8,128)(2,1)S(1)}, f32[8,128]{1,0:T(8,128)S(1)}) custom-call(f32[512,1152]{1,0:T(8,128)} %copy-done.2, bf16[512,384]{1,0:T(8,128)(2,1)S(1)} %get-tuple-element.114.q_ref, bf16[512,384]{1,0:T(8,128)(2,1)S(1)} %copy-done.14, bf16[512,384]{1,0:T(8,128)(2,1)S(1)} %copy-done.16, ...), custom_call_target="tpu_custom_call" | custom-call | flops 1006632960 | bytes 7864320 | tf_op jit(solution)/shard_map/self_backward/pallas_call | solution.py:217
  315.8 4.6 %collective-permute-done.35 = bf16[512,768]{1,0:T(8,128)(2,1)S(1)} collective-permute-done((bf16[512,768]{1,0:T(8,128)(2,1)S(1)}, bf16[512,768]{1,0:T(8,128)(2,1)S(1)}, u32[]{:S(2)}, u32[]{:S(2)}) %collective-permute-start.35) | collective-permute-done | bytes 786464 | tf_op jit(solution)/shard_map/ppermute | solution.py:375
  320.5 1.7 collective-permute-start.39
  322.2 1.7 collective-permute-start.40
  323.9 3.9 fusion.73
  327.9 2.4 convolution_convert_fusion.1
  333.7 2.6 pad_maximum_fusion
  336.3 4.4 %collective-permute-done.42 = bf16[128,1536]{1,0:T(8,128)(2,1)S(1)} collective-permute-done((bf16[128,1536]{1,0:T(8,128)(2,1)S(1)}, bf16[128,1536]{1,0:T(8,128)(2,1)S(1)}, u32[]{:S(2)}, u32[]{:S(2)}) %collective-permute-start.42) | collective-permute-done | bytes 393248 | tf_op jit(solution)/shard_map/ppermute | solution.py:412
  341.4 14.7 %collective-permute-start.45 = (bf16[512,768]{1,0:T(8,128)(2,1)}, bf16[512,768]{1,0:T(8,128)(2,1)}, u32[]{:S(2)}, u32[]{:S(2)}) collective-permute-start(bf16[512,768]{1,0:T(8,128)(2,1)} %collective-permute-done.41), channel_id=1, source_target_pairs={{0,4},{4,0},{8,12},{12,8},{16,20},{20,16},{24,28},{28,24},{1,5},{5... | collective-permute-start | bytes 2359304 | tf_op jit(solution)/shard_map/ppermute | solution.py:347
  358.6 1.9 broadcast_in_dim.96
  364.4 1.9 widen.3
  366.3 2.3 widen.4
  368.7 2.3 bitcast_dynamic-update-slice_fusion.2
  371.0 2.5 bitcast_dynamic-update-slice_fusion.1
  373.5 2.4 bitcast_dynamic-update-slice_fusion
  375.9 5.0 %fusion.74 = f32[512,768]{1,0:T(8,128)} fusion(bf16[2048,512]{1,0:T(8,128)(2,1)S(1)} %bitcast.80, bf16[2048,768]{1,0:T(8,128)(2,1)} %bitcast.25), kind=kOutput, calls=%fused_computation.204 | convolution fusion | flops 1610612736 | bytes 6815744 | tf_op jit(solution)/shard_map/dot_general | solution.py:36
  381.7 1.8 multiply_reduce_fusion.1
  383.7 3.5 select_reduce_fusion
  389.0 2.1 collective-permute-done.47
  392.7 2.0 concatenate.150
  396.2 2.2 collective-permute-done.52
  401.2 2.8 fusion.64
  404.1 2.9 collective-permute-start.51
  408.8 2.1 collective-permute-done.55
  413.5 2.0 collective-permute-done.56
  417.2 2.1 widen.5
  (410 shorter events, 98.5 us)
Async XLA Ops:
  7.2 115.8 %all-gather.3.cloned.1.call-start = ((), (), s32[]{:S(2)}) async-start(), calls=%async_computation.5 | async-start | bytes 5308416 | tf_op jit(solution)/shard_map/all_gather | solution.py:482
  9.4 119.2 %reduce-scatter.5.cloned.1.call-start = ((), (), s32[]{:S(2)}) async-start(), calls=%async_computation.6 | async-start | bytes 3538944 | tf_op jit(solution)/shard_map/reduce_scatter | solution.py:359
  41.4 11.3 %collective-permute-start.12 = (bf16[8,1,64,512]{3,2,1,0:T(8,128)(2,1)S(1)}, bf16[8,1,64,512]{3,2,1,0:T(8,128)(2,1)S(1)}, u32[]{:S(2)}, u32[]{:S(2)}) collective-permute-start(bf16[8,1,64,512]{3,2,1,0:T(8,128)(2,1)S(1)} %bitcast.83), channel_id=1, source_target_pairs={{0,1},{1,0},{2,3},{3,2},{4,5},{5,4},{6,7},{7,6},{8,9},{9,8},{10,11... | collective-permute-start | bytes 1572872 | tf_op jit(solution)/shard_map/ppermute | solution.py:392
  42.9 12.8 %collective-permute-start.13 = (bf16[8,1,64,512]{3,2,1,0:T(8,128)(2,1)S(1)}, bf16[8,1,64,512]{3,2,1,0:T(8,128)(2,1)S(1)}, u32[]{:S(2)}, u32[]{:S(2)}) collective-permute-start(bf16[8,1,64,512]{3,2,1,0:T(8,128)(2,1)S(1)} %bitcast.84), channel_id=1, source_target_pairs={{0,2},{1,3},{2,0},{3,1},{4,6},{5,7},{6,4},{7,5},{8,10},{9,11},{10,... | collective-permute-start | bytes 1572872 | tf_op jit(solution)/shard_map/ppermute | solution.py:392
  52.7 6.8 %collective-permute-start.14 = (bf16[8,1,32,512]{3,2,1,0:T(8,128)(2,1)S(1)}, bf16[8,1,32,512]{3,2,1,0:T(8,128)(2,1)S(1)}, u32[]{:S(2)}, u32[]{:S(2)}) collective-permute-start(bf16[8,1,32,512]{3,2,1,0:T(8,128)(2,1)S(1)} %slice.332), channel_id=1, source_target_pairs={{0,2},{1,3},{2,0},{3,1},{4,6},{5,7},{6,4},{7,5},{8,10},{9,11},{10,... | collective-permute-start | bytes 786440 | tf_op jit(solution)/shard_map/ppermute | solution.py:397
  55.7 6.4 %collective-permute-start.15 = (bf16[8,1,32,512]{3,2,1,0:T(8,128)(2,1)S(1)}, bf16[8,1,32,512]{3,2,1,0:T(8,128)(2,1)S(1)}, u32[]{:S(2)}, u32[]{:S(2)}) collective-permute-start(bf16[8,1,32,512]{3,2,1,0:T(8,128)(2,1)S(1)} %slice.333), channel_id=1, source_target_pairs={{0,1},{1,0},{2,3},{3,2},{4,5},{5,4},{6,7},{7,6},{8,9},{9,8},{10,11... | collective-permute-start | bytes 786440 | tf_op jit(solution)/shard_map/ppermute | solution.py:398
  67.4 137.8 %all-gather.5.cloned.1.call-start = ((), (), s32[]{:S(2)}) async-start(), calls=%async_computation.7 | async-start | bytes 10616832 | tf_op jit(solution)/shard_map/all_gather | solution.py:482
  69.7 187.8 %reduce-scatter.7.cloned.1.call-start = ((), (), s32[]{:S(2)}) async-start(), calls=%async_computation.8 | async-start | bytes 3538944 | tf_op jit(solution)/shard_map/reduce_scatter | solution.py:359
  69.8 9.3 %collective-permute-start.8 = (bf16[128,1536]{1,0:T(8,128)(2,1)S(1)}, bf16[128,1536]{1,0:T(8,128)(2,1)S(1)}, u32[]{:S(2)}, u32[]{:S(2)}) collective-permute-start(bf16[128,1536]{1,0:T(8,128)(2,1)S(1)} %copy-done.25), channel_id=1, source_target_pairs={{0,1},{1,0},{2,3},{3,2},{4,5},{5,4},{6,7},{7,6},{8,9},{9,8},{10,11... | collective-permute-start | bytes 1179656 | tf_op jit(solution)/shard_map/ppermute | solution.py:392
  70.2 10.6 %collective-permute-start.9 = (bf16[128,1536]{1,0:T(8,128)(2,1)S(1)}, bf16[128,1536]{1,0:T(8,128)(2,1)S(1)}, u32[]{:S(2)}, u32[]{:S(2)}) collective-permute-start(bf16[128,1536]{1,0:T(8,128)(2,1)S(1)} %copy-done.25), channel_id=1, source_target_pairs={{0,2},{1,3},{2,0},{3,1},{4,6},{5,7},{6,4},{7,5},{8,10},{9,11},{10,... | collective-permute-start | bytes 1179656 | tf_op jit(solution)/shard_map/ppermute | solution.py:392
  74.1 54.5 %copy-start.7 = (f32[512,64]{1,0:T(8,128)}, f32[512,64]{1,0:T(8,128)S(1)}, u32[]{:S(2)}) copy-start(f32[512,64]{1,0:T(8,128)S(1)} %pad_maximum_fusion.4.cos_ref) | copy-start | bytes 393220
  74.4 1.2 collective-permute-start
  75.6 5.7 %collective-permute-start.1 = (bf16[2,1024]{1,0:T(2,128)(2,1)S(1)}, bf16[2,1024]{1,0:T(2,128)(2,1)S(1)}, u32[]{:S(2)}, u32[]{:S(2)}) collective-permute-start(bf16[2,1024]{1,0:T(2,128)(2,1)S(1)} %pad_maximum_fusion.13), channel_id=1, source_target_pairs={{0,8},{4,12},{8,0},{12,4},{16,24},{20,28},{24,16},{28,20},{1,9},{5... | collective-permute-start | bytes 12296 | tf_op jit(solution)/shard_map/ppermute | solution.py:350
  79.2 16.0 %collective-permute-start.10 = (bf16[64,1536]{1,0:T(8,128)(2,1)S(1)}, bf16[64,1536]{1,0:T(8,128)(2,1)S(1)}, u32[]{:S(2)}, u32[]{:S(2)}) collective-permute-start(bf16[64,1536]{1,0:T(8,128)(2,1)S(1)} %slice.328), channel_id=1, source_target_pairs={{0,2},{1,3},{2,0},{3,1},{4,6},{5,7},{6,4},{7,5},{8,10},{9,11},{10,... | collective-permute-start | bytes 589832 | tf_op jit(solution)/shard_map/ppermute | solution.py:397
  80.8 18.6 %collective-permute-start.11 = (bf16[64,1536]{1,0:T(8,128)(2,1)S(1)}, bf16[64,1536]{1,0:T(8,128)(2,1)S(1)}, u32[]{:S(2)}, u32[]{:S(2)}) collective-permute-start(bf16[64,1536]{1,0:T(8,128)(2,1)S(1)} %slice.329), channel_id=1, source_target_pairs={{0,1},{1,0},{2,3},{3,2},{4,5},{5,4},{6,7},{7,6},{8,9},{9,8},{10,11... | collective-permute-start | bytes 589832 | tf_op jit(solution)/shard_map/ppermute | solution.py:398
  81.4 7.4 %collective-permute-start.2 = (bf16[4,1024]{1,0:T(4,128)(2,1)S(1)}, bf16[4,1024]{1,0:T(4,128)(2,1)S(1)}, u32[]{:S(2)}, u32[]{:S(2)}) collective-permute-start(bf16[4,1024]{1,0:T(4,128)(2,1)S(1)} %pad_maximum_fusion.11), channel_id=1, source_target_pairs={{0,16},{4,20},{8,24},{12,28},{16,0},{20,4},{24,8},{28,12},{1,17},{... | collective-permute-start | bytes 24584 | tf_op jit(solution)/shard_map/ppermute | solution.py:350
  89.0 6.0 %collective-permute-start.3 = (f32[4,1536]{1,0:T(4,128)S(1)}, f32[4,1536]{1,0:T(4,128)S(1)}, u32[]{:S(2)}, u32[]{:S(2)}) collective-permute-start(f32[4,1536]{1,0:T(4,128)S(1)} %slice.318), channel_id=1, source_target_pairs={{0,16},{4,20},{8,24},{12,28},{16,0},{20,4},{24,8},{28,12},{1,17},{... | collective-permute-start | bytes 73736 | tf_op jit(solution)/shard_map/ppermute | solution.py:350
  95.0 4.2 collective-permute-start.4
  99.3 1.2 collective-permute-start.5
  100.5 3.7 collective-permute-start.6
  104.2 3.8 collective-permute-start.7
  108.2 9.7 %collective-permute-start.23 = (bf16[128,1536]{1,0:T(8,128)(2,1)S(1)}, bf16[128,1536]{1,0:T(8,128)(2,1)S(1)}, u32[]{:S(2)}, u32[]{:S(2)}) collective-permute-start(bf16[128,1536]{1,0:T(8,128)(2,1)S(1)} %copy-done.28), channel_id=1, source_target_pairs={{0,1},{1,0},{2,3},{3,2},{4,5},{5,4},{6,7},{7,6},{8,9},{9,8},{10,11... | collective-permute-start | bytes 1179656 | tf_op jit(solution)/shard_map/ppermute | solution.py:392
  109.7 10.0 %collective-permute-start.24 = (bf16[128,1536]{1,0:T(8,128)(2,1)S(1)}, bf16[128,1536]{1,0:T(8,128)(2,1)S(1)}, u32[]{:S(2)}, u32[]{:S(2)}) collective-permute-start(bf16[128,1536]{1,0:T(8,128)(2,1)S(1)} %copy-done.28), channel_id=1, source_target_pairs={{0,2},{1,3},{2,0},{3,1},{4,6},{5,7},{6,4},{7,5},{8,10},{9,11},{10,... | collective-permute-start | bytes 1179656 | tf_op jit(solution)/shard_map/ppermute | solution.py:392
  118.7 34.1 %collective-permute-start.25 = (bf16[64,1536]{1,0:T(8,128)(2,1)}, bf16[64,1536]{1,0:T(8,128)(2,1)}, u32[]{:S(2)}, u32[]{:S(2)}) collective-permute-start(bf16[64,1536]{1,0:T(8,128)(2,1)} %slice.343), channel_id=1, source_target_pairs={{0,2},{1,3},{2,0},{3,1},{4,6},{5,7},{6,4},{7,5},{8,10},{9,11},{10,... | collective-permute-start | bytes 589832 | tf_op jit(solution)/shard_map/ppermute | solution.py:397
  120.4 34.0 %collective-permute-start.26 = (bf16[64,1536]{1,0:T(8,128)(2,1)}, bf16[64,1536]{1,0:T(8,128)(2,1)}, u32[]{:S(2)}, u32[]{:S(2)}) collective-permute-start(bf16[64,1536]{1,0:T(8,128)(2,1)} %slice.344), channel_id=1, source_target_pairs={{0,1},{1,0},{2,3},{3,2},{4,5},{5,4},{6,7},{7,6},{8,9},{9,8},{10,11... | collective-permute-start | bytes 589832 | tf_op jit(solution)/shard_map/ppermute | solution.py:398
  149.2 12.1 %collective-permute-start.16 = (bf16[128,1536]{1,0:T(8,128)(2,1)S(1)}, bf16[128,1536]{1,0:T(8,128)(2,1)S(1)}, u32[]{:S(2)}, u32[]{:S(2)}) collective-permute-start(bf16[128,1536]{1,0:T(8,128)(2,1)S(1)} %get-tuple-element.188), channel_id=1, source_target_pairs={{0,1},{1,0},{2,3},{3,2},{4,5},{5,4},{6,7},{7,6},{8,9},{9,8},{10,11... | collective-permute-start | bytes 1179656 | tf_op jit(solution)/shard_map/ppermute | solution.py:412
  150.3 11.9 %collective-permute-start.17 = (bf16[128,1536]{1,0:T(8,128)(2,1)S(1)}, bf16[128,1536]{1,0:T(8,128)(2,1)S(1)}, u32[]{:S(2)}, u32[]{:S(2)}) collective-permute-start(bf16[128,1536]{1,0:T(8,128)(2,1)S(1)} %get-tuple-element.190), channel_id=1, source_target_pairs={{0,2},{1,3},{2,0},{3,1},{4,6},{5,7},{6,4},{7,5},{8,10},{9,11},{10,... | collective-permute-start | bytes 1179656 | tf_op jit(solution)/shard_map/ppermute | solution.py:412
  151.1 15.3 %collective-permute-start.18 = (bf16[128,1536]{1,0:T(8,128)(2,1)S(1)}, bf16[128,1536]{1,0:T(8,128)(2,1)S(1)}, u32[]{:S(2)}, u32[]{:S(2)}) collective-permute-start(bf16[128,1536]{1,0:T(8,128)(2,1)S(1)} %get-tuple-element.189), channel_id=1, source_target_pairs={{0,3},{1,2},{2,1},{3,0},{4,7},{5,6},{6,5},{7,4},{8,11},{9,10},{10,... | collective-permute-start | bytes 1179656 | tf_op jit(solution)/shard_map/ppermute | solution.py:412
  168.2 9.2 %collective-permute-start.19 = (bf16[128,1536]{1,0:T(8,128)(2,1)S(1)}, bf16[128,1536]{1,0:T(8,128)(2,1)S(1)}, u32[]{:S(2)}, u32[]{:S(2)}) collective-permute-start(bf16[128,1536]{1,0:T(8,128)(2,1)S(1)} %get-tuple-element.173), channel_id=1, source_target_pairs={{0,1},{1,0},{2,3},{3,2},{4,5},{5,4},{6,7},{7,6},{8,9},{9,8},{10,11... | collective-permute-start | bytes 1179656 | tf_op jit(solution)/shard_map/ppermute | solution.py:392
  169.2 9.9 %collective-permute-start.20 = (bf16[128,1536]{1,0:T(8,128)(2,1)S(1)}, bf16[128,1536]{1,0:T(8,128)(2,1)S(1)}, u32[]{:S(2)}, u32[]{:S(2)}) collective-permute-start(bf16[128,1536]{1,0:T(8,128)(2,1)S(1)} %get-tuple-element.173), channel_id=1, source_target_pairs={{0,2},{1,3},{2,0},{3,1},{4,6},{5,7},{6,4},{7,5},{8,10},{9,11},{10,... | collective-permute-start | bytes 1179656 | tf_op jit(solution)/shard_map/ppermute | solution.py:392
  177.4 5.7 %collective-permute-start.21 = (bf16[64,1536]{1,0:T(8,128)(2,1)S(1)}, bf16[64,1536]{1,0:T(8,128)(2,1)S(1)}, u32[]{:S(2)}, u32[]{:S(2)}) collective-permute-start(bf16[64,1536]{1,0:T(8,128)(2,1)S(1)} %slice.341), channel_id=1, source_target_pairs={{0,2},{1,3},{2,0},{3,1},{4,6},{5,7},{6,4},{7,5},{8,10},{9,11},{10,... | collective-permute-start | bytes 589832 | tf_op jit(solution)/shard_map/ppermute | solution.py:397
  179.1 5.7 %collective-permute-start.22 = (bf16[64,1536]{1,0:T(8,128)(2,1)S(1)}, bf16[64,1536]{1,0:T(8,128)(2,1)S(1)}, u32[]{:S(2)}, u32[]{:S(2)}) collective-permute-start(bf16[64,1536]{1,0:T(8,128)(2,1)S(1)} %slice.342), channel_id=1, source_target_pairs={{0,1},{1,0},{2,3},{3,2},{4,5},{5,4},{6,7},{7,6},{8,9},{9,8},{10,11... | collective-permute-start | bytes 589832 | tf_op jit(solution)/shard_map/ppermute | solution.py:398
  218.5 122.1 %reduce-scatter.9.cloned.1.call-start = ((), (), s32[]{:S(2)}) async-start(), calls=%async_computation.9 | async-start | bytes 7077888 | tf_op jit(solution)/shard_map/reduce_scatter | solution.py:359
  232.2 12.3 %collective-permute-start.27 = (bf16[128,1536]{1,0:T(8,128)(2,1)}, bf16[128,1536]{1,0:T(8,128)(2,1)}, u32[]{:S(2)}, u32[]{:S(2)}) collective-permute-start(bf16[128,1536]{1,0:T(8,128)(2,1)} %get-tuple-element.187), channel_id=1, source_target_pairs={{0,1},{1,0},{2,3},{3,2},{4,5},{5,4},{6,7},{7,6},{8,9},{9,8},{10,11... | collective-permute-start | bytes 1179656 | tf_op jit(solution)/shard_map/ppermute | solution.py:412
  233.7 19.7 %collective-permute-start.28 = (bf16[128,1536]{1,0:T(8,128)(2,1)}, bf16[128,1536]{1,0:T(8,128)(2,1)}, u32[]{:S(2)}, u32[]{:S(2)}) collective-permute-start(bf16[128,1536]{1,0:T(8,128)(2,1)} %get-tuple-element.186), channel_id=1, source_target_pairs={{0,2},{1,3},{2,0},{3,1},{4,6},{5,7},{6,4},{7,5},{8,10},{9,11},{10,... | collective-permute-start | bytes 1179656 | tf_op jit(solution)/shard_map/ppermute | solution.py:412
  235.2 18.3 %collective-permute-start.29 = (bf16[128,1536]{1,0:T(8,128)(2,1)}, bf16[128,1536]{1,0:T(8,128)(2,1)}, u32[]{:S(2)}, u32[]{:S(2)}) collective-permute-start(bf16[128,1536]{1,0:T(8,128)(2,1)} %get-tuple-element.185), channel_id=1, source_target_pairs={{0,3},{1,2},{2,1},{3,0},{4,7},{5,6},{6,5},{7,4},{8,11},{9,10},{10,... | collective-permute-start | bytes 1179656 | tf_op jit(solution)/shard_map/ppermute | solution.py:412
  257.5 159.7 %reduce-scatter.11.cloned.1.call-start = ((), (), s32[]{:S(2)}) async-start(), calls=%async_computation.10 | async-start | bytes 5308416 | tf_op jit(solution)/shard_map/reduce_scatter | solution.py:359
  258.0 10.2 %collective-permute-start.30 = (bf16[128,1536]{1,0:T(8,128)(2,1)S(1)}, bf16[128,1536]{1,0:T(8,128)(2,1)S(1)}, u32[]{:S(2)}, u32[]{:S(2)}) collective-permute-start(bf16[128,1536]{1,0:T(8,128)(2,1)S(1)} %copy-done.35), channel_id=1, source_target_pairs={{0,1},{1,0},{2,3},{3,2},{4,5},{5,4},{6,7},{7,6},{8,9},{9,8},{10,11... | collective-permute-start | bytes 1179656 | tf_op jit(solution)/shard_map/ppermute | solution.py:392
  259.3 10.5 %collective-permute-start.31 = (bf16[128,1536]{1,0:T(8,128)(2,1)S(1)}, bf16[128,1536]{1,0:T(8,128)(2,1)}, u32[]{:S(2)}, u32[]{:S(2)}) collective-permute-start(bf16[128,1536]{1,0:T(8,128)(2,1)S(1)} %copy-done.35), channel_id=1, source_target_pairs={{0,2},{1,3},{2,0},{3,1},{4,6},{5,7},{6,4},{7,5},{8,10},{9,11},{10,... | collective-permute-start | bytes 1179656 | tf_op jit(solution)/shard_map/ppermute | solution.py:392
  268.2 5.7 %collective-permute-start.32 = (bf16[64,1536]{1,0:T(8,128)(2,1)S(1)}, bf16[64,1536]{1,0:T(8,128)(2,1)S(1)}, u32[]{:S(2)}, u32[]{:S(2)}) collective-permute-start(bf16[64,1536]{1,0:T(8,128)(2,1)S(1)} %slice.345), channel_id=1, source_target_pairs={{0,2},{1,3},{2,0},{3,1},{4,6},{5,7},{6,4},{7,5},{8,10},{9,11},{10,... | collective-permute-start | bytes 589832 | tf_op jit(solution)/shard_map/ppermute | solution.py:397
  270.7 5.7 %collective-permute-start.33 = (bf16[64,1536]{1,0:T(8,128)(2,1)S(1)}, bf16[64,1536]{1,0:T(8,128)(2,1)S(1)}, u32[]{:S(2)}, u32[]{:S(2)}) collective-permute-start(bf16[64,1536]{1,0:T(8,128)(2,1)S(1)} %slice.346), channel_id=1, source_target_pairs={{0,1},{1,0},{2,3},{3,2},{4,5},{5,4},{6,7},{7,6},{8,9},{9,8},{10,11... | collective-permute-start | bytes 589832 | tf_op jit(solution)/shard_map/ppermute | solution.py:398
  285.6 5.6 %collective-permute-start.34 = (bf16[256,768]{1,0:T(8,128)(2,1)S(1)}, bf16[256,768]{1,0:T(8,128)(2,1)S(1)}, u32[]{:S(2)}, u32[]{:S(2)}) collective-permute-start(bf16[256,768]{1,0:T(8,128)(2,1)S(1)} %get-tuple-element.120), channel_id=1, source_target_pairs={{0,4},{4,0},{8,12},{12,8},{16,20},{20,16},{24,28},{28,24},{1,5},{5... | collective-permute-start | bytes 1179656 | tf_op jit(solution)/shard_map/ppermute | solution.py:347
  291.3 29.2 %collective-permute-start.35 = (bf16[512,768]{1,0:T(8,128)(2,1)S(1)}, bf16[512,768]{1,0:T(8,128)(2,1)S(1)}, u32[]{:S(2)}, u32[]{:S(2)}) collective-permute-start(bf16[512,768]{1,0:T(8,128)(2,1)S(1)} %pad_maximum_fusion.2), channel_id=1, source_target_pairs={{0,8},{8,16},{16,24},{12,4},{20,12},{28,20},{1,9},{9,17},{17,25},{... | collective-permute-start | bytes 2359304 | tf_op jit(solution)/shard_map/ppermute | solution.py:375
  294.3 21.4 %collective-permute-start.36 = (bf16[128,1536]{1,0:T(8,128)(2,1)S(1)}, bf16[128,1536]{1,0:T(8,128)(2,1)S(1)}, u32[]{:S(2)}, u32[]{:S(2)}) collective-permute-start(bf16[128,1536]{1,0:T(8,128)(2,1)S(1)} %get-tuple-element.184), channel_id=1, source_target_pairs={{0,1},{1,0},{2,3},{3,2},{4,5},{5,4},{6,7},{7,6},{8,9},{9,8},{10,11... | collective-permute-start | bytes 1179656 | tf_op jit(solution)/shard_map/ppermute | solution.py:412
  296.1 19.7 %collective-permute-start.37 = (bf16[128,1536]{1,0:T(8,128)(2,1)S(1)}, bf16[128,1536]{1,0:T(8,128)(2,1)S(1)}, u32[]{:S(2)}, u32[]{:S(2)}) collective-permute-start(bf16[128,1536]{1,0:T(8,128)(2,1)S(1)} %get-tuple-element.183), channel_id=1, source_target_pairs={{0,2},{1,3},{2,0},{3,1},{4,6},{5,7},{6,4},{7,5},{8,10},{9,11},{10,... | collective-permute-start | bytes 1179656 | tf_op jit(solution)/shard_map/ppermute | solution.py:412
  296.4 19.4 %collective-permute-start.38 = (bf16[128,1536]{1,0:T(8,128)(2,1)S(1)}, bf16[128,1536]{1,0:T(8,128)(2,1)S(1)}, u32[]{:S(2)}, u32[]{:S(2)}) collective-permute-start(bf16[128,1536]{1,0:T(8,128)(2,1)S(1)} %get-tuple-element.182), channel_id=1, source_target_pairs={{0,3},{1,2},{2,1},{3,0},{4,7},{5,6},{6,5},{7,4},{8,11},{9,10},{10,... | collective-permute-start | bytes 1179656 | tf_op jit(solution)/shard_map/ppermute | solution.py:412
  320.5 9.7 %collective-permute-start.39 = (bf16[512,768]{1,0:T(8,128)(2,1)S(1)}, bf16[512,768]{1,0:T(8,128)(2,1)}, u32[]{:S(2)}, u32[]{:S(2)}) collective-permute-start(bf16[512,768]{1,0:T(8,128)(2,1)S(1)} %collective-permute-done.35), channel_id=1, source_target_pairs={{8,16},{16,24},{12,4},{20,12},{9,17},{17,25},{13,5},{21,13},{10,18... | collective-permute-start | bytes 2359304 | tf_op jit(solution)/shard_map/ppermute | solution.py:375
  322.2 8.1 %collective-permute-start.40 = (bf16[512,768]{1,0:T(8,128)(2,1)S(1)}, bf16[512,768]{1,0:T(8,128)(2,1)S(1)}, u32[]{:S(2)}, u32[]{:S(2)}) collective-permute-start(bf16[512,768]{1,0:T(8,128)(2,1)S(1)} %collective-permute-done.35), channel_id=1, source_target_pairs={{0,4},{4,0},{8,12},{12,8},{16,20},{20,16},{24,28},{28,24},{1,5},{5... | collective-permute-start | bytes 2359304 | tf_op jit(solution)/shard_map/ppermute | solution.py:347
  330.3 10.3 %collective-permute-start.41 = (bf16[512,768]{1,0:T(8,128)(2,1)}, bf16[512,768]{1,0:T(8,128)(2,1)}, u32[]{:S(2)}, u32[]{:S(2)}) collective-permute-start(bf16[512,768]{1,0:T(8,128)(2,1)} %collective-permute-done.39), channel_id=1, source_target_pairs={{16,24},{12,4},{17,25},{13,5},{18,26},{14,6},{19,27},{15,7}} | collective-permute-start | bytes 2359304 | tf_op jit(solution)/shard_map/ppermute | solution.py:375
  332.8 7.8 %collective-permute-start.42 = (bf16[128,1536]{1,0:T(8,128)(2,1)S(1)}, bf16[128,1536]{1,0:T(8,128)(2,1)S(1)}, u32[]{:S(2)}, u32[]{:S(2)}) collective-permute-start(bf16[128,1536]{1,0:T(8,128)(2,1)S(1)} %get-tuple-element.181), channel_id=1, source_target_pairs={{0,1},{1,0},{2,3},{3,2},{4,5},{5,4},{6,7},{7,6},{8,9},{9,8},{10,11... | collective-permute-start | bytes 1179656 | tf_op jit(solution)/shard_map/ppermute | solution.py:412
  341.4 27.3 %collective-permute-start.45 = (bf16[512,768]{1,0:T(8,128)(2,1)}, bf16[512,768]{1,0:T(8,128)(2,1)}, u32[]{:S(2)}, u32[]{:S(2)}) collective-permute-start(bf16[512,768]{1,0:T(8,128)(2,1)} %collective-permute-done.41), channel_id=1, source_target_pairs={{0,4},{4,0},{8,12},{12,8},{16,20},{20,16},{24,28},{28,24},{1,5},{5... | collective-permute-start | bytes 2359304 | tf_op jit(solution)/shard_map/ppermute | solution.py:347
  356.1 14.9 %collective-permute-start.46 = (bf16[512,768]{1,0:T(8,128)(2,1)}, bf16[512,768]{1,0:T(8,128)(2,1)}, u32[]{:S(2)}, u32[]{:S(2)}) collective-permute-start(bf16[512,768]{1,0:T(8,128)(2,1)} %collective-permute-done.39), channel_id=1, source_target_pairs={{0,4},{4,0},{8,12},{12,8},{16,20},{20,16},{24,28},{28,24},{1,5},{5... | collective-permute-start | bytes 2359304 | tf_op jit(solution)/shard_map/ppermute | solution.py:347
  361.5 20.1 %collective-permute-start.43 = (bf16[128,1536]{1,0:T(8,128)(2,1)}, bf16[128,1536]{1,0:T(8,128)(2,1)S(1)}, u32[]{:S(2)}, u32[]{:S(2)}) collective-permute-start(bf16[128,1536]{1,0:T(8,128)(2,1)} %get-tuple-element.180), channel_id=1, source_target_pairs={{0,2},{1,3},{2,0},{3,1},{4,6},{5,7},{6,4},{7,5},{8,10},{9,11},{10,... | collective-permute-start | bytes 1179656 | tf_op jit(solution)/shard_map/ppermute | solution.py:412
  363.0 18.6 %collective-permute-start.44 = (bf16[128,1536]{1,0:T(8,128)(2,1)}, bf16[128,1536]{1,0:T(8,128)(2,1)S(1)}, u32[]{:S(2)}, u32[]{:S(2)}) collective-permute-start(bf16[128,1536]{1,0:T(8,128)(2,1)} %get-tuple-element.179), channel_id=1, source_target_pairs={{0,3},{1,2},{2,1},{3,0},{4,7},{5,6},{6,5},{7,4},{8,11},{9,10},{10,... | collective-permute-start | bytes 1179656 | tf_op jit(solution)/shard_map/ppermute | solution.py:412
  387.3 3.8 collective-permute-start.47
  391.1 4.1 collective-permute-start.48
  394.7 3.7 collective-permute-start.52
  395.3 4.6 %collective-permute-start.49 = (bf16[1,1536]{1,0:T(2,128)(2,1)S(1)}, bf16[1,1536]{1,0:T(2,128)(2,1)S(1)}, u32[]{:S(2)}, u32[]{:S(2)}) collective-permute-start(bf16[1,1536]{1,0:T(2,128)(2,1)S(1)} %fusion.44), channel_id=1, source_target_pairs={{0,4},{4,0},{8,12},{12,8},{16,20},{20,16},{24,28},{28,24},{1,5},{5... | collective-permute-start | bytes 9224 | tf_op jit(solution)/shard_map/ppermute | solution.py:350
  398.4 5.5 %collective-permute-start.53 = (f32[3227]{0:T(1024)S(1)}, f32[3227]{0:T(1024)S(1)}, u32[]{:S(2)}, u32[]{:S(2)}) collective-permute-start(f32[3227]{0:T(1024)S(1)} %add.397), channel_id=1, source_target_pairs={{0,2},{1,3},{2,0},{3,1},{4,6},{5,7},{6,4},{7,5},{8,10},{9,11},{10,... | collective-permute-start | bytes 38732 | tf_op jit(solution)/shard_map/ppermute | solution.py:436
  400.0 4.1 collective-permute-start.50
  404.0 3.0 collective-permute-start.54
  404.1 8.1 %collective-permute-start.51 = (bf16[4,1536]{1,0:T(4,128)(2,1)S(1)}, bf16[4,1536]{1,0:T(4,128)(2,1)S(1)}, u32[]{:S(2)}, u32[]{:S(2)}) collective-permute-start(bf16[4,1536]{1,0:T(4,128)(2,1)S(1)} %pad_maximum_fusion.10), channel_id=1, source_target_pairs={{0,16},{4,20},{8,24},{12,28},{16,0},{20,4},{24,8},{28,12},{1,17},{... | collective-permute-start | bytes 36872 | tf_op jit(solution)/shard_map/ppermute | solution.py:350
  407.0 3.9 collective-permute-start.55
  410.9 4.6 %collective-permute-start.56 = (f32[3224]{0:T(1024)S(1)}, f32[3224]{0:T(1024)S(1)}, u32[]{:S(2)}, u32[]{:S(2)}) collective-permute-start(f32[3224]{0:T(1024)S(1)} %add.400), channel_id=1, source_target_pairs={{0,16},{4,20},{8,24},{12,28},{16,0},{20,4},{24,8},{28,12},{1,17},{... | collective-permute-start | bytes 38696 | tf_op jit(solution)/shard_map/ppermute | solution.py:436
  (95 other events, 757.5 us)
Sparse Core Ops, SparseCore 0:
  10.3 60.8 all-gather.2
  73.5 40.2 reduce-scatter.4
  115.4 89.7 all-gather.4
  218.7 38.7 reduce-scatter.6
  259.6 77.3 reduce-scatter.8
  340.8 71.8 reduce-scatter.10
